TPU v7x, 256 devices: a whole 4x4x8 slice. The times are simulated.
256 devices in a mesh: grp: 32 (over z_lo, x, core), blk: 8 (over z_hi, y).
Axes of the slice: x: 4, y: 4, z: 8 (z_hi: 2, z_lo: 4; z = z_hi * 4 + z_lo), core: 2. Of those that a mesh axis runs over, the one named last changes fastest.
Arguments:
- features: float32 [65536, 128], P(('grp', 'blk')), may hold values from -6 to 6
- w_neigh: float32 [128, 128], replicated, may hold values from -2 to 2
- w_root: float32 [128, 128], replicated, may hold values from -0.5 to 0.5
- bias: float32 [128], replicated, may hold values from -3 to 3
- grad_out: float32 [65536, 128], P(('grp', 'blk')), may hold values from -6 to 6
- tile_coord: int32 [32, 8, 8, 2, 6], P('grp', 'blk'), may hold values from 0 to 1
- tile_edge: int32 [32, 8, 8, 6, 2, 128], P('grp', 'blk'), may hold values from 0 to 127
- send_idx: int32 [32, 8, 32, 32], P('grp', 'blk'), may hold values from 0 to 255
- halo_dst: int32 [32, 8, 1024], P('grp', 'blk'), may hold values from 0 to 255
- halo_src: int32 [32, 8, 1024], P('grp', 'blk'), may hold values from 0 to 1023, as said below
- hub_idx: int32 [32, 8, 8], P('grp', 'blk'), may hold values from 0 to 255
- hub_dst: int32 [32, 8, 256], P('grp', 'blk'), may hold values from 0 to 255
- hub_src: int32 [32, 8, 256], P('grp', 'blk'), may hold values from 0 to 2047
Outputs:
- output: float32 [65536, 128], P(('grp', 'blk'))
- grad_features: float32 [65536, 128], P(('grp', 'blk'))
- grad_w_neigh: float32 [128, 128], replicated
- grad_w_root: float32 [128, 128], replicated
- grad_bias: float32 [128], replicated
Inputs may be any that keep to these rules, and one draw needn't show every extreme that they name: `halo_src`: A value q names slot q % 32 of the rows that partition q // 32 sends to this device's partition at the same blk index, never the device's own partition; from each source partition the named slots lie below a count of that pair, and every device names slot 31 of some source partition.
All inputs are finite; a program needn't handle non-finite values.
Results may differ from a plain program's by a relative error of at most 0.0003.
Values sent between devices are 32-bit elements; how exact they have to be, the bound alone decides.
No kernel may reach another device: no remote copies, remote signals or barrier semaphores. Data moves between devices by JAX's collectives and lax.ppermute only.
A program may use at most 64 MiB of HBM per device.

v0:
```python
import jax
import jax.numpy as jnp
from jax import lax
from jax.sharding import PartitionSpec as P

precise = lax.Precision.HIGHEST


def tile_product(values, read_tile, read_local, write_tile, write_local, tile_count):
    row_index = read_tile[:, None] * 128 + read_local
    picked = jnp.take(values, row_index, axis=0)
    chosen = (write_local[:, :, None] == jnp.arange(128, dtype=jnp.int32)[None, None, :]).astype(
        jnp.float32
    )
    partial_sum = jnp.einsum("tel,tef->tlf", chosen, picked, precision=precise)
    placing = (write_tile[:, None] == jnp.arange(tile_count, dtype=jnp.int32)[None, :]).astype(
        jnp.float32
    )
    blocks = jnp.einsum("tr,tlf->rlf", placing, partial_sum, precision=precise)
    return blocks.reshape(tile_count * 128, values.shape[1])


def per_device(
    features,
    w_neigh,
    w_root,
    bias,
    grad_out,
    tile_coord,
    tile_edge,
    send_idx,
    halo_dst,
    halo_src,
    hub_idx,
    hub_dst,
    hub_src,
):
    rows_dev = features.shape[0]
    width = features.shape[1]
    tile_count = rows_dev // 128
    coords = tile_coord.reshape(tile_coord.shape[2:])
    edge_lists = tile_edge.reshape(tile_edge.shape[2:])
    send_rows = send_idx.reshape(send_idx.shape[2:])
    halo_to = halo_dst.reshape(-1)
    halo_from = halo_src.reshape(-1)
    hub_rows = hub_idx.reshape(-1)
    hub_to = hub_dst.reshape(-1)
    hub_from = hub_src.reshape(-1)
    empty = jnp.zeros((rows_dev, width), jnp.float32)
    running = empty
    piece = lax.all_gather(features, "blk", axis=0, tiled=True)
    start = jnp.int32(0)
    for position in range(piece.shape[0] // rows_dev):
        source = start // rows_dev + position
        coord_now = lax.dynamic_index_in_dim(coords, source, 0, keepdims=False)
        edge_now = lax.dynamic_index_in_dim(edge_lists, source, 0, keepdims=False)
        block_rows = piece[position * rows_dev : (position + 1) * rows_dev]
        running = running + tile_product(
            block_rows, coord_now[1], edge_now[:, 1], coord_now[0], edge_now[:, 0], tile_count
        )
    neighbour_sum = running
    outgoing = jnp.take(features, send_rows, axis=0)
    incoming = lax.all_to_all(outgoing, "grp", split_axis=0, concat_axis=0, tiled=True)
    halo_values = jnp.take(incoming.reshape(-1, width), halo_from, axis=0)
    neighbour_sum = neighbour_sum + jax.ops.segment_sum(halo_values, halo_to, num_segments=rows_dev)
    hub_all = lax.all_gather(
        jnp.take(features, hub_rows, axis=0), ("grp", "blk"), axis=0, tiled=True
    )
    hub_values = jnp.take(hub_all, hub_from, axis=0)
    neighbour_sum = neighbour_sum + jax.ops.segment_sum(hub_values, hub_to, num_segments=rows_dev)
    intra_to = (coords[:, 0, :, None] * 128 + edge_lists[:, :, 0, :]).reshape(-1)
    all_to = jnp.concatenate([intra_to, halo_to, hub_to])
    degree = jax.ops.segment_sum(jnp.ones(all_to.shape, jnp.float32), all_to, num_segments=rows_dev)
    divisor = degree + 1.0
    mean_feat = neighbour_sum / divisor[:, None]
    pre = (
        jnp.dot(mean_feat, w_neigh, precision=precise)
        + jnp.dot(features, w_root, precision=precise)
        + bias
    )
    negative = jnp.minimum(pre, 0.0)
    output = jnp.where(pre > 0, pre, jnp.expm1(negative))
    grad_pre = grad_out * jnp.where(pre > 0, 1.0, jnp.exp(negative))
    grad_sum = jnp.dot(grad_pre, w_neigh.T, precision=precise) / divisor[:, None]
    grad_features = jnp.dot(grad_pre, w_root.T, precision=precise)
    local_wn = jnp.dot(mean_feat.T, grad_pre, precision=precise)
    local_wr = jnp.dot(features.T, grad_pre, precision=precise)
    local_bias = jnp.sum(grad_pre, axis=0)
    total_wn, total_wr, total_bias = lax.psum((local_wn, local_wr, local_bias), ("grp", "blk"))
    slot_terms = jax.ops.segment_sum(
        jnp.take(grad_sum, halo_to, axis=0),
        halo_from,
        num_segments=incoming.shape[0] * incoming.shape[1],
    )
    returned = lax.all_to_all(
        slot_terms.reshape(incoming.shape), "grp", split_axis=0, concat_axis=0, tiled=True
    )
    grad_features = grad_features + jax.ops.segment_sum(
        returned.reshape(-1, width), send_rows.reshape(-1), num_segments=rows_dev
    )
    hub_terms = jax.ops.segment_sum(
        jnp.take(grad_sum, hub_to, axis=0), hub_from, num_segments=hub_all.shape[0]
    )
    owned_grads = lax.psum_scatter(hub_terms, ("grp", "blk"), scatter_dimension=0, tiled=True)
    grad_features = grad_features + jax.ops.segment_sum(
        owned_grads, hub_rows, num_segments=rows_dev
    )
    start = jnp.int32(0)
    pieces = []
    for position in range(lax.axis_size("blk") * rows_dev // rows_dev):
        source = start // rows_dev + position
        coord_now = lax.dynamic_index_in_dim(coords, source, 0, keepdims=False)
        edge_now = lax.dynamic_index_in_dim(edge_lists, source, 0, keepdims=False)
        pieces.append(
            tile_product(
                grad_sum, coord_now[0], edge_now[:, 0], coord_now[1], edge_now[:, 1], tile_count
            )
        )
    grad_features = grad_features + lax.psum_scatter(
        jnp.concatenate(pieces, axis=0), "blk", scatter_dimension=0, tiled=True
    )
    node_total = rows_dev * lax.axis_size("grp") * lax.axis_size("blk")
    factor = node_total ** (-0.5)
    return (output, grad_features, total_wn * factor, total_wr * factor, total_bias * factor)


def solution(mesh):
    in_specs = (
        P(("grp", "blk"), None),
        P(),
        P(),
        P(),
        P(("grp", "blk"), None),
        P("grp", "blk", None, None, None),
        P("grp", "blk", None, None, None, None),
        P("grp", "blk", None, None),
        P("grp", "blk", None),
        P("grp", "blk", None),
        P("grp", "blk", None),
        P("grp", "blk", None),
        P("grp", "blk", None),
    )
    out_specs = (P(("grp", "blk"), None), P(("grp", "blk"), None), P(), P(), P())
    return jax.shard_map(
        per_device, mesh=mesh, in_specs=in_specs, out_specs=out_specs, check_vma=False
    )
```

profile of v0, /device:TPU:1, one launch (start us, length us, event | category | flops | bytes accessed | tf_op | source)
XLA Modules:
  0.0 990.1 jit_solution(17701557693415333533)
XLA Ops:
  8.7 2.8 gather_fusion
  12.6 10.1 %all-to-all-start = ((f32[32,32,128]{2,1,0:T(8,128)}), f32[32,32,128]{2,1,0:T(8,128)S(1)}, u32[]{:S(2)}, u32[]{:S(2)}) async-start(f32[32,32,128]{2,1,0:T(8,128)} %broadcast_select_fusion), calls=%async_computation | async-start | bytes 1048576 | tf_op jit(solution)/shard_map/all_to_all | solution.py:63
  24.8 1.9 slice_reduce_fusion.1
  31.8 52.2 %scatter_custom_fusion.2 = f32[256]{0:T(256)S(1)} fusion(s32[7424]{0:T(1024)S(1)} %pad_add_fusion, f32[7424]{0:T(1024)S(1)} %broadcast.261, f32[]{:T(128)} %constant.277.clone.1), kind=kCustom, calls=%fused_computation.387 | custom fusion | flops 7424 | bytes 1028 | tf_op jit(solution)/shard_map/scatter-add | solution.py:73
  84.1 1.4 fusion.236
  85.4 1.6 gather_fusion.2
  88.0 1.6 gather_fusion.3
  90.7 1.6 gather_fusion.4
  93.3 1.6 gather_fusion.5
  94.9 1.6 gather_fusion.6
  96.4 1.6 gather_fusion.7
  101.1 1.6 gather_fusion.8
  102.7 1.6 gather_fusion.9
  106.4 9.6 scatter_custom_fusion
  116.0 490.2 %all-gather.5.cloned.1.call-done = f32[2048,128]{1,0:T(8,128)} async-done(((f32[8,128]{1,0:T(8,128)}), f32[2048,128]{1,0:T(8,128)}) %all-gather.5.cloned.1.call-update) | async-done | bytes 1048592 | tf_op jit(solution)/shard_map/all_gather | solution.py:66
  606.2 3.4 scatter_custom_fusion.1
  613.8 1.8 gather_fusion.10
  616.7 1.6 gather_fusion.11
  619.3 1.6 gather_fusion.12
  621.9 1.6 gather_fusion.13
  624.6 1.6 gather_fusion.14
  627.2 1.6 gather_fusion.15
  629.8 1.6 gather_fusion.16
  632.4 1.6 gather_fusion.17
  635.0 3.4 scatter_custom_fusion.5
  639.7 10.3 %scatter_custom_fusion.3 = f32[1024,128]{1,0:T(8,128)} fusion(s32[1024]{0:T(1024)S(1)} %bitcast.338, f32[]{:T(128)} %constant.274.clone.1, f32[]{:T(128)} %constant.273.clone.1, pred[1024]{0:T(1024)(128)(4,1)S(1)} %compare_and_fusion.17, f32[256,128]{1,0:T(8,128)S(1)} %convolution_divide_fusion, s32[1024]{0:T(1024)S(1)} %get-tuple-element.87), kind=kCustom, calls=%fused_computation.67 | custom fusion | flops 262144 | bytes 660488 | tf_op jit(solution)/shard_map/scatter-add | solution.py:90
  650.0 7.1 all-to-all-start.1
  657.3 76.1 %psum.23 = f32[128]{0:T(128)S(1)} all-reduce(f32[128]{0:T(128)S(1)} %get-tuple-element.25), channel_id=1, replica_groups=mesh['grp'=32,'blk'=8] {'grp','blk'}, use_global_device_ids=true, to_apply=%region_12.14 | all-reduce | flops 128 | bytes 1024 | tf_op jit(solution)/shard_map/psum | solution.py:89
  734.2 158.0 %all-reduce.4.cloned.1.call-done = (f32[2048,128]{1,0:T(8,128)}, f32[128,128]{1,0:T(8,128)}, f32[128,128]{1,0:T(8,128)}) async-done(((f32[2048,128]{1,0:T(8,128)}, f32[128,128]{1,0:T(8,128)}, f32[128,128]{1,0:T(8,128)}), (f32[2048,128]{1,0:T(8,128)}, f32[128,128]{1,0:T(8,128)}, f32[128,128]{1,0:T(8,128)})) %all-reduce.4.cloned.1.call-update) | async-done | bytes 1179664
  894.5 6.1 scatter_fusion
  900.6 81.1 %reduce-scatter.2.cloned.1.call-done = f32[256,128]{1,0:T(8,128)} async-done(((f32[2048,128]{1,0:T(8,128)}), f32[256,128]{1,0:T(8,128)}) %reduce-scatter.2.cloned.1.call-update) | async-done | bytes 131088 | tf_op jit(solution)/shard_map/reduce_scatter | solution.py:119
  981.7 1.6 add_add_fusion
  (208 shorter events, 34.3 us)
Async XLA Ops:
  7.2 602.8 %copy-start = (f32[128,128]{1,0:T(8,128)S(1)}, f32[128,128]{1,0:T(8,128)}, u32[]{:S(2)}) copy-start(f32[128,128]{1,0:T(8,128)} %param.17) | copy-start | bytes 196612
  7.2 1.6 copy-start.1
  7.2 76.9 %all-gather.3.cloned.1.call-start = ((), (), s32[]{:S(2)}) async-start(), calls=%async_computation.3 | async-start | bytes 1179648 | tf_op jit(solution)/shard_map/all_gather | solution.py:51
  8.7 2.8 copy-start.4
  12.6 10.2 %copy-start.15 = (s32[1,1,8]{2,1,0:T(1,128)S(1)}, s32[1,1,8]{2,1,0:T(1,128)}, u32[]{:S(2)}) copy-start(s32[1,1,8]{2,1,0:T(1,128)} %param.25) | copy-start | bytes 100
  12.6 10.2 %copy-start.9 = (s32[1,1,1024]{2,1,0:T(1,128)S(1)}, s32[1,1,1024]{2,1,0:T(1,128)}, u32[]{:S(2)}) copy-start(s32[1,1,1024]{2,1,0:T(1,128)} %param.23) | copy-start | bytes 12292
  12.6 93.8 %all-to-all-start = ((f32[32,32,128]{2,1,0:T(8,128)}), f32[32,32,128]{2,1,0:T(8,128)S(1)}, u32[]{:S(2)}, u32[]{:S(2)}) async-start(f32[32,32,128]{2,1,0:T(8,128)} %broadcast_select_fusion), calls=%async_computation | async-start | bytes 1048576 | tf_op jit(solution)/shard_map/all_to_all | solution.py:63
  22.7 583.4 %all-gather.5.cloned.1.call-start = ((), (), s32[]{:S(2)}) async-start(), calls=%async_computation.4 | async-start | bytes 1052672 | tf_op jit(solution)/shard_map/all_gather | solution.py:66
  22.9 3.9 copy-start.6
  24.1 0.7 copy-start.3
  24.1 868.1 %all-reduce.4.cloned.1.call-start = ((), (), s32[]{:S(2)}) async-start(), calls=%async_computation.6 | async-start | bytes 2359296
  29.4 0.7 copy-start.10
  30.3 0.7 copy-start.12
  30.9 0.7 copy-start.11
  606.2 3.4 copy-start.14
  609.6 0.9 copy-start.5
  609.6 0.9 copy-start.13
  638.4 343.3 %reduce-scatter.2.cloned.1.call-start = ((), (), s32[]{:S(2)}) async-start(), calls=%async_computation.5 | async-start | bytes 1179648 | tf_op jit(solution)/shard_map/reduce_scatter | solution.py:119
  638.7 1.0 copy-start.2
  650.0 244.5 %all-to-all-start.1 = ((f32[32,32,128]{2,1,0:T(8,128)}), f32[32,32,128]{2,1,0:T(8,128)S(1)}, u32[]{:S(2)}, u32[]{:S(2)}) async-start(f32[32,32,128]{2,1,0:T(8,128)} %bitcast.54), calls=%async_computation.1 | async-start | bytes 1048576 | tf_op jit(solution)/shard_map/all_to_all | solution.py:95
  892.2 0.8 copy-start.8
  893.1 0.8 copy-start.7
Sparse Core Ops, SparseCore 0:
  10.7 66.2 all-gather.2
  79.3 526.8 all-gather.4
  638.5 253.6 all-reduce.3
  896.5 85.1 reduce-scatter.1
where the time goes:
time: 995 us; the launch traced here: 990 us
  waiting for transfers between devices  730 us (73%)
  other arithmetic  94.1 us (9%)
  blocking collectives  76.1 us (8%)
  local copies, waits for them, and re-layouts  37 us (4%)
  matrix products  20.3 us (2%)
  starting transfers between devices  17.5 us (2%)
  between operations  15.1 us (2%)
    all_gather x1, waiting for transfers between devices, per_device(): lax.all_gather(jnp.take(features, hub_rows, axis=0), ('grp', 'blk'), axis...  490 us
    unnamed x5, waiting for transfers between devices  159 us
    reduce_scatter x1, waiting for transfers between devices, per_device(): lax.psum_scatter(jnp.concatenate(pieces, axis=0), 'blk', scatter_dimensio...  81.1 us
    psum x1, blocking collectives, per_device(): lax.psum((local_wn, local_wr, local_bias), ('grp', 'blk'))  76.1 us
    scatter-add x1, other arithmetic, per_device(): jax.ops.segment_sum(jnp.ones(all_to.shape, jnp.float32), all_to, num_segm...  52.2 us
    gather x16, local copies, waits for them, and re-layouts, tile_product(): picked = jnp.take(values, row_index, axis=0)  25.4 us
  transfers between devices with their start and end apart: 6, of which 3 were waited for; matrix products, arithmetic and copies ran while one was open for 12% of the time, Pallas kernels for 0%

commit v1 on v0

v1 whole, which is shorter than its diff:
```python
import jax
import jax.numpy as jnp
from jax import lax
from jax.experimental import pallas as pl
from jax.experimental.pallas import tpu as pltpu
from jax.sharding import PartitionSpec as P

HIGH = lax.Precision.HIGHEST
F32, BF16, I32 = jnp.float32, jnp.bfloat16, jnp.int32
NT = (((1,), (1,)), ((), ()))
NN = (((1,), (0,)), ((), ()))
TN = (((0,), (0,)), ((), ()))


def dot(a, b, dims=NN, precision=None):
    return lax.dot_general(a, b, dims, precision=precision, preferred_element_type=F32)


def halves(x):
    high = x.astype(BF16)
    low = (x - high.astype(F32)).astype(BF16)
    return jnp.concatenate([high, low], axis=1)


def joined(y):
    n = y.shape[1] // 2
    return y[:, :n] + y[:, n:]


def one_hot(idx, rows):
    n = idx.shape[1]
    row = lax.broadcasted_iota(I32, (rows, n), 0)
    return jnp.where(row == idx, 1.0, 0.0).astype(BF16)


def lanes(ref_rows):
    return jnp.concatenate(ref_rows, axis=1)


def call(kernel, out_shape, args, specs=None, scratch=(), flops=1 << 28):
    whole = pl.BlockSpec(memory_space=pltpu.VMEM)
    size = sum(int(a.size) * a.dtype.itemsize for a in args)
    return pl.pallas_call(
        kernel,
        out_shape=out_shape,
        in_specs=[whole] * len(args) if specs is None else specs,
        out_specs=jax.tree.map(
            lambda s: pl.BlockSpec(memory_space=pltpu.SMEM if s.shape == (1,) else pltpu.VMEM), out_shape
        ),
        scratch_shapes=list(scratch),
        compiler_params=pltpu.CompilerParams(vmem_limit_bytes=40 << 20),
        cost_estimate=pl.CostEstimate(flops=flops, bytes_accessed=size, transcendentals=0),
    )(*args)


def shape(s, d=F32):
    return jax.ShapeDtypeStruct(s, d)


def expm1(x):
    series = x * (1 + x * (1 / 2) * (1 + x * (1 / 3) * (1 + x * (1 / 4) * (1 + x * (1 / 5) * (1 + x * (1 / 6) * (1 + x * (1 / 7)))))))
    return jnp.where(x > -0.35, series, jnp.exp(x) - 1.0)


def k_send(features, send, hub, out):
    x = halves(features[...])
    hot = lanes([one_hot(send[i : i + 1, :], 256) for i in range(8)])
    rows = joined(dot(hot, x, TN))
    out[:, 0:32, :] = rows.reshape(32, 32, 128)
    hub_rows = joined(dot(one_hot(hub[0:1, :], 256), x, TN))[0:8, :]
    for p in range(32):
        out[p, 32:40, :] = hub_rows


def k_index(pos, lists, own_to, halo_to, halo_from, hub_to,
            fwd, bwd, fwd_low, bwd_low, h_fwd, h_bwd, h_fwd_low, h_bwd_low, inv, flag):
    me = pos[0]
    zh, y = me // 4, me % 4
    top = jnp.float32(0.0)

    def keep(count, high_ref, low_ref, at):
        high = count.astype(BF16)
        high_ref[at] = high
        low_ref[at] = (count - high.astype(F32)).astype(BF16)

    for r in range(8):
        b = jnp.bitwise_xor(zh, r // 4) * 4 + (y + r % 4) % 4
        block = lists[b]
        to = lanes([one_hot(block[i : i + 1, :], 256) for i in range(6)])
        frm = lanes([one_hot(block[i : i + 1, :], 256) for i in range(6, 12)])
        h_to = lanes([one_hot(block[i : i + 1, :], 256) for i in range(12, 14)])
        codes = [block[i : i + 1, :] for i in range(14, 16)]
        rows = [jnp.where((c >> 3) % 8 == me, (c >> 6) * 8 + c % 8, -1) for c in codes]
        h_frm = lanes([one_hot(c, 256) for c in rows])
        count = jnp.concatenate([dot(to, frm, NT), dot(h_to, h_frm, NT)], axis=1)
        top = jnp.maximum(top, jnp.max(count))
        keep(count, fwd, fwd_low, r)
        count_t = jnp.concatenate([dot(frm, to, NT), dot(h_frm, h_to, NT)], axis=0)
        keep(count_t, bwd, bwd_low, r)
    to = lanes([one_hot(halo_to[i : i + 1, :], 256) for i in range(8)])
    frm = lanes([one_hot(halo_from[i : i + 1, :], 1024) for i in range(8)])
    count = dot(to, frm, NT)
    top = jnp.maximum(top, jnp.max(count))
    keep(count, h_fwd, h_fwd_low, ...)
    keep(dot(frm, to, NT), h_bwd, h_bwd_low, ...)
    flag[0] = (top > 256.0).astype(I32)
    row = lax.broadcasted_iota(I32, (256, 128), 0)
    degree = jnp.zeros((256, 128), F32)
    for ref, n in ((own_to, 48), (halo_to, 8), (hub_to, 2)):
        for i in range(n):
            degree = degree + jnp.where(row == ref[i : i + 1, :], 1.0, 0.0)
    degree = jnp.sum(degree, axis=1, keepdims=True)
    inv[...] = jnp.broadcast_to(1.0 / (degree + 1.0), (256, 128))


def k_partial(flag, features, incoming, fwd, fwd_low, *rest):
    outs, held = rest[:8], rest[8]
    hubs = incoming[:, 32:40, :].reshape(256, 128)
    x = jnp.concatenate([halves(features[...]), halves(hubs)], axis=0)
    for r in (5, 7, 6, 4, 1, 3, 2, 0):
        outs[r][...] = joined(dot(fwd[r], x))

    @pl.when(flag[0] != 0)
    def _():
        pltpu.sync_copy(fwd_low, held)
        for r in range(8):
            outs[r][...] += joined(dot(held[r], x))


def k_halo(flag, incoming, h_fwd, h_low, own, out, held):
    x = halves(incoming[:, 0:32, :].reshape(1024, 128))
    out[...] = own[...] + joined(dot(h_fwd[...], x))

    @pl.when(flag[0] != 0)
    def _():
        pltpu.sync_copy(h_low, held)
        out[...] += joined(dot(held[...], x))


def k_layer(a0, a1, a2, a3, a4, inv, features, w_neigh, w_root, bias, grad_out,
            output, grad_pre, grad_sum, mean):
    scale = inv[...]
    m = (a0[...] + a1[...] + a2[...] + a3[...] + a4[...]) * scale
    mean[...] = m
    pre = dot(m, w_neigh[...], NN, HIGH) + dot(features[...], w_root[...], NN, HIGH) + bias[...]
    negative = jnp.minimum(pre, 0.0)
    output[...] = jnp.where(pre > 0, pre, expm1(negative))
    g = grad_out[...] * jnp.where(pre > 0, 1.0, jnp.exp(negative))
    grad_pre[...] = g
    grad_sum[...] = dot(g, w_neigh[...], NT, HIGH) * scale


def k_weights(grad_pre, mean, features, out):
    g = grad_pre[...]
    wn = dot(mean[...], g, TN, HIGH)
    wr = dot(features[...], g, TN, HIGH)
    out[0:16, 0:8, :] = wn.reshape(16, 8, 128)
    out[16:32, 0:8, :] = wr.reshape(16, 8, 128)
    total = jnp.sum(g, axis=0, keepdims=True)
    fill = jnp.broadcast_to(total, (8, 128))
    for p in range(32):
        out[p, 8:16, :] = fill


def k_slots(flag, grad_sum, h_bwd, h_low, grad_pre, w_root, slots, root, held):
    x = halves(grad_sum[...])
    slots[...] = joined(dot(h_bwd[...], x))
    root[...] = dot(grad_pre[...], w_root[...], NT, HIGH)

    @pl.when(flag[0] != 0)
    def _():
        pltpu.sync_copy(h_low, held)
        slots[...] += joined(dot(held[...], x))


def k_back(flag, g0, g1, g2, g3, g4, g5, g6, g7, bwd, bwd_low, slots, root, out, local, held, total):
    xs = [halves(g[...]) for g in (g0, g1, g2, g3, g4, g5, g6, g7)]
    acc = dot(bwd[0], xs[0])
    for r in range(1, 8):
        acc = acc + dot(bwd[r], xs[r])
    total[...] = joined(acc)

    @pl.when(flag[0] != 0)
    def _():
        pltpu.sync_copy(bwd_low, held)
        for r in range(8):
            total[...] += joined(dot(held[r], xs[r]))

    out[:, 0:32, :] = slots[...].reshape(32, 32, 128)
    out[:, 32:40, :] = total[256:512, :].reshape(32, 8, 128)
    local[...] = root[...] + total[0:256, :]


def k_final(returned, send, hub, local, out):
    hot = lanes([one_hot(send[i : i + 1, :], 256) for i in range(8)])
    acc = dot(hot, halves(returned[:, 0:32, :].reshape(1024, 128)))
    hub_rows = jnp.sum(returned[:, 32:40, :], axis=0)
    hub_rows = jnp.concatenate([hub_rows, jnp.zeros((120, 128), F32)], axis=0)
    acc = acc + dot(one_hot(hub[0:1, :], 256), halves(hub_rows))
    out[...] = local[...] + joined(acc)


def per_device(features, w_neigh, w_root, bias, grad_out, tile_coord, tile_edge,
               send_idx, halo_dst, halo_src, hub_idx, hub_dst, hub_src):
    coords = tile_coord.reshape(8, 2, 6)
    edges = tile_edge.reshape(8, 6, 2, 128)
    own_to = coords[:, 0, :, None] * 128 + edges[:, :, 0, :]
    own_from = coords[:, 1, :, None] * 128 + edges[:, :, 1, :]
    hub_to = hub_dst.reshape(2, 128)
    hub_from = hub_src.reshape(2, 128)
    lists = jnp.concatenate(
        [own_to, own_from, jnp.broadcast_to(hub_to[None], (8, 2, 128)), jnp.broadcast_to(hub_from[None], (8, 2, 128))],
        axis=1,
    )
    send = send_idx.reshape(8, 128)
    hub = jnp.pad(hub_idx.reshape(1, 8), ((0, 0), (0, 120)), constant_values=-1)
    halo_to = halo_dst.reshape(8, 128)
    halo_from = halo_src.reshape(8, 128)
    pos = lax.axis_index("blk").astype(I32).reshape(1)

    def swap(v):
        return lax.ppermute(v, "blk", [(i, i ^ 4) for i in range(8)])

    def turn(v, k):
        return lax.ppermute(v, "blk", [(i, i // 4 * 4 + (i % 4 + k) % 4) for i in range(8)])

    def exchange(v, axis):
        return lax.all_to_all(v, axis, split_axis=0, concat_axis=0, tiled=True)

    vm, sm, hb = (pl.BlockSpec(memory_space=s) for s in (pltpu.VMEM, pltpu.SMEM, pl.ANY))

    outgoing = call(k_send, shape((32, 40, 128)), (features, send, hub))
    incoming = exchange(outgoing, "grp")
    lists = exchange(lists, "blk")
    fwd, bwd, fwd_low, bwd_low, h_fwd, h_bwd, h_fwd_low, h_bwd_low, inv, flag = call(
        k_index,
        (shape((8, 256, 512), BF16), shape((8, 512, 256), BF16), shape((8, 256, 512), BF16), shape((8, 512, 256), BF16),
         shape((256, 1024), BF16), shape((1024, 256), BF16), shape((256, 1024), BF16), shape((1024, 256), BF16),
         shape((256, 128)), shape((1,), I32)),
        (pos, lists, own_to.reshape(48, 128), halo_to, halo_from, hub_to),
        [sm, vm, vm, vm, vm, vm],
        flops=1 << 31,
    )
    part = call(
        k_partial, [shape((256, 128))] * 8, (flag, features, incoming, fwd, fwd_low), [sm, vm, vm, vm, hb],
        [pltpu.VMEM((8, 256, 512), BF16)], flops=1 << 29,
    )
    far = part[4] + turn(part[5], 1) + turn(part[7], 3) + turn(part[6], 2)
    far = swap(far)
    near = [turn(part[1], 1), turn(part[3], 3), turn(part[2], 2)]
    own = call(
        k_halo, shape((256, 128)), (flag, incoming, h_fwd, h_fwd_low, part[0]), [sm, vm, vm, hb, vm],
        [pltpu.VMEM((256, 1024), BF16)],
    )
    output, grad_pre, grad_sum, mean = call(
        k_layer, [shape((256, 128))] * 4,
        (own, *near, far, inv, features, w_neigh, w_root, bias.reshape(1, 128), grad_out),
    )
    other = swap(grad_sum)
    g1, g3, g2 = turn(grad_sum, 3), turn(grad_sum, 1), turn(grad_sum, 2)
    g5, g7, g6 = turn(other, 3), turn(other, 1), turn(other, 2)
    weights = call(k_weights, shape((32, 16, 128)), (grad_pre, mean, features))
    weights = exchange(weights, "grp").sum(axis=0)
    weights = exchange(jnp.broadcast_to(weights[None], (8, 16, 128)), "blk").sum(axis=0)
    slots, root = call(
        k_slots, [shape((1024, 128)), shape((256, 128))], (flag, grad_sum, h_bwd, h_bwd_low, grad_pre, w_root),
        [sm, vm, vm, hb, vm, vm], [pltpu.VMEM((1024, 256), BF16)],
    )
    back, local = call(
        k_back, [shape((32, 40, 128)), shape((256, 128))],
        (flag, grad_sum, g1, g2, g3, other, g5, g6, g7, bwd, bwd_low, slots, root),
        [sm] + [vm] * 8 + [vm, hb, vm, vm],
        [pltpu.VMEM((8, 512, 256), BF16), pltpu.VMEM((512, 128), F32)],
    )
    returned = exchange(back, "grp")
    grad_features = call(k_final, shape((256, 128)), (returned, send, hub, local))
    factor = (256 * lax.axis_size("grp") * lax.axis_size("blk")) ** (-0.5)
    full = exchange(jnp.broadcast_to(weights[None, 0:8], (32, 8, 128)), "grp") * factor
    full = full.reshape(256, 128)
    return output, grad_features, full[0:128], full[128:256], weights[8] * factor


def solution(mesh):
    rows = P(("grp", "blk"), None)
    in_specs = (
        rows, P(), P(), P(), rows,
        P("grp", "blk", None, None, None),
        P("grp", "blk", None, None, None, None),
        P("grp", "blk", None, None),
        P("grp", "blk", None), P("grp", "blk", None), P("grp", "blk", None), P("grp", "blk", None), P("grp", "blk", None),
    )
    return jax.shard_map(
        per_device, mesh=mesh, in_specs=in_specs, out_specs=(rows, rows, P(), P(), P()), check_vma=False
    )
```

time: 995 us -> 167 us (0.17)
  waiting for transfers between devices: 730 us -> 45.5 us
  other arithmetic: 94.1 us -> 4.03 us
  blocking collectives: 76.1 us -> 18.8 us
  starting transfers between devices: 17.5 us -> 58.8 us
  matrix products: 20.3 us -> 0 us
  Pallas kernels: 0 us -> 16.8 us
  local copies, waits for them, and re-layouts: 37 us -> 21.5 us
  between operations: 15.1 us -> 0.91 us
    all_gather x2 -> x0, waiting for transfers between devices: 490 us -> none  [the longest x1 490 us: per_device(): lax.all_gather(jnp.take(features, hub_rows, axis=0), ('grp', 'blk'), axis...]
    unnamed x5 -> x0, waiting for transfers between devices: 159 us -> none
    scatter-add x7 -> x0, other arithmetic: 85.8 us -> none  [the longest x1 52.2 us: per_device(): jax.ops.segment_sum(jnp.ones(all_to.shape, jnp.float32), all_to, num_segm...]
    reduce_scatter x1 -> x0, waiting for transfers between devices: 81.1 us -> none  [per_device(): lax.psum_scatter(jnp.concatenate(pieces, axis=0), 'blk', scatter_dimensio...]
    psum x1 -> x0, blocking collectives: 76.1 us -> none  [per_device(): lax.psum((local_wn, local_wr, local_bias), ('grp', 'blk'))]
    all_to_all x2 -> x5, waiting for transfers between devices: 0.01 us -> 30.4 us  [exchange(): return lax.all_to_all(v, axis, split_axis=0, concat_axis=0, tiled=True)]
    gather x18 -> x0, local copies, waits for them, and re-layouts: 28.7 us -> none  [the longest x16 25.4 us: tile_product(): picked = jnp.take(values, row_index, axis=0)]
    all_to_all x2 -> x5, starting transfers between devices: 17.3 us -> 40.4 us  [exchange(): return lax.all_to_all(v, axis, split_axis=0, concat_axis=0, tiled=True)]
  transfers between devices with their start and end apart: 6 -> 19, of which waited for: 3 -> 14; matrix products, arithmetic and copies ran while one was open for 12% -> 3% of each run, Pallas kernels for 0% -> 8%
where the time goes in v1:
time: 167 us; the launch traced here: 166 us
  starting transfers between devices  58.8 us (35%)
  waiting for transfers between devices  45.5 us (27%)
  local copies, waits for them, and re-layouts  21.5 us (13%)
  blocking collectives  18.8 us (11%)
  Pallas kernels  16.8 us (10%)
  other arithmetic  4.03 us (2%)
    all_to_all x5, starting transfers between devices, exchange(): return lax.all_to_all(v, axis, split_axis=0, concat_axis=0, tiled=True)  40.4 us
    all_to_all x5, waiting for transfers between devices, exchange(): return lax.all_to_all(v, axis, split_axis=0, concat_axis=0, tiled=True)  30.4 us
    all_to_all x1, blocking collectives, exchange(): return lax.all_to_all(v, axis, split_axis=0, concat_axis=0, tiled=True)  18.8 us
    pallas_call x9, Pallas kernels, call(): pl.pallas_call(kernel, out_shape=out_shape, in_specs=[whole] * len(args)...  16.8 us
    unnamed x55, local copies, waits for them, and re-layouts  16.4 us
    ppermute x12, waiting for transfers between devices, turn(): lax.ppermute(v, 'blk', [(i, i // 4 * 4 + (i % 4 + k) % 4) for i in range(...  12.9 us
    ppermute x12, starting transfers between devices, turn(): lax.ppermute(v, 'blk', [(i, i // 4 * 4 + (i % 4 + k) % 4) for i in range(...  12.5 us
    ppermute x2, starting transfers between devices, swap(): return lax.ppermute(v, 'blk', [(i, i ^ 4) for i in range(8)])  5.83 us
  transfers between devices with their start and end apart: 19, of which 14 were waited for; matrix products, arithmetic and copies ran while one was open for 3% of the time, Pallas kernels for 8%

profile of v1, /device:TPU:1, one launch (start us, length us, event | category | flops | bytes accessed | tf_op | source)
XLA Modules:
  0.0 166.3 jit_solution(13023205108260977014)
XLA Ops:
  4.5 11.6 %all-to-all-start = ((s32[8,16,128]{2,1,0:T(8,128)}), s32[8,16,128]{2,1,0:T(8,128)S(1)}, u32[]{:S(2)}, u32[]{:S(2)}) async-start(s32[8,16,128]{2,1,0:T(8,128)} %pad_add_fusion), calls=%async_computation | async-start | bytes 131072 | tf_op jit(solution)/shard_map/all_to_all | solution.py:228
  19.7 5.5 %all-to-all-done.lists = s32[8,16,128]{2,1,0:T(8,128)S(1)} async-done(((s32[8,16,128]{2,1,0:T(8,128)}), s32[8,16,128]{2,1,0:T(8,128)S(1)}, u32[]{:S(2)}, u32[]{:S(2)}) %all-to-all-start) | async-done | bytes 65568 | tf_op jit(solution)/shard_map/all_to_all | solution.py:228
  25.3 7.9 %all-to-all-start.1 = ((f32[32,40,128]{2,1,0:T(8,128)}), f32[32,40,128]{2,1,0:T(8,128)S(1)}, u32[]{:S(2)}, u32[]{:S(2)}) async-start(f32[32,40,128]{2,1,0:T(8,128)} %shard_map.165), calls=%async_computation.1 | async-start | bytes 1310720 | tf_op jit(solution)/shard_map/all_to_all | solution.py:228
  33.4 6.3 %shard_map.164 = (bf16[8,256,512]{2,1,0:T(8,128)(2,1)S(1)}, bf16[8,512,256]{2,1,0:T(8,128)(2,1)S(1)}, bf16[8,256,512]{2,1,0:T(8,128)(2,1)S(1)}, bf16[8,512,256]{...) custom-call(s32[1]{0:T(128)} %bitcast.pos, ...), custom_call_target="tpu_custom_call" | custom-call | flops 2147483648 | bytes 99332 | tf_op jit(solution)/shard_map/pallas_call | solution.py:43
  39.7 1.3 copy-done
  41.0 1.3 copy-done.2
  42.4 1.4 copy-done.4
  46.9 5.2 %all-to-all-done.1.incoming = f32[32,40,128]{2,1,0:T(8,128)S(1)} async-done(((f32[32,40,128]{2,1,0:T(8,128)}), f32[32,40,128]{2,1,0:T(8,128)S(1)}, u32[]{:S(2)}, u32[]{:S(2)}) %all-to-all-start.1) | async-done | bytes 655392 | tf_op jit(solution)/shard_map/all_to_all | solution.py:228
  52.1 1.6 copy-done.3
  53.7 1.6 copy-done.5
  55.3 1.4 shard_map.166
  57.2 2.4 %collective-permute-start.4 = (f32[256,128]{1,0:T(8,128)S(1)}, f32[256,128]{1,0:T(8,128)S(1)}, u32[]{:S(2)}, u32[]{:S(2)}) collective-permute-start(f32[256,128]{1,0:T(8,128)S(1)} %get-tuple-element.42), channel_id=1, source_target_pairs={{0,3},{1,0},{2,1},{3,2},{4,7},{5,4},{6,5},{7,6},{8,11},{9,8},{10,9... | collective-permute-start | bytes 393224 | tf_op jit(solution)/shard_map/ppermute | solution.py:225
  60.2 2.1 %collective-permute-start.1 = (f32[256,128]{1,0:T(8,128)S(1)}, f32[256,128]{1,0:T(8,128)S(1)}, u32[]{:S(2)}, u32[]{:S(2)}) collective-permute-start(f32[256,128]{1,0:T(8,128)S(1)} %get-tuple-element.38), channel_id=1, source_target_pairs={{0,3},{1,0},{2,1},{3,2},{4,7},{5,4},{6,5},{7,6},{8,11},{9,8},{10,9... | collective-permute-start | bytes 393224 | tf_op jit(solution)/shard_map/ppermute | solution.py:225
  62.3 1.3 collective-permute-done.3
  64.1 1.2 collective-permute-done.4
  68.9 2.0 %collective-permute-done.1.a2 = f32[256,128]{1,0:T(8,128)S(1)} collective-permute-done((f32[256,128]{1,0:T(8,128)S(1)}, f32[256,128]{1,0:T(8,128)S(1)}, u32[]{:S(2)}, u32[]{:S(2)}) %collective-permute-start.1) | collective-permute-done | bytes 131104 | tf_op jit(solution)/shard_map/ppermute | solution.py:225
  71.8 2.2 %collective-permute-done.6.a4 = f32[256,128]{1,0:T(8,128)S(1)} collective-permute-done((f32[256,128]{1,0:T(8,128)S(1)}, f32[256,128]{1,0:T(8,128)S(1)}, u32[]{:S(2)}, u32[]{:S(2)}) %collective-permute-start.6) | collective-permute-done | bytes 131104 | tf_op jit(solution)/shard_map/ppermute | solution.py:222
  74.1 1.2 shard_map.168
  76.0 18.8 %all_to_all.30 = f32[32,16,128]{2,1,0:T(8,128)} all-to-all(f32[32,16,128]{2,1,0:T(8,128)S(1)} %shard_map.172), channel_id=1, replica_groups=mesh['grp'=32,'blk'=8] {'grp'}, dimensions={0} | all-to-all | bytes 524288 | tf_op jit(solution)/shard_map/all_to_all | solution.py:228
  96.4 4.5 %all-to-all-start.4 = ((f32[8,16,128]{2,1,0:T(8,128)}), f32[8,16,128]{2,1,0:T(8,128)S(1)}, u32[]{:S(2)}, u32[]{:S(2)}) async-start(f32[8,16,128]{2,1,0:T(8,128)} %broadcast_in_dim.30), calls=%async_computation.4 | async-start | bytes 131072 | tf_op jit(solution)/shard_map/all_to_all | solution.py:228
  101.0 5.4 %collective-permute-start.10 = (f32[256,128]{1,0:T(8,128)S(1)}, f32[256,128]{1,0:T(8,128)}, u32[]{:S(2)}, u32[]{:S(2)}) collective-permute-start(f32[256,128]{1,0:T(8,128)S(1)} %get-tuple-element.46.grad_sum.g0), channel_id=1, source_target_pairs={{0,4},{1,5},{2,6},{3,7},{4,0},{5,1},{6,2},{7,3},{8,12},{9,13},{10,... | collective-permute-start | bytes 393224 | tf_op jit(solution)/shard_map/ppermute | solution.py:222
  107.5 2.8 %all-to-all-done.4 = f32[8,16,128]{2,1,0:T(8,128)S(1)} async-done(((f32[8,16,128]{2,1,0:T(8,128)}), f32[8,16,128]{2,1,0:T(8,128)S(1)}, u32[]{:S(2)}, u32[]{:S(2)}) %all-to-all-start.4) | async-done | bytes 65568 | tf_op jit(solution)/shard_map/all_to_all | solution.py:228
  111.0 7.8 %all-to-all-start.5 = ((f32[32,8,128]{2,1,0:T(8,128)}), f32[32,8,128]{2,1,0:T(8,128)}, u32[]{:S(2)}, u32[]{:S(2)}) async-start(f32[32,8,128]{2,1,0:T(8,128)} %broadcast_in_dim.31), calls=%async_computation.5 | async-start | bytes 262144 | tf_op jit(solution)/shard_map/all_to_all | solution.py:228
  119.4 2.1 %collective-permute-start.7 = (f32[256,128]{1,0:T(8,128)S(1)}, f32[256,128]{1,0:T(8,128)S(1)}, u32[]{:S(2)}, u32[]{:S(2)}) collective-permute-start(f32[256,128]{1,0:T(8,128)S(1)} %get-tuple-element.46.grad_sum.g0), channel_id=1, source_target_pairs={{0,3},{1,0},{2,1},{3,2},{4,7},{5,4},{6,5},{7,6},{8,11},{9,8},{10,9... | collective-permute-start | bytes 393224 | tf_op jit(solution)/shard_map/ppermute | solution.py:225
  121.5 1.8 %collective-permute-start.12 = (f32[256,128]{1,0:T(8,128)}, f32[256,128]{1,0:T(8,128)S(1)}, u32[]{:S(2)}, u32[]{:S(2)}) collective-permute-start(f32[256,128]{1,0:T(8,128)} %collective-permute-done.10.g4), channel_id=1, source_target_pairs={{0,2},{1,3},{2,0},{3,1},{4,6},{5,7},{6,4},{7,5},{8,10},{9,11},{10,... | collective-permute-start | bytes 393224 | tf_op jit(solution)/shard_map/ppermute | solution.py:225
  126.9 1.3 collective-permute-done.13.g7
  128.1 2.7 %collective-permute-done.12.g6 = f32[256,128]{1,0:T(8,128)S(1)} collective-permute-done((f32[256,128]{1,0:T(8,128)}, f32[256,128]{1,0:T(8,128)S(1)}, u32[]{:S(2)}, u32[]{:S(2)}) %collective-permute-start.12) | collective-permute-done | bytes 131104 | tf_op jit(solution)/shard_map/ppermute | solution.py:225
  130.8 1.3 collective-permute-done.11.g5
  132.1 1.6 copy-done.1
  134.6 3.2 %shard_map.170 = (f32[32,40,128]{2,1,0:T(8,128)}, f32[256,128]{1,0:T(8,128)S(1)}) custom-call(s32[1]{0:T(128)} %get-tuple-element.31.flag, f32[256,128]{1,0:T(8,128)S(1)} %get-tuple-element.46.grad_sum.g0, f32[256,128]{1,0:T(8,128)S(1)} %collective-permute-done.7.g1, f32[256,128]{1,0:T(8,128)S(1)} %collective-permute-done.8.g2, f32[256,128]{1,0:T(8,128)S(1)} %copy-done.21, ...), custom_call_target="tpu_custom_call" | custom-call | flops 268435456 | bytes 5898244 | tf_op jit(solution)/shard_map/pallas_call | solution.py:43
  137.8 8.5 %all-to-all-start.2 = ((f32[32,40,128]{2,1,0:T(8,128)}), f32[32,40,128]{2,1,0:T(8,128)S(1)}, u32[]{:S(2)}, u32[]{:S(2)}) async-start(f32[32,40,128]{2,1,0:T(8,128)} %get-tuple-element.54), calls=%async_computation.2 | async-start | bytes 1310720 | tf_op jit(solution)/shard_map/all_to_all | solution.py:228
  148.4 16.9 %all-to-all-done.2.returned = f32[32,40,128]{2,1,0:T(8,128)S(1)} async-done(((f32[32,40,128]{2,1,0:T(8,128)}), f32[32,40,128]{2,1,0:T(8,128)S(1)}, u32[]{:S(2)}, u32[]{:S(2)}) %all-to-all-start.2) | async-done | bytes 655392 | tf_op jit(solution)/shard_map/all_to_all | solution.py:228
  (93 shorter events, 29.0 us)
Async XLA Ops:
  0.6 32.7 %copy-start.23 = (s32[1,1,256]{2,1,0:T(1,128)S(1)}, s32[1,1,256]{2,1,0:T(1,128)}, u32[]{:S(2)}) copy-start(s32[1,1,256]{2,1,0:T(1,128)} %param.24) | copy-start | bytes 3076
  0.6 32.7 %copy-start.26 = (s32[1,1,1024]{2,1,0:T(1,128)S(1)}, s32[1,1,1024]{2,1,0:T(1,128)}, u32[]{:S(2)}) copy-start(s32[1,1,1024]{2,1,0:T(1,128)} %param.22) | copy-start | bytes 12292
  0.7 32.7 %copy-start.25 = (s32[1,1,1024]{2,1,0:T(1,128)S(1)}, s32[1,1,1024]{2,1,0:T(1,128)}, u32[]{:S(2)}) copy-start(s32[1,1,1024]{2,1,0:T(1,128)} %param.21) | copy-start | bytes 12292
  4.5 20.8 %all-to-all-start = ((s32[8,16,128]{2,1,0:T(8,128)}), s32[8,16,128]{2,1,0:T(8,128)S(1)}, u32[]{:S(2)}, u32[]{:S(2)}) async-start(s32[8,16,128]{2,1,0:T(8,128)} %pad_add_fusion), calls=%async_computation | async-start | bytes 131072 | tf_op jit(solution)/shard_map/all_to_all | solution.py:228
  25.3 26.9 %all-to-all-start.1 = ((f32[32,40,128]{2,1,0:T(8,128)}), f32[32,40,128]{2,1,0:T(8,128)S(1)}, u32[]{:S(2)}, u32[]{:S(2)}) async-start(f32[32,40,128]{2,1,0:T(8,128)} %shard_map.165), calls=%async_computation.1 | async-start | bytes 1310720 | tf_op jit(solution)/shard_map/all_to_all | solution.py:228
  33.4 18.8 %copy-start.13 = (f32[256,128]{1,0:T(8,128)S(1)}, f32[256,128]{1,0:T(8,128)}, u32[]{:S(2)}) copy-start(f32[256,128]{1,0:T(8,128)} %features.7) | copy-start | bytes 393220
  52.1 1.6 copy-start.3
  55.3 11.4 %copy-start.9 = (bf16[256,1024]{1,0:T(8,128)(2,1)S(1)}, bf16[256,1024]{1,0:T(8,128)(2,1)}, u32[]{:S(2)}) copy-start(bf16[256,1024]{1,0:T(8,128)(2,1)} %copy-done.8) | copy-start | bytes 1572868
  55.3 11.4 %copy-start.11 = (bf16[256,1024]{1,0:T(8,128)(2,1)S(1)}, bf16[256,1024]{1,0:T(8,128)(2,1)}, u32[]{:S(2)}) copy-start(bf16[256,1024]{1,0:T(8,128)(2,1)} %copy-done.10) | copy-start | bytes 1572868
  56.8 17.3 %copy-start.14 = (f32[128,128]{1,0:T(8,128)S(1)}, f32[128,128]{1,0:T(8,128)}, u32[]{:S(2)}) copy-start(f32[128,128]{1,0:T(8,128)} %w_root.3) | copy-start | bytes 196612
  56.8 17.3 %copy-start.15 = (f32[256,128]{1,0:T(8,128)S(1)}, f32[256,128]{1,0:T(8,128)}, u32[]{:S(2)}) copy-start(f32[256,128]{1,0:T(8,128)} %grad_out.1) | copy-start | bytes 393220
  56.8 17.3 %copy-start.17 = (f32[256,128]{1,0:T(8,128)S(1)}, f32[256,128]{1,0:T(8,128)}, u32[]{:S(2)}) copy-start(f32[256,128]{1,0:T(8,128)} %copy-done.16) | copy-start | bytes 393220
  56.8 17.2 %copy-start.22 = (f32[128,128]{1,0:T(8,128)S(1)}, f32[128,128]{1,0:T(8,128)}, u32[]{:S(2)}) copy-start(f32[128,128]{1,0:T(8,128)} %w_neigh.1) | copy-start | bytes 196612
  56.8 17.2 %copy-start.24 = (f32[128]{0:T(128)S(1)}, f32[128]{0:T(128)}, u32[]{:S(2)}) copy-start(f32[128]{0:T(128)} %param.16) | copy-start | bytes 1540
  56.8 6.8 %collective-permute-start.3 = (f32[256,128]{1,0:T(8,128)S(1)}, f32[256,128]{1,0:T(8,128)S(1)}, u32[]{:S(2)}, u32[]{:S(2)}) collective-permute-start(f32[256,128]{1,0:T(8,128)S(1)} %get-tuple-element.41), channel_id=1, source_target_pairs={{0,1},{1,2},{2,3},{3,0},{4,5},{5,6},{6,7},{7,4},{8,9},{9,10},{10,1... | collective-permute-start | bytes 393224 | tf_op jit(solution)/shard_map/ppermute | solution.py:225
  57.2 8.1 %collective-permute-start.4 = (f32[256,128]{1,0:T(8,128)S(1)}, f32[256,128]{1,0:T(8,128)S(1)}, u32[]{:S(2)}, u32[]{:S(2)}) collective-permute-start(f32[256,128]{1,0:T(8,128)S(1)} %get-tuple-element.42), channel_id=1, source_target_pairs={{0,3},{1,0},{2,1},{3,2},{4,7},{5,4},{6,5},{7,6},{8,11},{9,8},{10,9... | collective-permute-start | bytes 393224 | tf_op jit(solution)/shard_map/ppermute | solution.py:225
  59.6 6.6 %collective-permute-start.5 = (f32[256,128]{1,0:T(8,128)S(1)}, f32[256,128]{1,0:T(8,128)S(1)}, u32[]{:S(2)}, u32[]{:S(2)}) collective-permute-start(f32[256,128]{1,0:T(8,128)S(1)} %get-tuple-element.43), channel_id=1, source_target_pairs={{0,2},{1,3},{2,0},{3,1},{4,6},{5,7},{6,4},{7,5},{8,10},{9,11},{10,... | collective-permute-start | bytes 393224 | tf_op jit(solution)/shard_map/ppermute | solution.py:225
  59.6 9.3 %collective-permute-start = (f32[256,128]{1,0:T(8,128)S(1)}, f32[256,128]{1,0:T(8,128)S(1)}, u32[]{:S(2)}, u32[]{:S(2)}) collective-permute-start(f32[256,128]{1,0:T(8,128)S(1)} %get-tuple-element.37), channel_id=1, source_target_pairs={{0,1},{1,2},{2,3},{3,0},{4,5},{5,6},{6,7},{7,4},{8,9},{9,10},{10,1... | collective-permute-start | bytes 393224 | tf_op jit(solution)/shard_map/ppermute | solution.py:225
  60.2 10.7 %collective-permute-start.1 = (f32[256,128]{1,0:T(8,128)S(1)}, f32[256,128]{1,0:T(8,128)S(1)}, u32[]{:S(2)}, u32[]{:S(2)}) collective-permute-start(f32[256,128]{1,0:T(8,128)S(1)} %get-tuple-element.38), channel_id=1, source_target_pairs={{0,3},{1,0},{2,1},{3,2},{4,7},{5,4},{6,5},{7,6},{8,11},{9,8},{10,9... | collective-permute-start | bytes 393224 | tf_op jit(solution)/shard_map/ppermute | solution.py:225
  63.6 8.2 %collective-permute-start.2 = (f32[256,128]{1,0:T(8,128)S(1)}, f32[256,128]{1,0:T(8,128)S(1)}, u32[]{:S(2)}, u32[]{:S(2)}) collective-permute-start(f32[256,128]{1,0:T(8,128)S(1)} %get-tuple-element.39), channel_id=1, source_target_pairs={{0,2},{1,3},{2,0},{3,1},{4,6},{5,7},{6,4},{7,5},{8,10},{9,11},{10,... | collective-permute-start | bytes 393224 | tf_op jit(solution)/shard_map/ppermute | solution.py:225
  66.2 7.8 %collective-permute-start.6 = (f32[256,128]{1,0:T(8,128)S(1)}, f32[256,128]{1,0:T(8,128)S(1)}, u32[]{:S(2)}, u32[]{:S(2)}) collective-permute-start(f32[256,128]{1,0:T(8,128)S(1)} %add_add_fusion), channel_id=1, source_target_pairs={{0,4},{1,5},{2,6},{3,7},{4,0},{5,1},{6,2},{7,3},{8,12},{9,13},{10,... | collective-permute-start | bytes 393224 | tf_op jit(solution)/shard_map/ppermute | solution.py:222
  67.7 57.2 %copy-start.7 = (bf16[1024,256]{1,0:T(8,128)(2,1)S(1)}, bf16[1024,256]{1,0:T(8,128)(2,1)}, u32[]{:S(2)}) copy-start(bf16[1024,256]{1,0:T(8,128)(2,1)} %copy-done.6) | copy-start | bytes 1572868
  96.4 13.9 %all-to-all-start.4 = ((f32[8,16,128]{2,1,0:T(8,128)}), f32[8,16,128]{2,1,0:T(8,128)S(1)}, u32[]{:S(2)}, u32[]{:S(2)}) async-start(f32[8,16,128]{2,1,0:T(8,128)} %broadcast_in_dim.30), calls=%async_computation.4 | async-start | bytes 131072 | tf_op jit(solution)/shard_map/all_to_all | solution.py:228
  101.0 20.6 %collective-permute-start.10 = (f32[256,128]{1,0:T(8,128)S(1)}, f32[256,128]{1,0:T(8,128)}, u32[]{:S(2)}, u32[]{:S(2)}) collective-permute-start(f32[256,128]{1,0:T(8,128)S(1)} %get-tuple-element.46.grad_sum.g0), channel_id=1, source_target_pairs={{0,4},{1,5},{2,6},{3,7},{4,0},{5,1},{6,2},{7,3},{8,12},{9,13},{10,... | collective-permute-start | bytes 393224 | tf_op jit(solution)/shard_map/ppermute | solution.py:222
  106.3 17.0 %collective-permute-start.9 = (f32[256,128]{1,0:T(8,128)S(1)}, f32[256,128]{1,0:T(8,128)S(1)}, u32[]{:S(2)}, u32[]{:S(2)}) collective-permute-start(f32[256,128]{1,0:T(8,128)S(1)} %get-tuple-element.46.grad_sum.g0), channel_id=1, source_target_pairs={{0,1},{1,2},{2,3},{3,0},{4,5},{5,6},{6,7},{7,4},{8,9},{9,10},{10,1... | collective-permute-start | bytes 393224 | tf_op jit(solution)/shard_map/ppermute | solution.py:225
  111.0 26.8 %all-to-all-start.5 = ((f32[32,8,128]{2,1,0:T(8,128)}), f32[32,8,128]{2,1,0:T(8,128)}, u32[]{:S(2)}, u32[]{:S(2)}) async-start(f32[32,8,128]{2,1,0:T(8,128)} %broadcast_in_dim.31), calls=%async_computation.5 | async-start | bytes 262144 | tf_op jit(solution)/shard_map/all_to_all | solution.py:228
  118.8 8.1 %collective-permute-start.8 = (f32[256,128]{1,0:T(8,128)S(1)}, f32[256,128]{1,0:T(8,128)S(1)}, u32[]{:S(2)}, u32[]{:S(2)}) collective-permute-start(f32[256,128]{1,0:T(8,128)S(1)} %get-tuple-element.46.grad_sum.g0), channel_id=1, source_target_pairs={{0,2},{1,3},{2,0},{3,1},{4,6},{5,7},{6,4},{7,5},{8,10},{9,11},{10,... | collective-permute-start | bytes 393224 | tf_op jit(solution)/shard_map/ppermute | solution.py:225
  119.4 7.5 %collective-permute-start.7 = (f32[256,128]{1,0:T(8,128)S(1)}, f32[256,128]{1,0:T(8,128)S(1)}, u32[]{:S(2)}, u32[]{:S(2)}) collective-permute-start(f32[256,128]{1,0:T(8,128)S(1)} %get-tuple-element.46.grad_sum.g0), channel_id=1, source_target_pairs={{0,3},{1,0},{2,1},{3,2},{4,7},{5,4},{6,5},{7,6},{8,11},{9,8},{10,9... | collective-permute-start | bytes 393224 | tf_op jit(solution)/shard_map/ppermute | solution.py:225
  121.5 6.6 %collective-permute-start.13 = (f32[256,128]{1,0:T(8,128)}, f32[256,128]{1,0:T(8,128)S(1)}, u32[]{:S(2)}, u32[]{:S(2)}) collective-permute-start(f32[256,128]{1,0:T(8,128)} %collective-permute-done.10.g4), channel_id=1, source_target_pairs={{0,1},{1,2},{2,3},{3,0},{4,5},{5,6},{6,7},{7,4},{8,9},{9,10},{10,1... | collective-permute-start | bytes 393224 | tf_op jit(solution)/shard_map/ppermute | solution.py:225
  121.5 9.3 %collective-permute-start.12 = (f32[256,128]{1,0:T(8,128)}, f32[256,128]{1,0:T(8,128)S(1)}, u32[]{:S(2)}, u32[]{:S(2)}) collective-permute-start(f32[256,128]{1,0:T(8,128)} %collective-permute-done.10.g4), channel_id=1, source_target_pairs={{0,2},{1,3},{2,0},{3,1},{4,6},{5,7},{6,4},{7,5},{8,10},{9,11},{10,... | collective-permute-start | bytes 393224 | tf_op jit(solution)/shard_map/ppermute | solution.py:225
  124.0 8.1 %collective-permute-start.11 = (f32[256,128]{1,0:T(8,128)}, f32[256,128]{1,0:T(8,128)S(1)}, u32[]{:S(2)}, u32[]{:S(2)}) collective-permute-start(f32[256,128]{1,0:T(8,128)} %collective-permute-done.10.g4), channel_id=1, source_target_pairs={{0,3},{1,0},{2,1},{3,2},{4,7},{5,4},{6,5},{7,6},{8,11},{9,8},{10,9... | collective-permute-start | bytes 393224 | tf_op jit(solution)/shard_map/ppermute | solution.py:225
  137.8 27.5 %all-to-all-start.2 = ((f32[32,40,128]{2,1,0:T(8,128)}), f32[32,40,128]{2,1,0:T(8,128)S(1)}, u32[]{:S(2)}, u32[]{:S(2)}) async-start(f32[32,40,128]{2,1,0:T(8,128)} %get-tuple-element.54), calls=%async_computation.2 | async-start | bytes 1310720 | tf_op jit(solution)/shard_map/all_to_all | solution.py:228
  (14 other events, 14.4 us)

commit v2 on v1

v2 whole, which is shorter than its diff:
```python
import functools

import jax
import jax.numpy as jnp
from jax import lax
from jax.experimental import pallas as pl
from jax.experimental.pallas import tpu as pltpu
from jax.sharding import PartitionSpec as P

HIGH = lax.Precision.HIGHEST
F32, BF16, I32 = jnp.float32, jnp.bfloat16, jnp.int32
NT = (((1,), (1,)), ((), ()))
NN = (((1,), (0,)), ((), ()))
TN = (((0,), (0,)), ((), ()))


def dot(a, b, dims=NN, precision=None):
    return lax.dot_general(a, b, dims, precision=precision, preferred_element_type=F32)


def halves(x):
    high = x.astype(BF16)
    low = (x - high.astype(F32)).astype(BF16)
    return jnp.concatenate([high, low], axis=1)


def joined(y):
    n = y.shape[1] // 2
    return y[:, :n] + y[:, n:]


def one_hot(idx, rows):
    n = idx.shape[1]
    row = lax.broadcasted_iota(I32, (rows, n), 0)
    return jnp.where(row == idx, 1.0, 0.0).astype(BF16)


def lanes(ref_rows):
    return jnp.concatenate(ref_rows, axis=1)


def call(kernel, out_shape, args, specs=None, scratch=(), flops=1 << 28):
    whole = pl.BlockSpec(memory_space=pltpu.VMEM)
    size = sum(int(a.size) * a.dtype.itemsize for a in args)
    return pl.pallas_call(
        kernel,
        out_shape=out_shape,
        in_specs=[whole] * len(args) if specs is None else specs,
        out_specs=jax.tree.map(
            lambda s: pl.BlockSpec(memory_space=pltpu.SMEM if s.shape == (1,) else pltpu.VMEM), out_shape
        ),
        scratch_shapes=list(scratch),
        compiler_params=pltpu.CompilerParams(vmem_limit_bytes=16 << 20),
        cost_estimate=pl.CostEstimate(flops=flops, bytes_accessed=size, transcendentals=0),
    )(*args)


def shape(s, d=F32):
    return jax.ShapeDtypeStruct(s, d)


def expm1(x):
    series = x * (1 + x * (1 / 2) * (1 + x * (1 / 3) * (1 + x * (1 / 4) * (1 + x * (1 / 5) * (1 + x * (1 / 6) * (1 + x * (1 / 7)))))))
    return jnp.where(x > -0.35, series, jnp.exp(x) - 1.0)


def k_send(features, send, hub, out):
    x = halves(features[...])
    hot = lanes([one_hot(send[i : i + 1, :], 256) for i in range(8)])
    rows = joined(dot(hot, x, TN))
    out[:, 0:32, :] = rows.reshape(32, 32, 128)
    hub_rows = jnp.concatenate([features[pl.ds(hub[j], 1), :] for j in range(8)], axis=0)
    for p in range(32):
        out[p, 32:40, :] = hub_rows


def k_lists(pos, coord, edge, hub_to, hub_from, own_to, *outs):
    me = pos[0]
    for b in range(8):
        for t in range(6):
            own_to[b * 6 + t : b * 6 + t + 1, :] = edge[b, t, 0:1, :] + coord[b, 0, t] * 128
    for d in range(2):
        for k in range(4):
            b = jnp.bitwise_xor(me // 4, d) * 4 + (me % 4 + k) % 4
            at = d * 16
            for t in range(6):
                outs[k][at + t : at + t + 1, :] = edge[b, t, 0:1, :] + coord[b, 0, t] * 128
                outs[k][at + 6 + t : at + 7 + t, :] = edge[b, t, 1:2, :] + coord[b, 1, t] * 128
            outs[k][at + 12 : at + 14, :] = hub_to[...]
            outs[k][at + 14 : at + 16, :] = hub_from[...]


def hots(pos, block):
    me = pos[0]
    to = lanes([one_hot(block[i : i + 1, :], 256) for i in range(6)])
    frm = lanes([one_hot(block[i : i + 1, :], 256) for i in range(6, 12)])
    h_to = lanes([one_hot(block[i : i + 1, :], 256) for i in range(12, 14)])
    codes = [block[i : i + 1, :] for i in range(14, 16)]
    rows = [jnp.where((c >> 3) % 8 == me, (c >> 6) * 8 + c % 8, -1) for c in codes]
    return to, frm, h_to, lanes([one_hot(c, 256) for c in rows])


def blocks_of(lists):
    own, l1, l2, l3, far = lists
    return [ref[0:16, :] for ref in (own, l1, l2, l3)] + [far[16 * k : 16 * k + 16, :] for k in range(4)]


def halo_hots(halo_to, halo_from):
    to = lanes([one_hot(halo_to[i : i + 1, :], 256) for i in range(8)])
    return to, lanes([one_hot(halo_from[i : i + 1, :], 1024) for i in range(8)])


def rest(count):
    return (count - count.astype(BF16).astype(F32)).astype(BF16)


def forward_count(to, frm, h_to, h_frm):
    return jnp.concatenate([dot(to, frm, NT), dot(h_to, h_frm, NT)], axis=1)


def backward_count(to, frm, h_to, h_frm):
    return jnp.concatenate([dot(frm, to, NT), dot(h_frm, h_to, NT)], axis=0)


def k_fwd(pos, l0, l1, l2, l3, far, fwd, flag):
    top = jnp.float32(0.0)
    for r, block in enumerate(blocks_of((l0, l1, l2, l3, far))):
        count = forward_count(*hots(pos, block))
        top = jnp.maximum(top, jnp.max(count))
        fwd[r] = count.astype(BF16)
    flag[0] = (top > 256.0).astype(I32)


def k_bwd(pos, l0, l1, l2, l3, far, bwd):
    for r, block in enumerate(blocks_of((l0, l1, l2, l3, far))):
        bwd[r] = backward_count(*hots(pos, block)).astype(BF16)


def k_boundary(own_to, halo_to, halo_from, hub_to, h_fwd, h_bwd, inv, flag):
    to, frm = halo_hots(halo_to, halo_from)
    count = dot(to, frm, NT)
    h_fwd[...] = count.astype(BF16)
    h_bwd[...] = dot(frm, to, NT).astype(BF16)
    flag[0] = (jnp.max(count) > 256.0).astype(I32)
    row = lax.broadcasted_iota(I32, (256, 128), 0)
    degree = jnp.zeros((256, 128), F32)
    for ref, n in ((own_to, 48), (halo_to, 8), (hub_to, 2)):
        for i in range(n):
            degree = degree + jnp.where(row == ref[i : i + 1, :], 1.0, 0.0)
    degree = jnp.sum(degree, axis=1, keepdims=True)
    inv[...] = jnp.broadcast_to(1.0 / (degree + 1.0), (256, 128))


def k_partial(flag, pos, l0, l1, l2, l3, far, features, incoming, fwd, *outs):
    hubs = incoming[:, 32:40, :].reshape(256, 128)
    x = jnp.concatenate([halves(features[...]), halves(hubs)], axis=0)
    for r in range(8):
        outs[r][...] = joined(dot(fwd[r], x))

    @pl.when(flag[0] != 0)
    def _():
        for r, block in enumerate(blocks_of((l0, l1, l2, l3, far))):
            outs[r][...] += joined(dot(rest(forward_count(*hots(pos, block))), x))


def k_halo(flag, halo_to, halo_from, incoming, h_fwd, own, out):
    x = halves(incoming[:, 0:32, :].reshape(1024, 128))
    out[...] = own[...] + joined(dot(h_fwd[...], x))

    @pl.when(flag[0] != 0)
    def _():
        to, frm = halo_hots(halo_to, halo_from)
        out[...] += joined(dot(rest(dot(to, frm, NT)), x))


def k_layer(a0, a1, a2, a3, a4, inv, features, w_neigh, w_root, bias, grad_out,
            output, grad_pre, grad_sum, mean):
    scale = inv[...]
    m = (a0[...] + a1[...] + a2[...] + a3[...] + a4[...]) * scale
    mean[...] = m
    pre = dot(m, w_neigh[...], NN, HIGH) + dot(features[...], w_root[...], NN, HIGH) + bias[...]
    negative = jnp.minimum(pre, 0.0)
    output[...] = jnp.where(pre > 0, pre, expm1(negative))
    g = grad_out[...] * jnp.where(pre > 0, 1.0, jnp.exp(negative))
    grad_pre[...] = g
    grad_sum[...] = dot(g, w_neigh[...], NT, HIGH) * scale


def k_mid(flag, halo_to, halo_from, grad_sum, h_bwd, grad_pre, mean, features, out, held):
    x = halves(grad_sum[...])
    held[...] = joined(dot(h_bwd[...], x))

    @pl.when(flag[0] != 0)
    def _():
        to, frm = halo_hots(halo_to, halo_from)
        held[...] += joined(dot(rest(dot(frm, to, NT)), x))

    out[:, 0:32, :] = held[...].reshape(32, 32, 128)
    g = grad_pre[...]
    out[0:16, 32:40, :] = dot(mean[...], g, TN, HIGH).reshape(16, 8, 128)
    out[16:32, 32:40, :] = dot(features[...], g, TN, HIGH).reshape(16, 8, 128)
    fill = jnp.broadcast_to(jnp.sum(g, axis=0, keepdims=True), (8, 128))
    for p in range(32):
        out[p, 40:48, :] = fill


def k_back(flag, pos, l0, l1, l2, l3, far, g0, g1, g2, g3, g4, g5, g6, g7, bwd, intra, hubs, total):
    xs = [halves(g[...]) for g in (g0, g1, g2, g3, g4, g5, g6, g7)]
    acc = dot(bwd[0], xs[0])
    for r in range(1, 8):
        acc = acc + dot(bwd[r], xs[r])
    total[...] = joined(acc)

    @pl.when(flag[0] != 0)
    def _():
        for r, block in enumerate(blocks_of((l0, l1, l2, l3, far))):
            total[...] += joined(dot(rest(backward_count(*hots(pos, block))), xs[r]))

    hubs[...] = total[256:512, :].reshape(32, 8, 128)
    intra[...] = total[0:256, :]


def k_sum(returned, out):
    out[...] = jnp.sum(returned[:, 32:48, :], axis=0)


def k_pack(factor, hubs, near, far, out, bias):
    w = (near[...] + far[...]) * factor
    out[:, 0:8, :] = hubs[...]
    for p in range(32):
        out[p, 8:16, :] = w[0:8]
    bias[...] = w[8:9]


def k_slots(returned, send, intra, grad_pre, w_root, out):
    hot = lanes([one_hot(send[i : i + 1, :], 256) for i in range(8)])
    acc = joined(dot(hot, halves(returned[:, 0:32, :].reshape(1024, 128))))
    out[...] = intra[...] + dot(grad_pre[...], w_root[...], NT, HIGH) + acc


def k_final(final, hub, local, out, w_neigh, w_root):
    rows = jnp.sum(final[:, 0:8, :], axis=0)
    out[...] = local[...]
    for j in range(8):
        out[pl.ds(hub[j], 1), :] += rows[j : j + 1, :]
    w_neigh[...] = final[0:16, 8:16, :].reshape(128, 128)
    w_root[...] = final[16:32, 8:16, :].reshape(128, 128)


def per_device(features, w_neigh, w_root, bias, grad_out, tile_coord, tile_edge,
               send_idx, halo_dst, halo_src, hub_idx, hub_dst, hub_src):
    send = send_idx.reshape(8, 128)
    hub = hub_idx.reshape(8)
    hub_to = hub_dst.reshape(2, 128)
    hub_from = hub_src.reshape(2, 128)
    halo_to = halo_dst.reshape(8, 128)
    halo_from = halo_src.reshape(8, 128)
    pos = lax.axis_index("blk").astype(I32).reshape(1)
    block = shape((256, 128))

    def swap(v):
        return lax.ppermute(v, "blk", [(i, i ^ 4) for i in range(8)])

    def turn(v, k):
        return lax.ppermute(v, "blk", [(i, i // 4 * 4 + (i % 4 + k) % 4) for i in range(8)])

    def exchange(v, axis):
        return lax.all_to_all(v, axis, split_axis=0, concat_axis=0, tiled=True)

    vm, sm = (pl.BlockSpec(memory_space=s) for s in (pltpu.VMEM, pltpu.SMEM))

    outgoing = call(k_send, shape((32, 40, 128)), (features, send, hub), [vm, vm, sm])
    outgoing, coord = lax.optimization_barrier((outgoing, tile_coord.reshape(8, 2, 6)))
    incoming = exchange(outgoing, "grp")
    own_to, m0, m1, m2, m3 = call(
        k_lists, [shape((48, 128), I32)] + [shape((32, 128), I32)] * 4,
        (pos, coord, tile_edge.reshape(8, 6, 2, 128), hub_to, hub_from), [sm, sm, vm, vm, vm],
    )
    l3, l2, l1 = turn(m1, 1), turn(m2, 2), turn(m3, 3)
    far = swap(jnp.concatenate([m0[16:], l1[16:], l2[16:], l3[16:]], axis=0))
    lists = (pos, m0, l1, l2, l3, far)
    lm = [sm] + [vm] * 5
    h_fwd, h_bwd, inv, h_flag = call(
        k_boundary, (shape((256, 1024), BF16), shape((1024, 256), BF16), block, shape((1,), I32)),
        (own_to, halo_to, halo_from, hub_to), flops=1 << 31,
    )
    fwd, flag = call(k_fwd, (shape((8, 256, 512), BF16), shape((1,), I32)), lists, lm, flops=1 << 31)
    bwd = call(k_bwd, shape((8, 512, 256), BF16), lists, lm, flops=1 << 31)
    part = call(k_partial, [block] * 8, (flag, *lists, features, incoming, fwd), [sm, *lm, vm, vm, vm])
    other = part[4] + turn(part[5], 1) + turn(part[7], 3) + turn(part[6], 2)
    other = swap(other)
    near = [turn(part[1], 1), turn(part[3], 3), turn(part[2], 2)]
    own = call(k_halo, block, (h_flag, halo_to, halo_from, incoming, h_fwd, part[0]), [sm] + [vm] * 5)
    output, grad_pre, grad_sum, mean = call(
        k_layer, [block] * 4, (own, *near, other, inv, features, w_neigh, w_root, bias.reshape(1, 128), grad_out),
    )
    g4 = swap(grad_sum)
    g1, g3, g2 = turn(grad_sum, 3), turn(grad_sum, 1), turn(grad_sum, 2)
    mid = call(
        k_mid, shape((32, 48, 128)), (h_flag, halo_to, halo_from, grad_sum, h_bwd, grad_pre, mean, features),
        [sm] + [vm] * 7, [pltpu.VMEM((1024, 128), F32)],
    )
    returned = exchange(mid, "grp")
    g5, g7, g6 = turn(g4, 3), turn(g4, 1), turn(g4, 2)
    intra, hubs = call(
        k_back, [block, shape((32, 8, 128))],
        (flag, *lists, grad_sum, g1, g2, g3, g4, g5, g6, g7, bwd), [sm, *lm] + [vm] * 9,
        [pltpu.VMEM((512, 128), F32)],
    )
    returned, intra = lax.optimization_barrier((returned, intra))
    w = call(k_sum, shape((16, 128)), (returned,))
    w = w + turn(w, 1) + turn(w, 2) + turn(w, 3)
    factor = (256 * lax.axis_size("grp") * lax.axis_size("blk")) ** (-0.5)
    last, grad_bias = call(
        functools.partial(k_pack, factor), [shape((32, 16, 128)), shape((1, 128))], (hubs, w, swap(w))
    )
    last = exchange(last, "grp")
    local = call(k_slots, block, (returned, send, intra, grad_pre, w_root))
    grad_features, grad_wn, grad_wr = call(
        k_final, [block, shape((128, 128)), shape((128, 128))], (last, hub, local), [vm, sm, vm]
    )
    return output, grad_features, grad_wn, grad_wr, grad_bias.reshape(128)


def solution(mesh):
    rows = P(("grp", "blk"), None)
    in_specs = (
        rows, P(), P(), P(), rows,
        P("grp", "blk", None, None, None),
        P("grp", "blk", None, None, None, None),
        P("grp", "blk", None, None),
        P("grp", "blk", None), P("grp", "blk", None), P("grp", "blk", None), P("grp", "blk", None), P("grp", "blk", None),
    )
    return jax.shard_map(
        per_device, mesh=mesh, in_specs=in_specs, out_specs=(rows, rows, P(), P(), P()), check_vma=False
    )
```

time: 167 us -> 140 us (0.84)
  local copies, waits for them, and re-layouts: 21.5 us -> 2.52 us
  blocking collectives: 18.8 us -> 0 us
  starting transfers between devices: 58.8 us -> 67.1 us
  waiting for transfers between devices: 45.5 us -> 50.6 us
  other arithmetic: 4.03 us -> 0.04 us
    ppermute x2 -> x4, waiting for transfers between devices: 2.23 us -> 27.4 us  [swap(): return lax.ppermute(v, 'blk', [(i, i ^ 4) for i in range(8)])]
    all_to_all x5 -> x3, waiting for transfers between devices: 30.4 us -> 11.5 us  [exchange(): return lax.all_to_all(v, axis, split_axis=0, concat_axis=0, tiled=True)]
    all_to_all x1 -> x0, blocking collectives: 18.8 us -> none  [exchange(): return lax.all_to_all(v, axis, split_axis=0, concat_axis=0, tiled=True)]
    unnamed x55 -> x28, local copies, waits for them, and re-layouts: 16.4 us -> 1.62 us
    ppermute x12 -> x18, starting transfers between devices: 12.5 us -> 25.3 us  [turn(): lax.ppermute(v, 'blk', [(i, i // 4 * 4 + (i % 4 + k) % 4) for i in range(...]
    all_to_all x5 -> x3, starting transfers between devices: 40.4 us -> 28.2 us  [exchange(): return lax.all_to_all(v, axis, split_axis=0, concat_axis=0, tiled=True)]
    ppermute x2 -> x4, starting transfers between devices: 5.83 us -> 13.6 us  [swap(): return lax.ppermute(v, 'blk', [(i, i ^ 4) for i in range(8)])]
    broadcast_in_dim x4 -> x0, local copies, waits for them, and re-layouts: 2.66 us -> none  [the longest x1 0.68 us: per_device(): jnp.broadcast_to(hub_to[None], (8, 2, 128))]
  transfers between devices with their start and end apart: 19 -> 25, of which waited for: 14 -> 13; matrix products, arithmetic and copies ran while one was open for 3% -> 0% of each run, Pallas kernels for 8% -> 7%
where the time goes in v2:
time: 140 us
  starting transfers between devices  67.1 us (48%)
  waiting for transfers between devices  50.6 us (36%)
  Pallas kernels  18.4 us (13%)
  local copies, waits for them, and re-layouts  2.52 us (2%)
    all_to_all x3, starting transfers between devices, exchange(): return lax.all_to_all(v, axis, split_axis=0, concat_axis=0, tiled=True)  28.2 us
    ppermute x4, waiting for transfers between devices, swap(): return lax.ppermute(v, 'blk', [(i, i ^ 4) for i in range(8)])  27.4 us
    ppermute x18, starting transfers between devices, turn(): lax.ppermute(v, 'blk', [(i, i // 4 * 4 + (i % 4 + k) % 4) for i in range(...  25.3 us
    pallas_call x14, Pallas kernels, call(): pl.pallas_call(kernel, out_shape=out_shape, in_specs=[whole] * len(args)...  18.4 us
    ppermute x4, starting transfers between devices, swap(): return lax.ppermute(v, 'blk', [(i, i ^ 4) for i in range(8)])  13.6 us
    ppermute x18, waiting for transfers between devices, turn(): lax.ppermute(v, 'blk', [(i, i // 4 * 4 + (i % 4 + k) % 4) for i in range(...  11.7 us
    all_to_all x3, waiting for transfers between devices, exchange(): return lax.all_to_all(v, axis, split_axis=0, concat_axis=0, tiled=True)  11.5 us
  transfers between devices with their start and end apart: 25, of which 13 were waited for; matrix products, arithmetic and copies ran while one was open for 0% of the time, Pallas kernels for 7%

profile of v2, /device:TPU:1, one launch (start us, length us, event | category | flops | bytes accessed | tf_op | source)
XLA Modules:
  0.0 139.5 jit_solution(11096654726297940482)
XLA Ops:
  3.0 1.7 %shard_map.164 = f32[32,40,128]{2,1,0:T(8,128)} custom-call(f32[256,128]{1,0:T(8,128)S(1)} %copy-done, s32[8,128]{1,0:T(8,128)S(1)} %reshape.44.send, s32[8]{0:T(128)S(1)} %bitcast.23), custom_call_target="tpu_custom_call" | custom-call | flops 268435456 | bytes 135200 | tf_op jit(solution)/shard_map/pallas_call | solution.py:45
  4.8 10.0 %all-to-all-start = ((f32[32,40,128]{2,1,0:T(8,128)}), f32[32,40,128]{2,1,0:T(8,128)S(1)}, u32[]{:S(2)}, u32[]{:S(2)}) async-start(f32[32,40,128]{2,1,0:T(8,128)} %shard_map.164), calls=%async_computation | async-start | bytes 1310720 | tf_op jit(solution)/shard_map/all_to_all | solution.py:268
  15.7 2.8 %collective-permute-start = (s32[32,128]{1,0:T(8,128)S(1)}, s32[32,128]{1,0:T(8,128)S(1)}, u32[]{:S(2)}, u32[]{:S(2)}) collective-permute-start(s32[32,128]{1,0:T(8,128)S(1)} %get-tuple-element.45), channel_id=1, source_target_pairs={{0,3},{1,0},{2,1},{3,2},{4,7},{5,4},{6,5},{7,6},{8,11},{9,8},{10,9... | collective-permute-start | bytes 49160 | tf_op jit(solution)/shard_map/ppermute | solution.py:265
  19.6 3.3 %collective-permute-done.1.l2 = s32[32,128]{1,0:T(8,128)S(1)} collective-permute-done((s32[32,128]{1,0:T(8,128)S(1)}, s32[32,128]{1,0:T(8,128)S(1)}, u32[]{:S(2)}, u32[]{:S(2)}) %collective-permute-start.1) | collective-permute-done | bytes 16416 | tf_op jit(solution)/shard_map/ppermute | solution.py:265
  23.1 4.3 %collective-permute-start.3 = (s32[64,128]{1,0:T(8,128)S(1)}, s32[64,128]{1,0:T(8,128)S(1)}, u32[]{:S(2)}, u32[]{:S(2)}) collective-permute-start(s32[64,128]{1,0:T(8,128)S(1)} %pad_add_fusion), channel_id=1, source_target_pairs={{0,4},{1,5},{2,6},{3,7},{4,0},{5,1},{6,2},{7,3},{8,12},{9,13},{10,... | collective-permute-start | bytes 98312 | tf_op jit(solution)/shard_map/ppermute | solution.py:262
  27.4 3.8 %collective-permute-done.3.far = s32[64,128]{1,0:T(8,128)S(1)} collective-permute-done((s32[64,128]{1,0:T(8,128)S(1)}, s32[64,128]{1,0:T(8,128)S(1)}, u32[]{:S(2)}, u32[]{:S(2)}) %collective-permute-start.3) | collective-permute-done | bytes 32800 | tf_op jit(solution)/shard_map/ppermute | solution.py:262
  31.2 2.3 %shard_map.167 = (bf16[8,256,512]{2,1,0:T(8,128)(2,1)S(1)}, s32[1]{0:T(128)}) custom-call(s32[1]{0:T(128)} %bitcast.pos, s32[32,128]{1,0:T(8,128)S(1)} %get-tuple-element.44.l0, s32[32,128]{1,0:T(8,128)S(1)} %collective-permute-done.l1, s32[32,128]{1,0:T(8,128)S(1)} %collective-permute-done.1.l2, s32[32,128]{1,0:T(8,128)S(1)} %collective-permute-done.2.l3, ...), custom_call_target="tpu_custom_call" | custom-call | flops 2147483648 | bytes 98308 | tf_op jit(solution)/shard_map/pallas_call | solution.py:45
  34.5 1.4 shard_map.168
  35.8 2.1 %collective-permute-start.7 = (f32[256,128]{1,0:T(8,128)S(1)}, f32[256,128]{1,0:T(8,128)S(1)}, u32[]{:S(2)}, u32[]{:S(2)}) collective-permute-start(f32[256,128]{1,0:T(8,128)S(1)} %get-tuple-element.55), channel_id=1, source_target_pairs={{0,1},{1,2},{2,3},{3,0},{4,5},{5,6},{6,7},{7,4},{8,9},{9,10},{10,1... | collective-permute-start | bytes 393224 | tf_op jit(solution)/shard_map/ppermute | solution.py:265
  37.9 1.5 %collective-permute-start.8 = (f32[256,128]{1,0:T(8,128)S(1)}, f32[256,128]{1,0:T(8,128)S(1)}, u32[]{:S(2)}, u32[]{:S(2)}) collective-permute-start(f32[256,128]{1,0:T(8,128)S(1)} %get-tuple-element.56), channel_id=1, source_target_pairs={{0,3},{1,0},{2,1},{3,2},{4,7},{5,4},{6,5},{7,6},{8,11},{9,8},{10,9... | collective-permute-start | bytes 393224 | tf_op jit(solution)/shard_map/ppermute | solution.py:265
  39.4 1.6 %collective-permute-start.9 = (f32[256,128]{1,0:T(8,128)S(1)}, f32[256,128]{1,0:T(8,128)S(1)}, u32[]{:S(2)}, u32[]{:S(2)}) collective-permute-start(f32[256,128]{1,0:T(8,128)S(1)} %get-tuple-element.57), channel_id=1, source_target_pairs={{0,2},{1,3},{2,0},{3,1},{4,6},{5,7},{6,4},{7,5},{8,10},{9,11},{10,... | collective-permute-start | bytes 393224 | tf_op jit(solution)/shard_map/ppermute | solution.py:265
  41.4 2.3 %collective-permute-start.5 = (f32[256,128]{1,0:T(8,128)S(1)}, f32[256,128]{1,0:T(8,128)S(1)}, u32[]{:S(2)}, u32[]{:S(2)}) collective-permute-start(f32[256,128]{1,0:T(8,128)S(1)} %get-tuple-element.52), channel_id=1, source_target_pairs={{0,3},{1,0},{2,1},{3,2},{4,7},{5,4},{6,5},{7,6},{8,11},{9,8},{10,9... | collective-permute-start | bytes 393224 | tf_op jit(solution)/shard_map/ppermute | solution.py:265
  44.7 2.7 %collective-permute-done.9 = f32[256,128]{1,0:T(8,128)S(1)} collective-permute-done((f32[256,128]{1,0:T(8,128)S(1)}, f32[256,128]{1,0:T(8,128)S(1)}, u32[]{:S(2)}, u32[]{:S(2)}) %collective-permute-start.9) | collective-permute-done | bytes 131104 | tf_op jit(solution)/shard_map/ppermute | solution.py:265
  47.4 4.3 %collective-permute-start.10 = (f32[256,128]{1,0:T(8,128)S(1)}, f32[256,128]{1,0:T(8,128)S(1)}, u32[]{:S(2)}, u32[]{:S(2)}) collective-permute-start(f32[256,128]{1,0:T(8,128)S(1)} %add_add_fusion), channel_id=1, source_target_pairs={{0,4},{1,5},{2,6},{3,7},{4,0},{5,1},{6,2},{7,3},{8,12},{9,13},{10,... | collective-permute-start | bytes 393224 | tf_op jit(solution)/shard_map/ppermute | solution.py:262
  51.8 2.3 %shard_map.166 = (bf16[256,1024]{1,0:T(8,128)(2,1)S(1)}, bf16[1024,256]{1,0:T(8,128)(2,1)S(1)}, f32[256,128]{1,0:T(8,128)S(1)}, s32[1]{0:T(128)}) custom-call(s32[48,128]{1,0:T(8,128)S(1)} %get-tuple-element.40.own_to, s32[8,128]{1,0:T(8,128)S(1)} %bitcast.12, s32[8,128]{1,0:T(8,128)S(1)} %bitcast.15, s32[2,128]{1,0:T(2,128)S(1)} %bitcast.22), custom_call_target="tpu_custom_call" | custom-call | flops 2147483648 | bytes 33792 | tf_op jit(solution)/shard_map/pallas_call | solution.py:45
  55.1 2.4 %collective-permute-done.10.a4 = f32[256,128]{1,0:T(8,128)S(1)} collective-permute-done((f32[256,128]{1,0:T(8,128)S(1)}, f32[256,128]{1,0:T(8,128)S(1)}, u32[]{:S(2)}, u32[]{:S(2)}) %collective-permute-start.10) | collective-permute-done | bytes 131104 | tf_op jit(solution)/shard_map/ppermute | solution.py:262
  57.5 1.2 shard_map.170
  58.7 2.3 %shard_map.173 = f32[32,48,128]{2,1,0:T(8,128)} custom-call(s32[1]{0:T(128)} %get-tuple-element.41.flag, s32[8,128]{1,0:T(8,128)S(1)} %bitcast.14, s32[8,128]{1,0:T(8,128)S(1)} %bitcast.17, f32[256,128]{1,0:T(8,128)S(1)} %get-tuple-element.60.g0.grad_sum, bf16[1024,256]{1,0:T(8,128)(2,1)S(1)} %get-tuple-element.62.h_bwd, ...), custom_call_target="tpu_custom_call" | custom-call | flops 268435456 | bytes 1056772 | tf_op jit(solution)/shard_map/pallas_call | solution.py:45
  61.0 7.5 %all-to-all-start.1 = ((f32[32,48,128]{2,1,0:T(8,128)}), f32[32,48,128]{2,1,0:T(8,128)S(1)}, u32[]{:S(2)}, u32[]{:S(2)}) async-start(f32[32,48,128]{2,1,0:T(8,128)} %shard_map.173), calls=%async_computation.1 | async-start | bytes 1572864 | tf_op jit(solution)/shard_map/all_to_all | solution.py:268
  68.5 4.8 %collective-permute-start.14 = (f32[256,128]{1,0:T(8,128)S(1)}, f32[256,128]{1,0:T(8,128)S(1)}, u32[]{:S(2)}, u32[]{:S(2)}) collective-permute-start(f32[256,128]{1,0:T(8,128)S(1)} %get-tuple-element.60.g0.grad_sum), channel_id=1, source_target_pairs={{0,4},{1,5},{2,6},{3,7},{4,0},{5,1},{6,2},{7,3},{8,12},{9,13},{10,... | collective-permute-start | bytes 393224 | tf_op jit(solution)/shard_map/ppermute | solution.py:262
  74.3 2.3 %collective-permute-start.12 = (f32[256,128]{1,0:T(8,128)S(1)}, f32[256,128]{1,0:T(8,128)S(1)}, u32[]{:S(2)}, u32[]{:S(2)}) collective-permute-start(f32[256,128]{1,0:T(8,128)S(1)} %get-tuple-element.60.g0.grad_sum), channel_id=1, source_target_pairs={{0,2},{1,3},{2,0},{3,1},{4,6},{5,7},{6,4},{7,5},{8,10},{9,11},{10,... | collective-permute-start | bytes 393224 | tf_op jit(solution)/shard_map/ppermute | solution.py:265
  77.5 15.0 %collective-permute-done.14.g4 = f32[256,128]{1,0:T(8,128)S(1)} collective-permute-done((f32[256,128]{1,0:T(8,128)S(1)}, f32[256,128]{1,0:T(8,128)S(1)}, u32[]{:S(2)}, u32[]{:S(2)}) %collective-permute-start.14) | collective-permute-done | bytes 131104 | tf_op jit(solution)/shard_map/ppermute | solution.py:262
  93.6 2.3 %collective-permute-start.16 = (f32[256,128]{1,0:T(8,128)S(1)}, f32[256,128]{1,0:T(8,128)S(1)}, u32[]{:S(2)}, u32[]{:S(2)}) collective-permute-start(f32[256,128]{1,0:T(8,128)S(1)} %collective-permute-done.14.g4), channel_id=1, source_target_pairs={{0,2},{1,3},{2,0},{3,1},{4,6},{5,7},{6,4},{7,5},{8,10},{9,11},{10,... | collective-permute-start | bytes 393224 | tf_op jit(solution)/shard_map/ppermute | solution.py:265
  96.7 1.6 %shard_map.171.bwd = bf16[8,512,256]{2,1,0:T(8,128)(2,1)S(1)} custom-call(s32[1]{0:T(128)} %bitcast.pos, s32[32,128]{1,0:T(8,128)S(1)} %get-tuple-element.44.l0, s32[32,128]{1,0:T(8,128)S(1)} %collective-permute-done.l1, s32[32,128]{1,0:T(8,128)S(1)} %collective-permute-done.1.l2, s32[32,128]{1,0:T(8,128)S(1)} %collective-permute-done.2.l3, ...), custom_call_target="tpu_custom_call" | custom-call | flops 2147483648 | bytes 98308 | tf_op jit(solution)/shard_map/pallas_call | solution.py:45
  98.9 4.1 %collective-permute-done.17.g7 = f32[256,128]{1,0:T(8,128)S(1)} collective-permute-done((f32[256,128]{1,0:T(8,128)S(1)}, f32[256,128]{1,0:T(8,128)S(1)}, u32[]{:S(2)}, u32[]{:S(2)}) %collective-permute-start.17) | collective-permute-done | bytes 131104 | tf_op jit(solution)/shard_map/ppermute | solution.py:265
  103.0 1.4 shard_map.172
  104.7 1.9 %collective-permute-start.19 = (f32[16,128]{1,0:T(8,128)S(1)}, f32[16,128]{1,0:T(8,128)S(1)}, u32[]{:S(2)}, u32[]{:S(2)}) collective-permute-start(f32[16,128]{1,0:T(8,128)S(1)} %shard_map.174), channel_id=1, source_target_pairs={{0,2},{1,3},{2,0},{3,1},{4,6},{5,7},{6,4},{7,5},{8,10},{9,11},{10,... | collective-permute-start | bytes 24584 | tf_op jit(solution)/shard_map/ppermute | solution.py:265
  106.5 2.0 %collective-permute-start.20 = (f32[16,128]{1,0:T(8,128)S(1)}, f32[16,128]{1,0:T(8,128)S(1)}, u32[]{:S(2)}, u32[]{:S(2)}) collective-permute-start(f32[16,128]{1,0:T(8,128)S(1)} %shard_map.174), channel_id=1, source_target_pairs={{0,3},{1,0},{2,1},{3,2},{4,7},{5,4},{6,5},{7,6},{8,11},{9,8},{10,9... | collective-permute-start | bytes 24584 | tf_op jit(solution)/shard_map/ppermute | solution.py:265
  109.5 6.2 %collective-permute-done.21.far = f32[16,128]{1,0:T(8,128)S(1)} collective-permute-done((f32[16,128]{1,0:T(8,128)S(1)}, f32[16,128]{1,0:T(8,128)S(1)}, u32[]{:S(2)}, u32[]{:S(2)}) %collective-permute-start.21) | collective-permute-done | bytes 8224 | tf_op jit(solution)/shard_map/ppermute | solution.py:262
  116.5 10.7 %all-to-all-start.2 = ((f32[32,16,128]{2,1,0:T(8,128)}), f32[32,16,128]{2,1,0:T(8,128)S(1)}, u32[]{:S(2)}, u32[]{:S(2)}) async-start(f32[32,16,128]{2,1,0:T(8,128)} %get-tuple-element.67), calls=%async_computation.2 | async-start | bytes 524288 | tf_op jit(solution)/shard_map/all_to_all | solution.py:268
  127.6 10.7 %all-to-all-done.2.final = f32[32,16,128]{2,1,0:T(8,128)S(1)} async-done(((f32[32,16,128]{2,1,0:T(8,128)}), f32[32,16,128]{2,1,0:T(8,128)S(1)}, u32[]{:S(2)}, u32[]{:S(2)}) %all-to-all-start.2) | async-done | bytes 262176 | tf_op jit(solution)/shard_map/all_to_all | solution.py:268
  138.3 1.3 shard_map.177
  (69 shorter events, 14.7 us)
Async XLA Ops:
  0.6 14.2 %copy-start.13 = (s32[1,1,8,2,6]{2,3,4,1,0:T(2,128)S(1)}, s32[1,1,8,2,6]{2,3,4,1,0:T(2,128)}, u32[]{:S(2)}) copy-start(s32[1,1,8,2,6]{2,3,4,1,0:T(2,128)} %param.18) | copy-start | bytes 1156
  0.6 14.3 %copy-start.10 = (s32[1,1,256]{2,1,0:T(1,128)S(1)}, s32[1,1,256]{2,1,0:T(1,128)}, u32[]{:S(2)}) copy-start(s32[1,1,256]{2,1,0:T(1,128)} %param.24) | copy-start | bytes 3076
  0.7 14.3 %copy-start.9 = (s32[1,1,256]{2,1,0:T(1,128)S(1)}, s32[1,1,256]{2,1,0:T(1,128)}, u32[]{:S(2)}) copy-start(s32[1,1,256]{2,1,0:T(1,128)} %param.25) | copy-start | bytes 3076
  3.0 11.9 %copy-start.8 = (s32[1,1,8,6,2,128]{5,4,3,2,1,0:T(2,128)S(1)}, s32[1,1,8,6,2,128]{5,4,3,2,1,0:T(2,128)}, u32[]{:S(2)}) copy-start(s32[1,1,8,6,2,128]{5,4,3,2,1,0:T(2,128)} %param.19) | copy-start | bytes 147460
  4.8 29.7 %all-to-all-start = ((f32[32,40,128]{2,1,0:T(8,128)}), f32[32,40,128]{2,1,0:T(8,128)S(1)}, u32[]{:S(2)}, u32[]{:S(2)}) async-start(f32[32,40,128]{2,1,0:T(8,128)} %shard_map.164), calls=%async_computation | async-start | bytes 1310720 | tf_op jit(solution)/shard_map/all_to_all | solution.py:268
  15.7 3.9 %collective-permute-start = (s32[32,128]{1,0:T(8,128)S(1)}, s32[32,128]{1,0:T(8,128)S(1)}, u32[]{:S(2)}, u32[]{:S(2)}) collective-permute-start(s32[32,128]{1,0:T(8,128)S(1)} %get-tuple-element.45), channel_id=1, source_target_pairs={{0,3},{1,0},{2,1},{3,2},{4,7},{5,4},{6,5},{7,6},{8,11},{9,8},{10,9... | collective-permute-start | bytes 49160 | tf_op jit(solution)/shard_map/ppermute | solution.py:265
  18.5 4.4 %collective-permute-start.1 = (s32[32,128]{1,0:T(8,128)S(1)}, s32[32,128]{1,0:T(8,128)S(1)}, u32[]{:S(2)}, u32[]{:S(2)}) collective-permute-start(s32[32,128]{1,0:T(8,128)S(1)} %get-tuple-element.46), channel_id=1, source_target_pairs={{0,2},{1,3},{2,0},{3,1},{4,6},{5,7},{6,4},{7,5},{8,10},{9,11},{10,... | collective-permute-start | bytes 49160 | tf_op jit(solution)/shard_map/ppermute | solution.py:265
  18.9 4.2 %collective-permute-start.2 = (s32[32,128]{1,0:T(8,128)S(1)}, s32[32,128]{1,0:T(8,128)S(1)}, u32[]{:S(2)}, u32[]{:S(2)}) collective-permute-start(s32[32,128]{1,0:T(8,128)S(1)} %get-tuple-element.47), channel_id=1, source_target_pairs={{0,1},{1,2},{2,3},{3,0},{4,5},{5,6},{6,7},{7,4},{8,9},{9,10},{10,1... | collective-permute-start | bytes 49160 | tf_op jit(solution)/shard_map/ppermute | solution.py:265
  23.1 8.1 %collective-permute-start.3 = (s32[64,128]{1,0:T(8,128)S(1)}, s32[64,128]{1,0:T(8,128)S(1)}, u32[]{:S(2)}, u32[]{:S(2)}) collective-permute-start(s32[64,128]{1,0:T(8,128)S(1)} %pad_add_fusion), channel_id=1, source_target_pairs={{0,4},{1,5},{2,6},{3,7},{4,0},{5,1},{6,2},{7,3},{8,12},{9,13},{10,... | collective-permute-start | bytes 98312 | tf_op jit(solution)/shard_map/ppermute | solution.py:262
  33.6 18.2 %copy-start.5 = (s32[1,1,1024]{2,1,0:T(1,128)S(1)}, s32[1,1,1024]{2,1,0:T(1,128)}, u32[]{:S(2)}) copy-start(s32[1,1,1024]{2,1,0:T(1,128)} %param.21) | copy-start | bytes 12292
  33.6 18.2 %copy-start.6 = (s32[1,1,1024]{2,1,0:T(1,128)S(1)}, s32[1,1,1024]{2,1,0:T(1,128)}, u32[]{:S(2)}) copy-start(s32[1,1,1024]{2,1,0:T(1,128)} %param.22) | copy-start | bytes 12292
  35.8 7.8 %collective-permute-start.7 = (f32[256,128]{1,0:T(8,128)S(1)}, f32[256,128]{1,0:T(8,128)S(1)}, u32[]{:S(2)}, u32[]{:S(2)}) collective-permute-start(f32[256,128]{1,0:T(8,128)S(1)} %get-tuple-element.55), channel_id=1, source_target_pairs={{0,1},{1,2},{2,3},{3,0},{4,5},{5,6},{6,7},{7,4},{8,9},{9,10},{10,1... | collective-permute-start | bytes 393224 | tf_op jit(solution)/shard_map/ppermute | solution.py:265
  37.9 6.8 %collective-permute-start.8 = (f32[256,128]{1,0:T(8,128)S(1)}, f32[256,128]{1,0:T(8,128)S(1)}, u32[]{:S(2)}, u32[]{:S(2)}) collective-permute-start(f32[256,128]{1,0:T(8,128)S(1)} %get-tuple-element.56), channel_id=1, source_target_pairs={{0,3},{1,0},{2,1},{3,2},{4,7},{5,4},{6,5},{7,6},{8,11},{9,8},{10,9... | collective-permute-start | bytes 393224 | tf_op jit(solution)/shard_map/ppermute | solution.py:265
  39.4 8.0 %collective-permute-start.9 = (f32[256,128]{1,0:T(8,128)S(1)}, f32[256,128]{1,0:T(8,128)S(1)}, u32[]{:S(2)}, u32[]{:S(2)}) collective-permute-start(f32[256,128]{1,0:T(8,128)S(1)} %get-tuple-element.57), channel_id=1, source_target_pairs={{0,2},{1,3},{2,0},{3,1},{4,6},{5,7},{6,4},{7,5},{8,10},{9,11},{10,... | collective-permute-start | bytes 393224 | tf_op jit(solution)/shard_map/ppermute | solution.py:265
  41.0 14.1 %collective-permute-start.4 = (f32[256,128]{1,0:T(8,128)S(1)}, f32[256,128]{1,0:T(8,128)S(1)}, u32[]{:S(2)}, u32[]{:S(2)}) collective-permute-start(f32[256,128]{1,0:T(8,128)S(1)} %get-tuple-element.51), channel_id=1, source_target_pairs={{0,1},{1,2},{2,3},{3,0},{4,5},{5,6},{6,7},{7,4},{8,9},{9,10},{10,1... | collective-permute-start | bytes 393224 | tf_op jit(solution)/shard_map/ppermute | solution.py:265
  41.4 13.7 %collective-permute-start.5 = (f32[256,128]{1,0:T(8,128)S(1)}, f32[256,128]{1,0:T(8,128)S(1)}, u32[]{:S(2)}, u32[]{:S(2)}) collective-permute-start(f32[256,128]{1,0:T(8,128)S(1)} %get-tuple-element.52), channel_id=1, source_target_pairs={{0,3},{1,0},{2,1},{3,2},{4,7},{5,4},{6,5},{7,6},{8,11},{9,8},{10,9... | collective-permute-start | bytes 393224 | tf_op jit(solution)/shard_map/ppermute | solution.py:265
  43.7 11.4 %collective-permute-start.6 = (f32[256,128]{1,0:T(8,128)S(1)}, f32[256,128]{1,0:T(8,128)S(1)}, u32[]{:S(2)}, u32[]{:S(2)}) collective-permute-start(f32[256,128]{1,0:T(8,128)S(1)} %get-tuple-element.53), channel_id=1, source_target_pairs={{0,2},{1,3},{2,0},{3,1},{4,6},{5,7},{6,4},{7,5},{8,10},{9,11},{10,... | collective-permute-start | bytes 393224 | tf_op jit(solution)/shard_map/ppermute | solution.py:265
  47.4 10.0 %collective-permute-start.10 = (f32[256,128]{1,0:T(8,128)S(1)}, f32[256,128]{1,0:T(8,128)S(1)}, u32[]{:S(2)}, u32[]{:S(2)}) collective-permute-start(f32[256,128]{1,0:T(8,128)S(1)} %add_add_fusion), channel_id=1, source_target_pairs={{0,4},{1,5},{2,6},{3,7},{4,0},{5,1},{6,2},{7,3},{8,12},{9,13},{10,... | collective-permute-start | bytes 393224 | tf_op jit(solution)/shard_map/ppermute | solution.py:262
  61.0 43.4 %all-to-all-start.1 = ((f32[32,48,128]{2,1,0:T(8,128)}), f32[32,48,128]{2,1,0:T(8,128)S(1)}, u32[]{:S(2)}, u32[]{:S(2)}) async-start(f32[32,48,128]{2,1,0:T(8,128)} %shard_map.173), calls=%async_computation.1 | async-start | bytes 1572864 | tf_op jit(solution)/shard_map/all_to_all | solution.py:268
  68.5 24.0 %collective-permute-start.14 = (f32[256,128]{1,0:T(8,128)S(1)}, f32[256,128]{1,0:T(8,128)S(1)}, u32[]{:S(2)}, u32[]{:S(2)}) collective-permute-start(f32[256,128]{1,0:T(8,128)S(1)} %get-tuple-element.60.g0.grad_sum), channel_id=1, source_target_pairs={{0,4},{1,5},{2,6},{3,7},{4,0},{5,1},{6,2},{7,3},{8,12},{9,13},{10,... | collective-permute-start | bytes 393224 | tf_op jit(solution)/shard_map/ppermute | solution.py:262
  73.3 22.6 %collective-permute-start.11 = (f32[256,128]{1,0:T(8,128)S(1)}, f32[256,128]{1,0:T(8,128)S(1)}, u32[]{:S(2)}, u32[]{:S(2)}) collective-permute-start(f32[256,128]{1,0:T(8,128)S(1)} %get-tuple-element.60.g0.grad_sum), channel_id=1, source_target_pairs={{0,3},{1,0},{2,1},{3,2},{4,7},{5,4},{6,5},{7,6},{8,11},{9,8},{10,9... | collective-permute-start | bytes 393224 | tf_op jit(solution)/shard_map/ppermute | solution.py:265
  74.3 24.0 %collective-permute-start.12 = (f32[256,128]{1,0:T(8,128)S(1)}, f32[256,128]{1,0:T(8,128)S(1)}, u32[]{:S(2)}, u32[]{:S(2)}) collective-permute-start(f32[256,128]{1,0:T(8,128)S(1)} %get-tuple-element.60.g0.grad_sum), channel_id=1, source_target_pairs={{0,2},{1,3},{2,0},{3,1},{4,6},{5,7},{6,4},{7,5},{8,10},{9,11},{10,... | collective-permute-start | bytes 393224 | tf_op jit(solution)/shard_map/ppermute | solution.py:265
  76.7 21.7 %collective-permute-start.13 = (f32[256,128]{1,0:T(8,128)S(1)}, f32[256,128]{1,0:T(8,128)S(1)}, u32[]{:S(2)}, u32[]{:S(2)}) collective-permute-start(f32[256,128]{1,0:T(8,128)S(1)} %get-tuple-element.60.g0.grad_sum), channel_id=1, source_target_pairs={{0,1},{1,2},{2,3},{3,0},{4,5},{5,6},{6,7},{7,4},{8,9},{9,10},{10,1... | collective-permute-start | bytes 393224 | tf_op jit(solution)/shard_map/ppermute | solution.py:265
  92.5 5.8 %collective-permute-start.15 = (f32[256,128]{1,0:T(8,128)S(1)}, f32[256,128]{1,0:T(8,128)S(1)}, u32[]{:S(2)}, u32[]{:S(2)}) collective-permute-start(f32[256,128]{1,0:T(8,128)S(1)} %collective-permute-done.14.g4), channel_id=1, source_target_pairs={{0,3},{1,0},{2,1},{3,2},{4,7},{5,4},{6,5},{7,6},{8,11},{9,8},{10,9... | collective-permute-start | bytes 393224 | tf_op jit(solution)/shard_map/ppermute | solution.py:265
  93.6 5.3 %collective-permute-start.16 = (f32[256,128]{1,0:T(8,128)S(1)}, f32[256,128]{1,0:T(8,128)S(1)}, u32[]{:S(2)}, u32[]{:S(2)}) collective-permute-start(f32[256,128]{1,0:T(8,128)S(1)} %collective-permute-done.14.g4), channel_id=1, source_target_pairs={{0,2},{1,3},{2,0},{3,1},{4,6},{5,7},{6,4},{7,5},{8,10},{9,11},{10,... | collective-permute-start | bytes 393224 | tf_op jit(solution)/shard_map/ppermute | solution.py:265
  95.9 7.1 %collective-permute-start.17 = (f32[256,128]{1,0:T(8,128)S(1)}, f32[256,128]{1,0:T(8,128)S(1)}, u32[]{:S(2)}, u32[]{:S(2)}) collective-permute-start(f32[256,128]{1,0:T(8,128)S(1)} %collective-permute-done.14.g4), channel_id=1, source_target_pairs={{0,1},{1,2},{2,3},{3,0},{4,5},{5,6},{6,7},{7,4},{8,9},{9,10},{10,1... | collective-permute-start | bytes 393224 | tf_op jit(solution)/shard_map/ppermute | solution.py:265
  104.4 33.9 %copy-start.12 = (s32[1,1,8]{2,1,0:T(1,128)S(1)}, s32[1,1,8]{2,1,0:T(1,128)}, u32[]{:S(2)}) copy-start(s32[1,1,8]{2,1,0:T(1,128)} %param.23) | copy-start | bytes 100
  104.4 4.1 %collective-permute-start.18 = (f32[16,128]{1,0:T(8,128)S(1)}, f32[16,128]{1,0:T(8,128)S(1)}, u32[]{:S(2)}, u32[]{:S(2)}) collective-permute-start(f32[16,128]{1,0:T(8,128)S(1)} %shard_map.174), channel_id=1, source_target_pairs={{0,1},{1,2},{2,3},{3,0},{4,5},{5,6},{6,7},{7,4},{8,9},{9,10},{10,1... | collective-permute-start | bytes 24584 | tf_op jit(solution)/shard_map/ppermute | solution.py:265
  104.7 4.0 %collective-permute-start.19 = (f32[16,128]{1,0:T(8,128)S(1)}, f32[16,128]{1,0:T(8,128)S(1)}, u32[]{:S(2)}, u32[]{:S(2)}) collective-permute-start(f32[16,128]{1,0:T(8,128)S(1)} %shard_map.174), channel_id=1, source_target_pairs={{0,2},{1,3},{2,0},{3,1},{4,6},{5,7},{6,4},{7,5},{8,10},{9,11},{10,... | collective-permute-start | bytes 24584 | tf_op jit(solution)/shard_map/ppermute | solution.py:265
  106.5 2.8 %collective-permute-start.20 = (f32[16,128]{1,0:T(8,128)S(1)}, f32[16,128]{1,0:T(8,128)S(1)}, u32[]{:S(2)}, u32[]{:S(2)}) collective-permute-start(f32[16,128]{1,0:T(8,128)S(1)} %shard_map.174), channel_id=1, source_target_pairs={{0,3},{1,0},{2,1},{3,2},{4,7},{5,4},{6,5},{7,6},{8,11},{9,8},{10,9... | collective-permute-start | bytes 24584 | tf_op jit(solution)/shard_map/ppermute | solution.py:265
  109.3 6.4 %collective-permute-start.21 = (f32[16,128]{1,0:T(8,128)S(1)}, f32[16,128]{1,0:T(8,128)S(1)}, u32[]{:S(2)}, u32[]{:S(2)}) collective-permute-start(f32[16,128]{1,0:T(8,128)S(1)} %add_add_fusion.1.near), channel_id=1, source_target_pairs={{0,4},{1,5},{2,6},{3,7},{4,0},{5,1},{6,2},{7,3},{8,12},{9,13},{10,... | collective-permute-start | bytes 24584 | tf_op jit(solution)/shard_map/ppermute | solution.py:262
  116.5 21.8 %all-to-all-start.2 = ((f32[32,16,128]{2,1,0:T(8,128)}), f32[32,16,128]{2,1,0:T(8,128)S(1)}, u32[]{:S(2)}, u32[]{:S(2)}) async-start(f32[32,16,128]{2,1,0:T(8,128)} %get-tuple-element.67), calls=%async_computation.2 | async-start | bytes 524288 | tf_op jit(solution)/shard_map/all_to_all | solution.py:268
  (7 other events, 35.8 us)

commit v3 on v2

--- a/solution.py
+++ b/solution.py
@@ -186,25 +186,27 @@
     grad_sum[...] = dot(g, w_neigh[...], NT, HIGH) * scale
 
 
-def k_mid(flag, halo_to, halo_from, grad_sum, h_bwd, grad_pre, mean, features, out, held):
+def k_weights(grad_pre, mean, features, out):
+    g = grad_pre[...]
+    out[0:16, 0:8, :] = dot(mean[...], g, TN, HIGH).reshape(16, 8, 128)
+    out[16:32, 0:8, :] = dot(features[...], g, TN, HIGH).reshape(16, 8, 128)
+    fill = jnp.broadcast_to(jnp.sum(g, axis=0, keepdims=True), (8, 128))
+    for p in range(32):
+        out[p, 8:16, :] = fill
+
+
+def k_slots(flag, halo_to, halo_from, grad_sum, h_bwd, grad_pre, w_root, out, root):
     x = halves(grad_sum[...])
-    held[...] = joined(dot(h_bwd[...], x))
+    out[...] = joined(dot(h_bwd[...], x))
+    root[...] = dot(grad_pre[...], w_root[...], NT, HIGH)
 
     @pl.when(flag[0] != 0)
     def _():
         to, frm = halo_hots(halo_to, halo_from)
-        held[...] += joined(dot(rest(dot(frm, to, NT)), x))
-
-    out[:, 0:32, :] = held[...].reshape(32, 32, 128)
-    g = grad_pre[...]
-    out[0:16, 32:40, :] = dot(mean[...], g, TN, HIGH).reshape(16, 8, 128)
-    out[16:32, 32:40, :] = dot(features[...], g, TN, HIGH).reshape(16, 8, 128)
-    fill = jnp.broadcast_to(jnp.sum(g, axis=0, keepdims=True), (8, 128))
-    for p in range(32):
-        out[p, 40:48, :] = fill
-
-
-def k_back(flag, pos, l0, l1, l2, l3, far, g0, g1, g2, g3, g4, g5, g6, g7, bwd, intra, hubs, total):
+        out[...] += joined(dot(rest(dot(frm, to, NT)), x))
+
+
+def k_back(flag, pos, l0, l1, l2, l3, far, g0, g1, g2, g3, g4, g5, g6, g7, bwd, root, local, hubs, total):
     xs = [halves(g[...]) for g in (g0, g1, g2, g3, g4, g5, g6, g7)]
     acc = dot(bwd[0], xs[0])
     for r in range(1, 8):
@@ -217,34 +219,31 @@
             total[...] += joined(dot(rest(backward_count(*hots(pos, block))), xs[r]))
 
     hubs[...] = total[256:512, :].reshape(32, 8, 128)
-    intra[...] = total[0:256, :]
-
-
-def k_sum(returned, out):
-    out[...] = jnp.sum(returned[:, 32:48, :], axis=0)
-
-
-def k_pack(factor, hubs, near, far, out, bias):
+    local[...] = root[...] + total[0:256, :]
+
+
+def k_sum(weights, out):
+    out[...] = jnp.sum(weights[...], axis=0)
+
+
+def k_pack(factor, slots, hubs, near, far, out, bias):
     w = (near[...] + far[...]) * factor
-    out[:, 0:8, :] = hubs[...]
+    out[:, 0:32, :] = slots[...].reshape(32, 32, 128)
+    out[:, 32:40, :] = hubs[...]
     for p in range(32):
-        out[p, 8:16, :] = w[0:8]
+        out[p, 40:48, :] = w[0:8]
     bias[...] = w[8:9]
 
 
-def k_slots(returned, send, intra, grad_pre, w_root, out):
+def k_final(returned, send, hub, local, out, w_neigh, w_root):
     hot = lanes([one_hot(send[i : i + 1, :], 256) for i in range(8)])
     acc = joined(dot(hot, halves(returned[:, 0:32, :].reshape(1024, 128))))
-    out[...] = intra[...] + dot(grad_pre[...], w_root[...], NT, HIGH) + acc
-
-
-def k_final(final, hub, local, out, w_neigh, w_root):
-    rows = jnp.sum(final[:, 0:8, :], axis=0)
-    out[...] = local[...]
+    rows = jnp.sum(returned[:, 32:40, :], axis=0)
+    out[...] = local[...] + acc
     for j in range(8):
         out[pl.ds(hub[j], 1), :] += rows[j : j + 1, :]
-    w_neigh[...] = final[0:16, 8:16, :].reshape(128, 128)
-    w_root[...] = final[16:32, 8:16, :].reshape(128, 128)
+    w_neigh[...] = returned[0:16, 40:48, :].reshape(128, 128)
+    w_root[...] = returned[16:32, 40:48, :].reshape(128, 128)
 
 
 def per_device(features, w_neigh, w_root, bias, grad_out, tile_coord, tile_edge,
@@ -288,36 +287,37 @@
     bwd = call(k_bwd, shape((8, 512, 256), BF16), lists, lm, flops=1 << 31)
     part = call(k_partial, [block] * 8, (flag, *lists, features, incoming, fwd), [sm, *lm, vm, vm, vm])
     other = part[4] + turn(part[5], 1) + turn(part[7], 3) + turn(part[6], 2)
+    other, p1, p2, p3 = lax.optimization_barrier((other, part[1], part[2], part[3]))
     other = swap(other)
-    near = [turn(part[1], 1), turn(part[3], 3), turn(part[2], 2)]
+    near = [turn(p1, 1), turn(p3, 3), turn(p2, 2)]
     own = call(k_halo, block, (h_flag, halo_to, halo_from, incoming, h_fwd, part[0]), [sm] + [vm] * 5)
+    inv, bwd = lax.optimization_barrier((inv, bwd))
     output, grad_pre, grad_sum, mean = call(
-        k_layer, [block] * 4, (own, *near, other, inv, features, w_neigh, w_root, bias.reshape(1, 128), grad_out),
+        k_layer, [block] * 4, (own, other, *near, inv, features, w_neigh, w_root, bias.reshape(1, 128), grad_out),
     )
     g4 = swap(grad_sum)
     g1, g3, g2 = turn(grad_sum, 3), turn(grad_sum, 1), turn(grad_sum, 2)
-    mid = call(
-        k_mid, shape((32, 48, 128)), (h_flag, halo_to, halo_from, grad_sum, h_bwd, grad_pre, mean, features),
-        [sm] + [vm] * 7, [pltpu.VMEM((1024, 128), F32)],
-    )
-    returned = exchange(mid, "grp")
+    weights = exchange(call(k_weights, shape((32, 16, 128)), (grad_pre, mean, features)), "grp")
+    slots, root = call(
+        k_slots, [shape((1024, 128)), block], (h_flag, halo_to, halo_from, grad_sum, h_bwd, grad_pre, w_root),
+        [sm] + [vm] * 6,
+    )
     g5, g7, g6 = turn(g4, 3), turn(g4, 1), turn(g4, 2)
-    intra, hubs = call(
+    w = call(k_sum, shape((16, 128)), (weights,))
+    w = w + turn(w, 1) + turn(w, 2) + turn(w, 3)
+    w_far = swap(w)
+    local, hubs = call(
         k_back, [block, shape((32, 8, 128))],
-        (flag, *lists, grad_sum, g1, g2, g3, g4, g5, g6, g7, bwd), [sm, *lm] + [vm] * 9,
+        (flag, *lists, grad_sum, g1, g2, g3, g4, g5, g6, g7, bwd, root), [sm, *lm] + [vm] * 10,
         [pltpu.VMEM((512, 128), F32)],
     )
-    returned, intra = lax.optimization_barrier((returned, intra))
-    w = call(k_sum, shape((16, 128)), (returned,))
-    w = w + turn(w, 1) + turn(w, 2) + turn(w, 3)
     factor = (256 * lax.axis_size("grp") * lax.axis_size("blk")) ** (-0.5)
-    last, grad_bias = call(
-        functools.partial(k_pack, factor), [shape((32, 16, 128)), shape((1, 128))], (hubs, w, swap(w))
-    )
-    last = exchange(last, "grp")
-    local = call(k_slots, block, (returned, send, intra, grad_pre, w_root))
+    back, grad_bias = call(
+        functools.partial(k_pack, factor), [shape((32, 48, 128)), shape((1, 128))], (slots, hubs, w, w_far)
+    )
+    returned = exchange(back, "grp")
     grad_features, grad_wn, grad_wr = call(
-        k_final, [block, shape((128, 128)), shape((128, 128))], (last, hub, local), [vm, sm, vm]
+        k_final, [block, shape((128, 128)), shape((128, 128))], (returned, send, hub, local), [vm, vm, sm, vm]
     )
     return output, grad_features, grad_wn, grad_wr, grad_bias.reshape(128)
 

time: 140 us -> 135 us (0.964)
  blocking collectives: 0 us -> 25 us
  waiting for transfers between devices: 50.6 us -> 31.8 us
  starting transfers between devices: 67.1 us -> 55.1 us
    all_to_all x0 -> x1, blocking collectives: none -> 25 us  [exchange(): return lax.all_to_all(v, axis, split_axis=0, concat_axis=0, tiled=True)]
    ppermute x4, waiting for transfers between devices: 27.4 us -> 4.33 us  [swap(): return lax.ppermute(v, 'blk', [(i, i ^ 4) for i in range(8)])]
    all_to_all x3 -> x2, starting transfers between devices: 28.2 us -> 17.6 us  [exchange(): return lax.all_to_all(v, axis, split_axis=0, concat_axis=0, tiled=True)]
    all_to_all x3 -> x2, waiting for transfers between devices: 11.5 us -> 13.9 us  [exchange(): return lax.all_to_all(v, axis, split_axis=0, concat_axis=0, tiled=True)]
    ppermute x18, waiting for transfers between devices: 11.7 us -> 13.6 us  [turn(): lax.ppermute(v, 'blk', [(i, i // 4 * 4 + (i % 4 + k) % 4) for i in range(...]
  transfers between devices with their start and end apart: 25 -> 24, of which waited for: 13 -> 12; matrix products, arithmetic and copies ran while one was open for 0% -> 0% of each run, Pallas kernels for 7% -> 8%
where the time goes in v3:
time: 135 us; the launch traced here: 134 us
  starting transfers between devices  55.1 us (41%)
  waiting for transfers between devices  31.8 us (24%)
  blocking collectives  25 us (19%)
  Pallas kernels  18.1 us (13%)
  local copies, waits for them, and re-layouts  3.57 us (3%)
    all_to_all x1, blocking collectives, exchange(): return lax.all_to_all(v, axis, split_axis=0, concat_axis=0, tiled=True)  25 us
    ppermute x18, starting transfers between devices, turn(): lax.ppermute(v, 'blk', [(i, i // 4 * 4 + (i % 4 + k) % 4) for i in range(...  24.2 us
    pallas_call x14, Pallas kernels, call(): pl.pallas_call(kernel, out_shape=out_shape, in_specs=[whole] * len(args)...  18.1 us
    all_to_all x2, starting transfers between devices, exchange(): return lax.all_to_all(v, axis, split_axis=0, concat_axis=0, tiled=True)  17.6 us
    all_to_all x2, waiting for transfers between devices, exchange(): return lax.all_to_all(v, axis, split_axis=0, concat_axis=0, tiled=True)  13.9 us
    ppermute x18, waiting for transfers between devices, turn(): lax.ppermute(v, 'blk', [(i, i // 4 * 4 + (i % 4 + k) % 4) for i in range(...  13.6 us
    ppermute x4, starting transfers between devices, swap(): return lax.ppermute(v, 'blk', [(i, i ^ 4) for i in range(8)])  13.3 us
    ppermute x4, waiting for transfers between devices, swap(): return lax.ppermute(v, 'blk', [(i, i ^ 4) for i in range(8)])  4.33 us
  transfers between devices with their start and end apart: 24, of which 12 were waited for; matrix products, arithmetic and copies ran while one was open for 0% of the time, Pallas kernels for 8%

profile of v3, /device:TPU:1, one launch (start us, length us, event | category | flops | bytes accessed | tf_op | source)
XLA Modules:
  0.0 134.5 jit_solution(87762371620581252)
XLA Ops:
  3.0 1.8 %shard_map.164 = f32[32,40,128]{2,1,0:T(8,128)} custom-call(f32[256,128]{1,0:T(8,128)S(1)} %copy-done, s32[8,128]{1,0:T(8,128)S(1)} %reshape.44.send, s32[8]{0:T(128)S(1)} %bitcast.23), custom_call_target="tpu_custom_call" | custom-call | flops 268435456 | bytes 135200 | tf_op jit(solution)/shard_map/pallas_call | solution.py:45
  4.8 10.0 %all-to-all-start = ((f32[32,40,128]{2,1,0:T(8,128)}), f32[32,40,128]{2,1,0:T(8,128)S(1)}, u32[]{:S(2)}, u32[]{:S(2)}) async-start(f32[32,40,128]{2,1,0:T(8,128)} %shard_map.164), calls=%async_computation | async-start | bytes 1310720 | tf_op jit(solution)/shard_map/all_to_all | solution.py:267
  15.7 1.4 %collective-permute-start.2 = (s32[32,128]{1,0:T(8,128)S(1)}, s32[32,128]{1,0:T(8,128)S(1)}, u32[]{:S(2)}, u32[]{:S(2)}) collective-permute-start(s32[32,128]{1,0:T(8,128)S(1)} %get-tuple-element.53), channel_id=1, source_target_pairs={{0,1},{1,2},{2,3},{3,0},{4,5},{5,6},{6,7},{7,4},{8,9},{9,10},{10,1... | collective-permute-start | bytes 49160 | tf_op jit(solution)/shard_map/ppermute | solution.py:264
  17.1 2.6 %collective-permute-start.1 = (s32[32,128]{1,0:T(8,128)S(1)}, s32[32,128]{1,0:T(8,128)S(1)}, u32[]{:S(2)}, u32[]{:S(2)}) collective-permute-start(s32[32,128]{1,0:T(8,128)S(1)} %get-tuple-element.52), channel_id=1, source_target_pairs={{0,2},{1,3},{2,0},{3,1},{4,6},{5,7},{6,4},{7,5},{8,10},{9,11},{10,... | collective-permute-start | bytes 49160 | tf_op jit(solution)/shard_map/ppermute | solution.py:264
  21.2 1.4 %collective-permute-done.l1 = s32[32,128]{1,0:T(8,128)S(1)} collective-permute-done((s32[32,128]{1,0:T(8,128)S(1)}, s32[32,128]{1,0:T(8,128)S(1)}, u32[]{:S(2)}, u32[]{:S(2)}) %collective-permute-start) | collective-permute-done | bytes 16416 | tf_op jit(solution)/shard_map/ppermute | solution.py:264
  22.6 4.3 %collective-permute-start.3 = (s32[64,128]{1,0:T(8,128)S(1)}, s32[64,128]{1,0:T(8,128)S(1)}, u32[]{:S(2)}, u32[]{:S(2)}) collective-permute-start(s32[64,128]{1,0:T(8,128)S(1)} %pad_add_fusion), channel_id=1, source_target_pairs={{0,4},{1,5},{2,6},{3,7},{4,0},{5,1},{6,2},{7,3},{8,12},{9,13},{10,... | collective-permute-start | bytes 98312 | tf_op jit(solution)/shard_map/ppermute | solution.py:261
  26.9 4.3 %collective-permute-done.3.far = s32[64,128]{1,0:T(8,128)S(1)} collective-permute-done((s32[64,128]{1,0:T(8,128)S(1)}, s32[64,128]{1,0:T(8,128)S(1)}, u32[]{:S(2)}, u32[]{:S(2)}) %collective-permute-start.3) | collective-permute-done | bytes 32800 | tf_op jit(solution)/shard_map/ppermute | solution.py:261
  31.3 2.3 %shard_map.167 = (bf16[8,256,512]{2,1,0:T(8,128)(2,1)S(1)}, s32[1]{0:T(128)}) custom-call(s32[1]{0:T(128)} %bitcast.pos, s32[32,128]{1,0:T(8,128)S(1)} %get-tuple-element.50.l0, s32[32,128]{1,0:T(8,128)S(1)} %collective-permute-done.l1, s32[32,128]{1,0:T(8,128)S(1)} %collective-permute-done.1.l2, s32[32,128]{1,0:T(8,128)S(1)} %collective-permute-done.2.l3, ...), custom_call_target="tpu_custom_call" | custom-call | flops 2147483648 | bytes 98308 | tf_op jit(solution)/shard_map/pallas_call | solution.py:45
  34.5 1.4 %shard_map.168 = (f32[256,128]{1,0:T(8,128)S(1)}, f32[256,128]{1,0:T(8,128)S(1)}, f32[256,128]{1,0:T(8,128)S(1)}, f32[256,128]{1,0:T(8,128)S(1)}, f32[256,128]{1...) custom-call(s32[1]{0:T(128)} %get-tuple-element.54.flag, s32[1]{0:T(128)} %bitcast.pos, ...), custom_call_target="tpu_custom_call" | custom-call | flops 268435456 | bytes 2981896 | tf_op jit(solution)/shard_map/pallas_call | solution.py:45
  35.8 3.7 %collective-permute-start.6 = (f32[256,128]{1,0:T(8,128)S(1)}, f32[256,128]{1,0:T(8,128)S(1)}, u32[]{:S(2)}, u32[]{:S(2)}) collective-permute-start(f32[256,128]{1,0:T(8,128)S(1)} %get-tuple-element.60), channel_id=1, source_target_pairs={{0,2},{1,3},{2,0},{3,1},{4,6},{5,7},{6,4},{7,5},{8,10},{9,11},{10,... | collective-permute-start | bytes 393224 | tf_op jit(solution)/shard_map/ppermute | solution.py:264
  41.0 2.3 %shard_map.166 = (bf16[256,1024]{1,0:T(8,128)(2,1)S(1)}, bf16[1024,256]{1,0:T(8,128)(2,1)S(1)}, f32[256,128]{1,0:T(8,128)S(1)}, s32[1]{0:T(128)}) custom-call(s32[48,128]{1,0:T(8,128)S(1)} %get-tuple-element.46.own_to, s32[8,128]{1,0:T(8,128)S(1)} %bitcast.12, s32[8,128]{1,0:T(8,128)S(1)} %bitcast.15, s32[2,128]{1,0:T(2,128)S(1)} %bitcast.22), custom_call_target="tpu_custom_call" | custom-call | flops 2147483648 | bytes 33792 | tf_op jit(solution)/shard_map/pallas_call | solution.py:45
  43.4 3.0 %collective-permute-done.5 = f32[256,128]{1,0:T(8,128)S(1)} collective-permute-done((f32[256,128]{1,0:T(8,128)S(1)}, f32[256,128]{1,0:T(8,128)S(1)}, u32[]{:S(2)}, u32[]{:S(2)}) %collective-permute-start.5) | collective-permute-done | bytes 131104 | tf_op jit(solution)/shard_map/ppermute | solution.py:264
  46.9 4.1 %collective-permute-start.7 = (f32[256,128]{1,0:T(8,128)S(1)}, f32[256,128]{1,0:T(8,128)S(1)}, u32[]{:S(2)}, u32[]{:S(2)}) collective-permute-start(f32[256,128]{1,0:T(8,128)S(1)} %add_add_fusion), channel_id=1, source_target_pairs={{0,4},{1,5},{2,6},{3,7},{4,0},{5,1},{6,2},{7,3},{8,12},{9,13},{10,... | collective-permute-start | bytes 393224 | tf_op jit(solution)/shard_map/ppermute | solution.py:261
  51.0 1.2 collective-permute-start.8
  52.3 1.4 %collective-permute-start.9 = (f32[256,128]{1,0:T(8,128)S(1)}, f32[256,128]{1,0:T(8,128)S(1)}, u32[]{:S(2)}, u32[]{:S(2)}) collective-permute-start(f32[256,128]{1,0:T(8,128)S(1)} %get-tuple-element.66), channel_id=1, source_target_pairs={{0,3},{1,0},{2,1},{3,2},{4,7},{5,4},{6,5},{7,6},{8,11},{9,8},{10,9... | collective-permute-start | bytes 393224 | tf_op jit(solution)/shard_map/ppermute | solution.py:264
  53.7 1.5 %collective-permute-start.10 = (f32[256,128]{1,0:T(8,128)S(1)}, f32[256,128]{1,0:T(8,128)S(1)}, u32[]{:S(2)}, u32[]{:S(2)}) collective-permute-start(f32[256,128]{1,0:T(8,128)S(1)} %get-tuple-element.67), channel_id=1, source_target_pairs={{0,2},{1,3},{2,0},{3,1},{4,6},{5,7},{6,4},{7,5},{8,10},{9,11},{10,... | collective-permute-start | bytes 393224 | tf_op jit(solution)/shard_map/ppermute | solution.py:264
  55.2 1.6 %shard_map.170.bwd = bf16[8,512,256]{2,1,0:T(8,128)(2,1)S(1)} custom-call(s32[1]{0:T(128)} %bitcast.pos, s32[32,128]{1,0:T(8,128)S(1)} %get-tuple-element.50.l0, s32[32,128]{1,0:T(8,128)S(1)} %collective-permute-done.l1, s32[32,128]{1,0:T(8,128)S(1)} %collective-permute-done.1.l2, s32[32,128]{1,0:T(8,128)S(1)} %collective-permute-done.2.l3, ...), custom_call_target="tpu_custom_call" | custom-call | flops 2147483648 | bytes 98308 | tf_op jit(solution)/shard_map/pallas_call | solution.py:45
  57.8 1.8 %collective-permute-done.10.a4 = f32[256,128]{1,0:T(8,128)S(1)} collective-permute-done((f32[256,128]{1,0:T(8,128)S(1)}, f32[256,128]{1,0:T(8,128)S(1)}, u32[]{:S(2)}, u32[]{:S(2)}) %collective-permute-start.10) | collective-permute-done | bytes 131104 | tf_op jit(solution)/shard_map/ppermute | solution.py:264
  59.6 1.3 shard_map.171
  62.0 7.6 %all-to-all-start.1 = ((f32[32,16,128]{2,1,0:T(8,128)}), f32[32,16,128]{2,1,0:T(8,128)S(1)}, u32[]{:S(2)}, u32[]{:S(2)}) async-start(f32[32,16,128]{2,1,0:T(8,128)} %shard_map.174), calls=%async_computation.1 | async-start | bytes 524288 | tf_op jit(solution)/shard_map/all_to_all | solution.py:267
  69.5 1.3 collective-permute-start.11
  70.8 2.4 %collective-permute-start.14 = (f32[256,128]{1,0:T(8,128)S(1)}, f32[256,128]{1,0:T(8,128)S(1)}, u32[]{:S(2)}, u32[]{:S(2)}) collective-permute-start(f32[256,128]{1,0:T(8,128)S(1)} %get-tuple-element.71.grad_sum.g0), channel_id=1, source_target_pairs={{0,4},{1,5},{2,6},{3,7},{4,0},{5,1},{6,2},{7,3},{8,12},{9,13},{10,... | collective-permute-start | bytes 393224 | tf_op jit(solution)/shard_map/ppermute | solution.py:261
  73.2 13.0 %all-to-all-done.1.weights = f32[32,16,128]{2,1,0:T(8,128)S(1)} async-done(((f32[32,16,128]{2,1,0:T(8,128)}), f32[32,16,128]{2,1,0:T(8,128)S(1)}, u32[]{:S(2)}, u32[]{:S(2)}) %all-to-all-start.1) | async-done | bytes 262176 | tf_op jit(solution)/shard_map/all_to_all | solution.py:267
  86.3 1.3 collective-permute-start.20
  90.4 3.3 %collective-permute-start.12 = (f32[256,128]{1,0:T(8,128)S(1)}, f32[256,128]{1,0:T(8,128)S(1)}, u32[]{:S(2)}, u32[]{:S(2)}) collective-permute-start(f32[256,128]{1,0:T(8,128)S(1)} %get-tuple-element.71.grad_sum.g0), channel_id=1, source_target_pairs={{0,2},{1,3},{2,0},{3,1},{4,6},{5,7},{6,4},{7,5},{8,10},{9,11},{10,... | collective-permute-start | bytes 393224 | tf_op jit(solution)/shard_map/ppermute | solution.py:264
  93.6 2.7 %collective-permute-start.15 = (f32[256,128]{1,0:T(8,128)S(1)}, f32[256,128]{1,0:T(8,128)S(1)}, u32[]{:S(2)}, u32[]{:S(2)}) collective-permute-start(f32[256,128]{1,0:T(8,128)S(1)} %collective-permute-done.14.g4), channel_id=1, source_target_pairs={{0,3},{1,0},{2,1},{3,2},{4,7},{5,4},{6,5},{7,6},{8,11},{9,8},{10,9... | collective-permute-start | bytes 393224 | tf_op jit(solution)/shard_map/ppermute | solution.py:264
  97.0 2.4 %collective-permute-start.21 = (f32[16,128]{1,0:T(8,128)S(1)}, f32[16,128]{1,0:T(8,128)S(1)}, u32[]{:S(2)}, u32[]{:S(2)}) collective-permute-start(f32[16,128]{1,0:T(8,128)S(1)} %add_add_fusion.1.near), channel_id=1, source_target_pairs={{0,4},{1,5},{2,6},{3,7},{4,0},{5,1},{6,2},{7,3},{8,12},{9,13},{10,... | collective-permute-start | bytes 24584 | tf_op jit(solution)/shard_map/ppermute | solution.py:261
  99.8 2.1 %collective-permute-done.16.g6 = f32[256,128]{1,0:T(8,128)S(1)} collective-permute-done((f32[256,128]{1,0:T(8,128)S(1)}, f32[256,128]{1,0:T(8,128)S(1)}, u32[]{:S(2)}, u32[]{:S(2)}) %collective-permute-start.16) | collective-permute-done | bytes 131104 | tf_op jit(solution)/shard_map/ppermute | solution.py:264
  101.9 4.1 %collective-permute-done.17.g7 = f32[256,128]{1,0:T(8,128)S(1)} collective-permute-done((f32[256,128]{1,0:T(8,128)S(1)}, f32[256,128]{1,0:T(8,128)S(1)}, u32[]{:S(2)}, u32[]{:S(2)}) %collective-permute-start.17) | collective-permute-done | bytes 131104 | tf_op jit(solution)/shard_map/ppermute | solution.py:264
  106.0 1.4 %shard_map.173 = (f32[256,128]{1,0:T(8,128)S(1)}, f32[32,8,128]{2,1,0:T(8,128)S(1)}) custom-call(s32[1]{0:T(128)} %get-tuple-element.54.flag, s32[1]{0:T(128)} %bitcast.pos, s32[32,128]{1,0:T(8,128)S(1)} %get-tuple-element.50.l0, s32[32,128]{1,0:T(8,128)S(1)} %collective-permute-done.l1, s32[32,128]{1,0:T(8,128)S(1)} %collective-permute-done.1.l2, ...), custom_call_target="tpu_custom_call" | custom-call | flops 268435456 | bytes 3375112 | tf_op jit(solution)/shard_map/pallas_call | solution.py:45
  108.0 25.0 %all_to_all.15.returned = f32[32,48,128]{2,1,0:T(8,128)S(1)} all-to-all(f32[32,48,128]{2,1,0:T(8,128)S(1)} %get-tuple-element.79), channel_id=1, replica_groups=mesh['grp'=32,'blk'=8] {'grp'}, dimensions={0} | all-to-all | bytes 1572864 | tf_op jit(solution)/shard_map/all_to_all | solution.py:267
  132.9 1.5 %shard_map.177 = (f32[256,128]{1,0:T(8,128)}, f32[128,128]{1,0:T(8,128)}, f32[128,128]{1,0:T(8,128)}) custom-call(f32[32,48,128]{2,1,0:T(8,128)S(1)} %all_to_all.15.returned, s32[8,128]{1,0:T(8,128)S(1)} %reshape.44.send, s32[8]{0:T(128)S(1)} %bitcast.24, f32[256,128]{1,0:T(8,128)S(1)} %get-tuple-element.80.local), custom_call_target="tpu_custom_call" | custom-call | flops 268435456 | bytes 921632 | tf_op jit(solution)/shard_map/pallas_call | solution.py:45
  (72 shorter events, 14.3 us)
Async XLA Ops:
  0.6 14.2 %copy-start.15 = (s32[1,1,8,2,6]{2,3,4,1,0:T(2,128)S(1)}, s32[1,1,8,2,6]{2,3,4,1,0:T(2,128)}, u32[]{:S(2)}) copy-start(s32[1,1,8,2,6]{2,3,4,1,0:T(2,128)} %param.18) | copy-start | bytes 1156
  0.6 14.3 %copy-start.10 = (s32[1,1,256]{2,1,0:T(1,128)S(1)}, s32[1,1,256]{2,1,0:T(1,128)}, u32[]{:S(2)}) copy-start(s32[1,1,256]{2,1,0:T(1,128)} %param.24) | copy-start | bytes 3076
  0.7 14.3 %copy-start.9 = (s32[1,1,256]{2,1,0:T(1,128)S(1)}, s32[1,1,256]{2,1,0:T(1,128)}, u32[]{:S(2)}) copy-start(s32[1,1,256]{2,1,0:T(1,128)} %param.25) | copy-start | bytes 3076
  4.8 29.7 %all-to-all-start = ((f32[32,40,128]{2,1,0:T(8,128)}), f32[32,40,128]{2,1,0:T(8,128)S(1)}, u32[]{:S(2)}, u32[]{:S(2)}) async-start(f32[32,40,128]{2,1,0:T(8,128)} %shard_map.164), calls=%async_computation | async-start | bytes 1310720 | tf_op jit(solution)/shard_map/all_to_all | solution.py:267
  15.7 5.1 %collective-permute-start.2 = (s32[32,128]{1,0:T(8,128)S(1)}, s32[32,128]{1,0:T(8,128)S(1)}, u32[]{:S(2)}, u32[]{:S(2)}) collective-permute-start(s32[32,128]{1,0:T(8,128)S(1)} %get-tuple-element.53), channel_id=1, source_target_pairs={{0,1},{1,2},{2,3},{3,0},{4,5},{5,6},{6,7},{7,4},{8,9},{9,10},{10,1... | collective-permute-start | bytes 49160 | tf_op jit(solution)/shard_map/ppermute | solution.py:264
  17.1 4.1 %collective-permute-start.1 = (s32[32,128]{1,0:T(8,128)S(1)}, s32[32,128]{1,0:T(8,128)S(1)}, u32[]{:S(2)}, u32[]{:S(2)}) collective-permute-start(s32[32,128]{1,0:T(8,128)S(1)} %get-tuple-element.52), channel_id=1, source_target_pairs={{0,2},{1,3},{2,0},{3,1},{4,6},{5,7},{6,4},{7,5},{8,10},{9,11},{10,... | collective-permute-start | bytes 49160 | tf_op jit(solution)/shard_map/ppermute | solution.py:264
  19.7 2.9 %collective-permute-start = (s32[32,128]{1,0:T(8,128)S(1)}, s32[32,128]{1,0:T(8,128)S(1)}, u32[]{:S(2)}, u32[]{:S(2)}) collective-permute-start(s32[32,128]{1,0:T(8,128)S(1)} %get-tuple-element.51), channel_id=1, source_target_pairs={{0,3},{1,0},{2,1},{3,2},{4,7},{5,4},{6,5},{7,6},{8,11},{9,8},{10,9... | collective-permute-start | bytes 49160 | tf_op jit(solution)/shard_map/ppermute | solution.py:264
  22.6 8.6 %collective-permute-start.3 = (s32[64,128]{1,0:T(8,128)S(1)}, s32[64,128]{1,0:T(8,128)S(1)}, u32[]{:S(2)}, u32[]{:S(2)}) collective-permute-start(s32[64,128]{1,0:T(8,128)S(1)} %pad_add_fusion), channel_id=1, source_target_pairs={{0,4},{1,5},{2,6},{3,7},{4,0},{5,1},{6,2},{7,3},{8,12},{9,13},{10,... | collective-permute-start | bytes 98312 | tf_op jit(solution)/shard_map/ppermute | solution.py:261
  35.8 7.6 %collective-permute-start.6 = (f32[256,128]{1,0:T(8,128)S(1)}, f32[256,128]{1,0:T(8,128)S(1)}, u32[]{:S(2)}, u32[]{:S(2)}) collective-permute-start(f32[256,128]{1,0:T(8,128)S(1)} %get-tuple-element.60), channel_id=1, source_target_pairs={{0,2},{1,3},{2,0},{3,1},{4,6},{5,7},{6,4},{7,5},{8,10},{9,11},{10,... | collective-permute-start | bytes 393224 | tf_op jit(solution)/shard_map/ppermute | solution.py:264
  39.5 6.9 %collective-permute-start.5 = (f32[256,128]{1,0:T(8,128)S(1)}, f32[256,128]{1,0:T(8,128)S(1)}, u32[]{:S(2)}, u32[]{:S(2)}) collective-permute-start(f32[256,128]{1,0:T(8,128)S(1)} %get-tuple-element.59), channel_id=1, source_target_pairs={{0,3},{1,0},{2,1},{3,2},{4,7},{5,4},{6,5},{7,6},{8,11},{9,8},{10,9... | collective-permute-start | bytes 393224 | tf_op jit(solution)/shard_map/ppermute | solution.py:264
  40.3 6.5 %collective-permute-start.4 = (f32[256,128]{1,0:T(8,128)S(1)}, f32[256,128]{1,0:T(8,128)S(1)}, u32[]{:S(2)}, u32[]{:S(2)}) collective-permute-start(f32[256,128]{1,0:T(8,128)S(1)} %get-tuple-element.58), channel_id=1, source_target_pairs={{0,1},{1,2},{2,3},{3,0},{4,5},{5,6},{6,7},{7,4},{8,9},{9,10},{10,1... | collective-permute-start | bytes 393224 | tf_op jit(solution)/shard_map/ppermute | solution.py:264
  46.9 12.7 %copy-start.2 = (f32[256,128]{1,0:T(8,128)S(1)}, f32[256,128]{1,0:T(8,128)}, u32[]{:S(2)}) copy-start(f32[256,128]{1,0:T(8,128)} %grad_out.1) | copy-start | bytes 393220
  46.9 12.7 %copy-start.3 = (f32[128,128]{1,0:T(8,128)S(1)}, f32[128,128]{1,0:T(8,128)}, u32[]{:S(2)}) copy-start(f32[128,128]{1,0:T(8,128)} %w_neigh.1) | copy-start | bytes 196612
  46.9 12.7 %copy-start.4 = (f32[128,128]{1,0:T(8,128)S(1)}, f32[128,128]{1,0:T(8,128)}, u32[]{:S(2)}) copy-start(f32[128,128]{1,0:T(8,128)} %w_root.3) | copy-start | bytes 196612
  46.9 12.7 %copy-start.7 = (f32[128]{0:T(128)S(1)}, f32[128]{0:T(128)}, u32[]{:S(2)}) copy-start(f32[128]{0:T(128)} %param.16) | copy-start | bytes 1540
  46.9 10.8 %collective-permute-start.7 = (f32[256,128]{1,0:T(8,128)S(1)}, f32[256,128]{1,0:T(8,128)S(1)}, u32[]{:S(2)}, u32[]{:S(2)}) collective-permute-start(f32[256,128]{1,0:T(8,128)S(1)} %add_add_fusion), channel_id=1, source_target_pairs={{0,4},{1,5},{2,6},{3,7},{4,0},{5,1},{6,2},{7,3},{8,12},{9,13},{10,... | collective-permute-start | bytes 393224 | tf_op jit(solution)/shard_map/ppermute | solution.py:261
  51.0 6.7 %collective-permute-start.8 = (f32[256,128]{1,0:T(8,128)S(1)}, f32[256,128]{1,0:T(8,128)S(1)}, u32[]{:S(2)}, u32[]{:S(2)}) collective-permute-start(f32[256,128]{1,0:T(8,128)S(1)} %get-tuple-element.65), channel_id=1, source_target_pairs={{0,1},{1,2},{2,3},{3,0},{4,5},{5,6},{6,7},{7,4},{8,9},{9,10},{10,1... | collective-permute-start | bytes 393224 | tf_op jit(solution)/shard_map/ppermute | solution.py:264
  52.3 5.5 %collective-permute-start.9 = (f32[256,128]{1,0:T(8,128)S(1)}, f32[256,128]{1,0:T(8,128)S(1)}, u32[]{:S(2)}, u32[]{:S(2)}) collective-permute-start(f32[256,128]{1,0:T(8,128)S(1)} %get-tuple-element.66), channel_id=1, source_target_pairs={{0,3},{1,0},{2,1},{3,2},{4,7},{5,4},{6,5},{7,6},{8,11},{9,8},{10,9... | collective-permute-start | bytes 393224 | tf_op jit(solution)/shard_map/ppermute | solution.py:264
  53.7 5.8 %collective-permute-start.10 = (f32[256,128]{1,0:T(8,128)S(1)}, f32[256,128]{1,0:T(8,128)S(1)}, u32[]{:S(2)}, u32[]{:S(2)}) collective-permute-start(f32[256,128]{1,0:T(8,128)S(1)} %get-tuple-element.67), channel_id=1, source_target_pairs={{0,2},{1,3},{2,0},{3,1},{4,6},{5,7},{6,4},{7,5},{8,10},{9,11},{10,... | collective-permute-start | bytes 393224 | tf_op jit(solution)/shard_map/ppermute | solution.py:264
  62.0 24.3 %all-to-all-start.1 = ((f32[32,16,128]{2,1,0:T(8,128)}), f32[32,16,128]{2,1,0:T(8,128)S(1)}, u32[]{:S(2)}, u32[]{:S(2)}) async-start(f32[32,16,128]{2,1,0:T(8,128)} %shard_map.174), calls=%async_computation.1 | async-start | bytes 524288 | tf_op jit(solution)/shard_map/all_to_all | solution.py:267
  69.5 20.8 %collective-permute-start.11 = (f32[256,128]{1,0:T(8,128)S(1)}, f32[256,128]{1,0:T(8,128)S(1)}, u32[]{:S(2)}, u32[]{:S(2)}) collective-permute-start(f32[256,128]{1,0:T(8,128)S(1)} %get-tuple-element.71.grad_sum.g0), channel_id=1, source_target_pairs={{0,3},{1,0},{2,1},{3,2},{4,7},{5,4},{6,5},{7,6},{8,11},{9,8},{10,9... | collective-permute-start | bytes 393224 | tf_op jit(solution)/shard_map/ppermute | solution.py:264
  70.8 22.8 %collective-permute-start.14 = (f32[256,128]{1,0:T(8,128)S(1)}, f32[256,128]{1,0:T(8,128)S(1)}, u32[]{:S(2)}, u32[]{:S(2)}) collective-permute-start(f32[256,128]{1,0:T(8,128)S(1)} %get-tuple-element.71.grad_sum.g0), channel_id=1, source_target_pairs={{0,4},{1,5},{2,6},{3,7},{4,0},{5,1},{6,2},{7,3},{8,12},{9,13},{10,... | collective-permute-start | bytes 393224 | tf_op jit(solution)/shard_map/ppermute | solution.py:261
  86.3 7.3 %collective-permute-start.20 = (f32[16,128]{1,0:T(8,128)S(1)}, f32[16,128]{1,0:T(8,128)S(1)}, u32[]{:S(2)}, u32[]{:S(2)}) collective-permute-start(f32[16,128]{1,0:T(8,128)S(1)} %shard_map.175), channel_id=1, source_target_pairs={{0,3},{1,0},{2,1},{3,2},{4,7},{5,4},{6,5},{7,6},{8,11},{9,8},{10,9... | collective-permute-start | bytes 24584 | tf_op jit(solution)/shard_map/ppermute | solution.py:264
  87.6 8.8 %collective-permute-start.19 = (f32[16,128]{1,0:T(8,128)S(1)}, f32[16,128]{1,0:T(8,128)S(1)}, u32[]{:S(2)}, u32[]{:S(2)}) collective-permute-start(f32[16,128]{1,0:T(8,128)S(1)} %shard_map.175), channel_id=1, source_target_pairs={{0,2},{1,3},{2,0},{3,1},{4,6},{5,7},{6,4},{7,5},{8,10},{9,11},{10,... | collective-permute-start | bytes 24584 | tf_op jit(solution)/shard_map/ppermute | solution.py:264
  87.6 8.8 %collective-permute-start.18 = (f32[16,128]{1,0:T(8,128)S(1)}, f32[16,128]{1,0:T(8,128)S(1)}, u32[]{:S(2)}, u32[]{:S(2)}) collective-permute-start(f32[16,128]{1,0:T(8,128)S(1)} %shard_map.175), channel_id=1, source_target_pairs={{0,1},{1,2},{2,3},{3,0},{4,5},{5,6},{6,7},{7,4},{8,9},{9,10},{10,1... | collective-permute-start | bytes 24584 | tf_op jit(solution)/shard_map/ppermute | solution.py:264
  90.4 6.6 %collective-permute-start.12 = (f32[256,128]{1,0:T(8,128)S(1)}, f32[256,128]{1,0:T(8,128)S(1)}, u32[]{:S(2)}, u32[]{:S(2)}) collective-permute-start(f32[256,128]{1,0:T(8,128)S(1)} %get-tuple-element.71.grad_sum.g0), channel_id=1, source_target_pairs={{0,2},{1,3},{2,0},{3,1},{4,6},{5,7},{6,4},{7,5},{8,10},{9,11},{10,... | collective-permute-start | bytes 393224 | tf_op jit(solution)/shard_map/ppermute | solution.py:264
  93.6 6.2 %collective-permute-start.13 = (f32[256,128]{1,0:T(8,128)S(1)}, f32[256,128]{1,0:T(8,128)S(1)}, u32[]{:S(2)}, u32[]{:S(2)}) collective-permute-start(f32[256,128]{1,0:T(8,128)S(1)} %get-tuple-element.71.grad_sum.g0), channel_id=1, source_target_pairs={{0,1},{1,2},{2,3},{3,0},{4,5},{5,6},{6,7},{7,4},{8,9},{9,10},{10,1... | collective-permute-start | bytes 393224 | tf_op jit(solution)/shard_map/ppermute | solution.py:264
  93.6 6.2 %collective-permute-start.15 = (f32[256,128]{1,0:T(8,128)S(1)}, f32[256,128]{1,0:T(8,128)S(1)}, u32[]{:S(2)}, u32[]{:S(2)}) collective-permute-start(f32[256,128]{1,0:T(8,128)S(1)} %collective-permute-done.14.g4), channel_id=1, source_target_pairs={{0,3},{1,0},{2,1},{3,2},{4,7},{5,4},{6,5},{7,6},{8,11},{9,8},{10,9... | collective-permute-start | bytes 393224 | tf_op jit(solution)/shard_map/ppermute | solution.py:264
  96.3 5.6 %collective-permute-start.16 = (f32[256,128]{1,0:T(8,128)S(1)}, f32[256,128]{1,0:T(8,128)S(1)}, u32[]{:S(2)}, u32[]{:S(2)}) collective-permute-start(f32[256,128]{1,0:T(8,128)S(1)} %collective-permute-done.14.g4), channel_id=1, source_target_pairs={{0,2},{1,3},{2,0},{3,1},{4,6},{5,7},{6,4},{7,5},{8,10},{9,11},{10,... | collective-permute-start | bytes 393224 | tf_op jit(solution)/shard_map/ppermute | solution.py:264
  96.3 9.6 %collective-permute-start.17 = (f32[256,128]{1,0:T(8,128)S(1)}, f32[256,128]{1,0:T(8,128)S(1)}, u32[]{:S(2)}, u32[]{:S(2)}) collective-permute-start(f32[256,128]{1,0:T(8,128)S(1)} %collective-permute-done.14.g4), channel_id=1, source_target_pairs={{0,1},{1,2},{2,3},{3,0},{4,5},{5,6},{6,7},{7,4},{8,9},{9,10},{10,1... | collective-permute-start | bytes 393224 | tf_op jit(solution)/shard_map/ppermute | solution.py:264
  97.0 10.4 %collective-permute-start.21 = (f32[16,128]{1,0:T(8,128)S(1)}, f32[16,128]{1,0:T(8,128)S(1)}, u32[]{:S(2)}, u32[]{:S(2)}) collective-permute-start(f32[16,128]{1,0:T(8,128)S(1)} %add_add_fusion.1.near), channel_id=1, source_target_pairs={{0,4},{1,5},{2,6},{3,7},{4,0},{5,1},{6,2},{7,3},{8,12},{9,13},{10,... | collective-permute-start | bytes 24584 | tf_op jit(solution)/shard_map/ppermute | solution.py:261
  107.4 25.5 %copy-start.12 = (s32[1,1,8]{2,1,0:T(1,128)S(1)}, s32[1,1,8]{2,1,0:T(1,128)}, u32[]{:S(2)}) copy-start(s32[1,1,8]{2,1,0:T(1,128)} %param.23) | copy-start | bytes 100
  (8 other events, 44.7 us)

commit v4 on v3

--- a/solution.py
+++ b/solution.py
@@ -64,12 +64,15 @@
     return jnp.where(x > -0.35, series, jnp.exp(x) - 1.0)
 
 
+def send_hot(send):
+    return lanes([one_hot(lanes([send[4 * i + j : 4 * i + j + 1, :] for j in range(4)]), 256) for i in range(8)])
+
+
 def k_send(features, send, hub, out):
     x = halves(features[...])
-    hot = lanes([one_hot(send[i : i + 1, :], 256) for i in range(8)])
-    rows = joined(dot(hot, x, TN))
+    rows = joined(dot(send_hot(send), x, TN))
     out[:, 0:32, :] = rows.reshape(32, 32, 128)
-    hub_rows = jnp.concatenate([features[pl.ds(hub[j], 1), :] for j in range(8)], axis=0)
+    hub_rows = joined(dot(one_hot(hub[...], 256), x, TN))
     for p in range(32):
         out[p, 32:40, :] = hub_rows
 
@@ -206,7 +209,7 @@
         out[...] += joined(dot(rest(dot(frm, to, NT)), x))
 
 
-def k_back(flag, pos, l0, l1, l2, l3, far, g0, g1, g2, g3, g4, g5, g6, g7, bwd, root, local, hubs, total):
+def k_back(flag, pos, l0, l1, l2, l3, far, g0, g1, g2, g3, g4, g5, g6, g7, bwd, root, slots, local, out, total):
     xs = [halves(g[...]) for g in (g0, g1, g2, g3, g4, g5, g6, g7)]
     acc = dot(bwd[0], xs[0])
     for r in range(1, 8):
@@ -218,7 +221,8 @@
         for r, block in enumerate(blocks_of((l0, l1, l2, l3, far))):
             total[...] += joined(dot(rest(backward_count(*hots(pos, block))), xs[r]))
 
-    hubs[...] = total[256:512, :].reshape(32, 8, 128)
+    out[:, 0:32, :] = slots[...].reshape(32, 32, 128)
+    out[:, 32:40, :] = total[256:512, :].reshape(32, 8, 128)
     local[...] = root[...] + total[0:256, :]
 
 
@@ -226,29 +230,35 @@
     out[...] = jnp.sum(weights[...], axis=0)
 
 
-def k_pack(factor, slots, hubs, near, far, out, bias):
+def k_scale(factor, near, far, out, bias):
     w = (near[...] + far[...]) * factor
-    out[:, 0:32, :] = slots[...].reshape(32, 32, 128)
-    out[:, 32:40, :] = hubs[...]
-    for p in range(32):
-        out[p, 40:48, :] = w[0:8]
+    out[...] = w[0:8]
     bias[...] = w[8:9]
 
 
-def k_final(returned, send, hub, local, out, w_neigh, w_root):
-    hot = lanes([one_hot(send[i : i + 1, :], 256) for i in range(8)])
-    acc = joined(dot(hot, halves(returned[:, 0:32, :].reshape(1024, 128))))
+def k_place(here, a, b, w_neigh, w_root, held):
+    g = here[0]
+    zl, x, c = g // 8, g // 2 % 4, g % 2
+    for d, ref in enumerate((a, b)):
+        for k in range(4):
+            for m in range(4):
+                at = (jnp.bitwise_xor(zl, m) * 4 + (x + 4 - k) % 4) * 2 + jnp.bitwise_xor(c, d)
+                held[pl.ds(pl.multiple_of(at * 8, 8), 8), :] = ref[k * 32 + m * 8 : k * 32 + m * 8 + 8, :]
+    w_neigh[...] = held[0:128, :]
+    w_root[...] = held[128:256, :]
+
+
+def k_final(returned, send, hub, local, out):
+    acc = joined(dot(send_hot(send), halves(returned[:, 0:32, :].reshape(1024, 128))))
     rows = jnp.sum(returned[:, 32:40, :], axis=0)
     out[...] = local[...] + acc
     for j in range(8):
         out[pl.ds(hub[j], 1), :] += rows[j : j + 1, :]
-    w_neigh[...] = returned[0:16, 40:48, :].reshape(128, 128)
-    w_root[...] = returned[16:32, 40:48, :].reshape(128, 128)
 
 
 def per_device(features, w_neigh, w_root, bias, grad_out, tile_coord, tile_edge,
                send_idx, halo_dst, halo_src, hub_idx, hub_dst, hub_src):
-    send = send_idx.reshape(8, 128)
+    send = send_idx.reshape(32, 32)
     hub = hub_idx.reshape(8)
     hub_to = hub_dst.reshape(2, 128)
     hub_from = hub_src.reshape(2, 128)
@@ -268,7 +278,7 @@
 
     vm, sm = (pl.BlockSpec(memory_space=s) for s in (pltpu.VMEM, pltpu.SMEM))
 
-    outgoing = call(k_send, shape((32, 40, 128)), (features, send, hub), [vm, vm, sm])
+    outgoing = call(k_send, shape((32, 40, 128)), (features, send, hub_idx.reshape(1, 8)))
     outgoing, coord = lax.optimization_barrier((outgoing, tile_coord.reshape(8, 2, 6)))
     incoming = exchange(outgoing, "grp")
     own_to, m0, m1, m2, m3 = call(
@@ -303,22 +313,28 @@
         [sm] + [vm] * 6,
     )
     g5, g7, g6 = turn(g4, 3), turn(g4, 1), turn(g4, 2)
+    local, back = call(
+        k_back, [block, shape((32, 40, 128))],
+        (flag, *lists, grad_sum, g1, g2, g3, g4, g5, g6, g7, bwd, root, slots), [sm, *lm] + [vm] * 11,
+        [pltpu.VMEM((512, 128), F32)],
+    )
+    returned = exchange(back, "grp")
+    back, weights = lax.optimization_barrier((back, weights))
     w = call(k_sum, shape((16, 128)), (weights,))
     w = w + turn(w, 1) + turn(w, 2) + turn(w, 3)
-    w_far = swap(w)
-    local, hubs = call(
-        k_back, [block, shape((32, 8, 128))],
-        (flag, *lists, grad_sum, g1, g2, g3, g4, g5, g6, g7, bwd, root), [sm, *lm] + [vm] * 10,
-        [pltpu.VMEM((512, 128), F32)],
-    )
     factor = (256 * lax.axis_size("grp") * lax.axis_size("blk")) ** (-0.5)
-    back, grad_bias = call(
-        functools.partial(k_pack, factor), [shape((32, 48, 128)), shape((1, 128))], (slots, hubs, w, w_far)
-    )
-    returned = exchange(back, "grp")
-    grad_features, grad_wn, grad_wr = call(
-        k_final, [block, shape((128, 128)), shape((128, 128))], (returned, send, hub, local), [vm, vm, sm, vm]
-    )
+    w, grad_bias = call(functools.partial(k_scale, factor), [shape((8, 128)), shape((1, 128))], (w, swap(w)))
+    w = jnp.concatenate([w] + [lax.ppermute(w, "grp", [(i, i ^ (8 * m)) for i in range(32)]) for m in (1, 2, 3)], axis=0)
+    spin = [
+        lax.ppermute(w, "grp", [(i, i // 8 * 8 + (i % 8 + 2 * k) % 8) for i in range(32)]) for k in (1, 2, 3)
+    ]
+    w = jnp.concatenate([w] + spin, axis=0)
+    w_core = lax.ppermute(w, "grp", [(i, i ^ 1) for i in range(32)])
+    here = lax.axis_index("grp").astype(I32).reshape(1)
+    grad_wn, grad_wr = call(
+        k_place, [shape((128, 128))] * 2, (here, w, w_core), [sm, vm, vm], [pltpu.VMEM((256, 128), F32)]
+    )
+    grad_features = call(k_final, block, (returned, send, hub, local), [vm, vm, sm, vm])
     return output, grad_features, grad_wn, grad_wr, grad_bias.reshape(128)
 
 

time: 135 us -> 140 us (1.037)
  blocking collectives: 25 us -> 0 us
  starting transfers between devices: 55.1 us -> 77.4 us
  waiting for transfers between devices: 31.8 us -> 38.5 us
    all_to_all x1 -> x0, blocking collectives: 25 us -> none  [exchange(): return lax.all_to_all(v, axis, split_axis=0, concat_axis=0, tiled=True)]
    all_to_all x2 -> x3, waiting for transfers between devices: 13.9 us -> 0.87 us  [exchange(): return lax.all_to_all(v, axis, split_axis=0, concat_axis=0, tiled=True)]
    ppermute x0 -> x7, starting transfers between devices: none -> 12.6 us  [the longest x1 4.59 us: per_device(): w_core = lax.ppermute(w, 'grp', [(i, i ^ 1) for i in range(32)])]
    ppermute x4, waiting for transfers between devices: 4.33 us -> 16.7 us  [swap(): return lax.ppermute(v, 'blk', [(i, i ^ 4) for i in range(8)])]
    all_to_all x2 -> x3, starting transfers between devices: 17.6 us -> 28.2 us  [exchange(): return lax.all_to_all(v, axis, split_axis=0, concat_axis=0, tiled=True)]
    ppermute x0 -> x7, waiting for transfers between devices: none -> 6.5 us  [the longest x3 4.18 us: per_device(): lax.ppermute(w, 'grp', [(i, i ^ 8 * m) for i in range(32)])]
    ppermute x18, starting transfers between devices: 24.2 us -> 21.8 us  [turn(): lax.ppermute(v, 'blk', [(i, i // 4 * 4 + (i % 4 + k) % 4) for i in range(...]
    ppermute x4, starting transfers between devices: 13.3 us -> 14.9 us  [swap(): return lax.ppermute(v, 'blk', [(i, i ^ 4) for i in range(8)])]
  transfers between devices with their start and end apart: 24 -> 32, of which waited for: 12 -> 18; matrix products, arithmetic and copies ran while one was open for 0% -> 0% of each run, Pallas kernels for 8% -> 9%
where the time goes in v4:
time: 140 us
  starting transfers between devices  77.4 us (55%)
  waiting for transfers between devices  38.5 us (28%)
  Pallas kernels  19.3 us (14%)
  local copies, waits for them, and re-layouts  3.5 us (2%)
    all_to_all x3, starting transfers between devices, exchange(): return lax.all_to_all(v, axis, split_axis=0, concat_axis=0, tiled=True)  28.2 us
    ppermute x18, starting transfers between devices, turn(): lax.ppermute(v, 'blk', [(i, i // 4 * 4 + (i % 4 + k) % 4) for i in range(...  21.8 us
    pallas_call x15, Pallas kernels, call(): pl.pallas_call(kernel, out_shape=out_shape, in_specs=[whole] * len(args)...  19.3 us
    ppermute x4, waiting for transfers between devices, swap(): return lax.ppermute(v, 'blk', [(i, i ^ 4) for i in range(8)])  16.7 us
    ppermute x4, starting transfers between devices, swap(): return lax.ppermute(v, 'blk', [(i, i ^ 4) for i in range(8)])  14.9 us
    ppermute x18, waiting for transfers between devices, turn(): lax.ppermute(v, 'blk', [(i, i // 4 * 4 + (i % 4 + k) % 4) for i in range(...  14.4 us
    ppermute x1, starting transfers between devices, per_device(): w_core = lax.ppermute(w, 'grp', [(i, i ^ 1) for i in range(32)])  4.59 us
    ppermute x3, starting transfers between devices, per_device(): lax.ppermute(w, 'grp', [(i, i // 8 * 8 + (i % 8 + 2 * k) % 8) for i in ra...  4.49 us
  transfers between devices with their start and end apart: 32, of which 18 were waited for; matrix products, arithmetic and copies ran while one was open for 0% of the time, Pallas kernels for 9%

profile of v4, /device:TPU:1, one launch (start us, length us, event | category | flops | bytes accessed | tf_op | source)
XLA Modules:
  0.0 139.7 jit_solution(3899489316845276324)
XLA Ops:
  4.3 10.0 %all-to-all-start = ((f32[32,40,128]{2,1,0:T(8,128)}), f32[32,40,128]{2,1,0:T(8,128)S(1)}, u32[]{:S(2)}, u32[]{:S(2)}) async-start(f32[32,40,128]{2,1,0:T(8,128)} %shard_map.164), calls=%async_computation | async-start | bytes 1310720 | tf_op jit(solution)/shard_map/all_to_all | solution.py:277
  15.3 2.8 %collective-permute-start = (s32[32,128]{1,0:T(8,128)S(1)}, s32[32,128]{1,0:T(8,128)S(1)}, u32[]{:S(2)}, u32[]{:S(2)}) collective-permute-start(s32[32,128]{1,0:T(8,128)S(1)} %get-tuple-element.51), channel_id=1, source_target_pairs={{0,3},{1,0},{2,1},{3,2},{4,7},{5,4},{6,5},{7,6},{8,11},{9,8},{10,9... | collective-permute-start | bytes 49160 | tf_op jit(solution)/shard_map/ppermute | solution.py:274
  19.1 3.3 %collective-permute-done.1.l2 = s32[32,128]{1,0:T(8,128)S(1)} collective-permute-done((s32[32,128]{1,0:T(8,128)S(1)}, s32[32,128]{1,0:T(8,128)S(1)}, u32[]{:S(2)}, u32[]{:S(2)}) %collective-permute-start.1) | collective-permute-done | bytes 16416 | tf_op jit(solution)/shard_map/ppermute | solution.py:274
  22.7 4.3 %collective-permute-start.3 = (s32[64,128]{1,0:T(8,128)S(1)}, s32[64,128]{1,0:T(8,128)S(1)}, u32[]{:S(2)}, u32[]{:S(2)}) collective-permute-start(s32[64,128]{1,0:T(8,128)S(1)} %pad_add_fusion), channel_id=1, source_target_pairs={{0,4},{1,5},{2,6},{3,7},{4,0},{5,1},{6,2},{7,3},{8,12},{9,13},{10,... | collective-permute-start | bytes 98312 | tf_op jit(solution)/shard_map/ppermute | solution.py:271
  27.0 3.8 %collective-permute-done.3.far = s32[64,128]{1,0:T(8,128)S(1)} collective-permute-done((s32[64,128]{1,0:T(8,128)S(1)}, s32[64,128]{1,0:T(8,128)S(1)}, u32[]{:S(2)}, u32[]{:S(2)}) %collective-permute-start.3) | collective-permute-done | bytes 32800 | tf_op jit(solution)/shard_map/ppermute | solution.py:271
  30.8 2.3 %shard_map.167 = (bf16[8,256,512]{2,1,0:T(8,128)(2,1)S(1)}, s32[1]{0:T(128)}) custom-call(s32[1]{0:T(128)} %bitcast.pos, s32[32,128]{1,0:T(8,128)S(1)} %get-tuple-element.50.l0, s32[32,128]{1,0:T(8,128)S(1)} %collective-permute-done.l1, s32[32,128]{1,0:T(8,128)S(1)} %collective-permute-done.1.l2, s32[32,128]{1,0:T(8,128)S(1)} %collective-permute-done.2.l3, ...), custom_call_target="tpu_custom_call" | custom-call | flops 2147483648 | bytes 98308 | tf_op jit(solution)/shard_map/pallas_call | solution.py:45
  35.4 2.1 %collective-permute-start.4 = (f32[256,128]{1,0:T(8,128)S(1)}, f32[256,128]{1,0:T(8,128)S(1)}, u32[]{:S(2)}, u32[]{:S(2)}) collective-permute-start(f32[256,128]{1,0:T(8,128)S(1)} %get-tuple-element.58), channel_id=1, source_target_pairs={{0,1},{1,2},{2,3},{3,0},{4,5},{5,6},{6,7},{7,4},{8,9},{9,10},{10,1... | collective-permute-start | bytes 393224 | tf_op jit(solution)/shard_map/ppermute | solution.py:274
  37.4 1.5 %collective-permute-start.5 = (f32[256,128]{1,0:T(8,128)S(1)}, f32[256,128]{1,0:T(8,128)S(1)}, u32[]{:S(2)}, u32[]{:S(2)}) collective-permute-start(f32[256,128]{1,0:T(8,128)S(1)} %get-tuple-element.59), channel_id=1, source_target_pairs={{0,3},{1,0},{2,1},{3,2},{4,7},{5,4},{6,5},{7,6},{8,11},{9,8},{10,9... | collective-permute-start | bytes 393224 | tf_op jit(solution)/shard_map/ppermute | solution.py:274
  39.0 1.6 %collective-permute-start.6 = (f32[256,128]{1,0:T(8,128)S(1)}, f32[256,128]{1,0:T(8,128)S(1)}, u32[]{:S(2)}, u32[]{:S(2)}) collective-permute-start(f32[256,128]{1,0:T(8,128)S(1)} %get-tuple-element.60), channel_id=1, source_target_pairs={{0,2},{1,3},{2,0},{3,1},{4,6},{5,7},{6,4},{7,5},{8,10},{9,11},{10,... | collective-permute-start | bytes 393224 | tf_op jit(solution)/shard_map/ppermute | solution.py:274
  40.5 2.3 %shard_map.166 = (bf16[256,1024]{1,0:T(8,128)(2,1)S(1)}, bf16[1024,256]{1,0:T(8,128)(2,1)S(1)}, f32[256,128]{1,0:T(8,128)S(1)}, s32[1]{0:T(128)}) custom-call(s32[48,128]{1,0:T(8,128)S(1)} %get-tuple-element.46.own_to, s32[8,128]{1,0:T(8,128)S(1)} %bitcast.13, s32[8,128]{1,0:T(8,128)S(1)} %bitcast.16, s32[2,128]{1,0:T(2,128)S(1)} %bitcast.25), custom_call_target="tpu_custom_call" | custom-call | flops 2147483648 | bytes 33792 | tf_op jit(solution)/shard_map/pallas_call | solution.py:45
  42.9 4.0 %collective-permute-done.6 = f32[256,128]{1,0:T(8,128)S(1)} collective-permute-done((f32[256,128]{1,0:T(8,128)S(1)}, f32[256,128]{1,0:T(8,128)S(1)}, u32[]{:S(2)}, u32[]{:S(2)}) %collective-permute-start.6) | collective-permute-done | bytes 131104 | tf_op jit(solution)/shard_map/ppermute | solution.py:274
  47.5 4.1 %collective-permute-start.7 = (f32[256,128]{1,0:T(8,128)S(1)}, f32[256,128]{1,0:T(8,128)S(1)}, u32[]{:S(2)}, u32[]{:S(2)}) collective-permute-start(f32[256,128]{1,0:T(8,128)S(1)} %add_add_fusion), channel_id=1, source_target_pairs={{0,4},{1,5},{2,6},{3,7},{4,0},{5,1},{6,2},{7,3},{8,12},{9,13},{10,... | collective-permute-start | bytes 393224 | tf_op jit(solution)/shard_map/ppermute | solution.py:271
  52.9 1.4 collective-permute-start.9
  54.3 1.6 %shard_map.170.bwd = bf16[8,512,256]{2,1,0:T(8,128)(2,1)S(1)} custom-call(s32[1]{0:T(128)} %bitcast.pos, s32[32,128]{1,0:T(8,128)S(1)} %get-tuple-element.50.l0, s32[32,128]{1,0:T(8,128)S(1)} %collective-permute-done.l1, s32[32,128]{1,0:T(8,128)S(1)} %collective-permute-done.1.l2, s32[32,128]{1,0:T(8,128)S(1)} %collective-permute-done.2.l3, ...), custom_call_target="tpu_custom_call" | custom-call | flops 2147483648 | bytes 98308 | tf_op jit(solution)/shard_map/pallas_call | solution.py:45
  59.7 7.6 %all-to-all-start.2 = ((f32[32,16,128]{2,1,0:T(8,128)}), f32[32,16,128]{2,1,0:T(8,128)S(1)}, u32[]{:S(2)}, u32[]{:S(2)}) async-start(f32[32,16,128]{2,1,0:T(8,128)} %shard_map.175), calls=%async_computation.2 | async-start | bytes 524288 | tf_op jit(solution)/shard_map/all_to_all | solution.py:277
  67.3 3.4 %collective-permute-start.14 = (f32[256,128]{1,0:T(8,128)S(1)}, f32[256,128]{1,0:T(8,128)S(1)}, u32[]{:S(2)}, u32[]{:S(2)}) collective-permute-start(f32[256,128]{1,0:T(8,128)S(1)} %get-tuple-element.71.grad_sum.g0), channel_id=1, source_target_pairs={{0,4},{1,5},{2,6},{3,7},{4,0},{5,1},{6,2},{7,3},{8,12},{9,13},{10,... | collective-permute-start | bytes 393224 | tf_op jit(solution)/shard_map/ppermute | solution.py:271
  70.7 1.6 %collective-permute-start.11 = (f32[256,128]{1,0:T(8,128)S(1)}, f32[256,128]{1,0:T(8,128)S(1)}, u32[]{:S(2)}, u32[]{:S(2)}) collective-permute-start(f32[256,128]{1,0:T(8,128)S(1)} %get-tuple-element.71.grad_sum.g0), channel_id=1, source_target_pairs={{0,3},{1,0},{2,1},{3,2},{4,7},{5,4},{6,5},{7,6},{8,11},{9,8},{10,9... | collective-permute-start | bytes 393224 | tf_op jit(solution)/shard_map/ppermute | solution.py:274
  73.6 5.5 %collective-permute-done.14.g4 = f32[256,128]{1,0:T(8,128)S(1)} collective-permute-done((f32[256,128]{1,0:T(8,128)S(1)}, f32[256,128]{1,0:T(8,128)S(1)}, u32[]{:S(2)}, u32[]{:S(2)}) %collective-permute-start.14) | collective-permute-done | bytes 131104 | tf_op jit(solution)/shard_map/ppermute | solution.py:271
  79.1 1.8 %collective-permute-start.15 = (f32[256,128]{1,0:T(8,128)S(1)}, f32[256,128]{1,0:T(8,128)S(1)}, u32[]{:S(2)}, u32[]{:S(2)}) collective-permute-start(f32[256,128]{1,0:T(8,128)S(1)} %collective-permute-done.14.g4), channel_id=1, source_target_pairs={{0,3},{1,0},{2,1},{3,2},{4,7},{5,4},{6,5},{7,6},{8,11},{9,8},{10,9... | collective-permute-start | bytes 393224 | tf_op jit(solution)/shard_map/ppermute | solution.py:274
  84.4 1.9 %collective-permute-done.16.g6 = f32[256,128]{1,0:T(8,128)S(1)} collective-permute-done((f32[256,128]{1,0:T(8,128)S(1)}, f32[256,128]{1,0:T(8,128)S(1)}, u32[]{:S(2)}, u32[]{:S(2)}) %collective-permute-start.16) | collective-permute-done | bytes 131104 | tf_op jit(solution)/shard_map/ppermute | solution.py:274
  86.3 3.7 %collective-permute-done.17.g7 = f32[256,128]{1,0:T(8,128)S(1)} collective-permute-done((f32[256,128]{1,0:T(8,128)S(1)}, f32[256,128]{1,0:T(8,128)S(1)}, u32[]{:S(2)}, u32[]{:S(2)}) %collective-permute-start.17) | collective-permute-done | bytes 131104 | tf_op jit(solution)/shard_map/ppermute | solution.py:274
  90.0 2.3 %shard_map.173 = (f32[256,128]{1,0:T(8,128)S(1)}, f32[32,40,128]{2,1,0:T(8,128)}) custom-call(s32[1]{0:T(128)} %get-tuple-element.54.flag, s32[1]{0:T(128)} %bitcast.pos, s32[32,128]{1,0:T(8,128)S(1)} %get-tuple-element.50.l0, s32[32,128]{1,0:T(8,128)S(1)} %collective-permute-done.l1, s32[32,128]{1,0:T(8,128)S(1)} %collective-permute-done.1.l2, ...), custom_call_target="tpu_custom_call" | custom-call | flops 268435456 | bytes 3899400 | tf_op jit(solution)/shard_map/pallas_call | solution.py:45
  92.3 10.5 %all-to-all-start.1 = ((f32[32,40,128]{2,1,0:T(8,128)}), f32[32,40,128]{2,1,0:T(8,128)S(1)}, u32[]{:S(2)}, u32[]{:S(2)}) async-start(f32[32,40,128]{2,1,0:T(8,128)} %get-tuple-element.77), calls=%async_computation.1 | async-start | bytes 1310720 | tf_op jit(solution)/shard_map/all_to_all | solution.py:277
  103.0 1.5 %collective-permute-start.19 = (f32[16,128]{1,0:T(8,128)S(1)}, f32[16,128]{1,0:T(8,128)S(1)}, u32[]{:S(2)}, u32[]{:S(2)}) collective-permute-start(f32[16,128]{1,0:T(8,128)S(1)} %shard_map.176), channel_id=1, source_target_pairs={{0,2},{1,3},{2,0},{3,1},{4,6},{5,7},{6,4},{7,5},{8,10},{9,11},{10,... | collective-permute-start | bytes 24584 | tf_op jit(solution)/shard_map/ppermute | solution.py:274
  104.4 1.9 %collective-permute-start.20 = (f32[16,128]{1,0:T(8,128)S(1)}, f32[16,128]{1,0:T(8,128)S(1)}, u32[]{:S(2)}, u32[]{:S(2)}) collective-permute-start(f32[16,128]{1,0:T(8,128)S(1)} %shard_map.176), channel_id=1, source_target_pairs={{0,3},{1,0},{2,1},{3,2},{4,7},{5,4},{6,5},{7,6},{8,11},{9,8},{10,9... | collective-permute-start | bytes 24584 | tf_op jit(solution)/shard_map/ppermute | solution.py:274
  107.7 3.1 %collective-permute-start.21 = (f32[16,128]{1,0:T(8,128)S(1)}, f32[16,128]{1,0:T(8,128)S(1)}, u32[]{:S(2)}, u32[]{:S(2)}) collective-permute-start(f32[16,128]{1,0:T(8,128)S(1)} %add_add_fusion.1.near), channel_id=1, source_target_pairs={{0,4},{1,5},{2,6},{3,7},{4,0},{5,1},{6,2},{7,3},{8,12},{9,13},{10,... | collective-permute-start | bytes 24584 | tf_op jit(solution)/shard_map/ppermute | solution.py:271
  110.7 7.0 %collective-permute-done.21.far = f32[16,128]{1,0:T(8,128)S(1)} collective-permute-done((f32[16,128]{1,0:T(8,128)S(1)}, f32[16,128]{1,0:T(8,128)S(1)}, u32[]{:S(2)}, u32[]{:S(2)}) %collective-permute-start.21) | collective-permute-done | bytes 8224 | tf_op jit(solution)/shard_map/ppermute | solution.py:271
  118.2 3.5 %collective-permute-start.23 = (f32[8,128]{1,0:T(8,128)S(1)}, f32[8,128]{1,0:T(8,128)S(1)}, u32[]{:S(2)}, u32[]{:S(2)}) collective-permute-start(f32[8,128]{1,0:T(8,128)S(1)} %get-tuple-element.81), channel_id=1, source_target_pairs={{0,128},{8,136},{16,144},{24,152},{32,160},{40,168},{48,176},{56,1... | collective-permute-start | bytes 12296 | tf_op jit(solution)/shard_map/ppermute | solution.py:327
  122.7 3.3 %collective-permute-done.24 = f32[8,128]{1,0:T(8,128)S(1)} collective-permute-done((f32[8,128]{1,0:T(8,128)S(1)}, f32[8,128]{1,0:T(8,128)S(1)}, u32[]{:S(2)}, u32[]{:S(2)}) %collective-permute-start.24) | collective-permute-done | bytes 4128 | tf_op jit(solution)/shard_map/ppermute | solution.py:327
  126.9 2.4 %collective-permute-start.26 = (f32[32,128]{1,0:T(8,128)S(1)}, f32[32,128]{1,0:T(8,128)S(1)}, u32[]{:S(2)}, u32[]{:S(2)}) collective-permute-start(f32[32,128]{1,0:T(8,128)S(1)} %get-tuple-element.85), channel_id=1, source_target_pairs={{0,32},{8,40},{16,48},{24,56},{32,0},{40,8},{48,16},{56,24},{64,96... | collective-permute-start | bytes 49160 | tf_op jit(solution)/shard_map/ppermute | solution.py:329
  131.9 4.6 %collective-permute-start.28 = (f32[128,128]{1,0:T(8,128)S(1)}, f32[128,128]{1,0:T(8,128)S(1)}, u32[]{:S(2)}, u32[]{:S(2)}) collective-permute-start(f32[128,128]{1,0:T(8,128)S(1)} %constant_dynamic-update-slice_fusion.4.a), channel_id=1, source_target_pairs={{0,8},{8,0},{16,24},{24,16},{32,40},{40,32},{48,56},{56,48},{64,72... | collective-permute-start | bytes 196616 | tf_op jit(solution)/shard_map/ppermute | solution.py:332
  138.1 1.7 %shard_map.174 = f32[256,128]{1,0:T(8,128)} custom-call(f32[32,40,128]{2,1,0:T(8,128)S(1)} %all-to-all-done.1.returned, s32[32,32]{1,0:T(8,128)S(1)} %bitcast.22, s32[8]{0:T(128)S(1)} %bitcast.27, f32[256,128]{1,0:T(8,128)S(1)} %get-tuple-element.78.local), custom_call_target="tpu_custom_call" | custom-call | flops 268435456 | bytes 790560 | tf_op jit(solution)/shard_map/pallas_call | solution.py:45
  (98 shorter events, 26.5 us)
Async XLA Ops:
  4.3 29.7 %all-to-all-start = ((f32[32,40,128]{2,1,0:T(8,128)}), f32[32,40,128]{2,1,0:T(8,128)S(1)}, u32[]{:S(2)}, u32[]{:S(2)}) async-start(f32[32,40,128]{2,1,0:T(8,128)} %shard_map.164), calls=%async_computation | async-start | bytes 1310720 | tf_op jit(solution)/shard_map/all_to_all | solution.py:277
  15.3 3.9 %collective-permute-start = (s32[32,128]{1,0:T(8,128)S(1)}, s32[32,128]{1,0:T(8,128)S(1)}, u32[]{:S(2)}, u32[]{:S(2)}) collective-permute-start(s32[32,128]{1,0:T(8,128)S(1)} %get-tuple-element.51), channel_id=1, source_target_pairs={{0,3},{1,0},{2,1},{3,2},{4,7},{5,4},{6,5},{7,6},{8,11},{9,8},{10,9... | collective-permute-start | bytes 49160 | tf_op jit(solution)/shard_map/ppermute | solution.py:274
  18.1 4.4 %collective-permute-start.1 = (s32[32,128]{1,0:T(8,128)S(1)}, s32[32,128]{1,0:T(8,128)S(1)}, u32[]{:S(2)}, u32[]{:S(2)}) collective-permute-start(s32[32,128]{1,0:T(8,128)S(1)} %get-tuple-element.52), channel_id=1, source_target_pairs={{0,2},{1,3},{2,0},{3,1},{4,6},{5,7},{6,4},{7,5},{8,10},{9,11},{10,... | collective-permute-start | bytes 49160 | tf_op jit(solution)/shard_map/ppermute | solution.py:274
  18.4 4.2 %collective-permute-start.2 = (s32[32,128]{1,0:T(8,128)S(1)}, s32[32,128]{1,0:T(8,128)S(1)}, u32[]{:S(2)}, u32[]{:S(2)}) collective-permute-start(s32[32,128]{1,0:T(8,128)S(1)} %get-tuple-element.53), channel_id=1, source_target_pairs={{0,1},{1,2},{2,3},{3,0},{4,5},{5,6},{6,7},{7,4},{8,9},{9,10},{10,1... | collective-permute-start | bytes 49160 | tf_op jit(solution)/shard_map/ppermute | solution.py:274
  22.7 8.1 %collective-permute-start.3 = (s32[64,128]{1,0:T(8,128)S(1)}, s32[64,128]{1,0:T(8,128)S(1)}, u32[]{:S(2)}, u32[]{:S(2)}) collective-permute-start(s32[64,128]{1,0:T(8,128)S(1)} %pad_add_fusion), channel_id=1, source_target_pairs={{0,4},{1,5},{2,6},{3,7},{4,0},{5,1},{6,2},{7,3},{8,12},{9,13},{10,... | collective-permute-start | bytes 98312 | tf_op jit(solution)/shard_map/ppermute | solution.py:271
  35.4 7.5 %collective-permute-start.4 = (f32[256,128]{1,0:T(8,128)S(1)}, f32[256,128]{1,0:T(8,128)S(1)}, u32[]{:S(2)}, u32[]{:S(2)}) collective-permute-start(f32[256,128]{1,0:T(8,128)S(1)} %get-tuple-element.58), channel_id=1, source_target_pairs={{0,1},{1,2},{2,3},{3,0},{4,5},{5,6},{6,7},{7,4},{8,9},{9,10},{10,1... | collective-permute-start | bytes 393224 | tf_op jit(solution)/shard_map/ppermute | solution.py:274
  37.4 5.5 %collective-permute-start.5 = (f32[256,128]{1,0:T(8,128)S(1)}, f32[256,128]{1,0:T(8,128)S(1)}, u32[]{:S(2)}, u32[]{:S(2)}) collective-permute-start(f32[256,128]{1,0:T(8,128)S(1)} %get-tuple-element.59), channel_id=1, source_target_pairs={{0,3},{1,0},{2,1},{3,2},{4,7},{5,4},{6,5},{7,6},{8,11},{9,8},{10,9... | collective-permute-start | bytes 393224 | tf_op jit(solution)/shard_map/ppermute | solution.py:274
  39.0 7.9 %collective-permute-start.6 = (f32[256,128]{1,0:T(8,128)S(1)}, f32[256,128]{1,0:T(8,128)S(1)}, u32[]{:S(2)}, u32[]{:S(2)}) collective-permute-start(f32[256,128]{1,0:T(8,128)S(1)} %get-tuple-element.60), channel_id=1, source_target_pairs={{0,2},{1,3},{2,0},{3,1},{4,6},{5,7},{6,4},{7,5},{8,10},{9,11},{10,... | collective-permute-start | bytes 393224 | tf_op jit(solution)/shard_map/ppermute | solution.py:274
  47.0 9.8 %collective-permute-start.10 = (f32[256,128]{1,0:T(8,128)S(1)}, f32[256,128]{1,0:T(8,128)S(1)}, u32[]{:S(2)}, u32[]{:S(2)}) collective-permute-start(f32[256,128]{1,0:T(8,128)S(1)} %get-tuple-element.67), channel_id=1, source_target_pairs={{0,2},{1,3},{2,0},{3,1},{4,6},{5,7},{6,4},{7,5},{8,10},{9,11},{10,... | collective-permute-start | bytes 393224 | tf_op jit(solution)/shard_map/ppermute | solution.py:274
  47.5 9.8 %collective-permute-start.7 = (f32[256,128]{1,0:T(8,128)S(1)}, f32[256,128]{1,0:T(8,128)S(1)}, u32[]{:S(2)}, u32[]{:S(2)}) collective-permute-start(f32[256,128]{1,0:T(8,128)S(1)} %add_add_fusion), channel_id=1, source_target_pairs={{0,4},{1,5},{2,6},{3,7},{4,0},{5,1},{6,2},{7,3},{8,12},{9,13},{10,... | collective-permute-start | bytes 393224 | tf_op jit(solution)/shard_map/ppermute | solution.py:271
  51.6 5.7 %collective-permute-start.8 = (f32[256,128]{1,0:T(8,128)S(1)}, f32[256,128]{1,0:T(8,128)S(1)}, u32[]{:S(2)}, u32[]{:S(2)}) collective-permute-start(f32[256,128]{1,0:T(8,128)S(1)} %get-tuple-element.65), channel_id=1, source_target_pairs={{0,1},{1,2},{2,3},{3,0},{4,5},{5,6},{6,7},{7,4},{8,9},{9,10},{10,1... | collective-permute-start | bytes 393224 | tf_op jit(solution)/shard_map/ppermute | solution.py:274
  52.9 4.4 %collective-permute-start.9 = (f32[256,128]{1,0:T(8,128)S(1)}, f32[256,128]{1,0:T(8,128)S(1)}, u32[]{:S(2)}, u32[]{:S(2)}) collective-permute-start(f32[256,128]{1,0:T(8,128)S(1)} %get-tuple-element.66), channel_id=1, source_target_pairs={{0,3},{1,0},{2,1},{3,2},{4,7},{5,4},{6,5},{7,6},{8,11},{9,8},{10,9... | collective-permute-start | bytes 393224 | tf_op jit(solution)/shard_map/ppermute | solution.py:274
  59.7 32.6 %all-to-all-start.2 = ((f32[32,16,128]{2,1,0:T(8,128)}), f32[32,16,128]{2,1,0:T(8,128)S(1)}, u32[]{:S(2)}, u32[]{:S(2)}) async-start(f32[32,16,128]{2,1,0:T(8,128)} %shard_map.175), calls=%async_computation.2 | async-start | bytes 524288 | tf_op jit(solution)/shard_map/all_to_all | solution.py:277
  67.3 11.8 %collective-permute-start.14 = (f32[256,128]{1,0:T(8,128)S(1)}, f32[256,128]{1,0:T(8,128)S(1)}, u32[]{:S(2)}, u32[]{:S(2)}) collective-permute-start(f32[256,128]{1,0:T(8,128)S(1)} %get-tuple-element.71.grad_sum.g0), channel_id=1, source_target_pairs={{0,4},{1,5},{2,6},{3,7},{4,0},{5,1},{6,2},{7,3},{8,12},{9,13},{10,... | collective-permute-start | bytes 393224 | tf_op jit(solution)/shard_map/ppermute | solution.py:271
  70.7 11.6 %collective-permute-start.11 = (f32[256,128]{1,0:T(8,128)S(1)}, f32[256,128]{1,0:T(8,128)S(1)}, u32[]{:S(2)}, u32[]{:S(2)}) collective-permute-start(f32[256,128]{1,0:T(8,128)S(1)} %get-tuple-element.71.grad_sum.g0), channel_id=1, source_target_pairs={{0,3},{1,0},{2,1},{3,2},{4,7},{5,4},{6,5},{7,6},{8,11},{9,8},{10,9... | collective-permute-start | bytes 393224 | tf_op jit(solution)/shard_map/ppermute | solution.py:274
  72.2 12.2 %collective-permute-start.12 = (f32[256,128]{1,0:T(8,128)S(1)}, f32[256,128]{1,0:T(8,128)S(1)}, u32[]{:S(2)}, u32[]{:S(2)}) collective-permute-start(f32[256,128]{1,0:T(8,128)S(1)} %get-tuple-element.71.grad_sum.g0), channel_id=1, source_target_pairs={{0,2},{1,3},{2,0},{3,1},{4,6},{5,7},{6,4},{7,5},{8,10},{9,11},{10,... | collective-permute-start | bytes 393224 | tf_op jit(solution)/shard_map/ppermute | solution.py:274
  73.5 10.9 %collective-permute-start.13 = (f32[256,128]{1,0:T(8,128)S(1)}, f32[256,128]{1,0:T(8,128)S(1)}, u32[]{:S(2)}, u32[]{:S(2)}) collective-permute-start(f32[256,128]{1,0:T(8,128)S(1)} %get-tuple-element.71.grad_sum.g0), channel_id=1, source_target_pairs={{0,1},{1,2},{2,3},{3,0},{4,5},{5,6},{6,7},{7,4},{8,9},{9,10},{10,1... | collective-permute-start | bytes 393224 | tf_op jit(solution)/shard_map/ppermute | solution.py:274
  79.1 5.3 %collective-permute-start.15 = (f32[256,128]{1,0:T(8,128)S(1)}, f32[256,128]{1,0:T(8,128)S(1)}, u32[]{:S(2)}, u32[]{:S(2)}) collective-permute-start(f32[256,128]{1,0:T(8,128)S(1)} %collective-permute-done.14.g4), channel_id=1, source_target_pairs={{0,3},{1,0},{2,1},{3,2},{4,7},{5,4},{6,5},{7,6},{8,11},{9,8},{10,9... | collective-permute-start | bytes 393224 | tf_op jit(solution)/shard_map/ppermute | solution.py:274
  80.9 5.4 %collective-permute-start.16 = (f32[256,128]{1,0:T(8,128)S(1)}, f32[256,128]{1,0:T(8,128)S(1)}, u32[]{:S(2)}, u32[]{:S(2)}) collective-permute-start(f32[256,128]{1,0:T(8,128)S(1)} %collective-permute-done.14.g4), channel_id=1, source_target_pairs={{0,2},{1,3},{2,0},{3,1},{4,6},{5,7},{6,4},{7,5},{8,10},{9,11},{10,... | collective-permute-start | bytes 393224 | tf_op jit(solution)/shard_map/ppermute | solution.py:274
  82.3 7.7 %collective-permute-start.17 = (f32[256,128]{1,0:T(8,128)S(1)}, f32[256,128]{1,0:T(8,128)S(1)}, u32[]{:S(2)}, u32[]{:S(2)}) collective-permute-start(f32[256,128]{1,0:T(8,128)S(1)} %collective-permute-done.14.g4), channel_id=1, source_target_pairs={{0,1},{1,2},{2,3},{3,0},{4,5},{5,6},{6,7},{7,4},{8,9},{9,10},{10,1... | collective-permute-start | bytes 393224 | tf_op jit(solution)/shard_map/ppermute | solution.py:274
  92.3 45.8 %all-to-all-start.1 = ((f32[32,40,128]{2,1,0:T(8,128)}), f32[32,40,128]{2,1,0:T(8,128)S(1)}, u32[]{:S(2)}, u32[]{:S(2)}) async-start(f32[32,40,128]{2,1,0:T(8,128)} %get-tuple-element.77), calls=%async_computation.1 | async-start | bytes 1310720 | tf_op jit(solution)/shard_map/all_to_all | solution.py:277
  102.9 4.1 %collective-permute-start.18 = (f32[16,128]{1,0:T(8,128)S(1)}, f32[16,128]{1,0:T(8,128)S(1)}, u32[]{:S(2)}, u32[]{:S(2)}) collective-permute-start(f32[16,128]{1,0:T(8,128)S(1)} %shard_map.176), channel_id=1, source_target_pairs={{0,1},{1,2},{2,3},{3,0},{4,5},{5,6},{6,7},{7,4},{8,9},{9,10},{10,1... | collective-permute-start | bytes 24584 | tf_op jit(solution)/shard_map/ppermute | solution.py:274
  103.0 4.4 %collective-permute-start.19 = (f32[16,128]{1,0:T(8,128)S(1)}, f32[16,128]{1,0:T(8,128)S(1)}, u32[]{:S(2)}, u32[]{:S(2)}) collective-permute-start(f32[16,128]{1,0:T(8,128)S(1)} %shard_map.176), channel_id=1, source_target_pairs={{0,2},{1,3},{2,0},{3,1},{4,6},{5,7},{6,4},{7,5},{8,10},{9,11},{10,... | collective-permute-start | bytes 24584 | tf_op jit(solution)/shard_map/ppermute | solution.py:274
  104.4 3.2 %collective-permute-start.20 = (f32[16,128]{1,0:T(8,128)S(1)}, f32[16,128]{1,0:T(8,128)S(1)}, u32[]{:S(2)}, u32[]{:S(2)}) collective-permute-start(f32[16,128]{1,0:T(8,128)S(1)} %shard_map.176), channel_id=1, source_target_pairs={{0,3},{1,0},{2,1},{3,2},{4,7},{5,4},{6,5},{7,6},{8,11},{9,8},{10,9... | collective-permute-start | bytes 24584 | tf_op jit(solution)/shard_map/ppermute | solution.py:274
  107.7 10.0 %collective-permute-start.21 = (f32[16,128]{1,0:T(8,128)S(1)}, f32[16,128]{1,0:T(8,128)S(1)}, u32[]{:S(2)}, u32[]{:S(2)}) collective-permute-start(f32[16,128]{1,0:T(8,128)S(1)} %add_add_fusion.1.near), channel_id=1, source_target_pairs={{0,4},{1,5},{2,6},{3,7},{4,0},{5,1},{6,2},{7,3},{8,12},{9,13},{10,... | collective-permute-start | bytes 24584 | tf_op jit(solution)/shard_map/ppermute | solution.py:271
  118.2 3.6 %collective-permute-start.22 = (f32[8,128]{1,0:T(8,128)S(1)}, f32[8,128]{1,0:T(8,128)S(1)}, u32[]{:S(2)}, u32[]{:S(2)}) collective-permute-start(f32[8,128]{1,0:T(8,128)S(1)} %get-tuple-element.81), channel_id=1, source_target_pairs={{0,64},{8,72},{16,80},{24,88},{32,96},{40,104},{48,112},{56,120},{... | collective-permute-start | bytes 12296 | tf_op jit(solution)/shard_map/ppermute | solution.py:327
  118.2 4.5 %collective-permute-start.23 = (f32[8,128]{1,0:T(8,128)S(1)}, f32[8,128]{1,0:T(8,128)S(1)}, u32[]{:S(2)}, u32[]{:S(2)}) collective-permute-start(f32[8,128]{1,0:T(8,128)S(1)} %get-tuple-element.81), channel_id=1, source_target_pairs={{0,128},{8,136},{16,144},{24,152},{32,160},{40,168},{48,176},{56,1... | collective-permute-start | bytes 12296 | tf_op jit(solution)/shard_map/ppermute | solution.py:327
  121.7 4.3 %collective-permute-start.24 = (f32[8,128]{1,0:T(8,128)S(1)}, f32[8,128]{1,0:T(8,128)S(1)}, u32[]{:S(2)}, u32[]{:S(2)}) collective-permute-start(f32[8,128]{1,0:T(8,128)S(1)} %get-tuple-element.81), channel_id=1, source_target_pairs={{0,192},{8,200},{16,208},{24,216},{32,224},{40,232},{48,240},{56,2... | collective-permute-start | bytes 12296 | tf_op jit(solution)/shard_map/ppermute | solution.py:327
  126.0 4.5 %collective-permute-start.25 = (f32[32,128]{1,0:T(8,128)S(1)}, f32[32,128]{1,0:T(8,128)S(1)}, u32[]{:S(2)}, u32[]{:S(2)}) collective-permute-start(f32[32,128]{1,0:T(8,128)S(1)} %get-tuple-element.85), channel_id=1, source_target_pairs={{0,16},{8,24},{16,32},{24,40},{32,48},{40,56},{48,0},{56,8},{64,80... | collective-permute-start | bytes 49160 | tf_op jit(solution)/shard_map/ppermute | solution.py:329
  126.9 4.1 %collective-permute-start.26 = (f32[32,128]{1,0:T(8,128)S(1)}, f32[32,128]{1,0:T(8,128)S(1)}, u32[]{:S(2)}, u32[]{:S(2)}) collective-permute-start(f32[32,128]{1,0:T(8,128)S(1)} %get-tuple-element.85), channel_id=1, source_target_pairs={{0,32},{8,40},{16,48},{24,56},{32,0},{40,8},{48,16},{56,24},{64,96... | collective-permute-start | bytes 49160 | tf_op jit(solution)/shard_map/ppermute | solution.py:329
  129.3 2.6 %collective-permute-start.27 = (f32[32,128]{1,0:T(8,128)S(1)}, f32[32,128]{1,0:T(8,128)S(1)}, u32[]{:S(2)}, u32[]{:S(2)}) collective-permute-start(f32[32,128]{1,0:T(8,128)S(1)} %get-tuple-element.85), channel_id=1, source_target_pairs={{0,48},{8,56},{16,0},{24,8},{32,16},{40,24},{48,32},{56,40},{64,11... | collective-permute-start | bytes 49160 | tf_op jit(solution)/shard_map/ppermute | solution.py:329
  131.9 5.5 %collective-permute-start.28 = (f32[128,128]{1,0:T(8,128)S(1)}, f32[128,128]{1,0:T(8,128)S(1)}, u32[]{:S(2)}, u32[]{:S(2)}) collective-permute-start(f32[128,128]{1,0:T(8,128)S(1)} %constant_dynamic-update-slice_fusion.4.a), channel_id=1, source_target_pairs={{0,8},{8,0},{16,24},{24,16},{32,40},{40,32},{48,56},{56,48},{64,72... | collective-permute-start | bytes 196616 | tf_op jit(solution)/shard_map/ppermute | solution.py:332
  (18 other events, 217.0 us)

commit v5 on v3

--- a/solution.py
+++ b/solution.py
@@ -39,7 +39,7 @@
     return jnp.concatenate(ref_rows, axis=1)
 
 
-def call(kernel, out_shape, args, specs=None, scratch=(), flops=1 << 28):
+def call(kernel, out_shape, args, specs=None, scratch=(), flops=1 << 28, limit=16 << 20):
     whole = pl.BlockSpec(memory_space=pltpu.VMEM)
     size = sum(int(a.size) * a.dtype.itemsize for a in args)
     return pl.pallas_call(
@@ -50,7 +50,7 @@
             lambda s: pl.BlockSpec(memory_space=pltpu.SMEM if s.shape == (1,) else pltpu.VMEM), out_shape
         ),
         scratch_shapes=list(scratch),
-        compiler_params=pltpu.CompilerParams(vmem_limit_bytes=16 << 20),
+        compiler_params=pltpu.CompilerParams(vmem_limit_bytes=limit),
         cost_estimate=pl.CostEstimate(flops=flops, bytes_accessed=size, transcendentals=0),
     )(*args)
 
@@ -64,12 +64,20 @@
     return jnp.where(x > -0.35, series, jnp.exp(x) - 1.0)
 
 
-def k_send(features, send, hub, out):
+def send_hot(send):
+    return lanes([one_hot(lanes([send[4 * i + j : 4 * i + j + 1, :] for j in range(4)]), 256) for i in range(8)])
+
+
+def k_send(features_hbm, send_hbm, hub_hbm, out, features, send, hub, sems):
+    pairs = ((features_hbm, features), (send_hbm, send), (hub_hbm, hub))
+    copies = [pltpu.make_async_copy(src, dst, sems.at[n]) for n, (src, dst) in enumerate(pairs)]
+    for copy in copies:
+        copy.start()
+    for copy in copies:
+        copy.wait()
     x = halves(features[...])
-    hot = lanes([one_hot(send[i : i + 1, :], 256) for i in range(8)])
-    rows = joined(dot(hot, x, TN))
-    out[:, 0:32, :] = rows.reshape(32, 32, 128)
-    hub_rows = jnp.concatenate([features[pl.ds(hub[j], 1), :] for j in range(8)], axis=0)
+    out[:, 0:32, :] = joined(dot(send_hot(send), x, TN)).reshape(32, 32, 128)
+    hub_rows = joined(dot(one_hot(hub[...], 256), x, TN))
     for p in range(32):
         out[p, 32:40, :] = hub_rows
 
@@ -207,7 +215,7 @@
 
 
 def k_back(flag, pos, l0, l1, l2, l3, far, g0, g1, g2, g3, g4, g5, g6, g7, bwd, root, local, hubs, total):
-    xs = [halves(g[...]) for g in (g0, g1, g2, g3, g4, g5, g6, g7)]
+    xs = [halves(g[0:256, :]) for g in (g0, g1, g2, g3, g4, g5, g6, g7)]
     acc = dot(bwd[0], xs[0])
     for r in range(1, 8):
         acc = acc + dot(bwd[r], xs[r])
@@ -222,8 +230,13 @@
     local[...] = root[...] + total[0:256, :]
 
 
-def k_sum(weights, out):
-    out[...] = jnp.sum(weights[...], axis=0)
+def k_join(grad, weights, out):
+    out[0:256, :] = grad[...]
+    out[256:272, :] = jnp.sum(weights[...], axis=0)
+
+
+def k_sum(a, b, c, d, out):
+    out[...] = a[256:272, :] + b[256:272, :] + c[256:272, :] + d[256:272, :]
 
 
 def k_pack(factor, slots, hubs, near, far, out, bias):
@@ -236,8 +249,7 @@
 
 
 def k_final(returned, send, hub, local, out, w_neigh, w_root):
-    hot = lanes([one_hot(send[i : i + 1, :], 256) for i in range(8)])
-    acc = joined(dot(hot, halves(returned[:, 0:32, :].reshape(1024, 128))))
+    acc = joined(dot(send_hot(send), halves(returned[:, 0:32, :].reshape(1024, 128))))
     rows = jnp.sum(returned[:, 32:40, :], axis=0)
     out[...] = local[...] + acc
     for j in range(8):
@@ -248,7 +260,7 @@
 
 def per_device(features, w_neigh, w_root, bias, grad_out, tile_coord, tile_edge,
                send_idx, halo_dst, halo_src, hub_idx, hub_dst, hub_src):
-    send = send_idx.reshape(8, 128)
+    send = send_idx.reshape(32, 32)
     hub = hub_idx.reshape(8)
     hub_to = hub_dst.reshape(2, 128)
     hub_from = hub_src.reshape(2, 128)
@@ -266,9 +278,13 @@
     def exchange(v, axis):
         return lax.all_to_all(v, axis, split_axis=0, concat_axis=0, tiled=True)
 
-    vm, sm = (pl.BlockSpec(memory_space=s) for s in (pltpu.VMEM, pltpu.SMEM))
-
-    outgoing = call(k_send, shape((32, 40, 128)), (features, send, hub), [vm, vm, sm])
+    vm, sm, hb = (pl.BlockSpec(memory_space=s) for s in (pltpu.VMEM, pltpu.SMEM, pltpu.HBM))
+
+    outgoing = call(
+        k_send, shape((32, 40, 128)), (features, send, hub_idx.reshape(1, 8)), [hb] * 3,
+        [pltpu.VMEM((256, 128), F32), pltpu.VMEM((32, 32), I32), pltpu.VMEM((1, 8), I32), pltpu.SemaphoreType.DMA((3,))],
+        limit=60 << 20,
+    )
     outgoing, coord = lax.optimization_barrier((outgoing, tile_coord.reshape(8, 2, 6)))
     incoming = exchange(outgoing, "grp")
     own_to, m0, m1, m2, m3 = call(
@@ -302,9 +318,10 @@
         k_slots, [shape((1024, 128)), block], (h_flag, halo_to, halo_from, grad_sum, h_bwd, grad_pre, w_root),
         [sm] + [vm] * 6,
     )
+    g4, weights, g1, g2, g3, slots = lax.optimization_barrier((g4, weights, g1, g2, g3, slots))
+    g4 = call(k_join, shape((272, 128)), (g4, weights))
     g5, g7, g6 = turn(g4, 3), turn(g4, 1), turn(g4, 2)
-    w = call(k_sum, shape((16, 128)), (weights,))
-    w = w + turn(w, 1) + turn(w, 2) + turn(w, 3)
+    w = call(k_sum, shape((16, 128)), (g4, g5, g6, g7))
     w_far = swap(w)
     local, hubs = call(
         k_back, [block, shape((32, 8, 128))],

time: 135 us -> 131 us (0.970)
  starting transfers between devices: 55.1 us -> 50.4 us
  blocking collectives: 25 us -> 26.6 us
    all_to_all x2, waiting for transfers between devices: 13.9 us -> 3.41 us  [exchange(): return lax.all_to_all(v, axis, split_axis=0, concat_axis=0, tiled=True)]
    ppermute x18 -> x15, starting transfers between devices: 24.2 us -> 18.7 us  [turn(): lax.ppermute(v, 'blk', [(i, i // 4 * 4 + (i % 4 + k) % 4) for i in range(...]
    ppermute x18 -> x15, waiting for transfers between devices: 13.6 us -> 19 us  [turn(): lax.ppermute(v, 'blk', [(i, i // 4 * 4 + (i % 4 + k) % 4) for i in range(...]
    ppermute x4, waiting for transfers between devices: 4.33 us -> 8.56 us  [swap(): return lax.ppermute(v, 'blk', [(i, i ^ 4) for i in range(8)])]
    all_to_all x1, blocking collectives: 25 us -> 26.6 us  [exchange(): return lax.all_to_all(v, axis, split_axis=0, concat_axis=0, tiled=True)]
    pallas_call x14 -> x15, Pallas kernels: 18.1 us -> 19 us  [call(): pl.pallas_call(kernel, out_shape=out_shape, in_specs=[whole] * len(args)...]
    unnamed x32 -> x36, local copies, waits for them, and re-layouts: 2.67 us -> 2.76 us
  transfers between devices with their start and end apart: 24 -> 21, of which waited for: 12 -> 13; matrix products, arithmetic and copies ran while one was open for 0% -> 0% of each run, Pallas kernels for 8% -> 8%
where the time goes in v5:
time: 131 us
  starting transfers between devices  50.4 us (38%)
  waiting for transfers between devices  31 us (24%)
  blocking collectives  26.6 us (20%)
  Pallas kernels  19 us (15%)
  local copies, waits for them, and re-layouts  2.86 us (2%)
    all_to_all x1, blocking collectives, exchange(): return lax.all_to_all(v, axis, split_axis=0, concat_axis=0, tiled=True)  26.6 us
    ppermute x15, waiting for transfers between devices, turn(): lax.ppermute(v, 'blk', [(i, i // 4 * 4 + (i % 4 + k) % 4) for i in range(...  19 us
    pallas_call x15, Pallas kernels, call(): pl.pallas_call(kernel, out_shape=out_shape, in_specs=[whole] * len(args)...  19 us
    ppermute x15, starting transfers between devices, turn(): lax.ppermute(v, 'blk', [(i, i // 4 * 4 + (i % 4 + k) % 4) for i in range(...  18.7 us
    all_to_all x2, starting transfers between devices, exchange(): return lax.all_to_all(v, axis, split_axis=0, concat_axis=0, tiled=True)  17.6 us
    ppermute x4, starting transfers between devices, swap(): return lax.ppermute(v, 'blk', [(i, i ^ 4) for i in range(8)])  14.1 us
    ppermute x4, waiting for transfers between devices, swap(): return lax.ppermute(v, 'blk', [(i, i ^ 4) for i in range(8)])  8.56 us
    all_to_all x2, waiting for transfers between devices, exchange(): return lax.all_to_all(v, axis, split_axis=0, concat_axis=0, tiled=True)  3.41 us
  transfers between devices with their start and end apart: 21, of which 13 were waited for; matrix products, arithmetic and copies ran while one was open for 0% of the time, Pallas kernels for 8%

profile of v5, /device:TPU:1, one launch (start us, length us, event | category | flops | bytes accessed | tf_op | source)
XLA Modules:
  0.0 130.7 jit_solution(76867826205776309)
XLA Ops:
  0.7 2.3 %shard_map.164 = f32[32,40,128]{2,1,0:T(8,128)} custom-call(f32[256,128]{1,0:T(8,128)} %features.5, s32[32,32]{1,0:T(8,128)} %bitcast.20, s32[1,8]{1,0:T(1,128)} %bitcast.25), custom_call_target="tpu_custom_call" | custom-call | flops 268435456 | bytes 135200 | tf_op jit(solution)/shard_map/pallas_call | solution.py:45
  3.0 10.0 %all-to-all-start = ((f32[32,40,128]{2,1,0:T(8,128)}), f32[32,40,128]{2,1,0:T(8,128)S(1)}, u32[]{:S(2)}, u32[]{:S(2)}) async-start(f32[32,40,128]{2,1,0:T(8,128)} %shard_map.164), calls=%async_computation | async-start | bytes 1310720 | tf_op jit(solution)/shard_map/all_to_all | solution.py:279
  14.0 2.8 %collective-permute-start = (s32[32,128]{1,0:T(8,128)S(1)}, s32[32,128]{1,0:T(8,128)S(1)}, u32[]{:S(2)}, u32[]{:S(2)}) collective-permute-start(s32[32,128]{1,0:T(8,128)S(1)} %get-tuple-element.57), channel_id=1, source_target_pairs={{0,3},{1,0},{2,1},{3,2},{4,7},{5,4},{6,5},{7,6},{8,11},{9,8},{10,9... | collective-permute-start | bytes 49160 | tf_op jit(solution)/shard_map/ppermute | solution.py:276
  17.8 3.3 %collective-permute-done.1.l2 = s32[32,128]{1,0:T(8,128)S(1)} collective-permute-done((s32[32,128]{1,0:T(8,128)S(1)}, s32[32,128]{1,0:T(8,128)S(1)}, u32[]{:S(2)}, u32[]{:S(2)}) %collective-permute-start.1) | collective-permute-done | bytes 16416 | tf_op jit(solution)/shard_map/ppermute | solution.py:276
  21.3 4.3 %collective-permute-start.3 = (s32[64,128]{1,0:T(8,128)S(1)}, s32[64,128]{1,0:T(8,128)S(1)}, u32[]{:S(2)}, u32[]{:S(2)}) collective-permute-start(s32[64,128]{1,0:T(8,128)S(1)} %pad_add_fusion), channel_id=1, source_target_pairs={{0,4},{1,5},{2,6},{3,7},{4,0},{5,1},{6,2},{7,3},{8,12},{9,13},{10,... | collective-permute-start | bytes 98312 | tf_op jit(solution)/shard_map/ppermute | solution.py:273
  25.6 3.8 %collective-permute-done.3.far = s32[64,128]{1,0:T(8,128)S(1)} collective-permute-done((s32[64,128]{1,0:T(8,128)S(1)}, s32[64,128]{1,0:T(8,128)S(1)}, u32[]{:S(2)}, u32[]{:S(2)}) %collective-permute-start.3) | collective-permute-done | bytes 32800 | tf_op jit(solution)/shard_map/ppermute | solution.py:273
  29.5 2.3 %shard_map.167 = (bf16[8,256,512]{2,1,0:T(8,128)(2,1)S(1)}, s32[1]{0:T(128)}) custom-call(s32[1]{0:T(128)} %bitcast.pos, s32[32,128]{1,0:T(8,128)S(1)} %get-tuple-element.56.l0, s32[32,128]{1,0:T(8,128)S(1)} %collective-permute-done.l1, s32[32,128]{1,0:T(8,128)S(1)} %collective-permute-done.1.l2, s32[32,128]{1,0:T(8,128)S(1)} %collective-permute-done.2.l3, ...), custom_call_target="tpu_custom_call" | custom-call | flops 2147483648 | bytes 98308 | tf_op jit(solution)/shard_map/pallas_call | solution.py:45
  32.7 1.4 %shard_map.168 = (f32[256,128]{1,0:T(8,128)S(1)}, f32[256,128]{1,0:T(8,128)S(1)}, f32[256,128]{1,0:T(8,128)S(1)}, f32[256,128]{1,0:T(8,128)S(1)}, f32[256,128]{1...) custom-call(s32[1]{0:T(128)} %get-tuple-element.60.flag, s32[1]{0:T(128)} %bitcast.pos, ...), custom_call_target="tpu_custom_call" | custom-call | flops 268435456 | bytes 2981896 | tf_op jit(solution)/shard_map/pallas_call | solution.py:45
  34.1 2.1 %collective-permute-start.4 = (f32[256,128]{1,0:T(8,128)S(1)}, f32[256,128]{1,0:T(8,128)S(1)}, u32[]{:S(2)}, u32[]{:S(2)}) collective-permute-start(f32[256,128]{1,0:T(8,128)S(1)} %get-tuple-element.64), channel_id=1, source_target_pairs={{0,1},{1,2},{2,3},{3,0},{4,5},{5,6},{6,7},{7,4},{8,9},{9,10},{10,1... | collective-permute-start | bytes 393224 | tf_op jit(solution)/shard_map/ppermute | solution.py:276
  36.1 1.5 %collective-permute-start.5 = (f32[256,128]{1,0:T(8,128)S(1)}, f32[256,128]{1,0:T(8,128)S(1)}, u32[]{:S(2)}, u32[]{:S(2)}) collective-permute-start(f32[256,128]{1,0:T(8,128)S(1)} %get-tuple-element.65), channel_id=1, source_target_pairs={{0,3},{1,0},{2,1},{3,2},{4,7},{5,4},{6,5},{7,6},{8,11},{9,8},{10,9... | collective-permute-start | bytes 393224 | tf_op jit(solution)/shard_map/ppermute | solution.py:276
  37.7 1.6 %collective-permute-start.6 = (f32[256,128]{1,0:T(8,128)S(1)}, f32[256,128]{1,0:T(8,128)S(1)}, u32[]{:S(2)}, u32[]{:S(2)}) collective-permute-start(f32[256,128]{1,0:T(8,128)S(1)} %get-tuple-element.66), channel_id=1, source_target_pairs={{0,2},{1,3},{2,0},{3,1},{4,6},{5,7},{6,4},{7,5},{8,10},{9,11},{10,... | collective-permute-start | bytes 393224 | tf_op jit(solution)/shard_map/ppermute | solution.py:276
  39.2 2.3 %shard_map.166 = (bf16[256,1024]{1,0:T(8,128)(2,1)S(1)}, bf16[1024,256]{1,0:T(8,128)(2,1)S(1)}, f32[256,128]{1,0:T(8,128)S(1)}, s32[1]{0:T(128)}) custom-call(s32[48,128]{1,0:T(8,128)S(1)} %get-tuple-element.52.own_to, s32[8,128]{1,0:T(8,128)S(1)} %bitcast.12, s32[8,128]{1,0:T(8,128)S(1)} %bitcast.15, s32[2,128]{1,0:T(2,128)S(1)} %bitcast.24), custom_call_target="tpu_custom_call" | custom-call | flops 2147483648 | bytes 33792 | tf_op jit(solution)/shard_map/pallas_call | solution.py:45
  41.6 4.0 %collective-permute-done.6 = f32[256,128]{1,0:T(8,128)S(1)} collective-permute-done((f32[256,128]{1,0:T(8,128)S(1)}, f32[256,128]{1,0:T(8,128)S(1)}, u32[]{:S(2)}, u32[]{:S(2)}) %collective-permute-start.6) | collective-permute-done | bytes 131104 | tf_op jit(solution)/shard_map/ppermute | solution.py:276
  46.2 4.1 %collective-permute-start.7 = (f32[256,128]{1,0:T(8,128)S(1)}, f32[256,128]{1,0:T(8,128)S(1)}, u32[]{:S(2)}, u32[]{:S(2)}) collective-permute-start(f32[256,128]{1,0:T(8,128)S(1)} %add_add_fusion), channel_id=1, source_target_pairs={{0,4},{1,5},{2,6},{3,7},{4,0},{5,1},{6,2},{7,3},{8,12},{9,13},{10,... | collective-permute-start | bytes 393224 | tf_op jit(solution)/shard_map/ppermute | solution.py:273
  50.3 1.3 collective-permute-start.8
  51.6 1.4 %collective-permute-start.9 = (f32[256,128]{1,0:T(8,128)S(1)}, f32[256,128]{1,0:T(8,128)S(1)}, u32[]{:S(2)}, u32[]{:S(2)}) collective-permute-start(f32[256,128]{1,0:T(8,128)S(1)} %get-tuple-element.72), channel_id=1, source_target_pairs={{0,3},{1,0},{2,1},{3,2},{4,7},{5,4},{6,5},{7,6},{8,11},{9,8},{10,9... | collective-permute-start | bytes 393224 | tf_op jit(solution)/shard_map/ppermute | solution.py:276
  53.0 1.6 %shard_map.170.bwd = bf16[8,512,256]{2,1,0:T(8,128)(2,1)S(1)} custom-call(s32[1]{0:T(128)} %bitcast.pos, s32[32,128]{1,0:T(8,128)S(1)} %get-tuple-element.56.l0, s32[32,128]{1,0:T(8,128)S(1)} %collective-permute-done.l1, s32[32,128]{1,0:T(8,128)S(1)} %collective-permute-done.1.l2, s32[32,128]{1,0:T(8,128)S(1)} %collective-permute-done.2.l3, ...), custom_call_target="tpu_custom_call" | custom-call | flops 2147483648 | bytes 98308 | tf_op jit(solution)/shard_map/pallas_call | solution.py:45
  58.4 7.6 %all-to-all-start.1 = ((f32[32,16,128]{2,1,0:T(8,128)}), f32[32,16,128]{2,1,0:T(8,128)S(1)}, u32[]{:S(2)}, u32[]{:S(2)}) async-start(f32[32,16,128]{2,1,0:T(8,128)} %shard_map.172), calls=%async_computation.1 | async-start | bytes 524288 | tf_op jit(solution)/shard_map/all_to_all | solution.py:279
  66.0 3.4 %collective-permute-start.11 = (f32[256,128]{1,0:T(8,128)S(1)}, f32[256,128]{1,0:T(8,128)S(1)}, u32[]{:S(2)}, u32[]{:S(2)}) collective-permute-start(f32[256,128]{1,0:T(8,128)S(1)} %get-tuple-element.77.grad_sum.g0), channel_id=1, source_target_pairs={{0,4},{1,5},{2,6},{3,7},{4,0},{5,1},{6,2},{7,3},{8,12},{9,13},{10,... | collective-permute-start | bytes 393224 | tf_op jit(solution)/shard_map/ppermute | solution.py:273
  69.4 1.6 %collective-permute-start.12 = (f32[256,128]{1,0:T(8,128)S(1)}, f32[256,128]{1,0:T(8,128)S(1)}, u32[]{:S(2)}, u32[]{:S(2)}) collective-permute-start(f32[256,128]{1,0:T(8,128)S(1)} %get-tuple-element.77.grad_sum.g0), channel_id=1, source_target_pairs={{0,3},{1,0},{2,1},{3,2},{4,7},{5,4},{6,5},{7,6},{8,11},{9,8},{10,9... | collective-permute-start | bytes 393224 | tf_op jit(solution)/shard_map/ppermute | solution.py:276
  70.9 1.3 %collective-permute-start.13 = (f32[256,128]{1,0:T(8,128)S(1)}, f32[256,128]{1,0:T(8,128)S(1)}, u32[]{:S(2)}, u32[]{:S(2)}) collective-permute-start(f32[256,128]{1,0:T(8,128)S(1)} %get-tuple-element.77.grad_sum.g0), channel_id=1, source_target_pairs={{0,2},{1,3},{2,0},{3,1},{4,6},{5,7},{6,4},{7,5},{8,10},{9,11},{10,... | collective-permute-start | bytes 393224 | tf_op jit(solution)/shard_map/ppermute | solution.py:276
  76.3 1.5 %collective-permute-done.11.grad = f32[256,128]{1,0:T(8,128)S(1)} collective-permute-done((f32[256,128]{1,0:T(8,128)S(1)}, f32[256,128]{1,0:T(8,128)S(1)}, u32[]{:S(2)}, u32[]{:S(2)}) %collective-permute-start.11) | collective-permute-done | bytes 131104 | tf_op jit(solution)/shard_map/ppermute | solution.py:273
  77.8 2.3 %collective-permute-done.14.g3 = f32[256,128]{1,0:T(8,128)S(1)} collective-permute-done((f32[256,128]{1,0:T(8,128)S(1)}, f32[256,128]{1,0:T(8,128)S(1)}, u32[]{:S(2)}, u32[]{:S(2)}) %collective-permute-start.14) | collective-permute-done | bytes 131104 | tf_op jit(solution)/shard_map/ppermute | solution.py:276
  80.2 2.6 %all-to-all-done.1.weights = f32[32,16,128]{2,1,0:T(8,128)S(1)} async-done(((f32[32,16,128]{2,1,0:T(8,128)}), f32[32,16,128]{2,1,0:T(8,128)S(1)}, u32[]{:S(2)}, u32[]{:S(2)}) %all-to-all-start.1) | async-done | bytes 262176 | tf_op jit(solution)/shard_map/all_to_all | solution.py:279
  82.8 2.6 %collective-permute-start.15 = (f32[272,128]{1,0:T(8,128)S(1)}, f32[272,128]{1,0:T(8,128)S(1)}, u32[]{:S(2)}, u32[]{:S(2)}) collective-permute-start(f32[272,128]{1,0:T(8,128)S(1)} %shard_map.174.g4.a), channel_id=1, source_target_pairs={{0,3},{1,0},{2,1},{3,2},{4,7},{5,4},{6,5},{7,6},{8,11},{9,8},{10,9... | collective-permute-start | bytes 417800 | tf_op jit(solution)/shard_map/ppermute | solution.py:276
  86.3 4.7 %collective-permute-done.15.g5.b = f32[272,128]{1,0:T(8,128)S(1)} collective-permute-done((f32[272,128]{1,0:T(8,128)S(1)}, f32[272,128]{1,0:T(8,128)S(1)}, u32[]{:S(2)}, u32[]{:S(2)}) %collective-permute-start.15) | collective-permute-done | bytes 139296 | tf_op jit(solution)/shard_map/ppermute | solution.py:276
  91.6 3.9 %collective-permute-done.17.g7.d = f32[272,128]{1,0:T(8,128)S(1)} collective-permute-done((f32[272,128]{1,0:T(8,128)S(1)}, f32[272,128]{1,0:T(8,128)S(1)}, u32[]{:S(2)}, u32[]{:S(2)}) %collective-permute-start.17) | collective-permute-done | bytes 139296 | tf_op jit(solution)/shard_map/ppermute | solution.py:276
  95.5 2.3 %collective-permute-start.18 = (f32[16,128]{1,0:T(8,128)S(1)}, f32[16,128]{1,0:T(8,128)S(1)}, u32[]{:S(2)}, u32[]{:S(2)}) collective-permute-start(f32[16,128]{1,0:T(8,128)S(1)} %shard_map.176.near), channel_id=1, source_target_pairs={{0,4},{1,5},{2,6},{3,7},{4,0},{5,1},{6,2},{7,3},{8,12},{9,13},{10,... | collective-permute-start | bytes 24584 | tf_op jit(solution)/shard_map/ppermute | solution.py:273
  97.7 1.4 %shard_map.175 = (f32[256,128]{1,0:T(8,128)S(1)}, f32[32,8,128]{2,1,0:T(8,128)S(1)}) custom-call(s32[1]{0:T(128)} %get-tuple-element.60.flag, s32[1]{0:T(128)} %bitcast.pos, s32[32,128]{1,0:T(8,128)S(1)} %get-tuple-element.56.l0, s32[32,128]{1,0:T(8,128)S(1)} %collective-permute-done.l1, s32[32,128]{1,0:T(8,128)S(1)} %collective-permute-done.1.l2, ...), custom_call_target="tpu_custom_call" | custom-call | flops 268435456 | bytes 3407880 | tf_op jit(solution)/shard_map/pallas_call | solution.py:45
  99.2 2.8 %collective-permute-done.18.far = f32[16,128]{1,0:T(8,128)S(1)} collective-permute-done((f32[16,128]{1,0:T(8,128)S(1)}, f32[16,128]{1,0:T(8,128)S(1)}, u32[]{:S(2)}, u32[]{:S(2)}) %collective-permute-start.18) | collective-permute-done | bytes 8224 | tf_op jit(solution)/shard_map/ppermute | solution.py:273
  102.5 26.6 %all_to_all.15.returned = f32[32,48,128]{2,1,0:T(8,128)S(1)} all-to-all(f32[32,48,128]{2,1,0:T(8,128)S(1)} %get-tuple-element.91), channel_id=1, replica_groups=mesh['grp'=32,'blk'=8] {'grp'}, dimensions={0} | all-to-all | bytes 1572864 | tf_op jit(solution)/shard_map/all_to_all | solution.py:279
  129.1 1.7 %shard_map.178 = (f32[256,128]{1,0:T(8,128)}, f32[128,128]{1,0:T(8,128)}, f32[128,128]{1,0:T(8,128)}) custom-call(f32[32,48,128]{2,1,0:T(8,128)S(1)} %all_to_all.15.returned, s32[32,32]{1,0:T(8,128)S(1)} %bitcast.21, s32[8]{0:T(128)S(1)} %bitcast.26, f32[256,128]{1,0:T(8,128)S(1)} %get-tuple-element.92.local), custom_call_target="tpu_custom_call" | custom-call | flops 268435456 | bytes 921632 | tf_op jit(solution)/shard_map/pallas_call | solution.py:45
  (69 shorter events, 13.6 us)
Async XLA Ops:
  0.6 12.4 %copy-start.17 = (s32[1,1,8,2,6]{2,3,4,1,0:T(2,128)S(1)}, s32[1,1,8,2,6]{2,3,4,1,0:T(2,128)}, u32[]{:S(2)}) copy-start(s32[1,1,8,2,6]{2,3,4,1,0:T(2,128)} %param.18) | copy-start | bytes 1156
  0.6 12.5 %copy-start.11 = (s32[1,1,256]{2,1,0:T(1,128)S(1)}, s32[1,1,256]{2,1,0:T(1,128)}, u32[]{:S(2)}) copy-start(s32[1,1,256]{2,1,0:T(1,128)} %param.24) | copy-start | bytes 3076
  0.7 12.5 %copy-start.8 = (s32[1,1,8,6,2,128]{5,4,3,2,1,0:T(2,128)S(1)}, s32[1,1,8,6,2,128]{5,4,3,2,1,0:T(2,128)}, u32[]{:S(2)}) copy-start(s32[1,1,8,6,2,128]{5,4,3,2,1,0:T(2,128)} %param.19) | copy-start | bytes 147460
  0.7 12.5 %copy-start.10 = (s32[1,1,256]{2,1,0:T(1,128)S(1)}, s32[1,1,256]{2,1,0:T(1,128)}, u32[]{:S(2)}) copy-start(s32[1,1,256]{2,1,0:T(1,128)} %param.25) | copy-start | bytes 3076
  3.0 29.7 %all-to-all-start = ((f32[32,40,128]{2,1,0:T(8,128)}), f32[32,40,128]{2,1,0:T(8,128)S(1)}, u32[]{:S(2)}, u32[]{:S(2)}) async-start(f32[32,40,128]{2,1,0:T(8,128)} %shard_map.164), calls=%async_computation | async-start | bytes 1310720 | tf_op jit(solution)/shard_map/all_to_all | solution.py:279
  14.0 3.9 %collective-permute-start = (s32[32,128]{1,0:T(8,128)S(1)}, s32[32,128]{1,0:T(8,128)S(1)}, u32[]{:S(2)}, u32[]{:S(2)}) collective-permute-start(s32[32,128]{1,0:T(8,128)S(1)} %get-tuple-element.57), channel_id=1, source_target_pairs={{0,3},{1,0},{2,1},{3,2},{4,7},{5,4},{6,5},{7,6},{8,11},{9,8},{10,9... | collective-permute-start | bytes 49160 | tf_op jit(solution)/shard_map/ppermute | solution.py:276
  16.8 4.4 %collective-permute-start.1 = (s32[32,128]{1,0:T(8,128)S(1)}, s32[32,128]{1,0:T(8,128)S(1)}, u32[]{:S(2)}, u32[]{:S(2)}) collective-permute-start(s32[32,128]{1,0:T(8,128)S(1)} %get-tuple-element.58), channel_id=1, source_target_pairs={{0,2},{1,3},{2,0},{3,1},{4,6},{5,7},{6,4},{7,5},{8,10},{9,11},{10,... | collective-permute-start | bytes 49160 | tf_op jit(solution)/shard_map/ppermute | solution.py:276
  17.1 4.2 %collective-permute-start.2 = (s32[32,128]{1,0:T(8,128)S(1)}, s32[32,128]{1,0:T(8,128)S(1)}, u32[]{:S(2)}, u32[]{:S(2)}) collective-permute-start(s32[32,128]{1,0:T(8,128)S(1)} %get-tuple-element.59), channel_id=1, source_target_pairs={{0,1},{1,2},{2,3},{3,0},{4,5},{5,6},{6,7},{7,4},{8,9},{9,10},{10,1... | collective-permute-start | bytes 49160 | tf_op jit(solution)/shard_map/ppermute | solution.py:276
  21.3 11.3 %copy-start = (f32[256,128]{1,0:T(8,128)S(1)}, f32[256,128]{1,0:T(8,128)}, u32[]{:S(2)}) copy-start(f32[256,128]{1,0:T(8,128)} %features.5) | copy-start | bytes 393220
  21.3 8.1 %collective-permute-start.3 = (s32[64,128]{1,0:T(8,128)S(1)}, s32[64,128]{1,0:T(8,128)S(1)}, u32[]{:S(2)}, u32[]{:S(2)}) collective-permute-start(s32[64,128]{1,0:T(8,128)S(1)} %pad_add_fusion), channel_id=1, source_target_pairs={{0,4},{1,5},{2,6},{3,7},{4,0},{5,1},{6,2},{7,3},{8,12},{9,13},{10,... | collective-permute-start | bytes 98312 | tf_op jit(solution)/shard_map/ppermute | solution.py:273
  34.1 7.5 %collective-permute-start.4 = (f32[256,128]{1,0:T(8,128)S(1)}, f32[256,128]{1,0:T(8,128)S(1)}, u32[]{:S(2)}, u32[]{:S(2)}) collective-permute-start(f32[256,128]{1,0:T(8,128)S(1)} %get-tuple-element.64), channel_id=1, source_target_pairs={{0,1},{1,2},{2,3},{3,0},{4,5},{5,6},{6,7},{7,4},{8,9},{9,10},{10,1... | collective-permute-start | bytes 393224 | tf_op jit(solution)/shard_map/ppermute | solution.py:276
  36.1 5.5 %collective-permute-start.5 = (f32[256,128]{1,0:T(8,128)S(1)}, f32[256,128]{1,0:T(8,128)S(1)}, u32[]{:S(2)}, u32[]{:S(2)}) collective-permute-start(f32[256,128]{1,0:T(8,128)S(1)} %get-tuple-element.65), channel_id=1, source_target_pairs={{0,3},{1,0},{2,1},{3,2},{4,7},{5,4},{6,5},{7,6},{8,11},{9,8},{10,9... | collective-permute-start | bytes 393224 | tf_op jit(solution)/shard_map/ppermute | solution.py:276
  37.7 7.9 %collective-permute-start.6 = (f32[256,128]{1,0:T(8,128)S(1)}, f32[256,128]{1,0:T(8,128)S(1)}, u32[]{:S(2)}, u32[]{:S(2)}) collective-permute-start(f32[256,128]{1,0:T(8,128)S(1)} %get-tuple-element.66), channel_id=1, source_target_pairs={{0,2},{1,3},{2,0},{3,1},{4,6},{5,7},{6,4},{7,5},{8,10},{9,11},{10,... | collective-permute-start | bytes 393224 | tf_op jit(solution)/shard_map/ppermute | solution.py:276
  45.6 10.4 %copy-start.1 = (f32[256,128]{1,0:T(8,128)S(1)}, f32[256,128]{1,0:T(8,128)}, u32[]{:S(2)}) copy-start(f32[256,128]{1,0:T(8,128)} %grad_out.1) | copy-start | bytes 393220
  45.7 10.3 %copy-start.2 = (f32[128,128]{1,0:T(8,128)S(1)}, f32[128,128]{1,0:T(8,128)}, u32[]{:S(2)}) copy-start(f32[128,128]{1,0:T(8,128)} %w_neigh.1) | copy-start | bytes 196612
  45.7 10.3 %copy-start.3 = (f32[128,128]{1,0:T(8,128)S(1)}, f32[128,128]{1,0:T(8,128)}, u32[]{:S(2)}) copy-start(f32[128,128]{1,0:T(8,128)} %w_root.3) | copy-start | bytes 196612
  45.7 9.8 %collective-permute-start.10 = (f32[256,128]{1,0:T(8,128)S(1)}, f32[256,128]{1,0:T(8,128)S(1)}, u32[]{:S(2)}, u32[]{:S(2)}) collective-permute-start(f32[256,128]{1,0:T(8,128)S(1)} %get-tuple-element.73), channel_id=1, source_target_pairs={{0,2},{1,3},{2,0},{3,1},{4,6},{5,7},{6,4},{7,5},{8,10},{9,11},{10,... | collective-permute-start | bytes 393224 | tf_op jit(solution)/shard_map/ppermute | solution.py:276
  46.2 9.8 %collective-permute-start.7 = (f32[256,128]{1,0:T(8,128)S(1)}, f32[256,128]{1,0:T(8,128)S(1)}, u32[]{:S(2)}, u32[]{:S(2)}) collective-permute-start(f32[256,128]{1,0:T(8,128)S(1)} %add_add_fusion), channel_id=1, source_target_pairs={{0,4},{1,5},{2,6},{3,7},{4,0},{5,1},{6,2},{7,3},{8,12},{9,13},{10,... | collective-permute-start | bytes 393224 | tf_op jit(solution)/shard_map/ppermute | solution.py:273
  50.3 5.7 %collective-permute-start.8 = (f32[256,128]{1,0:T(8,128)S(1)}, f32[256,128]{1,0:T(8,128)S(1)}, u32[]{:S(2)}, u32[]{:S(2)}) collective-permute-start(f32[256,128]{1,0:T(8,128)S(1)} %get-tuple-element.71), channel_id=1, source_target_pairs={{0,1},{1,2},{2,3},{3,0},{4,5},{5,6},{6,7},{7,4},{8,9},{9,10},{10,1... | collective-permute-start | bytes 393224 | tf_op jit(solution)/shard_map/ppermute | solution.py:276
  51.6 4.4 %collective-permute-start.9 = (f32[256,128]{1,0:T(8,128)S(1)}, f32[256,128]{1,0:T(8,128)S(1)}, u32[]{:S(2)}, u32[]{:S(2)}) collective-permute-start(f32[256,128]{1,0:T(8,128)S(1)} %get-tuple-element.72), channel_id=1, source_target_pairs={{0,3},{1,0},{2,1},{3,2},{4,7},{5,4},{6,5},{7,6},{8,11},{9,8},{10,9... | collective-permute-start | bytes 393224 | tf_op jit(solution)/shard_map/ppermute | solution.py:276
  58.4 24.3 %all-to-all-start.1 = ((f32[32,16,128]{2,1,0:T(8,128)}), f32[32,16,128]{2,1,0:T(8,128)S(1)}, u32[]{:S(2)}, u32[]{:S(2)}) async-start(f32[32,16,128]{2,1,0:T(8,128)} %shard_map.172), calls=%async_computation.1 | async-start | bytes 524288 | tf_op jit(solution)/shard_map/all_to_all | solution.py:279
  66.0 11.8 %collective-permute-start.11 = (f32[256,128]{1,0:T(8,128)S(1)}, f32[256,128]{1,0:T(8,128)S(1)}, u32[]{:S(2)}, u32[]{:S(2)}) collective-permute-start(f32[256,128]{1,0:T(8,128)S(1)} %get-tuple-element.77.grad_sum.g0), channel_id=1, source_target_pairs={{0,4},{1,5},{2,6},{3,7},{4,0},{5,1},{6,2},{7,3},{8,12},{9,13},{10,... | collective-permute-start | bytes 393224 | tf_op jit(solution)/shard_map/ppermute | solution.py:273
  69.4 8.4 %collective-permute-start.12 = (f32[256,128]{1,0:T(8,128)S(1)}, f32[256,128]{1,0:T(8,128)S(1)}, u32[]{:S(2)}, u32[]{:S(2)}) collective-permute-start(f32[256,128]{1,0:T(8,128)S(1)} %get-tuple-element.77.grad_sum.g0), channel_id=1, source_target_pairs={{0,3},{1,0},{2,1},{3,2},{4,7},{5,4},{6,5},{7,6},{8,11},{9,8},{10,9... | collective-permute-start | bytes 393224 | tf_op jit(solution)/shard_map/ppermute | solution.py:276
  70.9 6.9 %collective-permute-start.13 = (f32[256,128]{1,0:T(8,128)S(1)}, f32[256,128]{1,0:T(8,128)S(1)}, u32[]{:S(2)}, u32[]{:S(2)}) collective-permute-start(f32[256,128]{1,0:T(8,128)S(1)} %get-tuple-element.77.grad_sum.g0), channel_id=1, source_target_pairs={{0,2},{1,3},{2,0},{3,1},{4,6},{5,7},{6,4},{7,5},{8,10},{9,11},{10,... | collective-permute-start | bytes 393224 | tf_op jit(solution)/shard_map/ppermute | solution.py:276
  72.3 7.9 %collective-permute-start.14 = (f32[256,128]{1,0:T(8,128)S(1)}, f32[256,128]{1,0:T(8,128)S(1)}, u32[]{:S(2)}, u32[]{:S(2)}) collective-permute-start(f32[256,128]{1,0:T(8,128)S(1)} %get-tuple-element.77.grad_sum.g0), channel_id=1, source_target_pairs={{0,1},{1,2},{2,3},{3,0},{4,5},{5,6},{6,7},{7,4},{8,9},{9,10},{10,1... | collective-permute-start | bytes 393224 | tf_op jit(solution)/shard_map/ppermute | solution.py:276
  82.8 19.2 %copy-start.16 = (f32[1024,128]{1,0:T(8,128)S(1)}, f32[1024,128]{1,0:T(8,128)}, u32[]{:S(2)}) copy-start(f32[1024,128]{1,0:T(8,128)} %copy-done.15) | copy-start | bytes 1572868
  82.8 8.3 %collective-permute-start.15 = (f32[272,128]{1,0:T(8,128)S(1)}, f32[272,128]{1,0:T(8,128)S(1)}, u32[]{:S(2)}, u32[]{:S(2)}) collective-permute-start(f32[272,128]{1,0:T(8,128)S(1)} %shard_map.174.g4.a), channel_id=1, source_target_pairs={{0,3},{1,0},{2,1},{3,2},{4,7},{5,4},{6,5},{7,6},{8,11},{9,8},{10,9... | collective-permute-start | bytes 417800 | tf_op jit(solution)/shard_map/ppermute | solution.py:276
  85.4 6.2 %collective-permute-start.16 = (f32[272,128]{1,0:T(8,128)S(1)}, f32[272,128]{1,0:T(8,128)S(1)}, u32[]{:S(2)}, u32[]{:S(2)}) collective-permute-start(f32[272,128]{1,0:T(8,128)S(1)} %shard_map.174.g4.a), channel_id=1, source_target_pairs={{0,2},{1,3},{2,0},{3,1},{4,6},{5,7},{6,4},{7,5},{8,10},{9,11},{10,... | collective-permute-start | bytes 417800 | tf_op jit(solution)/shard_map/ppermute | solution.py:276
  86.3 9.1 %collective-permute-start.17 = (f32[272,128]{1,0:T(8,128)S(1)}, f32[272,128]{1,0:T(8,128)S(1)}, u32[]{:S(2)}, u32[]{:S(2)}) collective-permute-start(f32[272,128]{1,0:T(8,128)S(1)} %shard_map.174.g4.a), channel_id=1, source_target_pairs={{0,1},{1,2},{2,3},{3,0},{4,5},{5,6},{6,7},{7,4},{8,9},{9,10},{10,1... | collective-permute-start | bytes 417800 | tf_op jit(solution)/shard_map/ppermute | solution.py:276
  95.5 6.5 %collective-permute-start.18 = (f32[16,128]{1,0:T(8,128)S(1)}, f32[16,128]{1,0:T(8,128)S(1)}, u32[]{:S(2)}, u32[]{:S(2)}) collective-permute-start(f32[16,128]{1,0:T(8,128)S(1)} %shard_map.176.near), channel_id=1, source_target_pairs={{0,4},{1,5},{2,6},{3,7},{4,0},{5,1},{6,2},{7,3},{8,12},{9,13},{10,... | collective-permute-start | bytes 24584 | tf_op jit(solution)/shard_map/ppermute | solution.py:273
  99.1 29.9 %copy-start.9 = (s32[1,1,32,32]{3,2,1,0:T(8,128)S(1)}, s32[1,1,32,32]{3,2,1,0:T(8,128)}, u32[]{:S(2)}) copy-start(s32[1,1,32,32]{3,2,1,0:T(8,128)} %param.20) | copy-start | bytes 12292
  99.2 29.9 %copy-start.12 = (s32[1,1,8]{2,1,0:T(1,128)S(1)}, s32[1,1,8]{2,1,0:T(1,128)}, u32[]{:S(2)}) copy-start(s32[1,1,8]{2,1,0:T(1,128)} %param.23) | copy-start | bytes 100
  (7 other events, 31.9 us)

commit v6 on v5

--- a/solution.py
+++ b/solution.py
@@ -230,32 +230,29 @@
     local[...] = root[...] + total[0:256, :]
 
 
-def k_join(grad, weights, out):
-    out[0:256, :] = grad[...]
-    out[256:272, :] = jnp.sum(weights[...], axis=0)
-
-
-def k_sum(a, b, c, d, out):
-    out[...] = a[256:272, :] + b[256:272, :] + c[256:272, :] + d[256:272, :]
-
-
-def k_pack(factor, slots, hubs, near, far, out, bias):
+def k_sum(weights, out):
+    out[...] = jnp.sum(weights[...], axis=0)
+
+
+def k_pack(factor, hubs, near, far, out, bias):
     w = (near[...] + far[...]) * factor
-    out[:, 0:32, :] = slots[...].reshape(32, 32, 128)
-    out[:, 32:40, :] = hubs[...]
+    out[:, 0:8, :] = hubs[...]
     for p in range(32):
-        out[p, 40:48, :] = w[0:8]
+        out[p, 8:16, :] = w[0:8]
     bias[...] = w[8:9]
 
 
-def k_final(returned, send, hub, local, out, w_neigh, w_root):
-    acc = joined(dot(send_hot(send), halves(returned[:, 0:32, :].reshape(1024, 128))))
-    rows = jnp.sum(returned[:, 32:40, :], axis=0)
-    out[...] = local[...] + acc
+def k_scatter(returned, send, local, out):
+    out[...] = local[...] + joined(dot(send_hot(send), halves(returned[...].reshape(1024, 128))))
+
+
+def k_final(last, hub, local, out, w_neigh, w_root):
+    rows = jnp.sum(last[:, 0:8, :], axis=0)
+    out[...] = local[...]
     for j in range(8):
         out[pl.ds(hub[j], 1), :] += rows[j : j + 1, :]
-    w_neigh[...] = returned[0:16, 40:48, :].reshape(128, 128)
-    w_root[...] = returned[16:32, 40:48, :].reshape(128, 128)
+    w_neigh[...] = last[0:16, 8:16, :].reshape(128, 128)
+    w_root[...] = last[16:32, 8:16, :].reshape(128, 128)
 
 
 def per_device(features, w_neigh, w_root, bias, grad_out, tile_coord, tile_edge,
@@ -319,22 +316,24 @@
         [sm] + [vm] * 6,
     )
     g4, weights, g1, g2, g3, slots = lax.optimization_barrier((g4, weights, g1, g2, g3, slots))
-    g4 = call(k_join, shape((272, 128)), (g4, weights))
+    returned = exchange(slots.reshape(32, 32, 128), "grp")
+    w = call(k_sum, shape((16, 128)), (weights,))
+    w = w + turn(w, 1) + turn(w, 2) + turn(w, 3)
+    w_far = swap(w)
     g5, g7, g6 = turn(g4, 3), turn(g4, 1), turn(g4, 2)
-    w = call(k_sum, shape((16, 128)), (g4, g5, g6, g7))
-    w_far = swap(w)
     local, hubs = call(
         k_back, [block, shape((32, 8, 128))],
         (flag, *lists, grad_sum, g1, g2, g3, g4, g5, g6, g7, bwd, root), [sm, *lm] + [vm] * 10,
         [pltpu.VMEM((512, 128), F32)],
     )
     factor = (256 * lax.axis_size("grp") * lax.axis_size("blk")) ** (-0.5)
-    back, grad_bias = call(
-        functools.partial(k_pack, factor), [shape((32, 48, 128)), shape((1, 128))], (slots, hubs, w, w_far)
-    )
-    returned = exchange(back, "grp")
+    last, grad_bias = call(
+        functools.partial(k_pack, factor), [shape((32, 16, 128)), shape((1, 128))], (hubs, w, w_far)
+    )
+    last = exchange(last, "grp")
+    local = call(k_scatter, block, (returned, send, local))
     grad_features, grad_wn, grad_wr = call(
-        k_final, [block, shape((128, 128)), shape((128, 128))], (returned, send, hub, local), [vm, vm, sm, vm]
+        k_final, [block, shape((128, 128)), shape((128, 128))], (last, hub, local), [vm, sm, vm]
     )
     return output, grad_features, grad_wn, grad_wr, grad_bias.reshape(128)
 

time: 131 us -> 129 us (0.985)
  blocking collectives: 26.6 us -> 0 us
  starting transfers between devices: 50.4 us -> 69.4 us
  local copies, waits for them, and re-layouts: 2.86 us -> 6.71 us
    all_to_all x1 -> x0, blocking collectives: 26.6 us -> none  [exchange(): return lax.all_to_all(v, axis, split_axis=0, concat_axis=0, tiled=True)]
    all_to_all x2 -> x4, starting transfers between devices: 17.6 us -> 33.3 us  [exchange(): return lax.all_to_all(v, axis, split_axis=0, concat_axis=0, tiled=True)]
    all_to_all x2 -> x4, waiting for transfers between devices: 3.41 us -> 12.5 us  [exchange(): return lax.all_to_all(v, axis, split_axis=0, concat_axis=0, tiled=True)]
    ppermute x15 -> x18, waiting for transfers between devices: 19 us -> 13.2 us  [turn(): lax.ppermute(v, 'blk', [(i, i // 4 * 4 + (i % 4 + k) % 4) for i in range(...]
    unnamed x36 -> x44, local copies, waits for them, and re-layouts: 2.76 us -> 6.61 us
    ppermute x4, waiting for transfers between devices: 8.56 us -> 5.15 us  [swap(): return lax.ppermute(v, 'blk', [(i, i ^ 4) for i in range(8)])]
    ppermute x15 -> x18, starting transfers between devices: 18.7 us -> 21.1 us  [turn(): lax.ppermute(v, 'blk', [(i, i // 4 * 4 + (i % 4 + k) % 4) for i in range(...]
  transfers between devices with their start and end apart: 21 -> 26, of which waited for: 13 -> 12; matrix products, arithmetic and copies ran while one was open for 0% -> 0% of each run, Pallas kernels for 8% -> 10%
where the time goes in v6:
time: 129 us; the launch traced here: 128 us
  starting transfers between devices  69.4 us (54%)
  waiting for transfers between devices  30.8 us (24%)
  Pallas kernels  20 us (16%)
  local copies, waits for them, and re-layouts  6.71 us (5%)
    all_to_all x4, starting transfers between devices, exchange(): return lax.all_to_all(v, axis, split_axis=0, concat_axis=0, tiled=True)  33.3 us
    ppermute x18, starting transfers between devices, turn(): lax.ppermute(v, 'blk', [(i, i // 4 * 4 + (i % 4 + k) % 4) for i in range(...  21.1 us
    pallas_call x15, Pallas kernels, call(): pl.pallas_call(kernel, out_shape=out_shape, in_specs=[whole] * len(args)...  20 us
    ppermute x4, starting transfers between devices, swap(): return lax.ppermute(v, 'blk', [(i, i ^ 4) for i in range(8)])  14.9 us
    ppermute x18, waiting for transfers between devices, turn(): lax.ppermute(v, 'blk', [(i, i // 4 * 4 + (i % 4 + k) % 4) for i in range(...  13.2 us
    all_to_all x4, waiting for transfers between devices, exchange(): return lax.all_to_all(v, axis, split_axis=0, concat_axis=0, tiled=True)  12.5 us
    unnamed x44, local copies, waits for them, and re-layouts  6.61 us
    ppermute x4, waiting for transfers between devices, swap(): return lax.ppermute(v, 'blk', [(i, i ^ 4) for i in range(8)])  5.15 us
  transfers between devices with their start and end apart: 26, of which 12 were waited for; matrix products, arithmetic and copies ran while one was open for 0% of the time, Pallas kernels for 10%

profile of v6, /device:TPU:1, one launch (start us, length us, event | category | flops | bytes accessed | tf_op | source)
XLA Modules:
  0.0 127.9 jit_solution(5174577589979424728)
XLA Ops:
  0.7 2.3 %shard_map.164 = f32[32,40,128]{2,1,0:T(8,128)} custom-call(f32[256,128]{1,0:T(8,128)} %features.5, s32[32,32]{1,0:T(8,128)} %bitcast.21, s32[1,8]{1,0:T(1,128)} %bitcast.26), custom_call_target="tpu_custom_call" | custom-call | flops 268435456 | bytes 135200 | tf_op jit(solution)/shard_map/pallas_call | solution.py:45
  3.0 10.0 %all-to-all-start = ((f32[32,40,128]{2,1,0:T(8,128)}), f32[32,40,128]{2,1,0:T(8,128)S(1)}, u32[]{:S(2)}, u32[]{:S(2)}) async-start(f32[32,40,128]{2,1,0:T(8,128)} %shard_map.164), calls=%async_computation | async-start | bytes 1310720 | tf_op jit(solution)/shard_map/all_to_all | solution.py:276
  14.0 2.8 %collective-permute-start = (s32[32,128]{1,0:T(8,128)S(1)}, s32[32,128]{1,0:T(8,128)S(1)}, u32[]{:S(2)}, u32[]{:S(2)}) collective-permute-start(s32[32,128]{1,0:T(8,128)S(1)} %get-tuple-element.57), channel_id=1, source_target_pairs={{0,3},{1,0},{2,1},{3,2},{4,7},{5,4},{6,5},{7,6},{8,11},{9,8},{10,9... | collective-permute-start | bytes 49160 | tf_op jit(solution)/shard_map/ppermute | solution.py:273
  17.8 3.3 %collective-permute-done.1.l2 = s32[32,128]{1,0:T(8,128)S(1)} collective-permute-done((s32[32,128]{1,0:T(8,128)S(1)}, s32[32,128]{1,0:T(8,128)S(1)}, u32[]{:S(2)}, u32[]{:S(2)}) %collective-permute-start.1) | collective-permute-done | bytes 16416 | tf_op jit(solution)/shard_map/ppermute | solution.py:273
  21.4 4.3 %collective-permute-start.3 = (s32[64,128]{1,0:T(8,128)S(1)}, s32[64,128]{1,0:T(8,128)S(1)}, u32[]{:S(2)}, u32[]{:S(2)}) collective-permute-start(s32[64,128]{1,0:T(8,128)S(1)} %pad_add_fusion), channel_id=1, source_target_pairs={{0,4},{1,5},{2,6},{3,7},{4,0},{5,1},{6,2},{7,3},{8,12},{9,13},{10,... | collective-permute-start | bytes 98312 | tf_op jit(solution)/shard_map/ppermute | solution.py:270
  25.7 3.8 %collective-permute-done.3.far = s32[64,128]{1,0:T(8,128)S(1)} collective-permute-done((s32[64,128]{1,0:T(8,128)S(1)}, s32[64,128]{1,0:T(8,128)S(1)}, u32[]{:S(2)}, u32[]{:S(2)}) %collective-permute-start.3) | collective-permute-done | bytes 32800 | tf_op jit(solution)/shard_map/ppermute | solution.py:270
  29.5 2.3 %shard_map.167 = (bf16[8,256,512]{2,1,0:T(8,128)(2,1)S(1)}, s32[1]{0:T(128)}) custom-call(s32[1]{0:T(128)} %bitcast.pos, s32[32,128]{1,0:T(8,128)S(1)} %get-tuple-element.56.l0, s32[32,128]{1,0:T(8,128)S(1)} %collective-permute-done.l1, s32[32,128]{1,0:T(8,128)S(1)} %collective-permute-done.1.l2, s32[32,128]{1,0:T(8,128)S(1)} %collective-permute-done.2.l3, ...), custom_call_target="tpu_custom_call" | custom-call | flops 2147483648 | bytes 98308 | tf_op jit(solution)/shard_map/pallas_call | solution.py:45
  32.7 1.4 %shard_map.168 = (f32[256,128]{1,0:T(8,128)S(1)}, f32[256,128]{1,0:T(8,128)S(1)}, f32[256,128]{1,0:T(8,128)S(1)}, f32[256,128]{1,0:T(8,128)S(1)}, f32[256,128]{1...) custom-call(s32[1]{0:T(128)} %get-tuple-element.60.flag, s32[1]{0:T(128)} %bitcast.pos, ...), custom_call_target="tpu_custom_call" | custom-call | flops 268435456 | bytes 2981896 | tf_op jit(solution)/shard_map/pallas_call | solution.py:45
  34.1 2.1 %collective-permute-start.4 = (f32[256,128]{1,0:T(8,128)S(1)}, f32[256,128]{1,0:T(8,128)S(1)}, u32[]{:S(2)}, u32[]{:S(2)}) collective-permute-start(f32[256,128]{1,0:T(8,128)S(1)} %get-tuple-element.64), channel_id=1, source_target_pairs={{0,1},{1,2},{2,3},{3,0},{4,5},{5,6},{6,7},{7,4},{8,9},{9,10},{10,1... | collective-permute-start | bytes 393224 | tf_op jit(solution)/shard_map/ppermute | solution.py:273
  36.1 1.5 %collective-permute-start.5 = (f32[256,128]{1,0:T(8,128)S(1)}, f32[256,128]{1,0:T(8,128)S(1)}, u32[]{:S(2)}, u32[]{:S(2)}) collective-permute-start(f32[256,128]{1,0:T(8,128)S(1)} %get-tuple-element.65), channel_id=1, source_target_pairs={{0,3},{1,0},{2,1},{3,2},{4,7},{5,4},{6,5},{7,6},{8,11},{9,8},{10,9... | collective-permute-start | bytes 393224 | tf_op jit(solution)/shard_map/ppermute | solution.py:273
  37.7 1.6 %collective-permute-start.6 = (f32[256,128]{1,0:T(8,128)S(1)}, f32[256,128]{1,0:T(8,128)S(1)}, u32[]{:S(2)}, u32[]{:S(2)}) collective-permute-start(f32[256,128]{1,0:T(8,128)S(1)} %get-tuple-element.66), channel_id=1, source_target_pairs={{0,2},{1,3},{2,0},{3,1},{4,6},{5,7},{6,4},{7,5},{8,10},{9,11},{10,... | collective-permute-start | bytes 393224 | tf_op jit(solution)/shard_map/ppermute | solution.py:273
  39.2 2.3 %shard_map.166 = (bf16[256,1024]{1,0:T(8,128)(2,1)S(1)}, bf16[1024,256]{1,0:T(8,128)(2,1)S(1)}, f32[256,128]{1,0:T(8,128)S(1)}, s32[1]{0:T(128)}) custom-call(s32[48,128]{1,0:T(8,128)S(1)} %get-tuple-element.52.own_to, s32[8,128]{1,0:T(8,128)S(1)} %bitcast.13, s32[8,128]{1,0:T(8,128)S(1)} %bitcast.16, s32[2,128]{1,0:T(2,128)S(1)} %bitcast.25), custom_call_target="tpu_custom_call" | custom-call | flops 2147483648 | bytes 33792 | tf_op jit(solution)/shard_map/pallas_call | solution.py:45
  41.6 4.0 %collective-permute-done.6 = f32[256,128]{1,0:T(8,128)S(1)} collective-permute-done((f32[256,128]{1,0:T(8,128)S(1)}, f32[256,128]{1,0:T(8,128)S(1)}, u32[]{:S(2)}, u32[]{:S(2)}) %collective-permute-start.6) | collective-permute-done | bytes 131104 | tf_op jit(solution)/shard_map/ppermute | solution.py:273
  46.2 4.1 %collective-permute-start.7 = (f32[256,128]{1,0:T(8,128)S(1)}, f32[256,128]{1,0:T(8,128)S(1)}, u32[]{:S(2)}, u32[]{:S(2)}) collective-permute-start(f32[256,128]{1,0:T(8,128)S(1)} %add_add_fusion), channel_id=1, source_target_pairs={{0,4},{1,5},{2,6},{3,7},{4,0},{5,1},{6,2},{7,3},{8,12},{9,13},{10,... | collective-permute-start | bytes 393224 | tf_op jit(solution)/shard_map/ppermute | solution.py:270
  51.6 1.4 %collective-permute-start.9 = (f32[256,128]{1,0:T(8,128)S(1)}, f32[256,128]{1,0:T(8,128)S(1)}, u32[]{:S(2)}, u32[]{:S(2)}) collective-permute-start(f32[256,128]{1,0:T(8,128)S(1)} %get-tuple-element.72), channel_id=1, source_target_pairs={{0,3},{1,0},{2,1},{3,2},{4,7},{5,4},{6,5},{7,6},{8,11},{9,8},{10,9... | collective-permute-start | bytes 393224 | tf_op jit(solution)/shard_map/ppermute | solution.py:273
  53.0 1.6 %shard_map.170.bwd = bf16[8,512,256]{2,1,0:T(8,128)(2,1)S(1)} custom-call(s32[1]{0:T(128)} %bitcast.pos, s32[32,128]{1,0:T(8,128)S(1)} %get-tuple-element.56.l0, s32[32,128]{1,0:T(8,128)S(1)} %collective-permute-done.l1, s32[32,128]{1,0:T(8,128)S(1)} %collective-permute-done.1.l2, s32[32,128]{1,0:T(8,128)S(1)} %collective-permute-done.2.l3, ...), custom_call_target="tpu_custom_call" | custom-call | flops 2147483648 | bytes 98308 | tf_op jit(solution)/shard_map/pallas_call | solution.py:45
  58.4 7.6 %all-to-all-start.1 = ((f32[32,16,128]{2,1,0:T(8,128)}), f32[32,16,128]{2,1,0:T(8,128)S(1)}, u32[]{:S(2)}, u32[]{:S(2)}) async-start(f32[32,16,128]{2,1,0:T(8,128)} %shard_map.172), calls=%async_computation.1 | async-start | bytes 524288 | tf_op jit(solution)/shard_map/all_to_all | solution.py:276
  66.0 3.4 %collective-permute-start.11 = (f32[256,128]{1,0:T(8,128)S(1)}, f32[256,128]{1,0:T(8,128)S(1)}, u32[]{:S(2)}, u32[]{:S(2)}) collective-permute-start(f32[256,128]{1,0:T(8,128)S(1)} %get-tuple-element.77.grad_sum.g0), channel_id=1, source_target_pairs={{0,4},{1,5},{2,6},{3,7},{4,0},{5,1},{6,2},{7,3},{8,12},{9,13},{10,... | collective-permute-start | bytes 393224 | tf_op jit(solution)/shard_map/ppermute | solution.py:270
  69.4 1.6 %collective-permute-start.12 = (f32[256,128]{1,0:T(8,128)S(1)}, f32[256,128]{1,0:T(8,128)S(1)}, u32[]{:S(2)}, u32[]{:S(2)}) collective-permute-start(f32[256,128]{1,0:T(8,128)S(1)} %get-tuple-element.77.grad_sum.g0), channel_id=1, source_target_pairs={{0,3},{1,0},{2,1},{3,2},{4,7},{5,4},{6,5},{7,6},{8,11},{9,8},{10,9... | collective-permute-start | bytes 393224 | tf_op jit(solution)/shard_map/ppermute | solution.py:273
  70.9 1.3 %collective-permute-start.13 = (f32[256,128]{1,0:T(8,128)S(1)}, f32[256,128]{1,0:T(8,128)S(1)}, u32[]{:S(2)}, u32[]{:S(2)}) collective-permute-start(f32[256,128]{1,0:T(8,128)S(1)} %get-tuple-element.77.grad_sum.g0), channel_id=1, source_target_pairs={{0,2},{1,3},{2,0},{3,1},{4,6},{5,7},{6,4},{7,5},{8,10},{9,11},{10,... | collective-permute-start | bytes 393224 | tf_op jit(solution)/shard_map/ppermute | solution.py:273
  74.2 2.1 %shard_map.173 = (f32[1024,128]{1,0:T(8,128)}, f32[256,128]{1,0:T(8,128)S(1)}) custom-call(s32[1]{0:T(128)} %get-tuple-element.53.flag, s32[8,128]{1,0:T(8,128)S(1)} %bitcast.15, s32[8,128]{1,0:T(8,128)S(1)} %bitcast.18, f32[256,128]{1,0:T(8,128)S(1)} %get-tuple-element.77.grad_sum.g0, bf16[1024,256]{1,0:T(8,128)(2,1)S(1)} %copy-done.20, ...), custom_call_target="tpu_custom_call" | custom-call | flops 268435456 | bytes 860164 | tf_op jit(solution)/shard_map/pallas_call | solution.py:45
  77.8 2.3 %collective-permute-done.14.g3 = f32[256,128]{1,0:T(8,128)S(1)} collective-permute-done((f32[256,128]{1,0:T(8,128)S(1)}, f32[256,128]{1,0:T(8,128)S(1)}, u32[]{:S(2)}, u32[]{:S(2)}) %collective-permute-start.14) | collective-permute-done | bytes 131104 | tf_op jit(solution)/shard_map/ppermute | solution.py:273
  80.8 1.9 %all-to-all-done.1.weights = f32[32,16,128]{2,1,0:T(8,128)S(1)} async-done(((f32[32,16,128]{2,1,0:T(8,128)}), f32[32,16,128]{2,1,0:T(8,128)S(1)}, u32[]{:S(2)}, u32[]{:S(2)}) %all-to-all-start.1) | async-done | bytes 262176 | tf_op jit(solution)/shard_map/all_to_all | solution.py:276
  82.7 6.5 %all-to-all-start.3 = ((f32[32,32,128]{2,1,0:T(8,128)}), f32[32,32,128]{2,1,0:T(8,128)S(1)}, u32[]{:S(2)}, u32[]{:S(2)}) async-start(f32[32,32,128]{2,1,0:T(8,128)} %bitcast.11), calls=%async_computation.3 | async-start | bytes 1048576 | tf_op jit(solution)/shard_map/all_to_all | solution.py:276
  90.1 1.6 %collective-permute-start.19 = (f32[16,128]{1,0:T(8,128)S(1)}, f32[16,128]{1,0:T(8,128)S(1)}, u32[]{:S(2)}, u32[]{:S(2)}) collective-permute-start(f32[16,128]{1,0:T(8,128)S(1)} %shard_map.175), channel_id=1, source_target_pairs={{0,2},{1,3},{2,0},{3,1},{4,6},{5,7},{6,4},{7,5},{8,10},{9,11},{10,... | collective-permute-start | bytes 24584 | tf_op jit(solution)/shard_map/ppermute | solution.py:273
  91.8 1.4 %collective-permute-start.20 = (f32[16,128]{1,0:T(8,128)S(1)}, f32[16,128]{1,0:T(8,128)S(1)}, u32[]{:S(2)}, u32[]{:S(2)}) collective-permute-start(f32[16,128]{1,0:T(8,128)S(1)} %shard_map.175), channel_id=1, source_target_pairs={{0,3},{1,0},{2,1},{3,2},{4,7},{5,4},{6,5},{7,6},{8,11},{9,8},{10,9... | collective-permute-start | bytes 24584 | tf_op jit(solution)/shard_map/ppermute | solution.py:273
  93.4 1.6 %collective-permute-start.16 = (f32[256,128]{1,0:T(8,128)S(1)}, f32[256,128]{1,0:T(8,128)S(1)}, u32[]{:S(2)}, u32[]{:S(2)}) collective-permute-start(f32[256,128]{1,0:T(8,128)S(1)} %collective-permute-done.11.g4), channel_id=1, source_target_pairs={{0,2},{1,3},{2,0},{3,1},{4,6},{5,7},{6,4},{7,5},{8,10},{9,11},{10,... | collective-permute-start | bytes 393224 | tf_op jit(solution)/shard_map/ppermute | solution.py:273
  95.2 3.2 %collective-permute-start.21 = (f32[16,128]{1,0:T(8,128)S(1)}, f32[16,128]{1,0:T(8,128)S(1)}, u32[]{:S(2)}, u32[]{:S(2)}) collective-permute-start(f32[16,128]{1,0:T(8,128)S(1)} %add_add_fusion.1.near), channel_id=1, source_target_pairs={{0,4},{1,5},{2,6},{3,7},{4,0},{5,1},{6,2},{7,3},{8,12},{9,13},{10,... | collective-permute-start | bytes 24584 | tf_op jit(solution)/shard_map/ppermute | solution.py:270
  99.0 2.7 %collective-permute-done.17.g7 = f32[256,128]{1,0:T(8,128)S(1)} collective-permute-done((f32[256,128]{1,0:T(8,128)S(1)}, f32[256,128]{1,0:T(8,128)S(1)}, u32[]{:S(2)}, u32[]{:S(2)}) %collective-permute-start.17) | collective-permute-done | bytes 131104 | tf_op jit(solution)/shard_map/ppermute | solution.py:273
  103.5 1.4 %shard_map.174 = (f32[256,128]{1,0:T(8,128)S(1)}, f32[32,8,128]{2,1,0:T(8,128)S(1)}) custom-call(s32[1]{0:T(128)} %get-tuple-element.60.flag, s32[1]{0:T(128)} %bitcast.pos, s32[32,128]{1,0:T(8,128)S(1)} %get-tuple-element.56.l0, s32[32,128]{1,0:T(8,128)S(1)} %collective-permute-done.l1, s32[32,128]{1,0:T(8,128)S(1)} %collective-permute-done.1.l2, ...), custom_call_target="tpu_custom_call" | custom-call | flops 268435456 | bytes 3375112 | tf_op jit(solution)/shard_map/pallas_call | solution.py:45
  106.3 9.2 %all-to-all-start.2 = ((f32[32,16,128]{2,1,0:T(8,128)}), f32[32,16,128]{2,1,0:T(8,128)S(1)}, u32[]{:S(2)}, u32[]{:S(2)}) async-start(f32[32,16,128]{2,1,0:T(8,128)} %get-tuple-element.90), calls=%async_computation.2 | async-start | bytes 524288 | tf_op jit(solution)/shard_map/all_to_all | solution.py:276
  116.9 9.7 %all-to-all-done.2.last = f32[32,16,128]{2,1,0:T(8,128)S(1)} async-done(((f32[32,16,128]{2,1,0:T(8,128)}), f32[32,16,128]{2,1,0:T(8,128)S(1)}, u32[]{:S(2)}, u32[]{:S(2)}) %all-to-all-start.2) | async-done | bytes 262176 | tf_op jit(solution)/shard_map/all_to_all | solution.py:276
  (87 shorter events, 20.5 us)
Async XLA Ops:
  0.6 12.4 %copy-start.21 = (s32[1,1,8,2,6]{2,3,4,1,0:T(2,128)S(1)}, s32[1,1,8,2,6]{2,3,4,1,0:T(2,128)}, u32[]{:S(2)}) copy-start(s32[1,1,8,2,6]{2,3,4,1,0:T(2,128)} %param.18) | copy-start | bytes 1156
  0.6 12.5 %copy-start.17 = (s32[1,1,256]{2,1,0:T(1,128)S(1)}, s32[1,1,256]{2,1,0:T(1,128)}, u32[]{:S(2)}) copy-start(s32[1,1,256]{2,1,0:T(1,128)} %param.24) | copy-start | bytes 3076
  0.7 12.5 %copy-start.14 = (s32[1,1,8,6,2,128]{5,4,3,2,1,0:T(2,128)S(1)}, s32[1,1,8,6,2,128]{5,4,3,2,1,0:T(2,128)}, u32[]{:S(2)}) copy-start(s32[1,1,8,6,2,128]{5,4,3,2,1,0:T(2,128)} %param.19) | copy-start | bytes 147460
  0.7 12.5 %copy-start.16 = (s32[1,1,256]{2,1,0:T(1,128)S(1)}, s32[1,1,256]{2,1,0:T(1,128)}, u32[]{:S(2)}) copy-start(s32[1,1,256]{2,1,0:T(1,128)} %param.25) | copy-start | bytes 3076
  3.0 29.7 %all-to-all-start = ((f32[32,40,128]{2,1,0:T(8,128)}), f32[32,40,128]{2,1,0:T(8,128)S(1)}, u32[]{:S(2)}, u32[]{:S(2)}) async-start(f32[32,40,128]{2,1,0:T(8,128)} %shard_map.164), calls=%async_computation | async-start | bytes 1310720 | tf_op jit(solution)/shard_map/all_to_all | solution.py:276
  14.0 3.9 %collective-permute-start = (s32[32,128]{1,0:T(8,128)S(1)}, s32[32,128]{1,0:T(8,128)S(1)}, u32[]{:S(2)}, u32[]{:S(2)}) collective-permute-start(s32[32,128]{1,0:T(8,128)S(1)} %get-tuple-element.57), channel_id=1, source_target_pairs={{0,3},{1,0},{2,1},{3,2},{4,7},{5,4},{6,5},{7,6},{8,11},{9,8},{10,9... | collective-permute-start | bytes 49160 | tf_op jit(solution)/shard_map/ppermute | solution.py:273
  16.8 4.4 %collective-permute-start.1 = (s32[32,128]{1,0:T(8,128)S(1)}, s32[32,128]{1,0:T(8,128)S(1)}, u32[]{:S(2)}, u32[]{:S(2)}) collective-permute-start(s32[32,128]{1,0:T(8,128)S(1)} %get-tuple-element.58), channel_id=1, source_target_pairs={{0,2},{1,3},{2,0},{3,1},{4,6},{5,7},{6,4},{7,5},{8,10},{9,11},{10,... | collective-permute-start | bytes 49160 | tf_op jit(solution)/shard_map/ppermute | solution.py:273
  17.1 4.2 %collective-permute-start.2 = (s32[32,128]{1,0:T(8,128)S(1)}, s32[32,128]{1,0:T(8,128)S(1)}, u32[]{:S(2)}, u32[]{:S(2)}) collective-permute-start(s32[32,128]{1,0:T(8,128)S(1)} %get-tuple-element.59), channel_id=1, source_target_pairs={{0,1},{1,2},{2,3},{3,0},{4,5},{5,6},{6,7},{7,4},{8,9},{9,10},{10,1... | collective-permute-start | bytes 49160 | tf_op jit(solution)/shard_map/ppermute | solution.py:273
  21.4 8.1 %collective-permute-start.3 = (s32[64,128]{1,0:T(8,128)S(1)}, s32[64,128]{1,0:T(8,128)S(1)}, u32[]{:S(2)}, u32[]{:S(2)}) collective-permute-start(s32[64,128]{1,0:T(8,128)S(1)} %pad_add_fusion), channel_id=1, source_target_pairs={{0,4},{1,5},{2,6},{3,7},{4,0},{5,1},{6,2},{7,3},{8,12},{9,13},{10,... | collective-permute-start | bytes 98312 | tf_op jit(solution)/shard_map/ppermute | solution.py:270
  34.1 7.5 %collective-permute-start.4 = (f32[256,128]{1,0:T(8,128)S(1)}, f32[256,128]{1,0:T(8,128)S(1)}, u32[]{:S(2)}, u32[]{:S(2)}) collective-permute-start(f32[256,128]{1,0:T(8,128)S(1)} %get-tuple-element.64), channel_id=1, source_target_pairs={{0,1},{1,2},{2,3},{3,0},{4,5},{5,6},{6,7},{7,4},{8,9},{9,10},{10,1... | collective-permute-start | bytes 393224 | tf_op jit(solution)/shard_map/ppermute | solution.py:273
  36.1 5.5 %collective-permute-start.5 = (f32[256,128]{1,0:T(8,128)S(1)}, f32[256,128]{1,0:T(8,128)S(1)}, u32[]{:S(2)}, u32[]{:S(2)}) collective-permute-start(f32[256,128]{1,0:T(8,128)S(1)} %get-tuple-element.65), channel_id=1, source_target_pairs={{0,3},{1,0},{2,1},{3,2},{4,7},{5,4},{6,5},{7,6},{8,11},{9,8},{10,9... | collective-permute-start | bytes 393224 | tf_op jit(solution)/shard_map/ppermute | solution.py:273
  37.7 7.9 %collective-permute-start.6 = (f32[256,128]{1,0:T(8,128)S(1)}, f32[256,128]{1,0:T(8,128)S(1)}, u32[]{:S(2)}, u32[]{:S(2)}) collective-permute-start(f32[256,128]{1,0:T(8,128)S(1)} %get-tuple-element.66), channel_id=1, source_target_pairs={{0,2},{1,3},{2,0},{3,1},{4,6},{5,7},{6,4},{7,5},{8,10},{9,11},{10,... | collective-permute-start | bytes 393224 | tf_op jit(solution)/shard_map/ppermute | solution.py:273
  45.7 9.8 %collective-permute-start.10 = (f32[256,128]{1,0:T(8,128)S(1)}, f32[256,128]{1,0:T(8,128)S(1)}, u32[]{:S(2)}, u32[]{:S(2)}) collective-permute-start(f32[256,128]{1,0:T(8,128)S(1)} %get-tuple-element.73), channel_id=1, source_target_pairs={{0,2},{1,3},{2,0},{3,1},{4,6},{5,7},{6,4},{7,5},{8,10},{9,11},{10,... | collective-permute-start | bytes 393224 | tf_op jit(solution)/shard_map/ppermute | solution.py:273
  46.2 9.8 %collective-permute-start.7 = (f32[256,128]{1,0:T(8,128)S(1)}, f32[256,128]{1,0:T(8,128)S(1)}, u32[]{:S(2)}, u32[]{:S(2)}) collective-permute-start(f32[256,128]{1,0:T(8,128)S(1)} %add_add_fusion), channel_id=1, source_target_pairs={{0,4},{1,5},{2,6},{3,7},{4,0},{5,1},{6,2},{7,3},{8,12},{9,13},{10,... | collective-permute-start | bytes 393224 | tf_op jit(solution)/shard_map/ppermute | solution.py:270
  50.3 5.7 %collective-permute-start.8 = (f32[256,128]{1,0:T(8,128)S(1)}, f32[256,128]{1,0:T(8,128)S(1)}, u32[]{:S(2)}, u32[]{:S(2)}) collective-permute-start(f32[256,128]{1,0:T(8,128)S(1)} %get-tuple-element.71), channel_id=1, source_target_pairs={{0,1},{1,2},{2,3},{3,0},{4,5},{5,6},{6,7},{7,4},{8,9},{9,10},{10,1... | collective-permute-start | bytes 393224 | tf_op jit(solution)/shard_map/ppermute | solution.py:273
  51.6 4.4 %collective-permute-start.9 = (f32[256,128]{1,0:T(8,128)S(1)}, f32[256,128]{1,0:T(8,128)S(1)}, u32[]{:S(2)}, u32[]{:S(2)}) collective-permute-start(f32[256,128]{1,0:T(8,128)S(1)} %get-tuple-element.72), channel_id=1, source_target_pairs={{0,3},{1,0},{2,1},{3,2},{4,7},{5,4},{6,5},{7,6},{8,11},{9,8},{10,9... | collective-permute-start | bytes 393224 | tf_op jit(solution)/shard_map/ppermute | solution.py:273
  58.4 24.3 %all-to-all-start.1 = ((f32[32,16,128]{2,1,0:T(8,128)}), f32[32,16,128]{2,1,0:T(8,128)S(1)}, u32[]{:S(2)}, u32[]{:S(2)}) async-start(f32[32,16,128]{2,1,0:T(8,128)} %shard_map.172), calls=%async_computation.1 | async-start | bytes 524288 | tf_op jit(solution)/shard_map/all_to_all | solution.py:276
  66.0 11.8 %collective-permute-start.11 = (f32[256,128]{1,0:T(8,128)S(1)}, f32[256,128]{1,0:T(8,128)S(1)}, u32[]{:S(2)}, u32[]{:S(2)}) collective-permute-start(f32[256,128]{1,0:T(8,128)S(1)} %get-tuple-element.77.grad_sum.g0), channel_id=1, source_target_pairs={{0,4},{1,5},{2,6},{3,7},{4,0},{5,1},{6,2},{7,3},{8,12},{9,13},{10,... | collective-permute-start | bytes 393224 | tf_op jit(solution)/shard_map/ppermute | solution.py:270
  69.4 8.4 %collective-permute-start.12 = (f32[256,128]{1,0:T(8,128)S(1)}, f32[256,128]{1,0:T(8,128)S(1)}, u32[]{:S(2)}, u32[]{:S(2)}) collective-permute-start(f32[256,128]{1,0:T(8,128)S(1)} %get-tuple-element.77.grad_sum.g0), channel_id=1, source_target_pairs={{0,3},{1,0},{2,1},{3,2},{4,7},{5,4},{6,5},{7,6},{8,11},{9,8},{10,9... | collective-permute-start | bytes 393224 | tf_op jit(solution)/shard_map/ppermute | solution.py:273
  70.9 6.9 %collective-permute-start.13 = (f32[256,128]{1,0:T(8,128)S(1)}, f32[256,128]{1,0:T(8,128)S(1)}, u32[]{:S(2)}, u32[]{:S(2)}) collective-permute-start(f32[256,128]{1,0:T(8,128)S(1)} %get-tuple-element.77.grad_sum.g0), channel_id=1, source_target_pairs={{0,2},{1,3},{2,0},{3,1},{4,6},{5,7},{6,4},{7,5},{8,10},{9,11},{10,... | collective-permute-start | bytes 393224 | tf_op jit(solution)/shard_map/ppermute | solution.py:273
  72.2 7.9 %collective-permute-start.14 = (f32[256,128]{1,0:T(8,128)S(1)}, f32[256,128]{1,0:T(8,128)S(1)}, u32[]{:S(2)}, u32[]{:S(2)}) collective-permute-start(f32[256,128]{1,0:T(8,128)S(1)} %get-tuple-element.77.grad_sum.g0), channel_id=1, source_target_pairs={{0,1},{1,2},{2,3},{3,0},{4,5},{5,6},{6,7},{7,4},{8,9},{9,10},{10,1... | collective-permute-start | bytes 393224 | tf_op jit(solution)/shard_map/ppermute | solution.py:273
  82.7 23.6 %all-to-all-start.3 = ((f32[32,32,128]{2,1,0:T(8,128)}), f32[32,32,128]{2,1,0:T(8,128)S(1)}, u32[]{:S(2)}, u32[]{:S(2)}) async-start(f32[32,32,128]{2,1,0:T(8,128)} %bitcast.11), calls=%async_computation.3 | async-start | bytes 1048576 | tf_op jit(solution)/shard_map/all_to_all | solution.py:276
  89.2 5.8 %collective-permute-start.18 = (f32[16,128]{1,0:T(8,128)S(1)}, f32[16,128]{1,0:T(8,128)S(1)}, u32[]{:S(2)}, u32[]{:S(2)}) collective-permute-start(f32[16,128]{1,0:T(8,128)S(1)} %shard_map.175), channel_id=1, source_target_pairs={{0,1},{1,2},{2,3},{3,0},{4,5},{5,6},{6,7},{7,4},{8,9},{9,10},{10,1... | collective-permute-start | bytes 24584 | tf_op jit(solution)/shard_map/ppermute | solution.py:273
  90.1 5.1 %collective-permute-start.19 = (f32[16,128]{1,0:T(8,128)S(1)}, f32[16,128]{1,0:T(8,128)S(1)}, u32[]{:S(2)}, u32[]{:S(2)}) collective-permute-start(f32[16,128]{1,0:T(8,128)S(1)} %shard_map.175), channel_id=1, source_target_pairs={{0,2},{1,3},{2,0},{3,1},{4,6},{5,7},{6,4},{7,5},{8,10},{9,11},{10,... | collective-permute-start | bytes 24584 | tf_op jit(solution)/shard_map/ppermute | solution.py:273
  91.8 3.5 %collective-permute-start.20 = (f32[16,128]{1,0:T(8,128)S(1)}, f32[16,128]{1,0:T(8,128)S(1)}, u32[]{:S(2)}, u32[]{:S(2)}) collective-permute-start(f32[16,128]{1,0:T(8,128)S(1)} %shard_map.175), channel_id=1, source_target_pairs={{0,3},{1,0},{2,1},{3,2},{4,7},{5,4},{6,5},{7,6},{8,11},{9,8},{10,9... | collective-permute-start | bytes 24584 | tf_op jit(solution)/shard_map/ppermute | solution.py:273
  93.2 5.2 %collective-permute-start.15 = (f32[256,128]{1,0:T(8,128)S(1)}, f32[256,128]{1,0:T(8,128)S(1)}, u32[]{:S(2)}, u32[]{:S(2)}) collective-permute-start(f32[256,128]{1,0:T(8,128)S(1)} %collective-permute-done.11.g4), channel_id=1, source_target_pairs={{0,3},{1,0},{2,1},{3,2},{4,7},{5,4},{6,5},{7,6},{8,11},{9,8},{10,9... | collective-permute-start | bytes 393224 | tf_op jit(solution)/shard_map/ppermute | solution.py:273
  93.4 5.6 %collective-permute-start.16 = (f32[256,128]{1,0:T(8,128)S(1)}, f32[256,128]{1,0:T(8,128)S(1)}, u32[]{:S(2)}, u32[]{:S(2)}) collective-permute-start(f32[256,128]{1,0:T(8,128)S(1)} %collective-permute-done.11.g4), channel_id=1, source_target_pairs={{0,2},{1,3},{2,0},{3,1},{4,6},{5,7},{6,4},{7,5},{8,10},{9,11},{10,... | collective-permute-start | bytes 393224 | tf_op jit(solution)/shard_map/ppermute | solution.py:273
  95.0 6.7 %collective-permute-start.17 = (f32[256,128]{1,0:T(8,128)S(1)}, f32[256,128]{1,0:T(8,128)S(1)}, u32[]{:S(2)}, u32[]{:S(2)}) collective-permute-start(f32[256,128]{1,0:T(8,128)S(1)} %collective-permute-done.11.g4), channel_id=1, source_target_pairs={{0,1},{1,2},{2,3},{3,0},{4,5},{5,6},{6,7},{7,4},{8,9},{9,10},{10,1... | collective-permute-start | bytes 393224 | tf_op jit(solution)/shard_map/ppermute | solution.py:273
  95.2 10.4 %collective-permute-start.21 = (f32[16,128]{1,0:T(8,128)S(1)}, f32[16,128]{1,0:T(8,128)S(1)}, u32[]{:S(2)}, u32[]{:S(2)}) collective-permute-start(f32[16,128]{1,0:T(8,128)S(1)} %add_add_fusion.1.near), channel_id=1, source_target_pairs={{0,4},{1,5},{2,6},{3,7},{4,0},{5,1},{6,2},{7,3},{8,12},{9,13},{10,... | collective-permute-start | bytes 24584 | tf_op jit(solution)/shard_map/ppermute | solution.py:270
  103.5 12.1 %copy-start.15 = (s32[1,1,32,32]{3,2,1,0:T(8,128)S(1)}, s32[1,1,32,32]{3,2,1,0:T(8,128)}, u32[]{:S(2)}) copy-start(s32[1,1,32,32]{3,2,1,0:T(8,128)} %param.20) | copy-start | bytes 12292
  105.6 21.1 %copy-start.18 = (s32[1,1,8]{2,1,0:T(1,128)S(1)}, s32[1,1,8]{2,1,0:T(1,128)}, u32[]{:S(2)}) copy-start(s32[1,1,8]{2,1,0:T(1,128)} %param.23) | copy-start | bytes 100
  106.3 20.4 %all-to-all-start.2 = ((f32[32,16,128]{2,1,0:T(8,128)}), f32[32,16,128]{2,1,0:T(8,128)S(1)}, u32[]{:S(2)}, u32[]{:S(2)}) async-start(f32[32,16,128]{2,1,0:T(8,128)} %get-tuple-element.90), calls=%async_computation.2 | async-start | bytes 524288 | tf_op jit(solution)/shard_map/all_to_all | solution.py:276
  (16 other events, 78.1 us)

commit v7 on v6

--- a/solution.py
+++ b/solution.py
@@ -130,9 +130,11 @@
     return jnp.concatenate([dot(frm, to, NT), dot(h_frm, h_to, NT)], axis=0)
 
 
-def k_fwd(pos, l0, l1, l2, l3, far, fwd, flag):
+def k_fwd(pos, *rest_refs):
+    *lists, fwd, flag = rest_refs
+    blocks = [ref[0:16, :] for ref in lists] if len(lists) == 4 else [lists[0][16 * k : 16 * k + 16, :] for k in range(4)]
     top = jnp.float32(0.0)
-    for r, block in enumerate(blocks_of((l0, l1, l2, l3, far))):
+    for r, block in enumerate(blocks):
         count = forward_count(*hots(pos, block))
         top = jnp.maximum(top, jnp.max(count))
         fwd[r] = count.astype(BF16)
@@ -159,15 +161,18 @@
     inv[...] = jnp.broadcast_to(1.0 / (degree + 1.0), (256, 128))
 
 
-def k_partial(flag, pos, l0, l1, l2, l3, far, features, incoming, fwd, *outs):
+def k_partial(flag, pos, *rest_refs):
+    *lists, features, incoming, fwd, o0, o1, o2, o3 = rest_refs
+    outs = (o0, o1, o2, o3)
     hubs = incoming[:, 32:40, :].reshape(256, 128)
     x = jnp.concatenate([halves(features[...]), halves(hubs)], axis=0)
-    for r in range(8):
+    for r in range(4):
         outs[r][...] = joined(dot(fwd[r], x))
 
     @pl.when(flag[0] != 0)
     def _():
-        for r, block in enumerate(blocks_of((l0, l1, l2, l3, far))):
+        blocks = [ref[0:16, :] for ref in lists] if len(lists) == 4 else [lists[0][16 * k : 16 * k + 16, :] for k in range(4)]
+        for r, block in enumerate(blocks):
             outs[r][...] += joined(dot(rest(forward_count(*hots(pos, block))), x))
 
 
@@ -203,10 +208,9 @@
         out[p, 8:16, :] = fill
 
 
-def k_slots(flag, halo_to, halo_from, grad_sum, h_bwd, grad_pre, w_root, out, root):
+def k_slots(flag, halo_to, halo_from, grad_sum, h_bwd, out):
     x = halves(grad_sum[...])
     out[...] = joined(dot(h_bwd[...], x))
-    root[...] = dot(grad_pre[...], w_root[...], NT, HIGH)
 
     @pl.when(flag[0] != 0)
     def _():
@@ -214,20 +218,20 @@
         out[...] += joined(dot(rest(dot(frm, to, NT)), x))
 
 
-def k_back(flag, pos, l0, l1, l2, l3, far, g0, g1, g2, g3, g4, g5, g6, g7, bwd, root, local, hubs, total):
+def k_back(flag, flag_far, pos, l0, l1, l2, l3, far, g0, g1, g2, g3, g4, g5, g6, g7, bwd, local, hubs, total):
     xs = [halves(g[0:256, :]) for g in (g0, g1, g2, g3, g4, g5, g6, g7)]
     acc = dot(bwd[0], xs[0])
     for r in range(1, 8):
         acc = acc + dot(bwd[r], xs[r])
     total[...] = joined(acc)
 
-    @pl.when(flag[0] != 0)
+    @pl.when(flag[0] + flag_far[0] != 0)
     def _():
         for r, block in enumerate(blocks_of((l0, l1, l2, l3, far))):
             total[...] += joined(dot(rest(backward_count(*hots(pos, block))), xs[r]))
 
     hubs[...] = total[256:512, :].reshape(32, 8, 128)
-    local[...] = root[...] + total[0:256, :]
+    local[...] = total[0:256, :]
 
 
 def k_sum(weights, out):
@@ -242,8 +246,9 @@
     bias[...] = w[8:9]
 
 
-def k_scatter(returned, send, local, out):
-    out[...] = local[...] + joined(dot(send_hot(send), halves(returned[...].reshape(1024, 128))))
+def k_scatter(returned, send, local, grad_pre, w_root, out):
+    root = dot(grad_pre[...], w_root[...], NT, HIGH)
+    out[...] = local[...] + root + joined(dot(send_hot(send), halves(returned[...].reshape(1024, 128))))
 
 
 def k_final(last, hub, local, out, w_neigh, w_root):
@@ -296,26 +301,30 @@
         k_boundary, (shape((256, 1024), BF16), shape((1024, 256), BF16), block, shape((1,), I32)),
         (own_to, halo_to, halo_from, hub_to), flops=1 << 31,
     )
-    fwd, flag = call(k_fwd, (shape((8, 256, 512), BF16), shape((1,), I32)), lists, lm, flops=1 << 31)
+    counts = (shape((4, 256, 512), BF16), shape((1,), I32))
+    fwd_near, flag_near = call(k_fwd, counts, lists[:5], lm[:5], flops=1 << 30)
+    fwd_far, flag_far = call(k_fwd, counts, (pos, far), lm[:2], flops=1 << 30)
     bwd = call(k_bwd, shape((8, 512, 256), BF16), lists, lm, flops=1 << 31)
-    part = call(k_partial, [block] * 8, (flag, *lists, features, incoming, fwd), [sm, *lm, vm, vm, vm])
-    other = part[4] + turn(part[5], 1) + turn(part[7], 3) + turn(part[6], 2)
+    part = call(k_partial, [block] * 4, (flag_far, pos, far, features, incoming, fwd_far), [sm, sm] + [vm] * 4)
+    o1, o3, o2 = turn(part[1], 1), turn(part[3], 3), turn(part[2], 2)
+    own_part = call(
+        k_partial, [block] * 4, (flag_near, *lists[:5], features, incoming, fwd_near), [sm, *lm[:5]] + [vm] * 3
+    )
+    other = part[0] + o1 + o3 + o2
+    part = own_part
     other, p1, p2, p3 = lax.optimization_barrier((other, part[1], part[2], part[3]))
     other = swap(other)
+    own = call(k_halo, block, (h_flag, halo_to, halo_from, incoming, h_fwd, part[0]), [sm] + [vm] * 5)
+    own, p2 = lax.optimization_barrier((own, p2))
     near = [turn(p1, 1), turn(p3, 3), turn(p2, 2)]
-    own = call(k_halo, block, (h_flag, halo_to, halo_from, incoming, h_fwd, part[0]), [sm] + [vm] * 5)
-    inv, bwd = lax.optimization_barrier((inv, bwd))
     output, grad_pre, grad_sum, mean = call(
         k_layer, [block] * 4, (own, other, *near, inv, features, w_neigh, w_root, bias.reshape(1, 128), grad_out),
     )
     g4 = swap(grad_sum)
     g1, g3, g2 = turn(grad_sum, 3), turn(grad_sum, 1), turn(grad_sum, 2)
     weights = exchange(call(k_weights, shape((32, 16, 128)), (grad_pre, mean, features)), "grp")
-    slots, root = call(
-        k_slots, [shape((1024, 128)), block], (h_flag, halo_to, halo_from, grad_sum, h_bwd, grad_pre, w_root),
-        [sm] + [vm] * 6,
-    )
-    g4, weights, g1, g2, g3, slots = lax.optimization_barrier((g4, weights, g1, g2, g3, slots))
+    slots = call(k_slots, shape((1024, 128)), (h_flag, halo_to, halo_from, grad_sum, h_bwd), [sm] + [vm] * 4)
+    weights, g1, g2, g3, g4, slots, bwd = lax.optimization_barrier((weights, g1, g2, g3, g4, slots, bwd))
     returned = exchange(slots.reshape(32, 32, 128), "grp")
     w = call(k_sum, shape((16, 128)), (weights,))
     w = w + turn(w, 1) + turn(w, 2) + turn(w, 3)
@@ -323,7 +332,7 @@
     g5, g7, g6 = turn(g4, 3), turn(g4, 1), turn(g4, 2)
     local, hubs = call(
         k_back, [block, shape((32, 8, 128))],
-        (flag, *lists, grad_sum, g1, g2, g3, g4, g5, g6, g7, bwd, root), [sm, *lm] + [vm] * 10,
+        (flag_near, flag_far, *lists, grad_sum, g1, g2, g3, g4, g5, g6, g7, bwd), [sm, sm, *lm] + [vm] * 9,
         [pltpu.VMEM((512, 128), F32)],
     )
     factor = (256 * lax.axis_size("grp") * lax.axis_size("blk")) ** (-0.5)
@@ -331,7 +340,7 @@
         functools.partial(k_pack, factor), [shape((32, 16, 128)), shape((1, 128))], (hubs, w, w_far)
     )
     last = exchange(last, "grp")
-    local = call(k_scatter, block, (returned, send, local))
+    local = call(k_scatter, block, (returned, send, local, grad_pre, w_root))
     grad_features, grad_wn, grad_wr = call(
         k_final, [block, shape((128, 128)), shape((128, 128))], (last, hub, local), [vm, sm, vm]
     )

time: 129 us -> 130 us (level)
  local copies, waits for them, and re-layouts: 6.71 us -> 8.98 us
  Pallas kernels: 20 us -> 22 us
  waiting for transfers between devices: 30.8 us -> 29 us
  starting transfers between devices: 69.4 us -> 68.1 us
    ppermute x18, waiting for transfers between devices: 13.2 us -> 8.23 us  [turn(): lax.ppermute(v, 'blk', [(i, i // 4 * 4 + (i % 4 + k) % 4) for i in range(...]
    all_to_all x4, waiting for transfers between devices: 12.5 us -> 16.1 us  [exchange(): return lax.all_to_all(v, axis, split_axis=0, concat_axis=0, tiled=True)]
    unnamed x44 -> x48, local copies, waits for them, and re-layouts: 6.61 us -> 8.88 us
    pallas_call x15 -> x17, Pallas kernels: 20 us -> 22 us  [call(): pl.pallas_call(kernel, out_shape=out_shape, in_specs=[whole] * len(args)...]
  transfers between devices with their start and end apart: 26 -> 26, of which waited for: 12 -> 11; matrix products, arithmetic and copies ran while one was open for 0% -> 0% of each run, Pallas kernels for 10% -> 12%
where the time goes in v7:
time: 130 us; the launch traced here: 129 us
  starting transfers between devices  68.1 us (52%)
  waiting for transfers between devices  29 us (22%)
  Pallas kernels  22 us (17%)
  local copies, waits for them, and re-layouts  8.98 us (7%)
    all_to_all x4, starting transfers between devices, exchange(): return lax.all_to_all(v, axis, split_axis=0, concat_axis=0, tiled=True)  32.3 us
    pallas_call x17, Pallas kernels, call(): pl.pallas_call(kernel, out_shape=out_shape, in_specs=[whole] * len(args)...  22 us
    ppermute x18, starting transfers between devices, turn(): lax.ppermute(v, 'blk', [(i, i // 4 * 4 + (i % 4 + k) % 4) for i in range(...  21.6 us
    all_to_all x4, waiting for transfers between devices, exchange(): return lax.all_to_all(v, axis, split_axis=0, concat_axis=0, tiled=True)  16.1 us
    ppermute x4, starting transfers between devices, swap(): return lax.ppermute(v, 'blk', [(i, i ^ 4) for i in range(8)])  14.1 us
    unnamed x48, local copies, waits for them, and re-layouts  8.88 us
    ppermute x18, waiting for transfers between devices, turn(): lax.ppermute(v, 'blk', [(i, i // 4 * 4 + (i % 4 + k) % 4) for i in range(...  8.23 us
    ppermute x4, waiting for transfers between devices, swap(): return lax.ppermute(v, 'blk', [(i, i ^ 4) for i in range(8)])  4.66 us
  transfers between devices with their start and end apart: 26, of which 11 were waited for; matrix products, arithmetic and copies ran while one was open for 0% of the time, Pallas kernels for 12%

profile of v7, /device:TPU:1, one launch (start us, length us, event | category | flops | bytes accessed | tf_op | source)
XLA Modules:
  0.0 129.1 jit_solution(9127526174572811154)
XLA Ops:
  0.7 2.3 %shard_map.164 = f32[32,40,128]{2,1,0:T(8,128)} custom-call(f32[256,128]{1,0:T(8,128)} %features.3, s32[32,32]{1,0:T(8,128)} %bitcast.13, s32[1,8]{1,0:T(1,128)} %bitcast.26), custom_call_target="tpu_custom_call" | custom-call | flops 268435456 | bytes 135200 | tf_op jit(solution)/shard_map/pallas_call | solution.py:45
  3.0 10.0 %all-to-all-start = ((f32[32,40,128]{2,1,0:T(8,128)}), f32[32,40,128]{2,1,0:T(8,128)S(1)}, u32[]{:S(2)}, u32[]{:S(2)}) async-start(f32[32,40,128]{2,1,0:T(8,128)} %shard_map.164), calls=%async_computation | async-start | bytes 1310720 | tf_op jit(solution)/shard_map/all_to_all | solution.py:281
  14.0 2.8 %collective-permute-start = (s32[32,128]{1,0:T(8,128)S(1)}, s32[32,128]{1,0:T(8,128)S(1)}, u32[]{:S(2)}, u32[]{:S(2)}) collective-permute-start(s32[32,128]{1,0:T(8,128)S(1)} %get-tuple-element.58), channel_id=1, source_target_pairs={{0,3},{1,0},{2,1},{3,2},{4,7},{5,4},{6,5},{7,6},{8,11},{9,8},{10,9... | collective-permute-start | bytes 49160 | tf_op jit(solution)/shard_map/ppermute | solution.py:278
  17.9 3.3 %collective-permute-done.1.rest_refs_2_.l2 = s32[32,128]{1,0:T(8,128)S(1)} collective-permute-done((s32[32,128]{1,0:T(8,128)S(1)}, s32[32,128]{1,0:T(8,128)S(1)}, u32[]{:S(2)}, u32[]{:S(2)}) %collective-permute-start.1) | collective-permute-done | bytes 16416 | tf_op jit(solution)/shard_map/ppermute | solution.py:278
  21.4 4.3 %collective-permute-start.3 = (s32[64,128]{1,0:T(8,128)S(1)}, s32[64,128]{1,0:T(8,128)S(1)}, u32[]{:S(2)}, u32[]{:S(2)}) collective-permute-start(s32[64,128]{1,0:T(8,128)S(1)} %pad_add_fusion), channel_id=1, source_target_pairs={{0,4},{1,5},{2,6},{3,7},{4,0},{5,1},{6,2},{7,3},{8,12},{9,13},{10,... | collective-permute-start | bytes 98312 | tf_op jit(solution)/shard_map/ppermute | solution.py:275
  25.7 2.3 %shard_map.166 = (bf16[256,1024]{1,0:T(8,128)(2,1)S(1)}, bf16[1024,256]{1,0:T(8,128)(2,1)S(1)}, f32[256,128]{1,0:T(8,128)S(1)}, s32[1]{0:T(128)}) custom-call(s32[48,128]{1,0:T(8,128)S(1)} %get-tuple-element.53.own_to, s32[8,128]{1,0:T(8,128)S(1)} %bitcast.15, s32[8,128]{1,0:T(8,128)S(1)} %bitcast.18, s32[2,128]{1,0:T(2,128)S(1)} %bitcast.25), custom_call_target="tpu_custom_call" | custom-call | flops 2147483648 | bytes 33792 | tf_op jit(solution)/shard_map/pallas_call | solution.py:45
  28.0 1.5 %collective-permute-done.3.rest_refs_0_.far = s32[64,128]{1,0:T(8,128)S(1)} collective-permute-done((s32[64,128]{1,0:T(8,128)S(1)}, s32[64,128]{1,0:T(8,128)S(1)}, u32[]{:S(2)}, u32[]{:S(2)}) %collective-permute-start.3) | collective-permute-done | bytes 32800 | tf_op jit(solution)/shard_map/ppermute | solution.py:275
  29.5 1.5 %shard_map.170 = (bf16[4,256,512]{2,1,0:T(8,128)(2,1)S(1)}, s32[1]{0:T(128)}) custom-call(s32[1]{0:T(128)} %bitcast.pos, s32[64,128]{1,0:T(8,128)S(1)} %collective-permute-done.3.rest_refs_0_.far), custom_call_target="tpu_custom_call" | custom-call | flops 1073741824 | bytes 32772 | tf_op jit(solution)/shard_map/pallas_call | solution.py:45
  31.1 1.7 %all-to-all-done.rest_refs_5_.incoming.rest_refs_2_ = f32[32,40,128]{2,1,0:T(8,128)S(1)} async-done(((f32[32,40,128]{2,1,0:T(8,128)}), f32[32,40,128]{2,1,0:T(8,128)S(1)}, u32[]{:S(2)}, u32[]{:S(2)}) %all-to-all-start) | async-done | bytes 655392 | tf_op jit(solution)/shard_map/all_to_all | solution.py:281
  33.8 2.1 %collective-permute-start.4 = (f32[256,128]{1,0:T(8,128)S(1)}, f32[256,128]{1,0:T(8,128)S(1)}, u32[]{:S(2)}, u32[]{:S(2)}) collective-permute-start(f32[256,128]{1,0:T(8,128)S(1)} %get-tuple-element.67), channel_id=1, source_target_pairs={{0,1},{1,2},{2,3},{3,0},{4,5},{5,6},{6,7},{7,4},{8,9},{9,10},{10,1... | collective-permute-start | bytes 393224 | tf_op jit(solution)/shard_map/ppermute | solution.py:278
  35.9 1.5 %collective-permute-start.5 = (f32[256,128]{1,0:T(8,128)S(1)}, f32[256,128]{1,0:T(8,128)S(1)}, u32[]{:S(2)}, u32[]{:S(2)}) collective-permute-start(f32[256,128]{1,0:T(8,128)S(1)} %get-tuple-element.68), channel_id=1, source_target_pairs={{0,3},{1,0},{2,1},{3,2},{4,7},{5,4},{6,5},{7,6},{8,11},{9,8},{10,9... | collective-permute-start | bytes 393224 | tf_op jit(solution)/shard_map/ppermute | solution.py:278
  37.4 1.6 %collective-permute-start.6 = (f32[256,128]{1,0:T(8,128)S(1)}, f32[256,128]{1,0:T(8,128)S(1)}, u32[]{:S(2)}, u32[]{:S(2)}) collective-permute-start(f32[256,128]{1,0:T(8,128)S(1)} %get-tuple-element.69), channel_id=1, source_target_pairs={{0,2},{1,3},{2,0},{3,1},{4,6},{5,7},{6,4},{7,5},{8,10},{9,11},{10,... | collective-permute-start | bytes 393224 | tf_op jit(solution)/shard_map/ppermute | solution.py:278
  39.0 1.5 %shard_map.167 = (bf16[4,256,512]{2,1,0:T(8,128)(2,1)S(1)}, s32[1]{0:T(128)}) custom-call(s32[1]{0:T(128)} %bitcast.pos, s32[32,128]{1,0:T(8,128)S(1)} %get-tuple-element.57.rest_refs_0_.l0, s32[32,128]{1,0:T(8,128)S(1)} %collective-permute-done.rest_refs_1_.l1, s32[32,128]{1,0:T(8,128)S(1)} %collective-permute-done.1.rest_refs_2_.l2, ...), custom_call_target="tpu_custom_call" | custom-call | flops 1073741824 | bytes 65540 | tf_op jit(solution)/shard_map/pallas_call | solution.py:45
  43.5 1.8 %collective-permute-done.6 = f32[256,128]{1,0:T(8,128)S(1)} collective-permute-done((f32[256,128]{1,0:T(8,128)S(1)}, f32[256,128]{1,0:T(8,128)S(1)}, u32[]{:S(2)}, u32[]{:S(2)}) %collective-permute-start.6) | collective-permute-done | bytes 131104 | tf_op jit(solution)/shard_map/ppermute | solution.py:278
  45.4 4.3 %collective-permute-start.7 = (f32[256,128]{1,0:T(8,128)S(1)}, f32[256,128]{1,0:T(8,128)S(1)}, u32[]{:S(2)}, u32[]{:S(2)}) collective-permute-start(f32[256,128]{1,0:T(8,128)S(1)} %add_add_fusion), channel_id=1, source_target_pairs={{0,4},{1,5},{2,6},{3,7},{4,0},{5,1},{6,2},{7,3},{8,12},{9,13},{10,... | collective-permute-start | bytes 393224 | tf_op jit(solution)/shard_map/ppermute | solution.py:275
  50.3 2.1 %collective-permute-start.9 = (f32[256,128]{1,0:T(8,128)S(1)}, f32[256,128]{1,0:T(8,128)S(1)}, u32[]{:S(2)}, u32[]{:S(2)}) collective-permute-start(f32[256,128]{1,0:T(8,128)S(1)} %get-tuple-element.77), channel_id=1, source_target_pairs={{0,3},{1,0},{2,1},{3,2},{4,7},{5,4},{6,5},{7,6},{8,11},{9,8},{10,9... | collective-permute-start | bytes 393224 | tf_op jit(solution)/shard_map/ppermute | solution.py:278
  52.5 3.0 %collective-permute-done.7.a1 = f32[256,128]{1,0:T(8,128)S(1)} collective-permute-done((f32[256,128]{1,0:T(8,128)S(1)}, f32[256,128]{1,0:T(8,128)S(1)}, u32[]{:S(2)}, u32[]{:S(2)}) %collective-permute-start.7) | collective-permute-done | bytes 131104 | tf_op jit(solution)/shard_map/ppermute | solution.py:275
  55.5 2.2 %collective-permute-done.10.a4 = f32[256,128]{1,0:T(8,128)S(1)} collective-permute-done((f32[256,128]{1,0:T(8,128)S(1)}, f32[256,128]{1,0:T(8,128)S(1)}, u32[]{:S(2)}, u32[]{:S(2)}) %collective-permute-start.10) | collective-permute-done | bytes 131104 | tf_op jit(solution)/shard_map/ppermute | solution.py:278
  60.1 7.4 %all-to-all-start.1 = ((f32[32,16,128]{2,1,0:T(8,128)}), f32[32,16,128]{2,1,0:T(8,128)S(1)}, u32[]{:S(2)}, u32[]{:S(2)}) async-start(f32[32,16,128]{2,1,0:T(8,128)} %shard_map.173), calls=%async_computation.1 | async-start | bytes 524288 | tf_op jit(solution)/shard_map/all_to_all | solution.py:281
  67.5 1.7 %collective-permute-start.14 = (f32[256,128]{1,0:T(8,128)S(1)}, f32[256,128]{1,0:T(8,128)S(1)}, u32[]{:S(2)}, u32[]{:S(2)}) collective-permute-start(f32[256,128]{1,0:T(8,128)S(1)} %get-tuple-element.81.grad_sum.g0), channel_id=1, source_target_pairs={{0,4},{1,5},{2,6},{3,7},{4,0},{5,1},{6,2},{7,3},{8,12},{9,13},{10,... | collective-permute-start | bytes 393224 | tf_op jit(solution)/shard_map/ppermute | solution.py:275
  69.2 2.0 %collective-permute-start.12 = (f32[256,128]{1,0:T(8,128)S(1)}, f32[256,128]{1,0:T(8,128)S(1)}, u32[]{:S(2)}, u32[]{:S(2)}) collective-permute-start(f32[256,128]{1,0:T(8,128)S(1)} %get-tuple-element.81.grad_sum.g0), channel_id=1, source_target_pairs={{0,2},{1,3},{2,0},{3,1},{4,6},{5,7},{6,4},{7,5},{8,10},{9,11},{10,... | collective-permute-start | bytes 393224 | tf_op jit(solution)/shard_map/ppermute | solution.py:278
  72.6 1.6 %shard_map.175.bwd = bf16[8,512,256]{2,1,0:T(8,128)(2,1)S(1)} custom-call(s32[1]{0:T(128)} %bitcast.pos, s32[32,128]{1,0:T(8,128)S(1)} %get-tuple-element.57.rest_refs_0_.l0, s32[32,128]{1,0:T(8,128)S(1)} %collective-permute-done.rest_refs_1_.l1, s32[32,128]{1,0:T(8,128)S(1)} %collective-permute-done.1.rest_refs_2_.l2, s32[32,128]{1,0:T(8,128)S(1)} %copy-done.10, ...), custom_call_target="tpu_custom_call" | custom-call | flops 2147483648 | bytes 98308 | tf_op jit(solution)/shard_map/pallas_call | solution.py:45
  75.5 1.8 %shard_map.174 = f32[1024,128]{1,0:T(8,128)} custom-call(s32[1]{0:T(128)} %get-tuple-element.54.flag, s32[8,128]{1,0:T(8,128)S(1)} %bitcast.17, s32[8,128]{1,0:T(8,128)S(1)} %bitcast.20, f32[256,128]{1,0:T(8,128)S(1)} %get-tuple-element.81.grad_sum.g0, bf16[1024,256]{1,0:T(8,128)(2,1)S(1)} %get-tuple-element.84.h_bwd), custom_call_target="tpu_custom_call" | custom-call | flops 268435456 | bytes 663556 | tf_op jit(solution)/shard_map/pallas_call | solution.py:45
  78.8 5.4 %all-to-all-done.1.weights = f32[32,16,128]{2,1,0:T(8,128)S(1)} async-done(((f32[32,16,128]{2,1,0:T(8,128)}), f32[32,16,128]{2,1,0:T(8,128)S(1)}, u32[]{:S(2)}, u32[]{:S(2)}) %all-to-all-start.1) | async-done | bytes 262176 | tf_op jit(solution)/shard_map/all_to_all | solution.py:281
  84.2 5.2 %all-to-all-start.3 = ((f32[32,32,128]{2,1,0:T(8,128)}), f32[32,32,128]{2,1,0:T(8,128)S(1)}, u32[]{:S(2)}, u32[]{:S(2)}) async-start(f32[32,32,128]{2,1,0:T(8,128)} %bitcast.11), calls=%async_computation.3 | async-start | bytes 1048576 | tf_op jit(solution)/shard_map/all_to_all | solution.py:281
  91.0 2.0 %collective-permute-start.17 = (f32[256,128]{1,0:T(8,128)S(1)}, f32[256,128]{1,0:T(8,128)S(1)}, u32[]{:S(2)}, u32[]{:S(2)}) collective-permute-start(f32[256,128]{1,0:T(8,128)S(1)} %collective-permute-done.14.g4), channel_id=1, source_target_pairs={{0,1},{1,2},{2,3},{3,0},{4,5},{5,6},{6,7},{7,4},{8,9},{9,10},{10,1... | collective-permute-start | bytes 393224 | tf_op jit(solution)/shard_map/ppermute | solution.py:278
  93.0 1.6 %collective-permute-start.16 = (f32[256,128]{1,0:T(8,128)S(1)}, f32[256,128]{1,0:T(8,128)S(1)}, u32[]{:S(2)}, u32[]{:S(2)}) collective-permute-start(f32[256,128]{1,0:T(8,128)S(1)} %collective-permute-done.14.g4), channel_id=1, source_target_pairs={{0,2},{1,3},{2,0},{3,1},{4,6},{5,7},{6,4},{7,5},{8,10},{9,11},{10,... | collective-permute-start | bytes 393224 | tf_op jit(solution)/shard_map/ppermute | solution.py:278
  94.6 2.0 %collective-permute-start.15 = (f32[256,128]{1,0:T(8,128)S(1)}, f32[256,128]{1,0:T(8,128)S(1)}, u32[]{:S(2)}, u32[]{:S(2)}) collective-permute-start(f32[256,128]{1,0:T(8,128)S(1)} %collective-permute-done.14.g4), channel_id=1, source_target_pairs={{0,3},{1,0},{2,1},{3,2},{4,7},{5,4},{6,5},{7,6},{8,11},{9,8},{10,9... | collective-permute-start | bytes 393224 | tf_op jit(solution)/shard_map/ppermute | solution.py:278
  96.6 3.8 %collective-permute-start.21 = (f32[16,128]{1,0:T(8,128)S(1)}, f32[16,128]{1,0:T(8,128)S(1)}, u32[]{:S(2)}, u32[]{:S(2)}) collective-permute-start(f32[16,128]{1,0:T(8,128)S(1)} %add_add_fusion.1.near), channel_id=1, source_target_pairs={{0,4},{1,5},{2,6},{3,7},{4,0},{5,1},{6,2},{7,3},{8,12},{9,13},{10,... | collective-permute-start | bytes 24584 | tf_op jit(solution)/shard_map/ppermute | solution.py:275
  103.0 2.0 %shard_map.176 = (f32[256,128]{1,0:T(8,128)S(1)}, f32[32,8,128]{2,1,0:T(8,128)S(1)}) custom-call(s32[1]{0:T(128)} %get-tuple-element.61.flag, s32[1]{0:T(128)} %get-tuple-element.64.flag.flag_far, s32[1]{0:T(128)} %bitcast.pos, s32[32,128]{1,0:T(8,128)S(1)} %get-tuple-element.57.rest_refs_0_.l0, s32[32,128]{1,0:T(8,128)S(1)} %collective-permute-done.rest_refs_1_.l1, ...), custom_call_target="tpu_custom_call" | custom-call | flops 268435456 | bytes 3244044 | tf_op jit(solution)/shard_map/pallas_call | solution.py:45
  106.4 9.7 %all-to-all-start.2 = ((f32[32,16,128]{2,1,0:T(8,128)}), f32[32,16,128]{2,1,0:T(8,128)S(1)}, u32[]{:S(2)}, u32[]{:S(2)}) async-start(f32[32,16,128]{2,1,0:T(8,128)} %get-tuple-element.92), calls=%async_computation.2 | async-start | bytes 524288 | tf_op jit(solution)/shard_map/all_to_all | solution.py:281
  118.1 9.0 %all-to-all-done.2.last = f32[32,16,128]{2,1,0:T(8,128)S(1)} async-done(((f32[32,16,128]{2,1,0:T(8,128)}), f32[32,16,128]{2,1,0:T(8,128)S(1)}, u32[]{:S(2)}, u32[]{:S(2)}) %all-to-all-start.2) | async-done | bytes 262176 | tf_op jit(solution)/shard_map/all_to_all | solution.py:281
  (93 shorter events, 23.0 us)
Async XLA Ops:
  0.7 25.0 %copy-start.16 = (s32[1,1,1024]{2,1,0:T(1,128)S(1)}, s32[1,1,1024]{2,1,0:T(1,128)}, u32[]{:S(2)}) copy-start(s32[1,1,1024]{2,1,0:T(1,128)} %param.22) | copy-start | bytes 12292
  0.7 25.0 %copy-start.14 = (s32[1,1,1024]{2,1,0:T(1,128)S(1)}, s32[1,1,1024]{2,1,0:T(1,128)}, u32[]{:S(2)}) copy-start(s32[1,1,1024]{2,1,0:T(1,128)} %param.21) | copy-start | bytes 12292
  3.0 29.7 %all-to-all-start = ((f32[32,40,128]{2,1,0:T(8,128)}), f32[32,40,128]{2,1,0:T(8,128)S(1)}, u32[]{:S(2)}, u32[]{:S(2)}) async-start(f32[32,40,128]{2,1,0:T(8,128)} %shard_map.164), calls=%async_computation | async-start | bytes 1310720 | tf_op jit(solution)/shard_map/all_to_all | solution.py:281
  14.0 3.9 %collective-permute-start = (s32[32,128]{1,0:T(8,128)S(1)}, s32[32,128]{1,0:T(8,128)S(1)}, u32[]{:S(2)}, u32[]{:S(2)}) collective-permute-start(s32[32,128]{1,0:T(8,128)S(1)} %get-tuple-element.58), channel_id=1, source_target_pairs={{0,3},{1,0},{2,1},{3,2},{4,7},{5,4},{6,5},{7,6},{8,11},{9,8},{10,9... | collective-permute-start | bytes 49160 | tf_op jit(solution)/shard_map/ppermute | solution.py:278
  16.8 4.4 %collective-permute-start.1 = (s32[32,128]{1,0:T(8,128)S(1)}, s32[32,128]{1,0:T(8,128)S(1)}, u32[]{:S(2)}, u32[]{:S(2)}) collective-permute-start(s32[32,128]{1,0:T(8,128)S(1)} %get-tuple-element.59), channel_id=1, source_target_pairs={{0,2},{1,3},{2,0},{3,1},{4,6},{5,7},{6,4},{7,5},{8,10},{9,11},{10,... | collective-permute-start | bytes 49160 | tf_op jit(solution)/shard_map/ppermute | solution.py:278
  17.2 4.2 %collective-permute-start.2 = (s32[32,128]{1,0:T(8,128)S(1)}, s32[32,128]{1,0:T(8,128)S(1)}, u32[]{:S(2)}, u32[]{:S(2)}) collective-permute-start(s32[32,128]{1,0:T(8,128)S(1)} %get-tuple-element.60), channel_id=1, source_target_pairs={{0,1},{1,2},{2,3},{3,0},{4,5},{5,6},{6,7},{7,4},{8,9},{9,10},{10,1... | collective-permute-start | bytes 49160 | tf_op jit(solution)/shard_map/ppermute | solution.py:278
  21.4 19.2 %copy-start.9 = (s32[32,128]{1,0:T(8,128)}, s32[32,128]{1,0:T(8,128)S(1)}, u32[]{:S(2)}) copy-start(s32[32,128]{1,0:T(8,128)S(1)} %collective-permute-done.2.rest_refs_3_.l3) | copy-start | bytes 49156
  21.4 8.1 %collective-permute-start.3 = (s32[64,128]{1,0:T(8,128)S(1)}, s32[64,128]{1,0:T(8,128)S(1)}, u32[]{:S(2)}, u32[]{:S(2)}) collective-permute-start(s32[64,128]{1,0:T(8,128)S(1)} %pad_add_fusion), channel_id=1, source_target_pairs={{0,4},{1,5},{2,6},{3,7},{4,0},{5,1},{6,2},{7,3},{8,12},{9,13},{10,... | collective-permute-start | bytes 98312 | tf_op jit(solution)/shard_map/ppermute | solution.py:275
  33.8 9.1 %collective-permute-start.4 = (f32[256,128]{1,0:T(8,128)S(1)}, f32[256,128]{1,0:T(8,128)S(1)}, u32[]{:S(2)}, u32[]{:S(2)}) collective-permute-start(f32[256,128]{1,0:T(8,128)S(1)} %get-tuple-element.67), channel_id=1, source_target_pairs={{0,1},{1,2},{2,3},{3,0},{4,5},{5,6},{6,7},{7,4},{8,9},{9,10},{10,1... | collective-permute-start | bytes 393224 | tf_op jit(solution)/shard_map/ppermute | solution.py:278
  35.9 7.7 %collective-permute-start.5 = (f32[256,128]{1,0:T(8,128)S(1)}, f32[256,128]{1,0:T(8,128)S(1)}, u32[]{:S(2)}, u32[]{:S(2)}) collective-permute-start(f32[256,128]{1,0:T(8,128)S(1)} %get-tuple-element.68), channel_id=1, source_target_pairs={{0,3},{1,0},{2,1},{3,2},{4,7},{5,4},{6,5},{7,6},{8,11},{9,8},{10,9... | collective-permute-start | bytes 393224 | tf_op jit(solution)/shard_map/ppermute | solution.py:278
  37.4 7.9 %collective-permute-start.6 = (f32[256,128]{1,0:T(8,128)S(1)}, f32[256,128]{1,0:T(8,128)S(1)}, u32[]{:S(2)}, u32[]{:S(2)}) collective-permute-start(f32[256,128]{1,0:T(8,128)S(1)} %get-tuple-element.69), channel_id=1, source_target_pairs={{0,2},{1,3},{2,0},{3,1},{4,6},{5,7},{6,4},{7,5},{8,10},{9,11},{10,... | collective-permute-start | bytes 393224 | tf_op jit(solution)/shard_map/ppermute | solution.py:278
  40.5 17.2 %copy-start.1 = (f32[128,128]{1,0:T(8,128)S(1)}, f32[128,128]{1,0:T(8,128)}, u32[]{:S(2)}) copy-start(f32[128,128]{1,0:T(8,128)} %w_root.3) | copy-start | bytes 196612
  40.5 17.2 %copy-start.2 = (f32[256,128]{1,0:T(8,128)S(1)}, f32[256,128]{1,0:T(8,128)}, u32[]{:S(2)}) copy-start(f32[256,128]{1,0:T(8,128)} %grad_out.1) | copy-start | bytes 393220
  40.5 17.1 %copy-start.12 = (f32[128,128]{1,0:T(8,128)S(1)}, f32[128,128]{1,0:T(8,128)}, u32[]{:S(2)}) copy-start(f32[128,128]{1,0:T(8,128)} %w_neigh.1) | copy-start | bytes 196612
  45.4 10.1 %collective-permute-start.7 = (f32[256,128]{1,0:T(8,128)S(1)}, f32[256,128]{1,0:T(8,128)S(1)}, u32[]{:S(2)}, u32[]{:S(2)}) collective-permute-start(f32[256,128]{1,0:T(8,128)S(1)} %add_add_fusion), channel_id=1, source_target_pairs={{0,4},{1,5},{2,6},{3,7},{4,0},{5,1},{6,2},{7,3},{8,12},{9,13},{10,... | collective-permute-start | bytes 393224 | tf_op jit(solution)/shard_map/ppermute | solution.py:275
  49.7 5.8 %collective-permute-start.8 = (f32[256,128]{1,0:T(8,128)S(1)}, f32[256,128]{1,0:T(8,128)S(1)}, u32[]{:S(2)}, u32[]{:S(2)}) collective-permute-start(f32[256,128]{1,0:T(8,128)S(1)} %get-tuple-element.76), channel_id=1, source_target_pairs={{0,1},{1,2},{2,3},{3,0},{4,5},{5,6},{6,7},{7,4},{8,9},{9,10},{10,1... | collective-permute-start | bytes 393224 | tf_op jit(solution)/shard_map/ppermute | solution.py:278
  50.3 5.2 %collective-permute-start.9 = (f32[256,128]{1,0:T(8,128)S(1)}, f32[256,128]{1,0:T(8,128)S(1)}, u32[]{:S(2)}, u32[]{:S(2)}) collective-permute-start(f32[256,128]{1,0:T(8,128)S(1)} %get-tuple-element.77), channel_id=1, source_target_pairs={{0,3},{1,0},{2,1},{3,2},{4,7},{5,4},{6,5},{7,6},{8,11},{9,8},{10,9... | collective-permute-start | bytes 393224 | tf_op jit(solution)/shard_map/ppermute | solution.py:278
  52.4 5.3 %collective-permute-start.10 = (f32[256,128]{1,0:T(8,128)S(1)}, f32[256,128]{1,0:T(8,128)S(1)}, u32[]{:S(2)}, u32[]{:S(2)}) collective-permute-start(f32[256,128]{1,0:T(8,128)S(1)} %get-tuple-element.78), channel_id=1, source_target_pairs={{0,2},{1,3},{2,0},{3,1},{4,6},{5,7},{6,4},{7,5},{8,10},{9,11},{10,... | collective-permute-start | bytes 393224 | tf_op jit(solution)/shard_map/ppermute | solution.py:278
  60.1 24.1 %all-to-all-start.1 = ((f32[32,16,128]{2,1,0:T(8,128)}), f32[32,16,128]{2,1,0:T(8,128)S(1)}, u32[]{:S(2)}, u32[]{:S(2)}) async-start(f32[32,16,128]{2,1,0:T(8,128)} %shard_map.173), calls=%async_computation.1 | async-start | bytes 524288 | tf_op jit(solution)/shard_map/all_to_all | solution.py:281
  67.5 10.0 %collective-permute-start.14 = (f32[256,128]{1,0:T(8,128)S(1)}, f32[256,128]{1,0:T(8,128)S(1)}, u32[]{:S(2)}, u32[]{:S(2)}) collective-permute-start(f32[256,128]{1,0:T(8,128)S(1)} %get-tuple-element.81.grad_sum.g0), channel_id=1, source_target_pairs={{0,4},{1,5},{2,6},{3,7},{4,0},{5,1},{6,2},{7,3},{8,12},{9,13},{10,... | collective-permute-start | bytes 393224 | tf_op jit(solution)/shard_map/ppermute | solution.py:275
  69.2 8.3 %collective-permute-start.13 = (f32[256,128]{1,0:T(8,128)S(1)}, f32[256,128]{1,0:T(8,128)S(1)}, u32[]{:S(2)}, u32[]{:S(2)}) collective-permute-start(f32[256,128]{1,0:T(8,128)S(1)} %get-tuple-element.81.grad_sum.g0), channel_id=1, source_target_pairs={{0,1},{1,2},{2,3},{3,0},{4,5},{5,6},{6,7},{7,4},{8,9},{9,10},{10,1... | collective-permute-start | bytes 393224 | tf_op jit(solution)/shard_map/ppermute | solution.py:278
  69.2 8.3 %collective-permute-start.12 = (f32[256,128]{1,0:T(8,128)S(1)}, f32[256,128]{1,0:T(8,128)S(1)}, u32[]{:S(2)}, u32[]{:S(2)}) collective-permute-start(f32[256,128]{1,0:T(8,128)S(1)} %get-tuple-element.81.grad_sum.g0), channel_id=1, source_target_pairs={{0,2},{1,3},{2,0},{3,1},{4,6},{5,7},{6,4},{7,5},{8,10},{9,11},{10,... | collective-permute-start | bytes 393224 | tf_op jit(solution)/shard_map/ppermute | solution.py:278
  71.2 6.9 %collective-permute-start.11 = (f32[256,128]{1,0:T(8,128)S(1)}, f32[256,128]{1,0:T(8,128)S(1)}, u32[]{:S(2)}, u32[]{:S(2)}) collective-permute-start(f32[256,128]{1,0:T(8,128)S(1)} %get-tuple-element.81.grad_sum.g0), channel_id=1, source_target_pairs={{0,3},{1,0},{2,1},{3,2},{4,7},{5,4},{6,5},{7,6},{8,11},{9,8},{10,9... | collective-permute-start | bytes 393224 | tf_op jit(solution)/shard_map/ppermute | solution.py:278
  84.2 22.2 %all-to-all-start.3 = ((f32[32,32,128]{2,1,0:T(8,128)}), f32[32,32,128]{2,1,0:T(8,128)S(1)}, u32[]{:S(2)}, u32[]{:S(2)}) async-start(f32[32,32,128]{2,1,0:T(8,128)} %bitcast.11), calls=%async_computation.3 | async-start | bytes 1048576 | tf_op jit(solution)/shard_map/all_to_all | solution.py:281
  89.4 5.2 %collective-permute-start.20 = (f32[16,128]{1,0:T(8,128)S(1)}, f32[16,128]{1,0:T(8,128)S(1)}, u32[]{:S(2)}, u32[]{:S(2)}) collective-permute-start(f32[16,128]{1,0:T(8,128)S(1)} %shard_map.177), channel_id=1, source_target_pairs={{0,3},{1,0},{2,1},{3,2},{4,7},{5,4},{6,5},{7,6},{8,11},{9,8},{10,9... | collective-permute-start | bytes 24584 | tf_op jit(solution)/shard_map/ppermute | solution.py:278
  90.3 6.3 %collective-permute-start.19 = (f32[16,128]{1,0:T(8,128)S(1)}, f32[16,128]{1,0:T(8,128)S(1)}, u32[]{:S(2)}, u32[]{:S(2)}) collective-permute-start(f32[16,128]{1,0:T(8,128)S(1)} %shard_map.177), channel_id=1, source_target_pairs={{0,2},{1,3},{2,0},{3,1},{4,6},{5,7},{6,4},{7,5},{8,10},{9,11},{10,... | collective-permute-start | bytes 24584 | tf_op jit(solution)/shard_map/ppermute | solution.py:278
  90.7 5.9 %collective-permute-start.18 = (f32[16,128]{1,0:T(8,128)S(1)}, f32[16,128]{1,0:T(8,128)S(1)}, u32[]{:S(2)}, u32[]{:S(2)}) collective-permute-start(f32[16,128]{1,0:T(8,128)S(1)} %shard_map.177), channel_id=1, source_target_pairs={{0,1},{1,2},{2,3},{3,0},{4,5},{5,6},{6,7},{7,4},{8,9},{9,10},{10,1... | collective-permute-start | bytes 24584 | tf_op jit(solution)/shard_map/ppermute | solution.py:278
  91.0 9.4 %collective-permute-start.17 = (f32[256,128]{1,0:T(8,128)S(1)}, f32[256,128]{1,0:T(8,128)S(1)}, u32[]{:S(2)}, u32[]{:S(2)}) collective-permute-start(f32[256,128]{1,0:T(8,128)S(1)} %collective-permute-done.14.g4), channel_id=1, source_target_pairs={{0,1},{1,2},{2,3},{3,0},{4,5},{5,6},{6,7},{7,4},{8,9},{9,10},{10,1... | collective-permute-start | bytes 393224 | tf_op jit(solution)/shard_map/ppermute | solution.py:278
  93.0 7.5 %collective-permute-start.16 = (f32[256,128]{1,0:T(8,128)S(1)}, f32[256,128]{1,0:T(8,128)S(1)}, u32[]{:S(2)}, u32[]{:S(2)}) collective-permute-start(f32[256,128]{1,0:T(8,128)S(1)} %collective-permute-done.14.g4), channel_id=1, source_target_pairs={{0,2},{1,3},{2,0},{3,1},{4,6},{5,7},{6,4},{7,5},{8,10},{9,11},{10,... | collective-permute-start | bytes 393224 | tf_op jit(solution)/shard_map/ppermute | solution.py:278
  94.6 5.8 %collective-permute-start.15 = (f32[256,128]{1,0:T(8,128)S(1)}, f32[256,128]{1,0:T(8,128)S(1)}, u32[]{:S(2)}, u32[]{:S(2)}) collective-permute-start(f32[256,128]{1,0:T(8,128)S(1)} %collective-permute-done.14.g4), channel_id=1, source_target_pairs={{0,3},{1,0},{2,1},{3,2},{4,7},{5,4},{6,5},{7,6},{8,11},{9,8},{10,9... | collective-permute-start | bytes 393224 | tf_op jit(solution)/shard_map/ppermute | solution.py:278
  96.6 9.0 %collective-permute-start.21 = (f32[16,128]{1,0:T(8,128)S(1)}, f32[16,128]{1,0:T(8,128)S(1)}, u32[]{:S(2)}, u32[]{:S(2)}) collective-permute-start(f32[16,128]{1,0:T(8,128)S(1)} %add_add_fusion.1.near), channel_id=1, source_target_pairs={{0,4},{1,5},{2,6},{3,7},{4,0},{5,1},{6,2},{7,3},{8,12},{9,13},{10,... | collective-permute-start | bytes 24584 | tf_op jit(solution)/shard_map/ppermute | solution.py:275
  106.4 20.8 %all-to-all-start.2 = ((f32[32,16,128]{2,1,0:T(8,128)}), f32[32,16,128]{2,1,0:T(8,128)S(1)}, u32[]{:S(2)}, u32[]{:S(2)}) async-start(f32[32,16,128]{2,1,0:T(8,128)} %get-tuple-element.92), calls=%async_computation.2 | async-start | bytes 524288 | tf_op jit(solution)/shard_map/all_to_all | solution.py:281
  (18 other events, 80.8 us)

commit v8 on v6

--- a/solution.py
+++ b/solution.py
@@ -203,10 +203,9 @@
         out[p, 8:16, :] = fill
 
 
-def k_slots(flag, halo_to, halo_from, grad_sum, h_bwd, grad_pre, w_root, out, root):
+def k_slots(flag, halo_to, halo_from, grad_sum, h_bwd, out):
     x = halves(grad_sum[...])
     out[...] = joined(dot(h_bwd[...], x))
-    root[...] = dot(grad_pre[...], w_root[...], NT, HIGH)
 
     @pl.when(flag[0] != 0)
     def _():
@@ -214,20 +213,30 @@
         out[...] += joined(dot(rest(dot(frm, to, NT)), x))
 
 
-def k_back(flag, pos, l0, l1, l2, l3, far, g0, g1, g2, g3, g4, g5, g6, g7, bwd, root, local, hubs, total):
-    xs = [halves(g[0:256, :]) for g in (g0, g1, g2, g3, g4, g5, g6, g7)]
-    acc = dot(bwd[0], xs[0])
-    for r in range(1, 8):
-        acc = acc + dot(bwd[r], xs[r])
-    total[...] = joined(acc)
-
-    @pl.when(flag[0] != 0)
+def back_sum(low, blocks, pos, grads, bwd, at, total):
+    xs = [halves(g[...]) for g in grads]
+    acc = dot(bwd[at], xs[0])
+    for r in range(1, 4):
+        acc = acc + dot(bwd[at + r], xs[r])
+    total[...] += joined(acc)
+
+    @pl.when(low)
     def _():
-        for r, block in enumerate(blocks_of((l0, l1, l2, l3, far))):
+        for r, block in enumerate(blocks()):
             total[...] += joined(dot(rest(backward_count(*hots(pos, block))), xs[r]))
 
+
+def k_back_near(flag, pos, l0, l1, l2, l3, g0, g1, g2, g3, bwd, total):
+    total[...] = jnp.zeros_like(total)
+    back_sum(flag[0] != 0, lambda: [ref[0:16, :] for ref in (l0, l1, l2, l3)], pos, (g0, g1, g2, g3), bwd, 0, total)
+
+
+def k_back(flag, pos, far, g4, g5, g6, g7, bwd, near, local, hubs, total):
+    total[...] = near[...]
+    blocks = lambda: [far[16 * k : 16 * k + 16, :] for k in range(4)]
+    back_sum(flag[0] != 0, blocks, pos, (g4, g5, g6, g7), bwd, 4, total)
     hubs[...] = total[256:512, :].reshape(32, 8, 128)
-    local[...] = root[...] + total[0:256, :]
+    local[...] = total[0:256, :]
 
 
 def k_sum(weights, out):
@@ -242,8 +251,9 @@
     bias[...] = w[8:9]
 
 
-def k_scatter(returned, send, local, out):
-    out[...] = local[...] + joined(dot(send_hot(send), halves(returned[...].reshape(1024, 128))))
+def k_scatter(returned, send, local, grad_pre, w_root, out):
+    root = dot(grad_pre[...], w_root[...], NT, HIGH)
+    out[...] = local[...] + root + joined(dot(send_hot(send), halves(returned[...].reshape(1024, 128))))
 
 
 def k_final(last, hub, local, out, w_neigh, w_root):
@@ -302,7 +312,7 @@
     other = part[4] + turn(part[5], 1) + turn(part[7], 3) + turn(part[6], 2)
     other, p1, p2, p3 = lax.optimization_barrier((other, part[1], part[2], part[3]))
     other = swap(other)
-    near = [turn(p1, 1), turn(p3, 3), turn(p2, 2)]
+    near = [turn(p2, 2), turn(p1, 1), turn(p3, 3)]
     own = call(k_halo, block, (h_flag, halo_to, halo_from, incoming, h_fwd, part[0]), [sm] + [vm] * 5)
     inv, bwd = lax.optimization_barrier((inv, bwd))
     output, grad_pre, grad_sum, mean = call(
@@ -311,19 +321,21 @@
     g4 = swap(grad_sum)
     g1, g3, g2 = turn(grad_sum, 3), turn(grad_sum, 1), turn(grad_sum, 2)
     weights = exchange(call(k_weights, shape((32, 16, 128)), (grad_pre, mean, features)), "grp")
-    slots, root = call(
-        k_slots, [shape((1024, 128)), block], (h_flag, halo_to, halo_from, grad_sum, h_bwd, grad_pre, w_root),
-        [sm] + [vm] * 6,
-    )
-    g4, weights, g1, g2, g3, slots = lax.optimization_barrier((g4, weights, g1, g2, g3, slots))
+    slots = call(k_slots, shape((1024, 128)), (h_flag, halo_to, halo_from, grad_sum, h_bwd), [sm] + [vm] * 4)
+    g4, g1, g2, g3 = lax.optimization_barrier((g4, g1, g2, g3))
+    back = call(
+        k_back_near, shape((512, 128)), (flag, *lists[:5], grad_sum, g1, g2, g3, bwd), [sm, *lm[:5]] + [vm] * 5
+    )
+    weights, back, slots = lax.optimization_barrier((weights, back, slots))
+    w = call(k_sum, shape((16, 128)), (weights,))
+    w, slots = lax.optimization_barrier((w, slots))
     returned = exchange(slots.reshape(32, 32, 128), "grp")
-    w = call(k_sum, shape((16, 128)), (weights,))
     w = w + turn(w, 1) + turn(w, 2) + turn(w, 3)
     w_far = swap(w)
     g5, g7, g6 = turn(g4, 3), turn(g4, 1), turn(g4, 2)
     local, hubs = call(
         k_back, [block, shape((32, 8, 128))],
-        (flag, *lists, grad_sum, g1, g2, g3, g4, g5, g6, g7, bwd, root), [sm, *lm] + [vm] * 10,
+        (flag, pos, far, g4, g5, g6, g7, bwd, back), [sm, sm] + [vm] * 7,
         [pltpu.VMEM((512, 128), F32)],
     )
     factor = (256 * lax.axis_size("grp") * lax.axis_size("blk")) ** (-0.5)
@@ -331,7 +343,7 @@
         functools.partial(k_pack, factor), [shape((32, 16, 128)), shape((1, 128))], (hubs, w, w_far)
     )
     last = exchange(last, "grp")
-    local = call(k_scatter, block, (returned, send, local))
+    local = call(k_scatter, block, (returned, send, local, grad_pre, w_root))
     grad_features, grad_wn, grad_wr = call(
         k_final, [block, shape((128, 128)), shape((128, 128))], (last, hub, local), [vm, sm, vm]
     )

time: 129 us -> 129 us (level)
  waiting for transfers between devices: 30.8 us -> 39.8 us
  starting transfers between devices: 69.4 us -> 63 us
  local copies, waits for them, and re-layouts: 6.71 us -> 2.94 us
  Pallas kernels: 20 us -> 21.6 us
    unnamed x44, local copies, waits for them, and re-layouts: 6.61 us -> 2.84 us
    all_to_all x4, starting transfers between devices: 33.3 us -> 30 us  [exchange(): return lax.all_to_all(v, axis, split_axis=0, concat_axis=0, tiled=True)]
    ppermute x18, waiting for transfers between devices: 13.2 us -> 16.5 us  [turn(): lax.ppermute(v, 'blk', [(i, i // 4 * 4 + (i % 4 + k) % 4) for i in range(...]
    all_to_all x4, waiting for transfers between devices: 12.5 us -> 15.5 us  [exchange(): return lax.all_to_all(v, axis, split_axis=0, concat_axis=0, tiled=True)]
    ppermute x4, waiting for transfers between devices: 5.15 us -> 7.83 us  [swap(): return lax.ppermute(v, 'blk', [(i, i ^ 4) for i in range(8)])]
    ppermute x18, starting transfers between devices: 21.1 us -> 19.1 us  [turn(): lax.ppermute(v, 'blk', [(i, i // 4 * 4 + (i % 4 + k) % 4) for i in range(...]
    pallas_call x15 -> x16, Pallas kernels: 20 us -> 21.6 us  [call(): pl.pallas_call(kernel, out_shape=out_shape, in_specs=[whole] * len(args)...]
  transfers between devices with their start and end apart: 26 -> 26, of which waited for: 12 -> 13; matrix products, arithmetic and copies ran while one was open for 0% -> 0% of each run, Pallas kernels for 10% -> 11%
where the time goes in v8:
time: 129 us; the launch traced here: 128 us
  starting transfers between devices  63 us (49%)
  waiting for transfers between devices  39.8 us (31%)
  Pallas kernels  21.6 us (17%)
  local copies, waits for them, and re-layouts  2.94 us (2%)
    all_to_all x4, starting transfers between devices, exchange(): return lax.all_to_all(v, axis, split_axis=0, concat_axis=0, tiled=True)  30 us
    pallas_call x16, Pallas kernels, call(): pl.pallas_call(kernel, out_shape=out_shape, in_specs=[whole] * len(args)...  21.6 us
    ppermute x18, starting transfers between devices, turn(): lax.ppermute(v, 'blk', [(i, i // 4 * 4 + (i % 4 + k) % 4) for i in range(...  19.1 us
    ppermute x18, waiting for transfers between devices, turn(): lax.ppermute(v, 'blk', [(i, i // 4 * 4 + (i % 4 + k) % 4) for i in range(...  16.5 us
    all_to_all x4, waiting for transfers between devices, exchange(): return lax.all_to_all(v, axis, split_axis=0, concat_axis=0, tiled=True)  15.5 us
    ppermute x4, starting transfers between devices, swap(): return lax.ppermute(v, 'blk', [(i, i ^ 4) for i in range(8)])  13.9 us
    ppermute x4, waiting for transfers between devices, swap(): return lax.ppermute(v, 'blk', [(i, i ^ 4) for i in range(8)])  7.83 us
    unnamed x44, local copies, waits for them, and re-layouts  2.84 us
  transfers between devices with their start and end apart: 26, of which 13 were waited for; matrix products, arithmetic and copies ran while one was open for 0% of the time, Pallas kernels for 11%

profile of v8, /device:TPU:1, one launch (start us, length us, event | category | flops | bytes accessed | tf_op | source)
XLA Modules:
  0.0 128.4 jit_solution(15945424130124775291)
XLA Ops:
  0.7 2.3 %shard_map.164 = f32[32,40,128]{2,1,0:T(8,128)} custom-call(f32[256,128]{1,0:T(8,128)} %features.5, s32[32,32]{1,0:T(8,128)} %bitcast.13, s32[1,8]{1,0:T(1,128)} %bitcast.26), custom_call_target="tpu_custom_call" | custom-call | flops 268435456 | bytes 135200 | tf_op jit(solution)/shard_map/pallas_call | solution.py:45
  3.0 10.0 %all-to-all-start = ((f32[32,40,128]{2,1,0:T(8,128)}), f32[32,40,128]{2,1,0:T(8,128)S(1)}, u32[]{:S(2)}, u32[]{:S(2)}) async-start(f32[32,40,128]{2,1,0:T(8,128)} %shard_map.164), calls=%async_computation | async-start | bytes 1310720 | tf_op jit(solution)/shard_map/all_to_all | solution.py:286
  14.0 2.8 %collective-permute-start = (s32[32,128]{1,0:T(8,128)S(1)}, s32[32,128]{1,0:T(8,128)S(1)}, u32[]{:S(2)}, u32[]{:S(2)}) collective-permute-start(s32[32,128]{1,0:T(8,128)S(1)} %get-tuple-element.58), channel_id=1, source_target_pairs={{0,3},{1,0},{2,1},{3,2},{4,7},{5,4},{6,5},{7,6},{8,11},{9,8},{10,9... | collective-permute-start | bytes 49160 | tf_op jit(solution)/shard_map/ppermute | solution.py:283
  17.8 3.3 %collective-permute-done.1.l2 = s32[32,128]{1,0:T(8,128)S(1)} collective-permute-done((s32[32,128]{1,0:T(8,128)S(1)}, s32[32,128]{1,0:T(8,128)S(1)}, u32[]{:S(2)}, u32[]{:S(2)}) %collective-permute-start.1) | collective-permute-done | bytes 16416 | tf_op jit(solution)/shard_map/ppermute | solution.py:283
  21.4 4.3 %collective-permute-start.3 = (s32[64,128]{1,0:T(8,128)S(1)}, s32[64,128]{1,0:T(8,128)S(1)}, u32[]{:S(2)}, u32[]{:S(2)}) collective-permute-start(s32[64,128]{1,0:T(8,128)S(1)} %pad_add_fusion), channel_id=1, source_target_pairs={{0,4},{1,5},{2,6},{3,7},{4,0},{5,1},{6,2},{7,3},{8,12},{9,13},{10,... | collective-permute-start | bytes 98312 | tf_op jit(solution)/shard_map/ppermute | solution.py:280
  25.7 3.8 %collective-permute-done.3.far = s32[64,128]{1,0:T(8,128)S(1)} collective-permute-done((s32[64,128]{1,0:T(8,128)S(1)}, s32[64,128]{1,0:T(8,128)S(1)}, u32[]{:S(2)}, u32[]{:S(2)}) %collective-permute-start.3) | collective-permute-done | bytes 32800 | tf_op jit(solution)/shard_map/ppermute | solution.py:280
  29.5 2.3 %shard_map.167 = (bf16[8,256,512]{2,1,0:T(8,128)(2,1)S(1)}, s32[1]{0:T(128)}) custom-call(s32[1]{0:T(128)} %bitcast.pos, s32[32,128]{1,0:T(8,128)S(1)} %get-tuple-element.57.l0, s32[32,128]{1,0:T(8,128)S(1)} %collective-permute-done.l1, s32[32,128]{1,0:T(8,128)S(1)} %collective-permute-done.1.l2, s32[32,128]{1,0:T(8,128)S(1)} %collective-permute-done.2.l3, ...), custom_call_target="tpu_custom_call" | custom-call | flops 2147483648 | bytes 98308 | tf_op jit(solution)/shard_map/pallas_call | solution.py:45
  32.7 1.4 %shard_map.168 = (f32[256,128]{1,0:T(8,128)S(1)}, f32[256,128]{1,0:T(8,128)S(1)}, f32[256,128]{1,0:T(8,128)S(1)}, f32[256,128]{1,0:T(8,128)S(1)}, f32[256,128]{1...) custom-call(s32[1]{0:T(128)} %get-tuple-element.61.flag, s32[1]{0:T(128)} %bitcast.pos, ...), custom_call_target="tpu_custom_call" | custom-call | flops 268435456 | bytes 2981896 | tf_op jit(solution)/shard_map/pallas_call | solution.py:45
  34.1 2.1 %collective-permute-start.4 = (f32[256,128]{1,0:T(8,128)S(1)}, f32[256,128]{1,0:T(8,128)S(1)}, u32[]{:S(2)}, u32[]{:S(2)}) collective-permute-start(f32[256,128]{1,0:T(8,128)S(1)} %get-tuple-element.65), channel_id=1, source_target_pairs={{0,1},{1,2},{2,3},{3,0},{4,5},{5,6},{6,7},{7,4},{8,9},{9,10},{10,1... | collective-permute-start | bytes 393224 | tf_op jit(solution)/shard_map/ppermute | solution.py:283
  36.2 1.5 %collective-permute-start.5 = (f32[256,128]{1,0:T(8,128)S(1)}, f32[256,128]{1,0:T(8,128)S(1)}, u32[]{:S(2)}, u32[]{:S(2)}) collective-permute-start(f32[256,128]{1,0:T(8,128)S(1)} %get-tuple-element.66), channel_id=1, source_target_pairs={{0,3},{1,0},{2,1},{3,2},{4,7},{5,4},{6,5},{7,6},{8,11},{9,8},{10,9... | collective-permute-start | bytes 393224 | tf_op jit(solution)/shard_map/ppermute | solution.py:283
  37.7 1.6 %collective-permute-start.6 = (f32[256,128]{1,0:T(8,128)S(1)}, f32[256,128]{1,0:T(8,128)S(1)}, u32[]{:S(2)}, u32[]{:S(2)}) collective-permute-start(f32[256,128]{1,0:T(8,128)S(1)} %get-tuple-element.67), channel_id=1, source_target_pairs={{0,2},{1,3},{2,0},{3,1},{4,6},{5,7},{6,4},{7,5},{8,10},{9,11},{10,... | collective-permute-start | bytes 393224 | tf_op jit(solution)/shard_map/ppermute | solution.py:283
  39.3 2.3 %shard_map.166 = (bf16[256,1024]{1,0:T(8,128)(2,1)S(1)}, bf16[1024,256]{1,0:T(8,128)(2,1)S(1)}, f32[256,128]{1,0:T(8,128)S(1)}, s32[1]{0:T(128)}) custom-call(s32[48,128]{1,0:T(8,128)S(1)} %get-tuple-element.53.own_to, s32[8,128]{1,0:T(8,128)S(1)} %bitcast.15, s32[8,128]{1,0:T(8,128)S(1)} %bitcast.18, s32[2,128]{1,0:T(2,128)S(1)} %bitcast.25), custom_call_target="tpu_custom_call" | custom-call | flops 2147483648 | bytes 33792 | tf_op jit(solution)/shard_map/pallas_call | solution.py:45
  41.7 4.0 %collective-permute-done.6 = f32[256,128]{1,0:T(8,128)S(1)} collective-permute-done((f32[256,128]{1,0:T(8,128)S(1)}, f32[256,128]{1,0:T(8,128)S(1)}, u32[]{:S(2)}, u32[]{:S(2)}) %collective-permute-start.6) | collective-permute-done | bytes 131104 | tf_op jit(solution)/shard_map/ppermute | solution.py:283
  47.0 4.0 %collective-permute-start.7 = (f32[256,128]{1,0:T(8,128)S(1)}, f32[256,128]{1,0:T(8,128)S(1)}, u32[]{:S(2)}, u32[]{:S(2)}) collective-permute-start(f32[256,128]{1,0:T(8,128)S(1)} %add_add_fusion), channel_id=1, source_target_pairs={{0,4},{1,5},{2,6},{3,7},{4,0},{5,1},{6,2},{7,3},{8,12},{9,13},{10,... | collective-permute-start | bytes 393224 | tf_op jit(solution)/shard_map/ppermute | solution.py:280
  51.1 1.4 %collective-permute-start.8 = (f32[256,128]{1,0:T(8,128)S(1)}, f32[256,128]{1,0:T(8,128)S(1)}, u32[]{:S(2)}, u32[]{:S(2)}) collective-permute-start(f32[256,128]{1,0:T(8,128)S(1)} %get-tuple-element.72), channel_id=1, source_target_pairs={{0,2},{1,3},{2,0},{3,1},{4,6},{5,7},{6,4},{7,5},{8,10},{9,11},{10,... | collective-permute-start | bytes 393224 | tf_op jit(solution)/shard_map/ppermute | solution.py:283
  52.4 1.6 %shard_map.170.bwd = bf16[8,512,256]{2,1,0:T(8,128)(2,1)S(1)} custom-call(s32[1]{0:T(128)} %bitcast.pos, s32[32,128]{1,0:T(8,128)S(1)} %get-tuple-element.57.l0, s32[32,128]{1,0:T(8,128)S(1)} %collective-permute-done.l1, s32[32,128]{1,0:T(8,128)S(1)} %collective-permute-done.1.l2, s32[32,128]{1,0:T(8,128)S(1)} %copy-done.6, ...), custom_call_target="tpu_custom_call" | custom-call | flops 2147483648 | bytes 98308 | tf_op jit(solution)/shard_map/pallas_call | solution.py:45
  55.0 1.7 %collective-permute-done.8.a2 = f32[256,128]{1,0:T(8,128)S(1)} collective-permute-done((f32[256,128]{1,0:T(8,128)S(1)}, f32[256,128]{1,0:T(8,128)S(1)}, u32[]{:S(2)}, u32[]{:S(2)}) %collective-permute-start.8) | collective-permute-done | bytes 131104 | tf_op jit(solution)/shard_map/ppermute | solution.py:283
  56.7 3.0 %collective-permute-done.9.a3 = f32[256,128]{1,0:T(8,128)S(1)} collective-permute-done((f32[256,128]{1,0:T(8,128)S(1)}, f32[256,128]{1,0:T(8,128)S(1)}, u32[]{:S(2)}, u32[]{:S(2)}) %collective-permute-start.9) | collective-permute-done | bytes 131104 | tf_op jit(solution)/shard_map/ppermute | solution.py:283
  62.7 6.0 %all-to-all-start.1 = ((f32[32,16,128]{2,1,0:T(8,128)}), f32[32,16,128]{2,1,0:T(8,128)S(1)}, u32[]{:S(2)}, u32[]{:S(2)}) async-start(f32[32,16,128]{2,1,0:T(8,128)} %shard_map.172), calls=%async_computation.1 | async-start | bytes 524288 | tf_op jit(solution)/shard_map/all_to_all | solution.py:286
  68.7 2.4 %collective-permute-start.11 = (f32[256,128]{1,0:T(8,128)S(1)}, f32[256,128]{1,0:T(8,128)}, u32[]{:S(2)}, u32[]{:S(2)}) collective-permute-start(f32[256,128]{1,0:T(8,128)S(1)} %get-tuple-element.78.g0.grad_sum), channel_id=1, source_target_pairs={{0,4},{1,5},{2,6},{3,7},{4,0},{5,1},{6,2},{7,3},{8,12},{9,13},{10,... | collective-permute-start | bytes 393224 | tf_op jit(solution)/shard_map/ppermute | solution.py:280
  74.0 2.0 %shard_map.174 = f32[1024,128]{1,0:T(8,128)} custom-call(s32[1]{0:T(128)} %get-tuple-element.54.flag, s32[8,128]{1,0:T(8,128)S(1)} %bitcast.17, s32[8,128]{1,0:T(8,128)S(1)} %bitcast.20, f32[256,128]{1,0:T(8,128)S(1)} %get-tuple-element.78.g0.grad_sum, bf16[1024,256]{1,0:T(8,128)(2,1)S(1)} %get-tuple-element.86.h_bwd), custom_call_target="tpu_custom_call" | custom-call | flops 268435456 | bytes 663556 | tf_op jit(solution)/shard_map/pallas_call | solution.py:45
  75.9 4.0 %collective-permute-done.11.g4 = f32[256,128]{1,0:T(8,128)} collective-permute-done((f32[256,128]{1,0:T(8,128)S(1)}, f32[256,128]{1,0:T(8,128)}, u32[]{:S(2)}, u32[]{:S(2)}) %collective-permute-start.11) | collective-permute-done | bytes 131104 | tf_op jit(solution)/shard_map/ppermute | solution.py:280
  82.8 2.6 %all-to-all-done.1.weights = f32[32,16,128]{2,1,0:T(8,128)S(1)} async-done(((f32[32,16,128]{2,1,0:T(8,128)}), f32[32,16,128]{2,1,0:T(8,128)S(1)}, u32[]{:S(2)}, u32[]{:S(2)}) %all-to-all-start.1) | async-done | bytes 262176 | tf_op jit(solution)/shard_map/all_to_all | solution.py:286
  85.4 6.6 %all-to-all-start.3 = ((f32[32,32,128]{2,1,0:T(8,128)}), f32[32,32,128]{2,1,0:T(8,128)S(1)}, u32[]{:S(2)}, u32[]{:S(2)}) async-start(f32[32,32,128]{2,1,0:T(8,128)} %bitcast.11), calls=%async_computation.3 | async-start | bytes 1048576 | tf_op jit(solution)/shard_map/all_to_all | solution.py:286
  92.1 1.5 %collective-permute-start.19 = (f32[16,128]{1,0:T(8,128)S(1)}, f32[16,128]{1,0:T(8,128)S(1)}, u32[]{:S(2)}, u32[]{:S(2)}) collective-permute-start(f32[16,128]{1,0:T(8,128)S(1)} %shard_map.176), channel_id=1, source_target_pairs={{0,2},{1,3},{2,0},{3,1},{4,6},{5,7},{6,4},{7,5},{8,10},{9,11},{10,... | collective-permute-start | bytes 24584 | tf_op jit(solution)/shard_map/ppermute | solution.py:283
  95.4 1.7 %collective-permute-start.16 = (f32[256,128]{1,0:T(8,128)}, f32[256,128]{1,0:T(8,128)S(1)}, u32[]{:S(2)}, u32[]{:S(2)}) collective-permute-start(f32[256,128]{1,0:T(8,128)} %collective-permute-done.11.g4), channel_id=1, source_target_pairs={{0,2},{1,3},{2,0},{3,1},{4,6},{5,7},{6,4},{7,5},{8,10},{9,11},{10,... | collective-permute-start | bytes 393224 | tf_op jit(solution)/shard_map/ppermute | solution.py:283
  98.0 3.1 %collective-permute-start.21 = (f32[16,128]{1,0:T(8,128)S(1)}, f32[16,128]{1,0:T(8,128)S(1)}, u32[]{:S(2)}, u32[]{:S(2)}) collective-permute-start(f32[16,128]{1,0:T(8,128)S(1)} %add_add_fusion.1.near), channel_id=1, source_target_pairs={{0,4},{1,5},{2,6},{3,7},{4,0},{5,1},{6,2},{7,3},{8,12},{9,13},{10,... | collective-permute-start | bytes 24584 | tf_op jit(solution)/shard_map/ppermute | solution.py:280
  101.2 3.3 %collective-permute-done.17.g7 = f32[256,128]{1,0:T(8,128)S(1)} collective-permute-done((f32[256,128]{1,0:T(8,128)}, f32[256,128]{1,0:T(8,128)S(1)}, u32[]{:S(2)}, u32[]{:S(2)}) %collective-permute-start.17) | collective-permute-done | bytes 131104 | tf_op jit(solution)/shard_map/ppermute | solution.py:283
  104.4 2.0 %shard_map.175 = (f32[256,128]{1,0:T(8,128)S(1)}, f32[32,8,128]{2,1,0:T(8,128)S(1)}) custom-call(s32[1]{0:T(128)} %get-tuple-element.61.flag, s32[1]{0:T(128)} %bitcast.pos, s32[64,128]{1,0:T(8,128)S(1)} %collective-permute-done.3.far, f32[256,128]{1,0:T(8,128)} %collective-permute-done.11.g4, f32[256,128]{1,0:T(8,128)S(1)} %collective-permute-done.15.g5, ...), custom_call_target="tpu_custom_call" | custom-call | flops 268435456 | bytes 2916360 | tf_op jit(solution)/shard_map/pallas_call | solution.py:45
  107.2 1.4 %all-to-all-done.3.returned = f32[32,32,128]{2,1,0:T(8,128)S(1)} async-done(((f32[32,32,128]{2,1,0:T(8,128)}), f32[32,32,128]{2,1,0:T(8,128)S(1)}, u32[]{:S(2)}, u32[]{:S(2)}) %all-to-all-start.3) | async-done | bytes 524320 | tf_op jit(solution)/shard_map/all_to_all | solution.py:286
  108.6 7.5 %all-to-all-start.2 = ((f32[32,16,128]{2,1,0:T(8,128)}), f32[32,16,128]{2,1,0:T(8,128)S(1)}, u32[]{:S(2)}, u32[]{:S(2)}) async-start(f32[32,16,128]{2,1,0:T(8,128)} %get-tuple-element.92), calls=%async_computation.2 | async-start | bytes 524288 | tf_op jit(solution)/shard_map/all_to_all | solution.py:286
  116.5 10.7 %all-to-all-done.2.last = f32[32,16,128]{2,1,0:T(8,128)S(1)} async-done(((f32[32,16,128]{2,1,0:T(8,128)}), f32[32,16,128]{2,1,0:T(8,128)S(1)}, u32[]{:S(2)}, u32[]{:S(2)}) %all-to-all-start.2) | async-done | bytes 262176 | tf_op jit(solution)/shard_map/all_to_all | solution.py:286
  (88 shorter events, 19.3 us)
Async XLA Ops:
  3.0 29.7 %all-to-all-start = ((f32[32,40,128]{2,1,0:T(8,128)}), f32[32,40,128]{2,1,0:T(8,128)S(1)}, u32[]{:S(2)}, u32[]{:S(2)}) async-start(f32[32,40,128]{2,1,0:T(8,128)} %shard_map.164), calls=%async_computation | async-start | bytes 1310720 | tf_op jit(solution)/shard_map/all_to_all | solution.py:286
  14.0 3.9 %collective-permute-start = (s32[32,128]{1,0:T(8,128)S(1)}, s32[32,128]{1,0:T(8,128)S(1)}, u32[]{:S(2)}, u32[]{:S(2)}) collective-permute-start(s32[32,128]{1,0:T(8,128)S(1)} %get-tuple-element.58), channel_id=1, source_target_pairs={{0,3},{1,0},{2,1},{3,2},{4,7},{5,4},{6,5},{7,6},{8,11},{9,8},{10,9... | collective-permute-start | bytes 49160 | tf_op jit(solution)/shard_map/ppermute | solution.py:283
  16.8 4.4 %collective-permute-start.1 = (s32[32,128]{1,0:T(8,128)S(1)}, s32[32,128]{1,0:T(8,128)S(1)}, u32[]{:S(2)}, u32[]{:S(2)}) collective-permute-start(s32[32,128]{1,0:T(8,128)S(1)} %get-tuple-element.59), channel_id=1, source_target_pairs={{0,2},{1,3},{2,0},{3,1},{4,6},{5,7},{6,4},{7,5},{8,10},{9,11},{10,... | collective-permute-start | bytes 49160 | tf_op jit(solution)/shard_map/ppermute | solution.py:283
  17.1 4.2 %collective-permute-start.2 = (s32[32,128]{1,0:T(8,128)S(1)}, s32[32,128]{1,0:T(8,128)S(1)}, u32[]{:S(2)}, u32[]{:S(2)}) collective-permute-start(s32[32,128]{1,0:T(8,128)S(1)} %get-tuple-element.60), channel_id=1, source_target_pairs={{0,1},{1,2},{2,3},{3,0},{4,5},{5,6},{6,7},{7,4},{8,9},{9,10},{10,1... | collective-permute-start | bytes 49160 | tf_op jit(solution)/shard_map/ppermute | solution.py:283
  21.4 8.1 %collective-permute-start.3 = (s32[64,128]{1,0:T(8,128)S(1)}, s32[64,128]{1,0:T(8,128)S(1)}, u32[]{:S(2)}, u32[]{:S(2)}) collective-permute-start(s32[64,128]{1,0:T(8,128)S(1)} %pad_add_fusion), channel_id=1, source_target_pairs={{0,4},{1,5},{2,6},{3,7},{4,0},{5,1},{6,2},{7,3},{8,12},{9,13},{10,... | collective-permute-start | bytes 98312 | tf_op jit(solution)/shard_map/ppermute | solution.py:280
  34.1 7.5 %collective-permute-start.4 = (f32[256,128]{1,0:T(8,128)S(1)}, f32[256,128]{1,0:T(8,128)S(1)}, u32[]{:S(2)}, u32[]{:S(2)}) collective-permute-start(f32[256,128]{1,0:T(8,128)S(1)} %get-tuple-element.65), channel_id=1, source_target_pairs={{0,1},{1,2},{2,3},{3,0},{4,5},{5,6},{6,7},{7,4},{8,9},{9,10},{10,1... | collective-permute-start | bytes 393224 | tf_op jit(solution)/shard_map/ppermute | solution.py:283
  36.2 5.5 %collective-permute-start.5 = (f32[256,128]{1,0:T(8,128)S(1)}, f32[256,128]{1,0:T(8,128)S(1)}, u32[]{:S(2)}, u32[]{:S(2)}) collective-permute-start(f32[256,128]{1,0:T(8,128)S(1)} %get-tuple-element.66), channel_id=1, source_target_pairs={{0,3},{1,0},{2,1},{3,2},{4,7},{5,4},{6,5},{7,6},{8,11},{9,8},{10,9... | collective-permute-start | bytes 393224 | tf_op jit(solution)/shard_map/ppermute | solution.py:283
  37.7 7.9 %collective-permute-start.6 = (f32[256,128]{1,0:T(8,128)S(1)}, f32[256,128]{1,0:T(8,128)S(1)}, u32[]{:S(2)}, u32[]{:S(2)}) collective-permute-start(f32[256,128]{1,0:T(8,128)S(1)} %get-tuple-element.67), channel_id=1, source_target_pairs={{0,2},{1,3},{2,0},{3,1},{4,6},{5,7},{6,4},{7,5},{8,10},{9,11},{10,... | collective-permute-start | bytes 393224 | tf_op jit(solution)/shard_map/ppermute | solution.py:283
  45.7 14.0 %copy-start.1 = (f32[128,128]{1,0:T(8,128)S(1)}, f32[128,128]{1,0:T(8,128)}, u32[]{:S(2)}) copy-start(f32[128,128]{1,0:T(8,128)} %w_root.3) | copy-start | bytes 196612
  45.7 14.0 %copy-start.2 = (f32[256,128]{1,0:T(8,128)S(1)}, f32[256,128]{1,0:T(8,128)}, u32[]{:S(2)}) copy-start(f32[256,128]{1,0:T(8,128)} %grad_out.1) | copy-start | bytes 393220
  45.7 14.0 %copy-start.8 = (f32[128,128]{1,0:T(8,128)S(1)}, f32[128,128]{1,0:T(8,128)}, u32[]{:S(2)}) copy-start(f32[128,128]{1,0:T(8,128)} %w_neigh.1) | copy-start | bytes 196612
  45.7 9.2 %collective-permute-start.10 = (f32[256,128]{1,0:T(8,128)S(1)}, f32[256,128]{1,0:T(8,128)S(1)}, u32[]{:S(2)}, u32[]{:S(2)}) collective-permute-start(f32[256,128]{1,0:T(8,128)S(1)} %get-tuple-element.74), channel_id=1, source_target_pairs={{0,3},{1,0},{2,1},{3,2},{4,7},{5,4},{6,5},{7,6},{8,11},{9,8},{10,9... | collective-permute-start | bytes 393224 | tf_op jit(solution)/shard_map/ppermute | solution.py:283
  47.0 8.0 %collective-permute-start.7 = (f32[256,128]{1,0:T(8,128)S(1)}, f32[256,128]{1,0:T(8,128)S(1)}, u32[]{:S(2)}, u32[]{:S(2)}) collective-permute-start(f32[256,128]{1,0:T(8,128)S(1)} %add_add_fusion), channel_id=1, source_target_pairs={{0,4},{1,5},{2,6},{3,7},{4,0},{5,1},{6,2},{7,3},{8,12},{9,13},{10,... | collective-permute-start | bytes 393224 | tf_op jit(solution)/shard_map/ppermute | solution.py:280
  51.1 5.6 %collective-permute-start.8 = (f32[256,128]{1,0:T(8,128)S(1)}, f32[256,128]{1,0:T(8,128)S(1)}, u32[]{:S(2)}, u32[]{:S(2)}) collective-permute-start(f32[256,128]{1,0:T(8,128)S(1)} %get-tuple-element.72), channel_id=1, source_target_pairs={{0,2},{1,3},{2,0},{3,1},{4,6},{5,7},{6,4},{7,5},{8,10},{9,11},{10,... | collective-permute-start | bytes 393224 | tf_op jit(solution)/shard_map/ppermute | solution.py:283
  52.4 7.2 %collective-permute-start.9 = (f32[256,128]{1,0:T(8,128)S(1)}, f32[256,128]{1,0:T(8,128)S(1)}, u32[]{:S(2)}, u32[]{:S(2)}) collective-permute-start(f32[256,128]{1,0:T(8,128)S(1)} %get-tuple-element.73), channel_id=1, source_target_pairs={{0,1},{1,2},{2,3},{3,0},{4,5},{5,6},{6,7},{7,4},{8,9},{9,10},{10,1... | collective-permute-start | bytes 393224 | tf_op jit(solution)/shard_map/ppermute | solution.py:283
  62.7 22.7 %all-to-all-start.1 = ((f32[32,16,128]{2,1,0:T(8,128)}), f32[32,16,128]{2,1,0:T(8,128)S(1)}, u32[]{:S(2)}, u32[]{:S(2)}) async-start(f32[32,16,128]{2,1,0:T(8,128)} %shard_map.172), calls=%async_computation.1 | async-start | bytes 524288 | tf_op jit(solution)/shard_map/all_to_all | solution.py:286
  68.7 11.3 %collective-permute-start.11 = (f32[256,128]{1,0:T(8,128)S(1)}, f32[256,128]{1,0:T(8,128)}, u32[]{:S(2)}, u32[]{:S(2)}) collective-permute-start(f32[256,128]{1,0:T(8,128)S(1)} %get-tuple-element.78.g0.grad_sum), channel_id=1, source_target_pairs={{0,4},{1,5},{2,6},{3,7},{4,0},{5,1},{6,2},{7,3},{8,12},{9,13},{10,... | collective-permute-start | bytes 393224 | tf_op jit(solution)/shard_map/ppermute | solution.py:280
  71.1 8.8 %collective-permute-start.12 = (f32[256,128]{1,0:T(8,128)S(1)}, f32[256,128]{1,0:T(8,128)S(1)}, u32[]{:S(2)}, u32[]{:S(2)}) collective-permute-start(f32[256,128]{1,0:T(8,128)S(1)} %get-tuple-element.78.g0.grad_sum), channel_id=1, source_target_pairs={{0,3},{1,0},{2,1},{3,2},{4,7},{5,4},{6,5},{7,6},{8,11},{9,8},{10,9... | collective-permute-start | bytes 393224 | tf_op jit(solution)/shard_map/ppermute | solution.py:283
  71.4 8.6 %collective-permute-start.13 = (f32[256,128]{1,0:T(8,128)S(1)}, f32[256,128]{1,0:T(8,128)S(1)}, u32[]{:S(2)}, u32[]{:S(2)}) collective-permute-start(f32[256,128]{1,0:T(8,128)S(1)} %get-tuple-element.78.g0.grad_sum), channel_id=1, source_target_pairs={{0,2},{1,3},{2,0},{3,1},{4,6},{5,7},{6,4},{7,5},{8,10},{9,11},{10,... | collective-permute-start | bytes 393224 | tf_op jit(solution)/shard_map/ppermute | solution.py:283
  72.4 8.5 %collective-permute-start.14 = (f32[256,128]{1,0:T(8,128)S(1)}, f32[256,128]{1,0:T(8,128)S(1)}, u32[]{:S(2)}, u32[]{:S(2)}) collective-permute-start(f32[256,128]{1,0:T(8,128)S(1)} %get-tuple-element.78.g0.grad_sum), channel_id=1, source_target_pairs={{0,1},{1,2},{2,3},{3,0},{4,5},{5,6},{6,7},{7,4},{8,9},{9,10},{10,1... | collective-permute-start | bytes 393224 | tf_op jit(solution)/shard_map/ppermute | solution.py:283
  85.4 23.1 %all-to-all-start.3 = ((f32[32,32,128]{2,1,0:T(8,128)}), f32[32,32,128]{2,1,0:T(8,128)S(1)}, u32[]{:S(2)}, u32[]{:S(2)}) async-start(f32[32,32,128]{2,1,0:T(8,128)} %bitcast.11), calls=%async_computation.3 | async-start | bytes 1048576 | tf_op jit(solution)/shard_map/all_to_all | solution.py:286
  92.0 5.2 %collective-permute-start.18 = (f32[16,128]{1,0:T(8,128)S(1)}, f32[16,128]{1,0:T(8,128)S(1)}, u32[]{:S(2)}, u32[]{:S(2)}) collective-permute-start(f32[16,128]{1,0:T(8,128)S(1)} %shard_map.176), channel_id=1, source_target_pairs={{0,1},{1,2},{2,3},{3,0},{4,5},{5,6},{6,7},{7,4},{8,9},{9,10},{10,1... | collective-permute-start | bytes 24584 | tf_op jit(solution)/shard_map/ppermute | solution.py:283
  92.1 5.9 %collective-permute-start.19 = (f32[16,128]{1,0:T(8,128)S(1)}, f32[16,128]{1,0:T(8,128)S(1)}, u32[]{:S(2)}, u32[]{:S(2)}) collective-permute-start(f32[16,128]{1,0:T(8,128)S(1)} %shard_map.176), channel_id=1, source_target_pairs={{0,2},{1,3},{2,0},{3,1},{4,6},{5,7},{6,4},{7,5},{8,10},{9,11},{10,... | collective-permute-start | bytes 24584 | tf_op jit(solution)/shard_map/ppermute | solution.py:283
  93.5 4.4 %collective-permute-start.20 = (f32[16,128]{1,0:T(8,128)S(1)}, f32[16,128]{1,0:T(8,128)S(1)}, u32[]{:S(2)}, u32[]{:S(2)}) collective-permute-start(f32[16,128]{1,0:T(8,128)S(1)} %shard_map.176), channel_id=1, source_target_pairs={{0,3},{1,0},{2,1},{3,2},{4,7},{5,4},{6,5},{7,6},{8,11},{9,8},{10,9... | collective-permute-start | bytes 24584 | tf_op jit(solution)/shard_map/ppermute | solution.py:283
  94.8 6.4 %collective-permute-start.15 = (f32[256,128]{1,0:T(8,128)}, f32[256,128]{1,0:T(8,128)S(1)}, u32[]{:S(2)}, u32[]{:S(2)}) collective-permute-start(f32[256,128]{1,0:T(8,128)} %collective-permute-done.11.g4), channel_id=1, source_target_pairs={{0,3},{1,0},{2,1},{3,2},{4,7},{5,4},{6,5},{7,6},{8,11},{9,8},{10,9... | collective-permute-start | bytes 393224 | tf_op jit(solution)/shard_map/ppermute | solution.py:283
  95.4 5.7 %collective-permute-start.16 = (f32[256,128]{1,0:T(8,128)}, f32[256,128]{1,0:T(8,128)S(1)}, u32[]{:S(2)}, u32[]{:S(2)}) collective-permute-start(f32[256,128]{1,0:T(8,128)} %collective-permute-done.11.g4), channel_id=1, source_target_pairs={{0,2},{1,3},{2,0},{3,1},{4,6},{5,7},{6,4},{7,5},{8,10},{9,11},{10,... | collective-permute-start | bytes 393224 | tf_op jit(solution)/shard_map/ppermute | solution.py:283
  97.2 7.3 %collective-permute-start.17 = (f32[256,128]{1,0:T(8,128)}, f32[256,128]{1,0:T(8,128)S(1)}, u32[]{:S(2)}, u32[]{:S(2)}) collective-permute-start(f32[256,128]{1,0:T(8,128)} %collective-permute-done.11.g4), channel_id=1, source_target_pairs={{0,1},{1,2},{2,3},{3,0},{4,5},{5,6},{6,7},{7,4},{8,9},{9,10},{10,1... | collective-permute-start | bytes 393224 | tf_op jit(solution)/shard_map/ppermute | solution.py:283
  98.0 18.1 %copy-start.4 = (f32[256,128]{1,0:T(8,128)S(1)}, f32[256,128]{1,0:T(8,128)}, u32[]{:S(2)}) copy-start(f32[256,128]{1,0:T(8,128)} %copy-done.3) | copy-start | bytes 393220
  98.0 18.1 %copy-start.9 = (s32[1,1,32,32]{3,2,1,0:T(8,128)S(1)}, s32[1,1,32,32]{3,2,1,0:T(8,128)}, u32[]{:S(2)}) copy-start(s32[1,1,32,32]{3,2,1,0:T(8,128)} %param.20) | copy-start | bytes 12292
  98.0 29.1 %copy-start.20 = (s32[1,1,8]{2,1,0:T(1,128)S(1)}, s32[1,1,8]{2,1,0:T(1,128)}, u32[]{:S(2)}) copy-start(s32[1,1,8]{2,1,0:T(1,128)} %param.23) | copy-start | bytes 100
  98.0 8.5 %collective-permute-start.21 = (f32[16,128]{1,0:T(8,128)S(1)}, f32[16,128]{1,0:T(8,128)S(1)}, u32[]{:S(2)}, u32[]{:S(2)}) collective-permute-start(f32[16,128]{1,0:T(8,128)S(1)} %add_add_fusion.1.near), channel_id=1, source_target_pairs={{0,4},{1,5},{2,6},{3,7},{4,0},{5,1},{6,2},{7,3},{8,12},{9,13},{10,... | collective-permute-start | bytes 24584 | tf_op jit(solution)/shard_map/ppermute | solution.py:280
  108.6 18.6 %all-to-all-start.2 = ((f32[32,16,128]{2,1,0:T(8,128)}), f32[32,16,128]{2,1,0:T(8,128)S(1)}, u32[]{:S(2)}, u32[]{:S(2)}) async-start(f32[32,16,128]{2,1,0:T(8,128)} %get-tuple-element.92), calls=%async_computation.2 | async-start | bytes 524288 | tf_op jit(solution)/shard_map/all_to_all | solution.py:286
  (16 other events, 134.0 us)

commit v9 on v6

--- a/solution.py
+++ b/solution.py
@@ -194,19 +194,45 @@
     grad_sum[...] = dot(g, w_neigh[...], NT, HIGH) * scale
 
 
-def k_weights(grad_pre, mean, features, out):
+def spot(n):
+    return pl.ds(pl.multiple_of(n * 8, 8), 8)
+
+
+def k_weights(here, grad_pre, mean, features, own, other, held):
+    c = here[0] % 2
     g = grad_pre[...]
-    out[0:16, 0:8, :] = dot(mean[...], g, TN, HIGH).reshape(16, 8, 128)
-    out[16:32, 0:8, :] = dot(features[...], g, TN, HIGH).reshape(16, 8, 128)
+    held[0:128, :] = dot(mean[...], g, TN, HIGH)
+    held[128:256, :] = dot(features[...], g, TN, HIGH)
     fill = jnp.broadcast_to(jnp.sum(g, axis=0, keepdims=True), (8, 128))
-    for p in range(32):
-        out[p, 8:16, :] = fill
-
-
-def k_slots(flag, halo_to, halo_from, grad_sum, h_bwd, grad_pre, w_root, out, root):
+    for d, out in enumerate((own, other)):
+        for n in range(16):
+            out[n * 8 : n * 8 + 8, :] = held[spot(n * 2 + jnp.bitwise_xor(c, d)), :]
+        out[128:136, :] = fill
+
+
+def k_over_core(here, a, b, o0, o1, o2, o3, held):
+    x = here[0] // 2 % 4
+    held[...] = a[...] + b[...]
+    for k, out in enumerate((o0, o1, o2, o3)):
+        for n in range(4):
+            out[n * 8 : n * 8 + 8, :] = held[spot(n * 4 + (x + k) % 4), :]
+        out[32:40, :] = held[128:136, :]
+
+
+def k_over_x(here, a, b, c, d, o0, o1, o2, o3, held):
+    held[...] = a[...] + b[...] + c[...] + d[...]
+    for m, out in enumerate((o0, o1, o2, o3)):
+        out[0:8, :] = held[spot(jnp.bitwise_xor(here[0] // 8, m)), :]
+        out[8:16, :] = held[32:40, :]
+
+
+def k_sum(a, b, c, d, out):
+    out[...] = a[...] + b[...] + c[...] + d[...]
+
+
+def k_slots(flag, halo_to, halo_from, grad_sum, h_bwd, out):
     x = halves(grad_sum[...])
     out[...] = joined(dot(h_bwd[...], x))
-    root[...] = dot(grad_pre[...], w_root[...], NT, HIGH)
 
     @pl.when(flag[0] != 0)
     def _():
@@ -214,7 +240,7 @@
         out[...] += joined(dot(rest(dot(frm, to, NT)), x))
 
 
-def k_back(flag, pos, l0, l1, l2, l3, far, g0, g1, g2, g3, g4, g5, g6, g7, bwd, root, local, hubs, total):
+def k_back(flag, pos, l0, l1, l2, l3, far, g0, g1, g2, g3, g4, g5, g6, g7, bwd, local, hubs, total):
     xs = [halves(g[0:256, :]) for g in (g0, g1, g2, g3, g4, g5, g6, g7)]
     acc = dot(bwd[0], xs[0])
     for r in range(1, 8):
@@ -227,11 +253,7 @@
             total[...] += joined(dot(rest(backward_count(*hots(pos, block))), xs[r]))
 
     hubs[...] = total[256:512, :].reshape(32, 8, 128)
-    local[...] = root[...] + total[0:256, :]
-
-
-def k_sum(weights, out):
-    out[...] = jnp.sum(weights[...], axis=0)
+    local[...] = total[0:256, :]
 
 
 def k_pack(factor, hubs, near, far, out, bias):
@@ -242,8 +264,9 @@
     bias[...] = w[8:9]
 
 
-def k_scatter(returned, send, local, out):
-    out[...] = local[...] + joined(dot(send_hot(send), halves(returned[...].reshape(1024, 128))))
+def k_scatter(returned, send, local, grad_pre, w_root, out):
+    root = dot(grad_pre[...], w_root[...], NT, HIGH)
+    out[...] = local[...] + root + joined(dot(send_hot(send), halves(returned[...].reshape(1024, 128))))
 
 
 def k_final(last, hub, local, out, w_neigh, w_root):
@@ -310,20 +333,31 @@
     )
     g4 = swap(grad_sum)
     g1, g3, g2 = turn(grad_sum, 3), turn(grad_sum, 1), turn(grad_sum, 2)
-    weights = exchange(call(k_weights, shape((32, 16, 128)), (grad_pre, mean, features)), "grp")
-    slots, root = call(
-        k_slots, [shape((1024, 128)), block], (h_flag, halo_to, halo_from, grad_sum, h_bwd, grad_pre, w_root),
-        [sm] + [vm] * 6,
-    )
-    g4, weights, g1, g2, g3, slots = lax.optimization_barrier((g4, weights, g1, g2, g3, slots))
+    slots = call(k_slots, shape((1024, 128)), (h_flag, halo_to, halo_from, grad_sum, h_bwd), [sm] + [vm] * 4)
     returned = exchange(slots.reshape(32, 32, 128), "grp")
-    w = call(k_sum, shape((16, 128)), (weights,))
-    w = w + turn(w, 1) + turn(w, 2) + turn(w, 3)
+    here = lax.axis_index("grp").astype(I32).reshape(1)
+
+    def move(v, to):
+        return lax.ppermute(v, "grp", [(i, to(i)) for i in range(32)])
+
+    mine, others = call(
+        k_weights, [shape((136, 128))] * 2, (here, grad_pre, mean, features), [sm, vm, vm, vm], [pltpu.VMEM((256, 128), F32)]
+    )
+    cut = call(
+        k_over_core, [shape((40, 128))] * 4, (here, mine, move(others, lambda i: i ^ 1)), [sm, vm, vm],
+        [pltpu.VMEM((136, 128), F32)],
+    )
+    spun = [move(cut[k], lambda i: i // 8 * 8 + (i % 8 + 2 * k) % 8) for k in (1, 2, 3)]
+    cut = call(
+        k_over_x, [shape((16, 128))] * 4, (here, cut[0], *spun), [sm] + [vm] * 4, [pltpu.VMEM((40, 128), F32)]
+    )
+    w = call(k_sum, shape((16, 128)), (cut[0], *[move(cut[m], lambda i: i ^ (8 * m)) for m in (1, 2, 3)]))
+    w = call(k_sum, shape((16, 128)), (w, turn(w, 1), turn(w, 2), turn(w, 3)))
     w_far = swap(w)
     g5, g7, g6 = turn(g4, 3), turn(g4, 1), turn(g4, 2)
     local, hubs = call(
         k_back, [block, shape((32, 8, 128))],
-        (flag, *lists, grad_sum, g1, g2, g3, g4, g5, g6, g7, bwd, root), [sm, *lm] + [vm] * 10,
+        (flag, *lists, grad_sum, g1, g2, g3, g4, g5, g6, g7, bwd), [sm, *lm] + [vm] * 9,
         [pltpu.VMEM((512, 128), F32)],
     )
     factor = (256 * lax.axis_size("grp") * lax.axis_size("blk")) ** (-0.5)
@@ -331,7 +365,7 @@
         functools.partial(k_pack, factor), [shape((32, 16, 128)), shape((1, 128))], (hubs, w, w_far)
     )
     last = exchange(last, "grp")
-    local = call(k_scatter, block, (returned, send, local))
+    local = call(k_scatter, block, (returned, send, local, grad_pre, w_root))
     grad_features, grad_wn, grad_wr = call(
         k_final, [block, shape((128, 128)), shape((128, 128))], (last, hub, local), [vm, sm, vm]
     )

time: 129 us -> 129 us (level)
  local copies, waits for them, and re-layouts: 6.71 us -> 0.17 us
  starting transfers between devices: 69.4 us -> 74.5 us
  waiting for transfers between devices: 30.8 us -> 34.3 us
    ppermute x0 -> x7, starting transfers between devices: none -> 9.34 us  [move(): return lax.ppermute(v, 'grp', [(i, to(i)) for i in range(32)])]
    unnamed x44 -> x26, local copies, waits for them, and re-layouts: 6.61 us -> 0.07 us
    ppermute x0 -> x7, waiting for transfers between devices: none -> 5.85 us  [move(): return lax.ppermute(v, 'grp', [(i, to(i)) for i in range(32)])]
    all_to_all x4 -> x3, starting transfers between devices: 33.3 us -> 27.6 us  [exchange(): return lax.all_to_all(v, axis, split_axis=0, concat_axis=0, tiled=True)]
    ppermute x18, starting transfers between devices: 21.1 us -> 22.7 us  [turn(): lax.ppermute(v, 'blk', [(i, i // 4 * 4 + (i % 4 + k) % 4) for i in range(...]
    pallas_call x15 -> x18, Pallas kernels: 20 us -> 18.9 us  [call(): pl.pallas_call(kernel, out_shape=out_shape, in_specs=[whole] * len(args)...]
    all_to_all x4 -> x3, waiting for transfers between devices: 12.5 us -> 11.5 us  [exchange(): return lax.all_to_all(v, axis, split_axis=0, concat_axis=0, tiled=True)]
  transfers between devices with their start and end apart: 26 -> 32, of which waited for: 12 -> 16; matrix products, arithmetic and copies ran while one was open for 0% -> 0% of each run, Pallas kernels for 10% -> 9%
where the time goes in v9:
time: 129 us
  starting transfers between devices  74.5 us (58%)
  waiting for transfers between devices  34.3 us (27%)
  Pallas kernels  18.9 us (15%)
    all_to_all x3, starting transfers between devices, exchange(): return lax.all_to_all(v, axis, split_axis=0, concat_axis=0, tiled=True)  27.6 us
    ppermute x18, starting transfers between devices, turn(): lax.ppermute(v, 'blk', [(i, i // 4 * 4 + (i % 4 + k) % 4) for i in range(...  22.7 us
    pallas_call x18, Pallas kernels, call(): pl.pallas_call(kernel, out_shape=out_shape, in_specs=[whole] * len(args)...  18.9 us
    ppermute x4, starting transfers between devices, swap(): return lax.ppermute(v, 'blk', [(i, i ^ 4) for i in range(8)])  14.9 us
    ppermute x18, waiting for transfers between devices, turn(): lax.ppermute(v, 'blk', [(i, i // 4 * 4 + (i % 4 + k) % 4) for i in range(...  12.7 us
    all_to_all x3, waiting for transfers between devices, exchange(): return lax.all_to_all(v, axis, split_axis=0, concat_axis=0, tiled=True)  11.5 us
    ppermute x7, starting transfers between devices, move(): return lax.ppermute(v, 'grp', [(i, to(i)) for i in range(32)])  9.34 us
    ppermute x7, waiting for transfers between devices, move(): return lax.ppermute(v, 'grp', [(i, to(i)) for i in range(32)])  5.85 us
  transfers between devices with their start and end apart: 32, of which 16 were waited for; matrix products, arithmetic and copies ran while one was open for 0% of the time, Pallas kernels for 9%

profile of v9, /device:TPU:1, one launch (start us, length us, event | category | flops | bytes accessed | tf_op | source)
XLA Modules:
  0.0 128.9 jit_solution(3262752725276836659)
XLA Ops:
  0.7 2.3 %shard_map.164 = f32[32,40,128]{2,1,0:T(8,128)} custom-call(f32[256,128]{1,0:T(8,128)} %features.5, s32[32,32]{1,0:T(8,128)} %bitcast.14, s32[1,8]{1,0:T(1,128)} %bitcast.27), custom_call_target="tpu_custom_call" | custom-call | flops 268435456 | bytes 135200 | tf_op jit(solution)/shard_map/pallas_call | solution.py:45
  3.0 10.0 %all-to-all-start = ((f32[32,40,128]{2,1,0:T(8,128)}), f32[32,40,128]{2,1,0:T(8,128)S(1)}, u32[]{:S(2)}, u32[]{:S(2)}) async-start(f32[32,40,128]{2,1,0:T(8,128)} %shard_map.164), calls=%async_computation | async-start | bytes 1310720 | tf_op jit(solution)/shard_map/all_to_all | solution.py:299
  14.0 2.8 %collective-permute-start = (s32[32,128]{1,0:T(8,128)S(1)}, s32[32,128]{1,0:T(8,128)S(1)}, u32[]{:S(2)}, u32[]{:S(2)}) collective-permute-start(s32[32,128]{1,0:T(8,128)S(1)} %get-tuple-element.59), channel_id=1, source_target_pairs={{0,3},{1,0},{2,1},{3,2},{4,7},{5,4},{6,5},{7,6},{8,11},{9,8},{10,9... | collective-permute-start | bytes 49160 | tf_op jit(solution)/shard_map/ppermute | solution.py:296
  17.8 3.3 %collective-permute-done.1.l2 = s32[32,128]{1,0:T(8,128)S(1)} collective-permute-done((s32[32,128]{1,0:T(8,128)S(1)}, s32[32,128]{1,0:T(8,128)S(1)}, u32[]{:S(2)}, u32[]{:S(2)}) %collective-permute-start.1) | collective-permute-done | bytes 16416 | tf_op jit(solution)/shard_map/ppermute | solution.py:296
  21.4 4.3 %collective-permute-start.3 = (s32[64,128]{1,0:T(8,128)S(1)}, s32[64,128]{1,0:T(8,128)S(1)}, u32[]{:S(2)}, u32[]{:S(2)}) collective-permute-start(s32[64,128]{1,0:T(8,128)S(1)} %pad_add_fusion), channel_id=1, source_target_pairs={{0,4},{1,5},{2,6},{3,7},{4,0},{5,1},{6,2},{7,3},{8,12},{9,13},{10,... | collective-permute-start | bytes 98312 | tf_op jit(solution)/shard_map/ppermute | solution.py:293
  25.7 3.8 %collective-permute-done.3.far = s32[64,128]{1,0:T(8,128)S(1)} collective-permute-done((s32[64,128]{1,0:T(8,128)S(1)}, s32[64,128]{1,0:T(8,128)S(1)}, u32[]{:S(2)}, u32[]{:S(2)}) %collective-permute-start.3) | collective-permute-done | bytes 32800 | tf_op jit(solution)/shard_map/ppermute | solution.py:293
  29.5 2.3 %shard_map.167 = (bf16[8,256,512]{2,1,0:T(8,128)(2,1)S(1)}, s32[1]{0:T(128)}) custom-call(s32[1]{0:T(128)} %bitcast.pos, s32[32,128]{1,0:T(8,128)S(1)} %get-tuple-element.58.l0, s32[32,128]{1,0:T(8,128)S(1)} %collective-permute-done.l1, s32[32,128]{1,0:T(8,128)S(1)} %collective-permute-done.1.l2, s32[32,128]{1,0:T(8,128)S(1)} %collective-permute-done.2.l3, ...), custom_call_target="tpu_custom_call" | custom-call | flops 2147483648 | bytes 98308 | tf_op jit(solution)/shard_map/pallas_call | solution.py:45
  32.7 1.4 %shard_map.168 = (f32[256,128]{1,0:T(8,128)S(1)}, f32[256,128]{1,0:T(8,128)S(1)}, f32[256,128]{1,0:T(8,128)S(1)}, f32[256,128]{1,0:T(8,128)S(1)}, f32[256,128]{1...) custom-call(s32[1]{0:T(128)} %get-tuple-element.62.flag, s32[1]{0:T(128)} %bitcast.pos, ...), custom_call_target="tpu_custom_call" | custom-call | flops 268435456 | bytes 2981896 | tf_op jit(solution)/shard_map/pallas_call | solution.py:45
  34.1 2.1 %collective-permute-start.4 = (f32[256,128]{1,0:T(8,128)S(1)}, f32[256,128]{1,0:T(8,128)S(1)}, u32[]{:S(2)}, u32[]{:S(2)}) collective-permute-start(f32[256,128]{1,0:T(8,128)S(1)} %get-tuple-element.66), channel_id=1, source_target_pairs={{0,1},{1,2},{2,3},{3,0},{4,5},{5,6},{6,7},{7,4},{8,9},{9,10},{10,1... | collective-permute-start | bytes 393224 | tf_op jit(solution)/shard_map/ppermute | solution.py:296
  36.1 1.5 %collective-permute-start.5 = (f32[256,128]{1,0:T(8,128)S(1)}, f32[256,128]{1,0:T(8,128)S(1)}, u32[]{:S(2)}, u32[]{:S(2)}) collective-permute-start(f32[256,128]{1,0:T(8,128)S(1)} %get-tuple-element.67), channel_id=1, source_target_pairs={{0,3},{1,0},{2,1},{3,2},{4,7},{5,4},{6,5},{7,6},{8,11},{9,8},{10,9... | collective-permute-start | bytes 393224 | tf_op jit(solution)/shard_map/ppermute | solution.py:296
  37.7 1.6 %collective-permute-start.6 = (f32[256,128]{1,0:T(8,128)S(1)}, f32[256,128]{1,0:T(8,128)S(1)}, u32[]{:S(2)}, u32[]{:S(2)}) collective-permute-start(f32[256,128]{1,0:T(8,128)S(1)} %get-tuple-element.68), channel_id=1, source_target_pairs={{0,2},{1,3},{2,0},{3,1},{4,6},{5,7},{6,4},{7,5},{8,10},{9,11},{10,... | collective-permute-start | bytes 393224 | tf_op jit(solution)/shard_map/ppermute | solution.py:296
  39.2 2.3 %shard_map.166 = (bf16[256,1024]{1,0:T(8,128)(2,1)S(1)}, bf16[1024,256]{1,0:T(8,128)(2,1)S(1)}, f32[256,128]{1,0:T(8,128)S(1)}, s32[1]{0:T(128)}) custom-call(s32[48,128]{1,0:T(8,128)S(1)} %get-tuple-element.54.own_to, s32[8,128]{1,0:T(8,128)S(1)} %bitcast.16, s32[8,128]{1,0:T(8,128)S(1)} %bitcast.19, s32[2,128]{1,0:T(2,128)S(1)} %bitcast.26), custom_call_target="tpu_custom_call" | custom-call | flops 2147483648 | bytes 33792 | tf_op jit(solution)/shard_map/pallas_call | solution.py:45
  41.6 4.0 %collective-permute-done.6 = f32[256,128]{1,0:T(8,128)S(1)} collective-permute-done((f32[256,128]{1,0:T(8,128)S(1)}, f32[256,128]{1,0:T(8,128)S(1)}, u32[]{:S(2)}, u32[]{:S(2)}) %collective-permute-start.6) | collective-permute-done | bytes 131104 | tf_op jit(solution)/shard_map/ppermute | solution.py:296
  46.2 4.1 %collective-permute-start.7 = (f32[256,128]{1,0:T(8,128)S(1)}, f32[256,128]{1,0:T(8,128)S(1)}, u32[]{:S(2)}, u32[]{:S(2)}) collective-permute-start(f32[256,128]{1,0:T(8,128)S(1)} %add_add_fusion), channel_id=1, source_target_pairs={{0,4},{1,5},{2,6},{3,7},{4,0},{5,1},{6,2},{7,3},{8,12},{9,13},{10,... | collective-permute-start | bytes 393224 | tf_op jit(solution)/shard_map/ppermute | solution.py:293
  51.6 1.4 %collective-permute-start.9 = (f32[256,128]{1,0:T(8,128)S(1)}, f32[256,128]{1,0:T(8,128)S(1)}, u32[]{:S(2)}, u32[]{:S(2)}) collective-permute-start(f32[256,128]{1,0:T(8,128)S(1)} %get-tuple-element.74), channel_id=1, source_target_pairs={{0,3},{1,0},{2,1},{3,2},{4,7},{5,4},{6,5},{7,6},{8,11},{9,8},{10,9... | collective-permute-start | bytes 393224 | tf_op jit(solution)/shard_map/ppermute | solution.py:296
  53.0 1.6 %shard_map.170.bwd = bf16[8,512,256]{2,1,0:T(8,128)(2,1)S(1)} custom-call(s32[1]{0:T(128)} %bitcast.pos, s32[32,128]{1,0:T(8,128)S(1)} %get-tuple-element.58.l0, s32[32,128]{1,0:T(8,128)S(1)} %collective-permute-done.l1, s32[32,128]{1,0:T(8,128)S(1)} %collective-permute-done.1.l2, s32[32,128]{1,0:T(8,128)S(1)} %collective-permute-done.2.l3, ...), custom_call_target="tpu_custom_call" | custom-call | flops 2147483648 | bytes 98308 | tf_op jit(solution)/shard_map/pallas_call | solution.py:45
  57.3 1.7 %shard_map.179 = f32[1024,128]{1,0:T(8,128)} custom-call(s32[1]{0:T(128)} %get-tuple-element.55.flag, s32[8,128]{1,0:T(8,128)S(1)} %bitcast.18, s32[8,128]{1,0:T(8,128)S(1)} %bitcast.21, f32[256,128]{1,0:T(8,128)S(1)} %get-tuple-element.79.g0.grad_sum, bf16[1024,256]{1,0:T(8,128)(2,1)S(1)} %get-tuple-element.95.h_bwd), custom_call_target="tpu_custom_call" | custom-call | flops 268435456 | bytes 663556 | tf_op jit(solution)/shard_map/pallas_call | solution.py:45
  59.0 7.6 %all-to-all-start.2 = ((f32[32,32,128]{2,1,0:T(8,128)}), f32[32,32,128]{2,1,0:T(8,128)S(1)}, u32[]{:S(2)}, u32[]{:S(2)}) async-start(f32[32,32,128]{2,1,0:T(8,128)} %bitcast.12), calls=%async_computation.2 | async-start | bytes 1048576 | tf_op jit(solution)/shard_map/all_to_all | solution.py:299
  67.4 3.3 %collective-permute-start.14 = (f32[256,128]{1,0:T(8,128)S(1)}, f32[256,128]{1,0:T(8,128)S(1)}, u32[]{:S(2)}, u32[]{:S(2)}) collective-permute-start(f32[256,128]{1,0:T(8,128)S(1)} %get-tuple-element.79.g0.grad_sum), channel_id=1, source_target_pairs={{0,4},{1,5},{2,6},{3,7},{4,0},{5,1},{6,2},{7,3},{8,12},{9,13},{10,... | collective-permute-start | bytes 393224 | tf_op jit(solution)/shard_map/ppermute | solution.py:293
  70.7 1.6 %collective-permute-start.11 = (f32[256,128]{1,0:T(8,128)S(1)}, f32[256,128]{1,0:T(8,128)S(1)}, u32[]{:S(2)}, u32[]{:S(2)}) collective-permute-start(f32[256,128]{1,0:T(8,128)S(1)} %get-tuple-element.79.g0.grad_sum), channel_id=1, source_target_pairs={{0,3},{1,0},{2,1},{3,2},{4,7},{5,4},{6,5},{7,6},{8,11},{9,8},{10,9... | collective-permute-start | bytes 393224 | tf_op jit(solution)/shard_map/ppermute | solution.py:296
  72.2 1.8 %collective-permute-start.19 = (f32[40,128]{1,0:T(8,128)S(1)}, f32[40,128]{1,0:T(8,128)S(1)}, u32[]{:S(2)}, u32[]{:S(2)}) collective-permute-start(f32[40,128]{1,0:T(8,128)S(1)} %get-tuple-element.87), channel_id=1, source_target_pairs={{0,16},{8,24},{16,32},{24,40},{32,48},{40,56},{48,0},{56,8},{64,80... | collective-permute-start | bytes 61448 | tf_op jit(solution)/shard_map/ppermute | solution.py:341
  74.1 2.4 %collective-permute-start.20 = (f32[40,128]{1,0:T(8,128)S(1)}, f32[40,128]{1,0:T(8,128)S(1)}, u32[]{:S(2)}, u32[]{:S(2)}) collective-permute-start(f32[40,128]{1,0:T(8,128)S(1)} %get-tuple-element.88), channel_id=1, source_target_pairs={{0,32},{8,40},{16,48},{24,56},{32,0},{40,8},{48,16},{56,24},{64,96... | collective-permute-start | bytes 61448 | tf_op jit(solution)/shard_map/ppermute | solution.py:341
  80.7 2.2 %collective-permute-start.23 = (f32[16,128]{1,0:T(8,128)S(1)}, f32[16,128]{1,0:T(8,128)S(1)}, u32[]{:S(2)}, u32[]{:S(2)}) collective-permute-start(f32[16,128]{1,0:T(8,128)S(1)} %get-tuple-element.92), channel_id=1, source_target_pairs={{0,128},{8,136},{16,144},{24,152},{32,160},{40,168},{48,176},{56,1... | collective-permute-start | bytes 24584 | tf_op jit(solution)/shard_map/ppermute | solution.py:341
  83.0 3.6 %collective-permute-done.23.c = f32[16,128]{1,0:T(8,128)S(1)} collective-permute-done((f32[16,128]{1,0:T(8,128)S(1)}, f32[16,128]{1,0:T(8,128)S(1)}, u32[]{:S(2)}, u32[]{:S(2)}) %collective-permute-start.23) | collective-permute-done | bytes 8224 | tf_op jit(solution)/shard_map/ppermute | solution.py:341
  87.1 1.4 %collective-permute-start.25 = (f32[16,128]{1,0:T(8,128)S(1)}, f32[16,128]{1,0:T(8,128)S(1)}, u32[]{:S(2)}, u32[]{:S(2)}) collective-permute-start(f32[16,128]{1,0:T(8,128)S(1)} %shard_map.176.a), channel_id=1, source_target_pairs={{0,1},{1,2},{2,3},{3,0},{4,5},{5,6},{6,7},{7,4},{8,9},{9,10},{10,1... | collective-permute-start | bytes 24584 | tf_op jit(solution)/shard_map/ppermute | solution.py:296
  88.6 2.0 %collective-permute-start.26 = (f32[16,128]{1,0:T(8,128)S(1)}, f32[16,128]{1,0:T(8,128)S(1)}, u32[]{:S(2)}, u32[]{:S(2)}) collective-permute-start(f32[16,128]{1,0:T(8,128)S(1)} %shard_map.176.a), channel_id=1, source_target_pairs={{0,2},{1,3},{2,0},{3,1},{4,6},{5,7},{6,4},{7,5},{8,10},{9,11},{10,... | collective-permute-start | bytes 24584 | tf_op jit(solution)/shard_map/ppermute | solution.py:296
  92.7 2.6 %collective-permute-start.15 = (f32[256,128]{1,0:T(8,128)S(1)}, f32[256,128]{1,0:T(8,128)S(1)}, u32[]{:S(2)}, u32[]{:S(2)}) collective-permute-start(f32[256,128]{1,0:T(8,128)S(1)} %collective-permute-done.14.g4), channel_id=1, source_target_pairs={{0,3},{1,0},{2,1},{3,2},{4,7},{5,4},{6,5},{7,6},{8,11},{9,8},{10,9... | collective-permute-start | bytes 393224 | tf_op jit(solution)/shard_map/ppermute | solution.py:296
  96.6 3.2 %collective-permute-start.28 = (f32[16,128]{1,0:T(8,128)S(1)}, f32[16,128]{1,0:T(8,128)S(1)}, u32[]{:S(2)}, u32[]{:S(2)}) collective-permute-start(f32[16,128]{1,0:T(8,128)S(1)} %shard_map.177.near), channel_id=1, source_target_pairs={{0,4},{1,5},{2,6},{3,7},{4,0},{5,1},{6,2},{7,3},{8,12},{9,13},{10,... | collective-permute-start | bytes 24584 | tf_op jit(solution)/shard_map/ppermute | solution.py:293
  100.7 3.8 %collective-permute-done.17.g7 = f32[256,128]{1,0:T(8,128)S(1)} collective-permute-done((f32[256,128]{1,0:T(8,128)S(1)}, f32[256,128]{1,0:T(8,128)S(1)}, u32[]{:S(2)}, u32[]{:S(2)}) %collective-permute-start.17) | collective-permute-done | bytes 131104 | tf_op jit(solution)/shard_map/ppermute | solution.py:296
  104.4 1.4 %shard_map.172 = (f32[256,128]{1,0:T(8,128)S(1)}, f32[32,8,128]{2,1,0:T(8,128)S(1)}) custom-call(s32[1]{0:T(128)} %get-tuple-element.62.flag, s32[1]{0:T(128)} %bitcast.pos, s32[32,128]{1,0:T(8,128)S(1)} %get-tuple-element.58.l0, s32[32,128]{1,0:T(8,128)S(1)} %collective-permute-done.l1, s32[32,128]{1,0:T(8,128)S(1)} %collective-permute-done.1.l2, ...), custom_call_target="tpu_custom_call" | custom-call | flops 268435456 | bytes 3244040 | tf_op jit(solution)/shard_map/pallas_call | solution.py:45
  106.6 9.9 %all-to-all-start.1 = ((f32[32,16,128]{2,1,0:T(8,128)}), f32[32,16,128]{2,1,0:T(8,128)S(1)}, u32[]{:S(2)}, u32[]{:S(2)}) async-start(f32[32,16,128]{2,1,0:T(8,128)} %get-tuple-element.94), calls=%async_computation.1 | async-start | bytes 524288 | tf_op jit(solution)/shard_map/all_to_all | solution.py:299
  117.0 10.7 %all-to-all-done.1.last = f32[32,16,128]{2,1,0:T(8,128)S(1)} async-done(((f32[32,16,128]{2,1,0:T(8,128)}), f32[32,16,128]{2,1,0:T(8,128)S(1)}, u32[]{:S(2)}, u32[]{:S(2)}) %all-to-all-start.1) | async-done | bytes 262176 | tf_op jit(solution)/shard_map/all_to_all | solution.py:299
  (83 shorter events, 20.1 us)
Async XLA Ops:
  3.0 29.7 %all-to-all-start = ((f32[32,40,128]{2,1,0:T(8,128)}), f32[32,40,128]{2,1,0:T(8,128)S(1)}, u32[]{:S(2)}, u32[]{:S(2)}) async-start(f32[32,40,128]{2,1,0:T(8,128)} %shard_map.164), calls=%async_computation | async-start | bytes 1310720 | tf_op jit(solution)/shard_map/all_to_all | solution.py:299
  14.0 3.9 %collective-permute-start = (s32[32,128]{1,0:T(8,128)S(1)}, s32[32,128]{1,0:T(8,128)S(1)}, u32[]{:S(2)}, u32[]{:S(2)}) collective-permute-start(s32[32,128]{1,0:T(8,128)S(1)} %get-tuple-element.59), channel_id=1, source_target_pairs={{0,3},{1,0},{2,1},{3,2},{4,7},{5,4},{6,5},{7,6},{8,11},{9,8},{10,9... | collective-permute-start | bytes 49160 | tf_op jit(solution)/shard_map/ppermute | solution.py:296
  16.8 4.4 %collective-permute-start.1 = (s32[32,128]{1,0:T(8,128)S(1)}, s32[32,128]{1,0:T(8,128)S(1)}, u32[]{:S(2)}, u32[]{:S(2)}) collective-permute-start(s32[32,128]{1,0:T(8,128)S(1)} %get-tuple-element.60), channel_id=1, source_target_pairs={{0,2},{1,3},{2,0},{3,1},{4,6},{5,7},{6,4},{7,5},{8,10},{9,11},{10,... | collective-permute-start | bytes 49160 | tf_op jit(solution)/shard_map/ppermute | solution.py:296
  17.1 4.2 %collective-permute-start.2 = (s32[32,128]{1,0:T(8,128)S(1)}, s32[32,128]{1,0:T(8,128)S(1)}, u32[]{:S(2)}, u32[]{:S(2)}) collective-permute-start(s32[32,128]{1,0:T(8,128)S(1)} %get-tuple-element.61), channel_id=1, source_target_pairs={{0,1},{1,2},{2,3},{3,0},{4,5},{5,6},{6,7},{7,4},{8,9},{9,10},{10,1... | collective-permute-start | bytes 49160 | tf_op jit(solution)/shard_map/ppermute | solution.py:296
  21.4 8.1 %collective-permute-start.3 = (s32[64,128]{1,0:T(8,128)S(1)}, s32[64,128]{1,0:T(8,128)S(1)}, u32[]{:S(2)}, u32[]{:S(2)}) collective-permute-start(s32[64,128]{1,0:T(8,128)S(1)} %pad_add_fusion), channel_id=1, source_target_pairs={{0,4},{1,5},{2,6},{3,7},{4,0},{5,1},{6,2},{7,3},{8,12},{9,13},{10,... | collective-permute-start | bytes 98312 | tf_op jit(solution)/shard_map/ppermute | solution.py:293
  34.1 7.5 %collective-permute-start.4 = (f32[256,128]{1,0:T(8,128)S(1)}, f32[256,128]{1,0:T(8,128)S(1)}, u32[]{:S(2)}, u32[]{:S(2)}) collective-permute-start(f32[256,128]{1,0:T(8,128)S(1)} %get-tuple-element.66), channel_id=1, source_target_pairs={{0,1},{1,2},{2,3},{3,0},{4,5},{5,6},{6,7},{7,4},{8,9},{9,10},{10,1... | collective-permute-start | bytes 393224 | tf_op jit(solution)/shard_map/ppermute | solution.py:296
  36.1 5.5 %collective-permute-start.5 = (f32[256,128]{1,0:T(8,128)S(1)}, f32[256,128]{1,0:T(8,128)S(1)}, u32[]{:S(2)}, u32[]{:S(2)}) collective-permute-start(f32[256,128]{1,0:T(8,128)S(1)} %get-tuple-element.67), channel_id=1, source_target_pairs={{0,3},{1,0},{2,1},{3,2},{4,7},{5,4},{6,5},{7,6},{8,11},{9,8},{10,9... | collective-permute-start | bytes 393224 | tf_op jit(solution)/shard_map/ppermute | solution.py:296
  37.7 7.9 %collective-permute-start.6 = (f32[256,128]{1,0:T(8,128)S(1)}, f32[256,128]{1,0:T(8,128)S(1)}, u32[]{:S(2)}, u32[]{:S(2)}) collective-permute-start(f32[256,128]{1,0:T(8,128)S(1)} %get-tuple-element.68), channel_id=1, source_target_pairs={{0,2},{1,3},{2,0},{3,1},{4,6},{5,7},{6,4},{7,5},{8,10},{9,11},{10,... | collective-permute-start | bytes 393224 | tf_op jit(solution)/shard_map/ppermute | solution.py:296
  45.7 9.8 %collective-permute-start.10 = (f32[256,128]{1,0:T(8,128)S(1)}, f32[256,128]{1,0:T(8,128)S(1)}, u32[]{:S(2)}, u32[]{:S(2)}) collective-permute-start(f32[256,128]{1,0:T(8,128)S(1)} %get-tuple-element.75), channel_id=1, source_target_pairs={{0,2},{1,3},{2,0},{3,1},{4,6},{5,7},{6,4},{7,5},{8,10},{9,11},{10,... | collective-permute-start | bytes 393224 | tf_op jit(solution)/shard_map/ppermute | solution.py:296
  46.2 9.8 %collective-permute-start.7 = (f32[256,128]{1,0:T(8,128)S(1)}, f32[256,128]{1,0:T(8,128)S(1)}, u32[]{:S(2)}, u32[]{:S(2)}) collective-permute-start(f32[256,128]{1,0:T(8,128)S(1)} %add_add_fusion), channel_id=1, source_target_pairs={{0,4},{1,5},{2,6},{3,7},{4,0},{5,1},{6,2},{7,3},{8,12},{9,13},{10,... | collective-permute-start | bytes 393224 | tf_op jit(solution)/shard_map/ppermute | solution.py:293
  50.3 5.7 %collective-permute-start.8 = (f32[256,128]{1,0:T(8,128)S(1)}, f32[256,128]{1,0:T(8,128)S(1)}, u32[]{:S(2)}, u32[]{:S(2)}) collective-permute-start(f32[256,128]{1,0:T(8,128)S(1)} %get-tuple-element.73), channel_id=1, source_target_pairs={{0,1},{1,2},{2,3},{3,0},{4,5},{5,6},{6,7},{7,4},{8,9},{9,10},{10,1... | collective-permute-start | bytes 393224 | tf_op jit(solution)/shard_map/ppermute | solution.py:296
  51.6 4.4 %collective-permute-start.9 = (f32[256,128]{1,0:T(8,128)S(1)}, f32[256,128]{1,0:T(8,128)S(1)}, u32[]{:S(2)}, u32[]{:S(2)}) collective-permute-start(f32[256,128]{1,0:T(8,128)S(1)} %get-tuple-element.74), channel_id=1, source_target_pairs={{0,3},{1,0},{2,1},{3,2},{4,7},{5,4},{6,5},{7,6},{8,11},{9,8},{10,9... | collective-permute-start | bytes 393224 | tf_op jit(solution)/shard_map/ppermute | solution.py:296
  59.0 47.6 %all-to-all-start.2 = ((f32[32,32,128]{2,1,0:T(8,128)}), f32[32,32,128]{2,1,0:T(8,128)S(1)}, u32[]{:S(2)}, u32[]{:S(2)}) async-start(f32[32,32,128]{2,1,0:T(8,128)} %bitcast.12), calls=%async_computation.2 | async-start | bytes 1048576 | tf_op jit(solution)/shard_map/all_to_all | solution.py:299
  67.0 5.2 %collective-permute-start.18 = (f32[136,128]{1,0:T(8,128)S(1)}, f32[136,128]{1,0:T(8,128)S(1)}, u32[]{:S(2)}, u32[]{:S(2)}) collective-permute-start(f32[136,128]{1,0:T(8,128)S(1)} %get-tuple-element.85), channel_id=1, source_target_pairs={{0,8},{8,0},{16,24},{24,16},{32,40},{40,32},{48,56},{56,48},{64,72... | collective-permute-start | bytes 208904 | tf_op jit(solution)/shard_map/ppermute | solution.py:341
  67.4 25.3 %collective-permute-start.14 = (f32[256,128]{1,0:T(8,128)S(1)}, f32[256,128]{1,0:T(8,128)S(1)}, u32[]{:S(2)}, u32[]{:S(2)}) collective-permute-start(f32[256,128]{1,0:T(8,128)S(1)} %get-tuple-element.79.g0.grad_sum), channel_id=1, source_target_pairs={{0,4},{1,5},{2,6},{3,7},{4,0},{5,1},{6,2},{7,3},{8,12},{9,13},{10,... | collective-permute-start | bytes 393224 | tf_op jit(solution)/shard_map/ppermute | solution.py:293
  70.7 25.4 %collective-permute-start.11 = (f32[256,128]{1,0:T(8,128)S(1)}, f32[256,128]{1,0:T(8,128)S(1)}, u32[]{:S(2)}, u32[]{:S(2)}) collective-permute-start(f32[256,128]{1,0:T(8,128)S(1)} %get-tuple-element.79.g0.grad_sum), channel_id=1, source_target_pairs={{0,3},{1,0},{2,1},{3,2},{4,7},{5,4},{6,5},{7,6},{8,11},{9,8},{10,9... | collective-permute-start | bytes 393224 | tf_op jit(solution)/shard_map/ppermute | solution.py:296
  72.2 5.4 %collective-permute-start.19 = (f32[40,128]{1,0:T(8,128)S(1)}, f32[40,128]{1,0:T(8,128)S(1)}, u32[]{:S(2)}, u32[]{:S(2)}) collective-permute-start(f32[40,128]{1,0:T(8,128)S(1)} %get-tuple-element.87), channel_id=1, source_target_pairs={{0,16},{8,24},{16,32},{24,40},{32,48},{40,56},{48,0},{56,8},{64,80... | collective-permute-start | bytes 61448 | tf_op jit(solution)/shard_map/ppermute | solution.py:341
  74.1 4.5 %collective-permute-start.20 = (f32[40,128]{1,0:T(8,128)S(1)}, f32[40,128]{1,0:T(8,128)S(1)}, u32[]{:S(2)}, u32[]{:S(2)}) collective-permute-start(f32[40,128]{1,0:T(8,128)S(1)} %get-tuple-element.88), channel_id=1, source_target_pairs={{0,32},{8,40},{16,48},{24,56},{32,0},{40,8},{48,16},{56,24},{64,96... | collective-permute-start | bytes 61448 | tf_op jit(solution)/shard_map/ppermute | solution.py:341
  76.4 2.9 %collective-permute-start.21 = (f32[40,128]{1,0:T(8,128)S(1)}, f32[40,128]{1,0:T(8,128)S(1)}, u32[]{:S(2)}, u32[]{:S(2)}) collective-permute-start(f32[40,128]{1,0:T(8,128)S(1)} %get-tuple-element.89), channel_id=1, source_target_pairs={{0,48},{8,56},{16,0},{24,8},{32,16},{40,24},{48,32},{56,40},{64,11... | collective-permute-start | bytes 61448 | tf_op jit(solution)/shard_map/ppermute | solution.py:341
  79.4 3.6 %collective-permute-start.22 = (f32[16,128]{1,0:T(8,128)S(1)}, f32[16,128]{1,0:T(8,128)S(1)}, u32[]{:S(2)}, u32[]{:S(2)}) collective-permute-start(f32[16,128]{1,0:T(8,128)S(1)} %get-tuple-element.91), channel_id=1, source_target_pairs={{0,64},{8,72},{16,80},{24,88},{32,96},{40,104},{48,112},{56,120},{... | collective-permute-start | bytes 24584 | tf_op jit(solution)/shard_map/ppermute | solution.py:341
  80.7 5.9 %collective-permute-start.23 = (f32[16,128]{1,0:T(8,128)S(1)}, f32[16,128]{1,0:T(8,128)S(1)}, u32[]{:S(2)}, u32[]{:S(2)}) collective-permute-start(f32[16,128]{1,0:T(8,128)S(1)} %get-tuple-element.92), channel_id=1, source_target_pairs={{0,128},{8,136},{16,144},{24,152},{32,160},{40,168},{48,176},{56,1... | collective-permute-start | bytes 24584 | tf_op jit(solution)/shard_map/ppermute | solution.py:341
  82.8 4.3 %collective-permute-start.24 = (f32[16,128]{1,0:T(8,128)S(1)}, f32[16,128]{1,0:T(8,128)S(1)}, u32[]{:S(2)}, u32[]{:S(2)}) collective-permute-start(f32[16,128]{1,0:T(8,128)S(1)} %get-tuple-element.93), channel_id=1, source_target_pairs={{0,192},{8,200},{16,208},{24,216},{32,224},{40,232},{48,240},{56,2... | collective-permute-start | bytes 24584 | tf_op jit(solution)/shard_map/ppermute | solution.py:341
  87.1 3.9 %collective-permute-start.25 = (f32[16,128]{1,0:T(8,128)S(1)}, f32[16,128]{1,0:T(8,128)S(1)}, u32[]{:S(2)}, u32[]{:S(2)}) collective-permute-start(f32[16,128]{1,0:T(8,128)S(1)} %shard_map.176.a), channel_id=1, source_target_pairs={{0,1},{1,2},{2,3},{3,0},{4,5},{5,6},{6,7},{7,4},{8,9},{9,10},{10,1... | collective-permute-start | bytes 24584 | tf_op jit(solution)/shard_map/ppermute | solution.py:296
  88.6 4.0 %collective-permute-start.26 = (f32[16,128]{1,0:T(8,128)S(1)}, f32[16,128]{1,0:T(8,128)S(1)}, u32[]{:S(2)}, u32[]{:S(2)}) collective-permute-start(f32[16,128]{1,0:T(8,128)S(1)} %shard_map.176.a), channel_id=1, source_target_pairs={{0,2},{1,3},{2,0},{3,1},{4,6},{5,7},{6,4},{7,5},{8,10},{9,11},{10,... | collective-permute-start | bytes 24584 | tf_op jit(solution)/shard_map/ppermute | solution.py:296
  90.6 4.7 %collective-permute-start.27 = (f32[16,128]{1,0:T(8,128)S(1)}, f32[16,128]{1,0:T(8,128)S(1)}, u32[]{:S(2)}, u32[]{:S(2)}) collective-permute-start(f32[16,128]{1,0:T(8,128)S(1)} %shard_map.176.a), channel_id=1, source_target_pairs={{0,3},{1,0},{2,1},{3,2},{4,7},{5,4},{6,5},{7,6},{8,11},{9,8},{10,9... | collective-permute-start | bytes 24584 | tf_op jit(solution)/shard_map/ppermute | solution.py:296
  91.1 5.5 %collective-permute-start.12 = (f32[256,128]{1,0:T(8,128)S(1)}, f32[256,128]{1,0:T(8,128)S(1)}, u32[]{:S(2)}, u32[]{:S(2)}) collective-permute-start(f32[256,128]{1,0:T(8,128)S(1)} %get-tuple-element.79.g0.grad_sum), channel_id=1, source_target_pairs={{0,2},{1,3},{2,0},{3,1},{4,6},{5,7},{6,4},{7,5},{8,10},{9,11},{10,... | collective-permute-start | bytes 393224 | tf_op jit(solution)/shard_map/ppermute | solution.py:296
  92.6 7.2 %collective-permute-start.13 = (f32[256,128]{1,0:T(8,128)S(1)}, f32[256,128]{1,0:T(8,128)S(1)}, u32[]{:S(2)}, u32[]{:S(2)}) collective-permute-start(f32[256,128]{1,0:T(8,128)S(1)} %get-tuple-element.79.g0.grad_sum), channel_id=1, source_target_pairs={{0,1},{1,2},{2,3},{3,0},{4,5},{5,6},{6,7},{7,4},{8,9},{9,10},{10,1... | collective-permute-start | bytes 393224 | tf_op jit(solution)/shard_map/ppermute | solution.py:296
  92.7 7.4 %collective-permute-start.15 = (f32[256,128]{1,0:T(8,128)S(1)}, f32[256,128]{1,0:T(8,128)S(1)}, u32[]{:S(2)}, u32[]{:S(2)}) collective-permute-start(f32[256,128]{1,0:T(8,128)S(1)} %collective-permute-done.14.g4), channel_id=1, source_target_pairs={{0,3},{1,0},{2,1},{3,2},{4,7},{5,4},{6,5},{7,6},{8,11},{9,8},{10,9... | collective-permute-start | bytes 393224 | tf_op jit(solution)/shard_map/ppermute | solution.py:296
  95.3 5.4 %collective-permute-start.16 = (f32[256,128]{1,0:T(8,128)S(1)}, f32[256,128]{1,0:T(8,128)S(1)}, u32[]{:S(2)}, u32[]{:S(2)}) collective-permute-start(f32[256,128]{1,0:T(8,128)S(1)} %collective-permute-done.14.g4), channel_id=1, source_target_pairs={{0,2},{1,3},{2,0},{3,1},{4,6},{5,7},{6,4},{7,5},{8,10},{9,11},{10,... | collective-permute-start | bytes 393224 | tf_op jit(solution)/shard_map/ppermute | solution.py:296
  96.1 8.4 %collective-permute-start.17 = (f32[256,128]{1,0:T(8,128)S(1)}, f32[256,128]{1,0:T(8,128)S(1)}, u32[]{:S(2)}, u32[]{:S(2)}) collective-permute-start(f32[256,128]{1,0:T(8,128)S(1)} %collective-permute-done.14.g4), channel_id=1, source_target_pairs={{0,1},{1,2},{2,3},{3,0},{4,5},{5,6},{6,7},{7,4},{8,9},{9,10},{10,1... | collective-permute-start | bytes 393224 | tf_op jit(solution)/shard_map/ppermute | solution.py:296
  96.6 9.2 %collective-permute-start.28 = (f32[16,128]{1,0:T(8,128)S(1)}, f32[16,128]{1,0:T(8,128)S(1)}, u32[]{:S(2)}, u32[]{:S(2)}) collective-permute-start(f32[16,128]{1,0:T(8,128)S(1)} %shard_map.177.near), channel_id=1, source_target_pairs={{0,4},{1,5},{2,6},{3,7},{4,0},{5,1},{6,2},{7,3},{8,12},{9,13},{10,... | collective-permute-start | bytes 24584 | tf_op jit(solution)/shard_map/ppermute | solution.py:293
  106.6 21.1 %all-to-all-start.1 = ((f32[32,16,128]{2,1,0:T(8,128)}), f32[32,16,128]{2,1,0:T(8,128)S(1)}, u32[]{:S(2)}, u32[]{:S(2)}) async-start(f32[32,16,128]{2,1,0:T(8,128)} %get-tuple-element.94), calls=%async_computation.1 | async-start | bytes 524288 | tf_op jit(solution)/shard_map/all_to_all | solution.py:299
  (13 other events, 168.6 us)

commit v10 on v9

--- a/solution.py
+++ b/solution.py
@@ -351,6 +351,7 @@
     cut = call(
         k_over_x, [shape((16, 128))] * 4, (here, cut[0], *spun), [sm] + [vm] * 4, [pltpu.VMEM((40, 128), F32)]
     )
+    cut, g1, g2, g3 = lax.optimization_barrier((cut, g1, g2, g3))
     w = call(k_sum, shape((16, 128)), (cut[0], *[move(cut[m], lambda i: i ^ (8 * m)) for m in (1, 2, 3)]))
     w = call(k_sum, shape((16, 128)), (w, turn(w, 1), turn(w, 2), turn(w, 3)))
     w_far = swap(w)

time: 129 us -> 139 us (1.078)
  starting transfers between devices: 74.5 us -> 81.8 us
  waiting for transfers between devices: 34.3 us -> 36.8 us
    all_to_all x3, starting transfers between devices: 27.6 us -> 34 us  [exchange(): return lax.all_to_all(v, axis, split_axis=0, concat_axis=0, tiled=True)]
    ppermute x4, waiting for transfers between devices: 4.28 us -> 7.92 us  [swap(): return lax.ppermute(v, 'blk', [(i, i ^ 4) for i in range(8)])]
    ppermute x18, waiting for transfers between devices: 12.7 us -> 10.1 us  [turn(): lax.ppermute(v, 'blk', [(i, i // 4 * 4 + (i % 4 + k) % 4) for i in range(...]
    ppermute x7, starting transfers between devices: 9.34 us -> 11.2 us  [move(): return lax.ppermute(v, 'grp', [(i, to(i)) for i in range(32)])]
    ppermute x7, waiting for transfers between devices: 5.85 us -> 7.25 us  [move(): return lax.ppermute(v, 'grp', [(i, to(i)) for i in range(32)])]
  transfers between devices with their start and end apart: 32 -> 32, of which waited for: 16 -> 15; matrix products, arithmetic and copies ran while one was open for 0% -> 0% of each run, Pallas kernels for 9% -> 8%
where the time goes in v10:
time: 139 us
  starting transfers between devices  81.8 us (59%)
  waiting for transfers between devices  36.8 us (26%)
  Pallas kernels  18.9 us (14%)
    all_to_all x3, starting transfers between devices, exchange(): return lax.all_to_all(v, axis, split_axis=0, concat_axis=0, tiled=True)  34 us
    ppermute x18, starting transfers between devices, turn(): lax.ppermute(v, 'blk', [(i, i // 4 * 4 + (i % 4 + k) % 4) for i in range(...  22.4 us
    pallas_call x18, Pallas kernels, call(): pl.pallas_call(kernel, out_shape=out_shape, in_specs=[whole] * len(args)...  18.9 us
    ppermute x4, starting transfers between devices, swap(): return lax.ppermute(v, 'blk', [(i, i ^ 4) for i in range(8)])  14.3 us
    all_to_all x3, waiting for transfers between devices, exchange(): return lax.all_to_all(v, axis, split_axis=0, concat_axis=0, tiled=True)  11.5 us
    ppermute x7, starting transfers between devices, move(): return lax.ppermute(v, 'grp', [(i, to(i)) for i in range(32)])  11.2 us
    ppermute x18, waiting for transfers between devices, turn(): lax.ppermute(v, 'blk', [(i, i // 4 * 4 + (i % 4 + k) % 4) for i in range(...  10.1 us
    ppermute x4, waiting for transfers between devices, swap(): return lax.ppermute(v, 'blk', [(i, i ^ 4) for i in range(8)])  7.92 us
  transfers between devices with their start and end apart: 32, of which 15 were waited for; matrix products, arithmetic and copies ran while one was open for 0% of the time, Pallas kernels for 8%

profile of v10, /device:TPU:1, one launch (start us, length us, event | category | flops | bytes accessed | tf_op | source)
XLA Modules:
  0.0 138.8 jit_solution(17809133898678049861)
XLA Ops:
  0.7 2.3 %shard_map.164 = f32[32,40,128]{2,1,0:T(8,128)} custom-call(f32[256,128]{1,0:T(8,128)} %features.5, s32[32,32]{1,0:T(8,128)} %bitcast.14, s32[1,8]{1,0:T(1,128)} %bitcast.27), custom_call_target="tpu_custom_call" | custom-call | flops 268435456 | bytes 135200 | tf_op jit(solution)/shard_map/pallas_call | solution.py:45
  3.0 10.0 %all-to-all-start = ((f32[32,40,128]{2,1,0:T(8,128)}), f32[32,40,128]{2,1,0:T(8,128)S(1)}, u32[]{:S(2)}, u32[]{:S(2)}) async-start(f32[32,40,128]{2,1,0:T(8,128)} %shard_map.164), calls=%async_computation | async-start | bytes 1310720 | tf_op jit(solution)/shard_map/all_to_all | solution.py:299
  14.0 2.8 %collective-permute-start = (s32[32,128]{1,0:T(8,128)S(1)}, s32[32,128]{1,0:T(8,128)S(1)}, u32[]{:S(2)}, u32[]{:S(2)}) collective-permute-start(s32[32,128]{1,0:T(8,128)S(1)} %get-tuple-element.66), channel_id=1, source_target_pairs={{0,3},{1,0},{2,1},{3,2},{4,7},{5,4},{6,5},{7,6},{8,11},{9,8},{10,9... | collective-permute-start | bytes 49160 | tf_op jit(solution)/shard_map/ppermute | solution.py:296
  17.8 3.3 %collective-permute-done.1.l2 = s32[32,128]{1,0:T(8,128)S(1)} collective-permute-done((s32[32,128]{1,0:T(8,128)S(1)}, s32[32,128]{1,0:T(8,128)S(1)}, u32[]{:S(2)}, u32[]{:S(2)}) %collective-permute-start.1) | collective-permute-done | bytes 16416 | tf_op jit(solution)/shard_map/ppermute | solution.py:296
  21.4 4.3 %collective-permute-start.3 = (s32[64,128]{1,0:T(8,128)S(1)}, s32[64,128]{1,0:T(8,128)S(1)}, u32[]{:S(2)}, u32[]{:S(2)}) collective-permute-start(s32[64,128]{1,0:T(8,128)S(1)} %pad_add_fusion), channel_id=1, source_target_pairs={{0,4},{1,5},{2,6},{3,7},{4,0},{5,1},{6,2},{7,3},{8,12},{9,13},{10,... | collective-permute-start | bytes 98312 | tf_op jit(solution)/shard_map/ppermute | solution.py:293
  25.7 3.8 %collective-permute-done.3.far = s32[64,128]{1,0:T(8,128)S(1)} collective-permute-done((s32[64,128]{1,0:T(8,128)S(1)}, s32[64,128]{1,0:T(8,128)S(1)}, u32[]{:S(2)}, u32[]{:S(2)}) %collective-permute-start.3) | collective-permute-done | bytes 32800 | tf_op jit(solution)/shard_map/ppermute | solution.py:293
  29.5 2.3 %shard_map.167 = (bf16[8,256,512]{2,1,0:T(8,128)(2,1)S(1)}, s32[1]{0:T(128)}) custom-call(s32[1]{0:T(128)} %bitcast.pos, s32[32,128]{1,0:T(8,128)S(1)} %get-tuple-element.65.l0, s32[32,128]{1,0:T(8,128)S(1)} %collective-permute-done.l1, s32[32,128]{1,0:T(8,128)S(1)} %collective-permute-done.1.l2, s32[32,128]{1,0:T(8,128)S(1)} %collective-permute-done.2.l3, ...), custom_call_target="tpu_custom_call" | custom-call | flops 2147483648 | bytes 98308 | tf_op jit(solution)/shard_map/pallas_call | solution.py:45
  34.1 2.1 %collective-permute-start.4 = (f32[256,128]{1,0:T(8,128)S(1)}, f32[256,128]{1,0:T(8,128)S(1)}, u32[]{:S(2)}, u32[]{:S(2)}) collective-permute-start(f32[256,128]{1,0:T(8,128)S(1)} %get-tuple-element.73), channel_id=1, source_target_pairs={{0,1},{1,2},{2,3},{3,0},{4,5},{5,6},{6,7},{7,4},{8,9},{9,10},{10,1... | collective-permute-start | bytes 393224 | tf_op jit(solution)/shard_map/ppermute | solution.py:296
  36.1 1.5 %collective-permute-start.5 = (f32[256,128]{1,0:T(8,128)S(1)}, f32[256,128]{1,0:T(8,128)S(1)}, u32[]{:S(2)}, u32[]{:S(2)}) collective-permute-start(f32[256,128]{1,0:T(8,128)S(1)} %get-tuple-element.74), channel_id=1, source_target_pairs={{0,3},{1,0},{2,1},{3,2},{4,7},{5,4},{6,5},{7,6},{8,11},{9,8},{10,9... | collective-permute-start | bytes 393224 | tf_op jit(solution)/shard_map/ppermute | solution.py:296
  37.7 1.6 %collective-permute-start.6 = (f32[256,128]{1,0:T(8,128)S(1)}, f32[256,128]{1,0:T(8,128)S(1)}, u32[]{:S(2)}, u32[]{:S(2)}) collective-permute-start(f32[256,128]{1,0:T(8,128)S(1)} %get-tuple-element.75), channel_id=1, source_target_pairs={{0,2},{1,3},{2,0},{3,1},{4,6},{5,7},{6,4},{7,5},{8,10},{9,11},{10,... | collective-permute-start | bytes 393224 | tf_op jit(solution)/shard_map/ppermute | solution.py:296
  39.2 2.3 %shard_map.166 = (bf16[256,1024]{1,0:T(8,128)(2,1)S(1)}, bf16[1024,256]{1,0:T(8,128)(2,1)S(1)}, f32[256,128]{1,0:T(8,128)S(1)}, s32[1]{0:T(128)}) custom-call(s32[48,128]{1,0:T(8,128)S(1)} %get-tuple-element.61.own_to, s32[8,128]{1,0:T(8,128)S(1)} %bitcast.16, s32[8,128]{1,0:T(8,128)S(1)} %bitcast.19, s32[2,128]{1,0:T(2,128)S(1)} %bitcast.26), custom_call_target="tpu_custom_call" | custom-call | flops 2147483648 | bytes 33792 | tf_op jit(solution)/shard_map/pallas_call | solution.py:45
  41.6 4.0 %collective-permute-done.6 = f32[256,128]{1,0:T(8,128)S(1)} collective-permute-done((f32[256,128]{1,0:T(8,128)S(1)}, f32[256,128]{1,0:T(8,128)S(1)}, u32[]{:S(2)}, u32[]{:S(2)}) %collective-permute-start.6) | collective-permute-done | bytes 131104 | tf_op jit(solution)/shard_map/ppermute | solution.py:296
  46.2 4.1 %collective-permute-start.7 = (f32[256,128]{1,0:T(8,128)S(1)}, f32[256,128]{1,0:T(8,128)S(1)}, u32[]{:S(2)}, u32[]{:S(2)}) collective-permute-start(f32[256,128]{1,0:T(8,128)S(1)} %add_add_fusion), channel_id=1, source_target_pairs={{0,4},{1,5},{2,6},{3,7},{4,0},{5,1},{6,2},{7,3},{8,12},{9,13},{10,... | collective-permute-start | bytes 393224 | tf_op jit(solution)/shard_map/ppermute | solution.py:293
  53.0 1.6 %shard_map.170.bwd = bf16[8,512,256]{2,1,0:T(8,128)(2,1)S(1)} custom-call(s32[1]{0:T(128)} %bitcast.pos, s32[32,128]{1,0:T(8,128)S(1)} %get-tuple-element.65.l0, s32[32,128]{1,0:T(8,128)S(1)} %collective-permute-done.l1, s32[32,128]{1,0:T(8,128)S(1)} %collective-permute-done.1.l2, s32[32,128]{1,0:T(8,128)S(1)} %collective-permute-done.2.l3, ...), custom_call_target="tpu_custom_call" | custom-call | flops 2147483648 | bytes 98308 | tf_op jit(solution)/shard_map/pallas_call | solution.py:45
  57.3 1.7 %shard_map.179 = f32[1024,128]{1,0:T(8,128)} custom-call(s32[1]{0:T(128)} %get-tuple-element.62.flag, s32[8,128]{1,0:T(8,128)S(1)} %bitcast.18, s32[8,128]{1,0:T(8,128)S(1)} %bitcast.21, f32[256,128]{1,0:T(8,128)S(1)} %get-tuple-element.86.g0.grad_sum, bf16[1024,256]{1,0:T(8,128)(2,1)S(1)} %get-tuple-element.109.h_bwd), custom_call_target="tpu_custom_call" | custom-call | flops 268435456 | bytes 663556 | tf_op jit(solution)/shard_map/pallas_call | solution.py:45
  59.0 7.6 %all-to-all-start.2 = ((f32[32,32,128]{2,1,0:T(8,128)}), f32[32,32,128]{2,1,0:T(8,128)S(1)}, u32[]{:S(2)}, u32[]{:S(2)}) async-start(f32[32,32,128]{2,1,0:T(8,128)} %bitcast.12), calls=%async_computation.2 | async-start | bytes 1048576 | tf_op jit(solution)/shard_map/all_to_all | solution.py:299
  67.4 3.3 %collective-permute-start.18 = (f32[256,128]{1,0:T(8,128)S(1)}, f32[256,128]{1,0:T(8,128)S(1)}, u32[]{:S(2)}, u32[]{:S(2)}) collective-permute-start(f32[256,128]{1,0:T(8,128)S(1)} %get-tuple-element.86.g0.grad_sum), channel_id=1, source_target_pairs={{0,4},{1,5},{2,6},{3,7},{4,0},{5,1},{6,2},{7,3},{8,12},{9,13},{10,... | collective-permute-start | bytes 393224 | tf_op jit(solution)/shard_map/ppermute | solution.py:293
  70.7 1.6 %collective-permute-start.15 = (f32[256,128]{1,0:T(8,128)S(1)}, f32[256,128]{1,0:T(8,128)S(1)}, u32[]{:S(2)}, u32[]{:S(2)}) collective-permute-start(f32[256,128]{1,0:T(8,128)S(1)} %get-tuple-element.86.g0.grad_sum), channel_id=1, source_target_pairs={{0,3},{1,0},{2,1},{3,2},{4,7},{5,4},{6,5},{7,6},{8,11},{9,8},{10,9... | collective-permute-start | bytes 393224 | tf_op jit(solution)/shard_map/ppermute | solution.py:296
  73.6 1.6 %collective-permute-start.12 = (f32[40,128]{1,0:T(8,128)S(1)}, f32[40,128]{1,0:T(8,128)S(1)}, u32[]{:S(2)}, u32[]{:S(2)}) collective-permute-start(f32[40,128]{1,0:T(8,128)S(1)} %get-tuple-element.92), channel_id=1, source_target_pairs={{0,16},{8,24},{16,32},{24,40},{32,48},{40,56},{48,0},{56,8},{64,80... | collective-permute-start | bytes 61448 | tf_op jit(solution)/shard_map/ppermute | solution.py:341
  75.2 2.7 %collective-permute-done.12.b = f32[40,128]{1,0:T(8,128)S(1)} collective-permute-done((f32[40,128]{1,0:T(8,128)S(1)}, f32[40,128]{1,0:T(8,128)S(1)}, u32[]{:S(2)}, u32[]{:S(2)}) %collective-permute-start.12) | collective-permute-done | bytes 20512 | tf_op jit(solution)/shard_map/ppermute | solution.py:341
  78.0 1.7 %collective-permute-start.13 = (f32[40,128]{1,0:T(8,128)S(1)}, f32[40,128]{1,0:T(8,128)S(1)}, u32[]{:S(2)}, u32[]{:S(2)}) collective-permute-start(f32[40,128]{1,0:T(8,128)S(1)} %get-tuple-element.93), channel_id=1, source_target_pairs={{0,32},{8,40},{16,48},{24,56},{32,0},{40,8},{48,16},{56,24},{64,96... | collective-permute-start | bytes 61448 | tf_op jit(solution)/shard_map/ppermute | solution.py:341
  79.7 2.7 %collective-permute-done.13.c = f32[40,128]{1,0:T(8,128)S(1)} collective-permute-done((f32[40,128]{1,0:T(8,128)S(1)}, f32[40,128]{1,0:T(8,128)S(1)}, u32[]{:S(2)}, u32[]{:S(2)}) %collective-permute-start.13) | collective-permute-done | bytes 20512 | tf_op jit(solution)/shard_map/ppermute | solution.py:341
  85.0 1.6 %collective-permute-start.19 = (f32[256,128]{1,0:T(8,128)S(1)}, f32[256,128]{1,0:T(8,128)S(1)}, u32[]{:S(2)}, u32[]{:S(2)}) collective-permute-start(f32[256,128]{1,0:T(8,128)S(1)} %collective-permute-done.18.g4), channel_id=1, source_target_pairs={{0,3},{1,0},{2,1},{3,2},{4,7},{5,4},{6,5},{7,6},{8,11},{9,8},{10,9... | collective-permute-start | bytes 393224 | tf_op jit(solution)/shard_map/ppermute | solution.py:296
  88.6 2.1 %collective-permute-start.22 = (f32[16,128]{1,0:T(8,128)S(1)}, f32[16,128]{1,0:T(8,128)S(1)}, u32[]{:S(2)}, u32[]{:S(2)}) collective-permute-start(f32[16,128]{1,0:T(8,128)S(1)} %get-tuple-element.105), channel_id=1, source_target_pairs={{0,64},{8,72},{16,80},{24,88},{32,96},{40,104},{48,112},{56,120},{... | collective-permute-start | bytes 24584 | tf_op jit(solution)/shard_map/ppermute | solution.py:341
  92.2 2.5 %collective-permute-start.24 = (f32[16,128]{1,0:T(8,128)S(1)}, f32[16,128]{1,0:T(8,128)S(1)}, u32[]{:S(2)}, u32[]{:S(2)}) collective-permute-start(f32[16,128]{1,0:T(8,128)S(1)} %get-tuple-element.107), channel_id=1, source_target_pairs={{0,192},{8,200},{16,208},{24,216},{32,224},{40,232},{48,240},{56,2... | collective-permute-start | bytes 24584 | tf_op jit(solution)/shard_map/ppermute | solution.py:341
  94.7 1.8 %collective-permute-done.24.d = f32[16,128]{1,0:T(8,128)S(1)} collective-permute-done((f32[16,128]{1,0:T(8,128)S(1)}, f32[16,128]{1,0:T(8,128)S(1)}, u32[]{:S(2)}, u32[]{:S(2)}) %collective-permute-start.24) | collective-permute-done | bytes 8224 | tf_op jit(solution)/shard_map/ppermute | solution.py:341
  97.0 2.6 %collective-permute-start.26 = (f32[16,128]{1,0:T(8,128)S(1)}, f32[16,128]{1,0:T(8,128)S(1)}, u32[]{:S(2)}, u32[]{:S(2)}) collective-permute-start(f32[16,128]{1,0:T(8,128)S(1)} %shard_map.176.a), channel_id=1, source_target_pairs={{0,2},{1,3},{2,0},{3,1},{4,6},{5,7},{6,4},{7,5},{8,10},{9,11},{10,... | collective-permute-start | bytes 24584 | tf_op jit(solution)/shard_map/ppermute | solution.py:296
  101.0 1.7 %collective-permute-done.27.d = f32[16,128]{1,0:T(8,128)S(1)} collective-permute-done((f32[16,128]{1,0:T(8,128)S(1)}, f32[16,128]{1,0:T(8,128)S(1)}, u32[]{:S(2)}, u32[]{:S(2)}) %collective-permute-start.27) | collective-permute-done | bytes 8224 | tf_op jit(solution)/shard_map/ppermute | solution.py:296
  102.7 2.6 %collective-permute-start.28 = (f32[16,128]{1,0:T(8,128)S(1)}, f32[16,128]{1,0:T(8,128)S(1)}, u32[]{:S(2)}, u32[]{:S(2)}) collective-permute-start(f32[16,128]{1,0:T(8,128)S(1)} %shard_map.177.near), channel_id=1, source_target_pairs={{0,4},{1,5},{2,6},{3,7},{4,0},{5,1},{6,2},{7,3},{8,12},{9,13},{10,... | collective-permute-start | bytes 24584 | tf_op jit(solution)/shard_map/ppermute | solution.py:293
  106.7 2.5 %collective-permute-done.28.far = f32[16,128]{1,0:T(8,128)S(1)} collective-permute-done((f32[16,128]{1,0:T(8,128)S(1)}, f32[16,128]{1,0:T(8,128)S(1)}, u32[]{:S(2)}, u32[]{:S(2)}) %collective-permute-start.28) | collective-permute-done | bytes 8224 | tf_op jit(solution)/shard_map/ppermute | solution.py:293
  110.0 16.4 %all-to-all-start.1 = ((f32[32,16,128]{2,1,0:T(8,128)}), f32[32,16,128]{2,1,0:T(8,128)S(1)}, u32[]{:S(2)}, u32[]{:S(2)}) async-start(f32[32,16,128]{2,1,0:T(8,128)} %get-tuple-element.108), calls=%async_computation.1 | async-start | bytes 524288 | tf_op jit(solution)/shard_map/all_to_all | solution.py:299
  126.8 10.7 %all-to-all-done.1.last = f32[32,16,128]{2,1,0:T(8,128)S(1)} async-done(((f32[32,16,128]{2,1,0:T(8,128)}), f32[32,16,128]{2,1,0:T(8,128)S(1)}, u32[]{:S(2)}, u32[]{:S(2)}) %all-to-all-start.1) | async-done | bytes 262176 | tf_op jit(solution)/shard_map/all_to_all | solution.py:299
  (83 shorter events, 24.4 us)
Async XLA Ops:
  3.0 29.7 %all-to-all-start = ((f32[32,40,128]{2,1,0:T(8,128)}), f32[32,40,128]{2,1,0:T(8,128)S(1)}, u32[]{:S(2)}, u32[]{:S(2)}) async-start(f32[32,40,128]{2,1,0:T(8,128)} %shard_map.164), calls=%async_computation | async-start | bytes 1310720 | tf_op jit(solution)/shard_map/all_to_all | solution.py:299
  14.0 3.9 %collective-permute-start = (s32[32,128]{1,0:T(8,128)S(1)}, s32[32,128]{1,0:T(8,128)S(1)}, u32[]{:S(2)}, u32[]{:S(2)}) collective-permute-start(s32[32,128]{1,0:T(8,128)S(1)} %get-tuple-element.66), channel_id=1, source_target_pairs={{0,3},{1,0},{2,1},{3,2},{4,7},{5,4},{6,5},{7,6},{8,11},{9,8},{10,9... | collective-permute-start | bytes 49160 | tf_op jit(solution)/shard_map/ppermute | solution.py:296
  16.8 4.4 %collective-permute-start.1 = (s32[32,128]{1,0:T(8,128)S(1)}, s32[32,128]{1,0:T(8,128)S(1)}, u32[]{:S(2)}, u32[]{:S(2)}) collective-permute-start(s32[32,128]{1,0:T(8,128)S(1)} %get-tuple-element.67), channel_id=1, source_target_pairs={{0,2},{1,3},{2,0},{3,1},{4,6},{5,7},{6,4},{7,5},{8,10},{9,11},{10,... | collective-permute-start | bytes 49160 | tf_op jit(solution)/shard_map/ppermute | solution.py:296
  17.1 4.2 %collective-permute-start.2 = (s32[32,128]{1,0:T(8,128)S(1)}, s32[32,128]{1,0:T(8,128)S(1)}, u32[]{:S(2)}, u32[]{:S(2)}) collective-permute-start(s32[32,128]{1,0:T(8,128)S(1)} %get-tuple-element.68), channel_id=1, source_target_pairs={{0,1},{1,2},{2,3},{3,0},{4,5},{5,6},{6,7},{7,4},{8,9},{9,10},{10,1... | collective-permute-start | bytes 49160 | tf_op jit(solution)/shard_map/ppermute | solution.py:296
  21.4 8.1 %collective-permute-start.3 = (s32[64,128]{1,0:T(8,128)S(1)}, s32[64,128]{1,0:T(8,128)S(1)}, u32[]{:S(2)}, u32[]{:S(2)}) collective-permute-start(s32[64,128]{1,0:T(8,128)S(1)} %pad_add_fusion), channel_id=1, source_target_pairs={{0,4},{1,5},{2,6},{3,7},{4,0},{5,1},{6,2},{7,3},{8,12},{9,13},{10,... | collective-permute-start | bytes 98312 | tf_op jit(solution)/shard_map/ppermute | solution.py:293
  34.1 7.5 %collective-permute-start.4 = (f32[256,128]{1,0:T(8,128)S(1)}, f32[256,128]{1,0:T(8,128)S(1)}, u32[]{:S(2)}, u32[]{:S(2)}) collective-permute-start(f32[256,128]{1,0:T(8,128)S(1)} %get-tuple-element.73), channel_id=1, source_target_pairs={{0,1},{1,2},{2,3},{3,0},{4,5},{5,6},{6,7},{7,4},{8,9},{9,10},{10,1... | collective-permute-start | bytes 393224 | tf_op jit(solution)/shard_map/ppermute | solution.py:296
  36.1 5.5 %collective-permute-start.5 = (f32[256,128]{1,0:T(8,128)S(1)}, f32[256,128]{1,0:T(8,128)S(1)}, u32[]{:S(2)}, u32[]{:S(2)}) collective-permute-start(f32[256,128]{1,0:T(8,128)S(1)} %get-tuple-element.74), channel_id=1, source_target_pairs={{0,3},{1,0},{2,1},{3,2},{4,7},{5,4},{6,5},{7,6},{8,11},{9,8},{10,9... | collective-permute-start | bytes 393224 | tf_op jit(solution)/shard_map/ppermute | solution.py:296
  37.7 7.9 %collective-permute-start.6 = (f32[256,128]{1,0:T(8,128)S(1)}, f32[256,128]{1,0:T(8,128)S(1)}, u32[]{:S(2)}, u32[]{:S(2)}) collective-permute-start(f32[256,128]{1,0:T(8,128)S(1)} %get-tuple-element.75), channel_id=1, source_target_pairs={{0,2},{1,3},{2,0},{3,1},{4,6},{5,7},{6,4},{7,5},{8,10},{9,11},{10,... | collective-permute-start | bytes 393224 | tf_op jit(solution)/shard_map/ppermute | solution.py:296
  45.7 9.8 %collective-permute-start.10 = (f32[256,128]{1,0:T(8,128)S(1)}, f32[256,128]{1,0:T(8,128)S(1)}, u32[]{:S(2)}, u32[]{:S(2)}) collective-permute-start(f32[256,128]{1,0:T(8,128)S(1)} %get-tuple-element.82), channel_id=1, source_target_pairs={{0,2},{1,3},{2,0},{3,1},{4,6},{5,7},{6,4},{7,5},{8,10},{9,11},{10,... | collective-permute-start | bytes 393224 | tf_op jit(solution)/shard_map/ppermute | solution.py:296
  46.2 9.8 %collective-permute-start.7 = (f32[256,128]{1,0:T(8,128)S(1)}, f32[256,128]{1,0:T(8,128)S(1)}, u32[]{:S(2)}, u32[]{:S(2)}) collective-permute-start(f32[256,128]{1,0:T(8,128)S(1)} %add_add_fusion), channel_id=1, source_target_pairs={{0,4},{1,5},{2,6},{3,7},{4,0},{5,1},{6,2},{7,3},{8,12},{9,13},{10,... | collective-permute-start | bytes 393224 | tf_op jit(solution)/shard_map/ppermute | solution.py:293
  50.3 5.7 %collective-permute-start.8 = (f32[256,128]{1,0:T(8,128)S(1)}, f32[256,128]{1,0:T(8,128)S(1)}, u32[]{:S(2)}, u32[]{:S(2)}) collective-permute-start(f32[256,128]{1,0:T(8,128)S(1)} %get-tuple-element.80), channel_id=1, source_target_pairs={{0,1},{1,2},{2,3},{3,0},{4,5},{5,6},{6,7},{7,4},{8,9},{9,10},{10,1... | collective-permute-start | bytes 393224 | tf_op jit(solution)/shard_map/ppermute | solution.py:296
  51.6 4.4 %collective-permute-start.9 = (f32[256,128]{1,0:T(8,128)S(1)}, f32[256,128]{1,0:T(8,128)S(1)}, u32[]{:S(2)}, u32[]{:S(2)}) collective-permute-start(f32[256,128]{1,0:T(8,128)S(1)} %get-tuple-element.81), channel_id=1, source_target_pairs={{0,3},{1,0},{2,1},{3,2},{4,7},{5,4},{6,5},{7,6},{8,11},{9,8},{10,9... | collective-permute-start | bytes 393224 | tf_op jit(solution)/shard_map/ppermute | solution.py:296
  59.0 51.0 %all-to-all-start.2 = ((f32[32,32,128]{2,1,0:T(8,128)}), f32[32,32,128]{2,1,0:T(8,128)S(1)}, u32[]{:S(2)}, u32[]{:S(2)}) async-start(f32[32,32,128]{2,1,0:T(8,128)} %bitcast.12), calls=%async_computation.2 | async-start | bytes 1048576 | tf_op jit(solution)/shard_map/all_to_all | solution.py:299
  67.0 6.6 %collective-permute-start.11 = (f32[136,128]{1,0:T(8,128)S(1)}, f32[136,128]{1,0:T(8,128)S(1)}, u32[]{:S(2)}, u32[]{:S(2)}) collective-permute-start(f32[136,128]{1,0:T(8,128)S(1)} %get-tuple-element.90), channel_id=1, source_target_pairs={{0,8},{8,0},{16,24},{24,16},{32,40},{40,32},{48,56},{56,48},{64,72... | collective-permute-start | bytes 208904 | tf_op jit(solution)/shard_map/ppermute | solution.py:341
  67.4 17.6 %collective-permute-start.18 = (f32[256,128]{1,0:T(8,128)S(1)}, f32[256,128]{1,0:T(8,128)S(1)}, u32[]{:S(2)}, u32[]{:S(2)}) collective-permute-start(f32[256,128]{1,0:T(8,128)S(1)} %get-tuple-element.86.g0.grad_sum), channel_id=1, source_target_pairs={{0,4},{1,5},{2,6},{3,7},{4,0},{5,1},{6,2},{7,3},{8,12},{9,13},{10,... | collective-permute-start | bytes 393224 | tf_op jit(solution)/shard_map/ppermute | solution.py:293
  70.7 17.2 %collective-permute-start.15 = (f32[256,128]{1,0:T(8,128)S(1)}, f32[256,128]{1,0:T(8,128)S(1)}, u32[]{:S(2)}, u32[]{:S(2)}) collective-permute-start(f32[256,128]{1,0:T(8,128)S(1)} %get-tuple-element.86.g0.grad_sum), channel_id=1, source_target_pairs={{0,3},{1,0},{2,1},{3,2},{4,7},{5,4},{6,5},{7,6},{8,11},{9,8},{10,9... | collective-permute-start | bytes 393224 | tf_op jit(solution)/shard_map/ppermute | solution.py:296
  72.2 16.4 %collective-permute-start.16 = (f32[256,128]{1,0:T(8,128)S(1)}, f32[256,128]{1,0:T(8,128)S(1)}, u32[]{:S(2)}, u32[]{:S(2)}) collective-permute-start(f32[256,128]{1,0:T(8,128)S(1)} %get-tuple-element.86.g0.grad_sum), channel_id=1, source_target_pairs={{0,2},{1,3},{2,0},{3,1},{4,6},{5,7},{6,4},{7,5},{8,10},{9,11},{10,... | collective-permute-start | bytes 393224 | tf_op jit(solution)/shard_map/ppermute | solution.py:296
  73.6 15.0 %collective-permute-start.17 = (f32[256,128]{1,0:T(8,128)S(1)}, f32[256,128]{1,0:T(8,128)S(1)}, u32[]{:S(2)}, u32[]{:S(2)}) collective-permute-start(f32[256,128]{1,0:T(8,128)S(1)} %get-tuple-element.86.g0.grad_sum), channel_id=1, source_target_pairs={{0,1},{1,2},{2,3},{3,0},{4,5},{5,6},{6,7},{7,4},{8,9},{9,10},{10,1... | collective-permute-start | bytes 393224 | tf_op jit(solution)/shard_map/ppermute | solution.py:296
  73.6 4.3 %collective-permute-start.12 = (f32[40,128]{1,0:T(8,128)S(1)}, f32[40,128]{1,0:T(8,128)S(1)}, u32[]{:S(2)}, u32[]{:S(2)}) collective-permute-start(f32[40,128]{1,0:T(8,128)S(1)} %get-tuple-element.92), channel_id=1, source_target_pairs={{0,16},{8,24},{16,32},{24,40},{32,48},{40,56},{48,0},{56,8},{64,80... | collective-permute-start | bytes 61448 | tf_op jit(solution)/shard_map/ppermute | solution.py:341
  78.0 4.4 %collective-permute-start.13 = (f32[40,128]{1,0:T(8,128)S(1)}, f32[40,128]{1,0:T(8,128)S(1)}, u32[]{:S(2)}, u32[]{:S(2)}) collective-permute-start(f32[40,128]{1,0:T(8,128)S(1)} %get-tuple-element.93), channel_id=1, source_target_pairs={{0,32},{8,40},{16,48},{24,56},{32,0},{40,8},{48,16},{56,24},{64,96... | collective-permute-start | bytes 61448 | tf_op jit(solution)/shard_map/ppermute | solution.py:341
  82.4 4.1 %collective-permute-start.14 = (f32[40,128]{1,0:T(8,128)S(1)}, f32[40,128]{1,0:T(8,128)S(1)}, u32[]{:S(2)}, u32[]{:S(2)}) collective-permute-start(f32[40,128]{1,0:T(8,128)S(1)} %get-tuple-element.94), channel_id=1, source_target_pairs={{0,48},{8,56},{16,0},{24,8},{32,16},{40,24},{48,32},{56,40},{64,11... | collective-permute-start | bytes 61448 | tf_op jit(solution)/shard_map/ppermute | solution.py:341
  85.0 20.3 %collective-permute-start.19 = (f32[256,128]{1,0:T(8,128)S(1)}, f32[256,128]{1,0:T(8,128)S(1)}, u32[]{:S(2)}, u32[]{:S(2)}) collective-permute-start(f32[256,128]{1,0:T(8,128)S(1)} %collective-permute-done.18.g4), channel_id=1, source_target_pairs={{0,3},{1,0},{2,1},{3,2},{4,7},{5,4},{6,5},{7,6},{8,11},{9,8},{10,9... | collective-permute-start | bytes 393224 | tf_op jit(solution)/shard_map/ppermute | solution.py:296
  86.5 18.8 %collective-permute-start.20 = (f32[256,128]{1,0:T(8,128)S(1)}, f32[256,128]{1,0:T(8,128)S(1)}, u32[]{:S(2)}, u32[]{:S(2)}) collective-permute-start(f32[256,128]{1,0:T(8,128)S(1)} %collective-permute-done.18.g4), channel_id=1, source_target_pairs={{0,2},{1,3},{2,0},{3,1},{4,6},{5,7},{6,4},{7,5},{8,10},{9,11},{10,... | collective-permute-start | bytes 393224 | tf_op jit(solution)/shard_map/ppermute | solution.py:296
  87.9 17.4 %collective-permute-start.21 = (f32[256,128]{1,0:T(8,128)S(1)}, f32[256,128]{1,0:T(8,128)S(1)}, u32[]{:S(2)}, u32[]{:S(2)}) collective-permute-start(f32[256,128]{1,0:T(8,128)S(1)} %collective-permute-done.18.g4), channel_id=1, source_target_pairs={{0,1},{1,2},{2,3},{3,0},{4,5},{5,6},{6,7},{7,4},{8,9},{9,10},{10,1... | collective-permute-start | bytes 393224 | tf_op jit(solution)/shard_map/ppermute | solution.py:296
  88.6 3.6 %collective-permute-start.22 = (f32[16,128]{1,0:T(8,128)S(1)}, f32[16,128]{1,0:T(8,128)S(1)}, u32[]{:S(2)}, u32[]{:S(2)}) collective-permute-start(f32[16,128]{1,0:T(8,128)S(1)} %get-tuple-element.105), channel_id=1, source_target_pairs={{0,64},{8,72},{16,80},{24,88},{32,96},{40,104},{48,112},{56,120},{... | collective-permute-start | bytes 24584 | tf_op jit(solution)/shard_map/ppermute | solution.py:341
  90.7 4.0 %collective-permute-start.23 = (f32[16,128]{1,0:T(8,128)S(1)}, f32[16,128]{1,0:T(8,128)S(1)}, u32[]{:S(2)}, u32[]{:S(2)}) collective-permute-start(f32[16,128]{1,0:T(8,128)S(1)} %get-tuple-element.106), channel_id=1, source_target_pairs={{0,128},{8,136},{16,144},{24,152},{32,160},{40,168},{48,176},{56,1... | collective-permute-start | bytes 24584 | tf_op jit(solution)/shard_map/ppermute | solution.py:341
  92.2 4.3 %collective-permute-start.24 = (f32[16,128]{1,0:T(8,128)S(1)}, f32[16,128]{1,0:T(8,128)S(1)}, u32[]{:S(2)}, u32[]{:S(2)}) collective-permute-start(f32[16,128]{1,0:T(8,128)S(1)} %get-tuple-element.107), channel_id=1, source_target_pairs={{0,192},{8,200},{16,208},{24,216},{32,224},{40,232},{48,240},{56,2... | collective-permute-start | bytes 24584 | tf_op jit(solution)/shard_map/ppermute | solution.py:341
  96.5 3.7 %collective-permute-start.25 = (f32[16,128]{1,0:T(8,128)S(1)}, f32[16,128]{1,0:T(8,128)S(1)}, u32[]{:S(2)}, u32[]{:S(2)}) collective-permute-start(f32[16,128]{1,0:T(8,128)S(1)} %shard_map.176.a), channel_id=1, source_target_pairs={{0,1},{1,2},{2,3},{3,0},{4,5},{5,6},{6,7},{7,4},{8,9},{9,10},{10,1... | collective-permute-start | bytes 24584 | tf_op jit(solution)/shard_map/ppermute | solution.py:296
  97.0 4.0 %collective-permute-start.26 = (f32[16,128]{1,0:T(8,128)S(1)}, f32[16,128]{1,0:T(8,128)S(1)}, u32[]{:S(2)}, u32[]{:S(2)}) collective-permute-start(f32[16,128]{1,0:T(8,128)S(1)} %shard_map.176.a), channel_id=1, source_target_pairs={{0,2},{1,3},{2,0},{3,1},{4,6},{5,7},{6,4},{7,5},{8,10},{9,11},{10,... | collective-permute-start | bytes 24584 | tf_op jit(solution)/shard_map/ppermute | solution.py:296
  100.2 2.5 %collective-permute-start.27 = (f32[16,128]{1,0:T(8,128)S(1)}, f32[16,128]{1,0:T(8,128)S(1)}, u32[]{:S(2)}, u32[]{:S(2)}) collective-permute-start(f32[16,128]{1,0:T(8,128)S(1)} %shard_map.176.a), channel_id=1, source_target_pairs={{0,3},{1,0},{2,1},{3,2},{4,7},{5,4},{6,5},{7,6},{8,11},{9,8},{10,9... | collective-permute-start | bytes 24584 | tf_op jit(solution)/shard_map/ppermute | solution.py:296
  102.7 6.5 %collective-permute-start.28 = (f32[16,128]{1,0:T(8,128)S(1)}, f32[16,128]{1,0:T(8,128)S(1)}, u32[]{:S(2)}, u32[]{:S(2)}) collective-permute-start(f32[16,128]{1,0:T(8,128)S(1)} %shard_map.177.near), channel_id=1, source_target_pairs={{0,4},{1,5},{2,6},{3,7},{4,0},{5,1},{6,2},{7,3},{8,12},{9,13},{10,... | collective-permute-start | bytes 24584 | tf_op jit(solution)/shard_map/ppermute | solution.py:293
  110.0 27.5 %all-to-all-start.1 = ((f32[32,16,128]{2,1,0:T(8,128)}), f32[32,16,128]{2,1,0:T(8,128)S(1)}, u32[]{:S(2)}, u32[]{:S(2)}) async-start(f32[32,16,128]{2,1,0:T(8,128)} %get-tuple-element.108), calls=%async_computation.1 | async-start | bytes 524288 | tf_op jit(solution)/shard_map/all_to_all | solution.py:299
  (13 other events, 176.0 us)

commit v11 on v6

--- a/solution.py
+++ b/solution.py
@@ -203,10 +203,9 @@
         out[p, 8:16, :] = fill
 
 
-def k_slots(flag, halo_to, halo_from, grad_sum, h_bwd, grad_pre, w_root, out, root):
+def k_slots(flag, halo_to, halo_from, grad_sum, h_bwd, out):
     x = halves(grad_sum[...])
     out[...] = joined(dot(h_bwd[...], x))
-    root[...] = dot(grad_pre[...], w_root[...], NT, HIGH)
 
     @pl.when(flag[0] != 0)
     def _():
@@ -214,7 +213,7 @@
         out[...] += joined(dot(rest(dot(frm, to, NT)), x))
 
 
-def k_back(flag, pos, l0, l1, l2, l3, far, g0, g1, g2, g3, g4, g5, g6, g7, bwd, root, local, hubs, total):
+def k_back(flag, pos, l0, l1, l2, l3, far, g0, g1, g2, g3, g4, g5, g6, g7, bwd, local, hubs, total):
     xs = [halves(g[0:256, :]) for g in (g0, g1, g2, g3, g4, g5, g6, g7)]
     acc = dot(bwd[0], xs[0])
     for r in range(1, 8):
@@ -227,7 +226,7 @@
             total[...] += joined(dot(rest(backward_count(*hots(pos, block))), xs[r]))
 
     hubs[...] = total[256:512, :].reshape(32, 8, 128)
-    local[...] = root[...] + total[0:256, :]
+    local[...] = total[0:256, :]
 
 
 def k_sum(weights, out):
@@ -242,8 +241,9 @@
     bias[...] = w[8:9]
 
 
-def k_scatter(returned, send, local, out):
-    out[...] = local[...] + joined(dot(send_hot(send), halves(returned[...].reshape(1024, 128))))
+def k_scatter(returned, send, local, grad_pre, w_root, out):
+    root = dot(grad_pre[...], w_root[...], NT, HIGH)
+    out[...] = local[...] + root + joined(dot(send_hot(send), halves(returned[...].reshape(1024, 128))))
 
 
 def k_final(last, hub, local, out, w_neigh, w_root):
@@ -302,7 +302,7 @@
     other = part[4] + turn(part[5], 1) + turn(part[7], 3) + turn(part[6], 2)
     other, p1, p2, p3 = lax.optimization_barrier((other, part[1], part[2], part[3]))
     other = swap(other)
-    near = [turn(p1, 1), turn(p3, 3), turn(p2, 2)]
+    near = [turn(p2, 2), turn(p1, 1), turn(p3, 3)]
     own = call(k_halo, block, (h_flag, halo_to, halo_from, incoming, h_fwd, part[0]), [sm] + [vm] * 5)
     inv, bwd = lax.optimization_barrier((inv, bwd))
     output, grad_pre, grad_sum, mean = call(
@@ -311,10 +311,7 @@
     g4 = swap(grad_sum)
     g1, g3, g2 = turn(grad_sum, 3), turn(grad_sum, 1), turn(grad_sum, 2)
     weights = exchange(call(k_weights, shape((32, 16, 128)), (grad_pre, mean, features)), "grp")
-    slots, root = call(
-        k_slots, [shape((1024, 128)), block], (h_flag, halo_to, halo_from, grad_sum, h_bwd, grad_pre, w_root),
-        [sm] + [vm] * 6,
-    )
+    slots = call(k_slots, shape((1024, 128)), (h_flag, halo_to, halo_from, grad_sum, h_bwd), [sm] + [vm] * 4)
     g4, weights, g1, g2, g3, slots = lax.optimization_barrier((g4, weights, g1, g2, g3, slots))
     returned = exchange(slots.reshape(32, 32, 128), "grp")
     w = call(k_sum, shape((16, 128)), (weights,))
@@ -323,7 +320,7 @@
     g5, g7, g6 = turn(g4, 3), turn(g4, 1), turn(g4, 2)
     local, hubs = call(
         k_back, [block, shape((32, 8, 128))],
-        (flag, *lists, grad_sum, g1, g2, g3, g4, g5, g6, g7, bwd, root), [sm, *lm] + [vm] * 10,
+        (flag, *lists, grad_sum, g1, g2, g3, g4, g5, g6, g7, bwd), [sm, *lm] + [vm] * 9,
         [pltpu.VMEM((512, 128), F32)],
     )
     factor = (256 * lax.axis_size("grp") * lax.axis_size("blk")) ** (-0.5)
@@ -331,7 +328,7 @@
         functools.partial(k_pack, factor), [shape((32, 16, 128)), shape((1, 128))], (hubs, w, w_far)
     )
     last = exchange(last, "grp")
-    local = call(k_scatter, block, (returned, send, local))
+    local = call(k_scatter, block, (returned, send, local, grad_pre, w_root))
     grad_features, grad_wn, grad_wr = call(
         k_final, [block, shape((128, 128)), shape((128, 128))], (last, hub, local), [vm, sm, vm]
     )

time: 129 us -> 133 us (1.031)
  waiting for transfers between devices: 30.8 us -> 36.7 us
  starting transfers between devices: 69.4 us -> 64.6 us
  local copies, waits for them, and re-layouts: 6.71 us -> 9.45 us
    unnamed x44 -> x64, local copies, waits for them, and re-layouts: 6.61 us -> 9.35 us
    ppermute x4, waiting for transfers between devices: 5.15 us -> 7.84 us  [swap(): return lax.ppermute(v, 'blk', [(i, i ^ 4) for i in range(8)])]
    ppermute x18, waiting for transfers between devices: 13.2 us -> 15.5 us  [turn(): lax.ppermute(v, 'blk', [(i, i // 4 * 4 + (i % 4 + k) % 4) for i in range(...]
    ppermute x18, starting transfers between devices: 21.1 us -> 19.1 us  [turn(): lax.ppermute(v, 'blk', [(i, i // 4 * 4 + (i % 4 + k) % 4) for i in range(...]
    all_to_all x4, starting transfers between devices: 33.3 us -> 31.6 us  [exchange(): return lax.all_to_all(v, axis, split_axis=0, concat_axis=0, tiled=True)]
where the time goes in v11:
time: 133 us
  starting transfers between devices  64.6 us (49%)
  waiting for transfers between devices  36.7 us (28%)
  Pallas kernels  20.7 us (16%)
  local copies, waits for them, and re-layouts  9.45 us (7%)
    all_to_all x4, starting transfers between devices, exchange(): return lax.all_to_all(v, axis, split_axis=0, concat_axis=0, tiled=True)  31.6 us
    pallas_call x15, Pallas kernels, call(): pl.pallas_call(kernel, out_shape=out_shape, in_specs=[whole] * len(args)...  20.7 us
    ppermute x18, starting transfers between devices, turn(): lax.ppermute(v, 'blk', [(i, i // 4 * 4 + (i % 4 + k) % 4) for i in range(...  19.1 us
    ppermute x18, waiting for transfers between devices, turn(): lax.ppermute(v, 'blk', [(i, i // 4 * 4 + (i % 4 + k) % 4) for i in range(...  15.5 us
    ppermute x4, starting transfers between devices, swap(): return lax.ppermute(v, 'blk', [(i, i ^ 4) for i in range(8)])  13.9 us
    all_to_all x4, waiting for transfers between devices, exchange(): return lax.all_to_all(v, axis, split_axis=0, concat_axis=0, tiled=True)  13.4 us
    unnamed x64, local copies, waits for them, and re-layouts  9.35 us
    ppermute x4, waiting for transfers between devices, swap(): return lax.ppermute(v, 'blk', [(i, i ^ 4) for i in range(8)])  7.84 us
  transfers between devices with their start and end apart: 26, of which 12 were waited for; matrix products, arithmetic and copies ran while one was open for 0% of the time, Pallas kernels for 10%

profile of v11, /device:TPU:1, one launch (start us, length us, event | category | flops | bytes accessed | tf_op | source)
XLA Modules:
  0.0 132.5 jit_solution(5217859253772377133)
XLA Ops:
  0.7 2.3 %shard_map.164 = f32[32,40,128]{2,1,0:T(8,128)} custom-call(f32[256,128]{1,0:T(8,128)} %features.5, s32[32,32]{1,0:T(8,128)} %bitcast.13, s32[1,8]{1,0:T(1,128)} %bitcast.26), custom_call_target="tpu_custom_call" | custom-call | flops 268435456 | bytes 135200 | tf_op jit(solution)/shard_map/pallas_call | solution.py:45
  3.0 10.0 %all-to-all-start = ((f32[32,40,128]{2,1,0:T(8,128)}), f32[32,40,128]{2,1,0:T(8,128)S(1)}, u32[]{:S(2)}, u32[]{:S(2)}) async-start(f32[32,40,128]{2,1,0:T(8,128)} %shard_map.164), calls=%async_computation | async-start | bytes 1310720 | tf_op jit(solution)/shard_map/all_to_all | solution.py:276
  14.0 2.8 %collective-permute-start = (s32[32,128]{1,0:T(8,128)S(1)}, s32[32,128]{1,0:T(8,128)S(1)}, u32[]{:S(2)}, u32[]{:S(2)}) collective-permute-start(s32[32,128]{1,0:T(8,128)S(1)} %get-tuple-element.55), channel_id=1, source_target_pairs={{0,3},{1,0},{2,1},{3,2},{4,7},{5,4},{6,5},{7,6},{8,11},{9,8},{10,9... | collective-permute-start | bytes 49160 | tf_op jit(solution)/shard_map/ppermute | solution.py:273
  17.9 3.3 %collective-permute-done.1.l2 = s32[32,128]{1,0:T(8,128)S(1)} collective-permute-done((s32[32,128]{1,0:T(8,128)S(1)}, s32[32,128]{1,0:T(8,128)S(1)}, u32[]{:S(2)}, u32[]{:S(2)}) %collective-permute-start.1) | collective-permute-done | bytes 16416 | tf_op jit(solution)/shard_map/ppermute | solution.py:273
  21.4 4.3 %collective-permute-start.3 = (s32[64,128]{1,0:T(8,128)S(1)}, s32[64,128]{1,0:T(8,128)S(1)}, u32[]{:S(2)}, u32[]{:S(2)}) collective-permute-start(s32[64,128]{1,0:T(8,128)S(1)} %pad_add_fusion), channel_id=1, source_target_pairs={{0,4},{1,5},{2,6},{3,7},{4,0},{5,1},{6,2},{7,3},{8,12},{9,13},{10,... | collective-permute-start | bytes 98312 | tf_op jit(solution)/shard_map/ppermute | solution.py:270
  25.7 3.8 %collective-permute-done.3.far = s32[64,128]{1,0:T(8,128)S(1)} collective-permute-done((s32[64,128]{1,0:T(8,128)S(1)}, s32[64,128]{1,0:T(8,128)S(1)}, u32[]{:S(2)}, u32[]{:S(2)}) %collective-permute-start.3) | collective-permute-done | bytes 32800 | tf_op jit(solution)/shard_map/ppermute | solution.py:270
  29.5 2.3 %shard_map.167 = (bf16[8,256,512]{2,1,0:T(8,128)(2,1)S(1)}, s32[1]{0:T(128)}) custom-call(s32[1]{0:T(128)} %bitcast.pos, s32[32,128]{1,0:T(8,128)S(1)} %get-tuple-element.54.l0, s32[32,128]{1,0:T(8,128)S(1)} %collective-permute-done.l1, s32[32,128]{1,0:T(8,128)S(1)} %collective-permute-done.1.l2, s32[32,128]{1,0:T(8,128)S(1)} %collective-permute-done.2.l3, ...), custom_call_target="tpu_custom_call" | custom-call | flops 2147483648 | bytes 98308 | tf_op jit(solution)/shard_map/pallas_call | solution.py:45
  32.7 1.3 %shard_map.168 = (f32[256,128]{1,0:T(8,128)S(1)}, f32[256,128]{1,0:T(8,128)S(1)}, f32[256,128]{1,0:T(8,128)S(1)}, f32[256,128]{1,0:T(8,128)S(1)}, f32[256,128]{1...) custom-call(s32[1]{0:T(128)} %get-tuple-element.58.flag, s32[1]{0:T(128)} %bitcast.pos, ...), custom_call_target="tpu_custom_call" | custom-call | flops 268435456 | bytes 2981896 | tf_op jit(solution)/shard_map/pallas_call | solution.py:45
  34.1 2.1 %collective-permute-start.4 = (f32[256,128]{1,0:T(8,128)S(1)}, f32[256,128]{1,0:T(8,128)S(1)}, u32[]{:S(2)}, u32[]{:S(2)}) collective-permute-start(f32[256,128]{1,0:T(8,128)S(1)} %get-tuple-element.62), channel_id=1, source_target_pairs={{0,1},{1,2},{2,3},{3,0},{4,5},{5,6},{6,7},{7,4},{8,9},{9,10},{10,1... | collective-permute-start | bytes 393224 | tf_op jit(solution)/shard_map/ppermute | solution.py:273
  36.1 1.5 %collective-permute-start.5 = (f32[256,128]{1,0:T(8,128)S(1)}, f32[256,128]{1,0:T(8,128)S(1)}, u32[]{:S(2)}, u32[]{:S(2)}) collective-permute-start(f32[256,128]{1,0:T(8,128)S(1)} %get-tuple-element.63), channel_id=1, source_target_pairs={{0,3},{1,0},{2,1},{3,2},{4,7},{5,4},{6,5},{7,6},{8,11},{9,8},{10,9... | collective-permute-start | bytes 393224 | tf_op jit(solution)/shard_map/ppermute | solution.py:273
  37.7 1.6 %collective-permute-start.6 = (f32[256,128]{1,0:T(8,128)S(1)}, f32[256,128]{1,0:T(8,128)S(1)}, u32[]{:S(2)}, u32[]{:S(2)}) collective-permute-start(f32[256,128]{1,0:T(8,128)S(1)} %get-tuple-element.64), channel_id=1, source_target_pairs={{0,2},{1,3},{2,0},{3,1},{4,6},{5,7},{6,4},{7,5},{8,10},{9,11},{10,... | collective-permute-start | bytes 393224 | tf_op jit(solution)/shard_map/ppermute | solution.py:273
  39.2 2.3 %shard_map.166 = (bf16[256,1024]{1,0:T(8,128)(2,1)S(1)}, bf16[1024,256]{1,0:T(8,128)(2,1)S(1)}, f32[256,128]{1,0:T(8,128)S(1)}, s32[1]{0:T(128)}) custom-call(s32[48,128]{1,0:T(8,128)S(1)} %get-tuple-element.50.own_to, s32[8,128]{1,0:T(8,128)S(1)} %bitcast.15, s32[8,128]{1,0:T(8,128)S(1)} %bitcast.18, s32[2,128]{1,0:T(2,128)S(1)} %bitcast.25), custom_call_target="tpu_custom_call" | custom-call | flops 2147483648 | bytes 33792 | tf_op jit(solution)/shard_map/pallas_call | solution.py:45
  41.6 4.0 %collective-permute-done.6 = f32[256,128]{1,0:T(8,128)S(1)} collective-permute-done((f32[256,128]{1,0:T(8,128)S(1)}, f32[256,128]{1,0:T(8,128)S(1)}, u32[]{:S(2)}, u32[]{:S(2)}) %collective-permute-start.6) | collective-permute-done | bytes 131104 | tf_op jit(solution)/shard_map/ppermute | solution.py:273
  45.7 1.3 collective-permute-start.10
  47.0 4.1 %collective-permute-start.7 = (f32[256,128]{1,0:T(8,128)S(1)}, f32[256,128]{1,0:T(8,128)S(1)}, u32[]{:S(2)}, u32[]{:S(2)}) collective-permute-start(f32[256,128]{1,0:T(8,128)S(1)} %add_add_fusion), channel_id=1, source_target_pairs={{0,4},{1,5},{2,6},{3,7},{4,0},{5,1},{6,2},{7,3},{8,12},{9,13},{10,... | collective-permute-start | bytes 393224 | tf_op jit(solution)/shard_map/ppermute | solution.py:270
  51.0 1.4 %collective-permute-start.8 = (f32[256,128]{1,0:T(8,128)S(1)}, f32[256,128]{1,0:T(8,128)S(1)}, u32[]{:S(2)}, u32[]{:S(2)}) collective-permute-start(f32[256,128]{1,0:T(8,128)S(1)} %get-tuple-element.69), channel_id=1, source_target_pairs={{0,2},{1,3},{2,0},{3,1},{4,6},{5,7},{6,4},{7,5},{8,10},{9,11},{10,... | collective-permute-start | bytes 393224 | tf_op jit(solution)/shard_map/ppermute | solution.py:273
  52.4 1.6 %shard_map.170.bwd = bf16[8,512,256]{2,1,0:T(8,128)(2,1)S(1)} custom-call(s32[1]{0:T(128)} %bitcast.pos, s32[32,128]{1,0:T(8,128)S(1)} %get-tuple-element.54.l0, s32[32,128]{1,0:T(8,128)S(1)} %collective-permute-done.l1, s32[32,128]{1,0:T(8,128)S(1)} %collective-permute-done.1.l2, s32[32,128]{1,0:T(8,128)S(1)} %copy-done.16, ...), custom_call_target="tpu_custom_call" | custom-call | flops 2147483648 | bytes 98308 | tf_op jit(solution)/shard_map/pallas_call | solution.py:45
  55.0 1.7 %collective-permute-done.8.a2 = f32[256,128]{1,0:T(8,128)S(1)} collective-permute-done((f32[256,128]{1,0:T(8,128)S(1)}, f32[256,128]{1,0:T(8,128)S(1)}, u32[]{:S(2)}, u32[]{:S(2)}) %collective-permute-start.8) | collective-permute-done | bytes 131104 | tf_op jit(solution)/shard_map/ppermute | solution.py:273
  56.6 3.0 %collective-permute-done.9.a3 = f32[256,128]{1,0:T(8,128)S(1)} collective-permute-done((f32[256,128]{1,0:T(8,128)S(1)}, f32[256,128]{1,0:T(8,128)S(1)}, u32[]{:S(2)}, u32[]{:S(2)}) %collective-permute-start.9) | collective-permute-done | bytes 131104 | tf_op jit(solution)/shard_map/ppermute | solution.py:273
  62.7 6.0 %all-to-all-start.1 = ((f32[32,16,128]{2,1,0:T(8,128)}), f32[32,16,128]{2,1,0:T(8,128)S(1)}, u32[]{:S(2)}, u32[]{:S(2)}) async-start(f32[32,16,128]{2,1,0:T(8,128)} %shard_map.172), calls=%async_computation.1 | async-start | bytes 524288 | tf_op jit(solution)/shard_map/all_to_all | solution.py:276
  68.6 2.4 %collective-permute-start.11 = (f32[256,128]{1,0:T(8,128)S(1)}, f32[256,128]{1,0:T(8,128)}, u32[]{:S(2)}, u32[]{:S(2)}) collective-permute-start(f32[256,128]{1,0:T(8,128)S(1)} %get-tuple-element.75.grad_sum.g0), channel_id=1, source_target_pairs={{0,4},{1,5},{2,6},{3,7},{4,0},{5,1},{6,2},{7,3},{8,12},{9,13},{10,... | collective-permute-start | bytes 393224 | tf_op jit(solution)/shard_map/ppermute | solution.py:270
  73.9 2.0 %shard_map.173 = f32[1024,128]{1,0:T(8,128)} custom-call(s32[1]{0:T(128)} %get-tuple-element.51.flag, s32[8,128]{1,0:T(8,128)S(1)} %bitcast.17, s32[8,128]{1,0:T(8,128)S(1)} %bitcast.20, f32[256,128]{1,0:T(8,128)S(1)} %get-tuple-element.75.grad_sum.g0, bf16[1024,256]{1,0:T(8,128)(2,1)S(1)} %get-tuple-element.78.h_bwd), custom_call_target="tpu_custom_call" | custom-call | flops 268435456 | bytes 663556 | tf_op jit(solution)/shard_map/pallas_call | solution.py:45
  75.9 4.0 %collective-permute-done.11.g4 = f32[256,128]{1,0:T(8,128)} collective-permute-done((f32[256,128]{1,0:T(8,128)S(1)}, f32[256,128]{1,0:T(8,128)}, u32[]{:S(2)}, u32[]{:S(2)}) %collective-permute-start.11) | collective-permute-done | bytes 131104 | tf_op jit(solution)/shard_map/ppermute | solution.py:270
  81.9 3.5 %all-to-all-done.1.weights = f32[32,16,128]{2,1,0:T(8,128)S(1)} async-done(((f32[32,16,128]{2,1,0:T(8,128)}), f32[32,16,128]{2,1,0:T(8,128)S(1)}, u32[]{:S(2)}, u32[]{:S(2)}) %all-to-all-start.1) | async-done | bytes 262176 | tf_op jit(solution)/shard_map/all_to_all | solution.py:276
  86.1 6.8 %all-to-all-start.3 = ((f32[32,32,128]{2,1,0:T(8,128)}), f32[32,32,128]{2,1,0:T(8,128)S(1)}, u32[]{:S(2)}, u32[]{:S(2)}) async-start(f32[32,32,128]{2,1,0:T(8,128)} %bitcast.11), calls=%async_computation.3 | async-start | bytes 1048576 | tf_op jit(solution)/shard_map/all_to_all | solution.py:276
  93.9 1.5 %collective-permute-start.19 = (f32[16,128]{1,0:T(8,128)S(1)}, f32[16,128]{1,0:T(8,128)S(1)}, u32[]{:S(2)}, u32[]{:S(2)}) collective-permute-start(f32[16,128]{1,0:T(8,128)S(1)} %shard_map.175), channel_id=1, source_target_pairs={{0,2},{1,3},{2,0},{3,1},{4,6},{5,7},{6,4},{7,5},{8,10},{9,11},{10,... | collective-permute-start | bytes 24584 | tf_op jit(solution)/shard_map/ppermute | solution.py:273
  97.3 1.7 %collective-permute-start.16 = (f32[256,128]{1,0:T(8,128)}, f32[256,128]{1,0:T(8,128)S(1)}, u32[]{:S(2)}, u32[]{:S(2)}) collective-permute-start(f32[256,128]{1,0:T(8,128)} %collective-permute-done.11.g4), channel_id=1, source_target_pairs={{0,2},{1,3},{2,0},{3,1},{4,6},{5,7},{6,4},{7,5},{8,10},{9,11},{10,... | collective-permute-start | bytes 393224 | tf_op jit(solution)/shard_map/ppermute | solution.py:273
  99.8 3.1 %collective-permute-start.21 = (f32[16,128]{1,0:T(8,128)S(1)}, f32[16,128]{1,0:T(8,128)S(1)}, u32[]{:S(2)}, u32[]{:S(2)}) collective-permute-start(f32[16,128]{1,0:T(8,128)S(1)} %add_add_fusion.1.near), channel_id=1, source_target_pairs={{0,4},{1,5},{2,6},{3,7},{4,0},{5,1},{6,2},{7,3},{8,12},{9,13},{10,... | collective-permute-start | bytes 24584 | tf_op jit(solution)/shard_map/ppermute | solution.py:270
  103.1 3.2 %collective-permute-done.17.g7 = f32[256,128]{1,0:T(8,128)S(1)} collective-permute-done((f32[256,128]{1,0:T(8,128)}, f32[256,128]{1,0:T(8,128)S(1)}, u32[]{:S(2)}, u32[]{:S(2)}) %collective-permute-start.17) | collective-permute-done | bytes 131104 | tf_op jit(solution)/shard_map/ppermute | solution.py:273
  107.0 2.3 %shard_map.174 = (f32[256,128]{1,0:T(8,128)S(1)}, f32[32,8,128]{2,1,0:T(8,128)S(1)}) custom-call(s32[1]{0:T(128)} %get-tuple-element.58.flag, s32[1]{0:T(128)} %bitcast.pos, s32[32,128]{1,0:T(8,128)S(1)} %get-tuple-element.54.l0, s32[32,128]{1,0:T(8,128)S(1)} %collective-permute-done.l1, s32[32,128]{1,0:T(8,128)S(1)} %collective-permute-done.1.l2, ...), custom_call_target="tpu_custom_call" | custom-call | flops 268435456 | bytes 3244040 | tf_op jit(solution)/shard_map/pallas_call | solution.py:45
  110.7 8.8 %all-to-all-start.2 = ((f32[32,16,128]{2,1,0:T(8,128)}), f32[32,16,128]{2,1,0:T(8,128)S(1)}, u32[]{:S(2)}, u32[]{:S(2)}) async-start(f32[32,16,128]{2,1,0:T(8,128)} %get-tuple-element.86), calls=%async_computation.2 | async-start | bytes 524288 | tf_op jit(solution)/shard_map/all_to_all | solution.py:276
  121.6 9.0 %all-to-all-done.2.last = f32[32,16,128]{2,1,0:T(8,128)S(1)} async-done(((f32[32,16,128]{2,1,0:T(8,128)}), f32[32,16,128]{2,1,0:T(8,128)S(1)}, u32[]{:S(2)}, u32[]{:S(2)}) %all-to-all-start.2) | async-done | bytes 262176 | tf_op jit(solution)/shard_map/all_to_all | solution.py:276
  (107 shorter events, 22.6 us)
Async XLA Ops:
  3.0 29.7 %all-to-all-start = ((f32[32,40,128]{2,1,0:T(8,128)}), f32[32,40,128]{2,1,0:T(8,128)S(1)}, u32[]{:S(2)}, u32[]{:S(2)}) async-start(f32[32,40,128]{2,1,0:T(8,128)} %shard_map.164), calls=%async_computation | async-start | bytes 1310720 | tf_op jit(solution)/shard_map/all_to_all | solution.py:276
  14.0 3.9 %collective-permute-start = (s32[32,128]{1,0:T(8,128)S(1)}, s32[32,128]{1,0:T(8,128)S(1)}, u32[]{:S(2)}, u32[]{:S(2)}) collective-permute-start(s32[32,128]{1,0:T(8,128)S(1)} %get-tuple-element.55), channel_id=1, source_target_pairs={{0,3},{1,0},{2,1},{3,2},{4,7},{5,4},{6,5},{7,6},{8,11},{9,8},{10,9... | collective-permute-start | bytes 49160 | tf_op jit(solution)/shard_map/ppermute | solution.py:273
  16.8 4.4 %collective-permute-start.1 = (s32[32,128]{1,0:T(8,128)S(1)}, s32[32,128]{1,0:T(8,128)S(1)}, u32[]{:S(2)}, u32[]{:S(2)}) collective-permute-start(s32[32,128]{1,0:T(8,128)S(1)} %get-tuple-element.56), channel_id=1, source_target_pairs={{0,2},{1,3},{2,0},{3,1},{4,6},{5,7},{6,4},{7,5},{8,10},{9,11},{10,... | collective-permute-start | bytes 49160 | tf_op jit(solution)/shard_map/ppermute | solution.py:273
  17.2 4.2 %collective-permute-start.2 = (s32[32,128]{1,0:T(8,128)S(1)}, s32[32,128]{1,0:T(8,128)S(1)}, u32[]{:S(2)}, u32[]{:S(2)}) collective-permute-start(s32[32,128]{1,0:T(8,128)S(1)} %get-tuple-element.57), channel_id=1, source_target_pairs={{0,1},{1,2},{2,3},{3,0},{4,5},{5,6},{6,7},{7,4},{8,9},{9,10},{10,1... | collective-permute-start | bytes 49160 | tf_op jit(solution)/shard_map/ppermute | solution.py:273
  21.4 8.1 %collective-permute-start.3 = (s32[64,128]{1,0:T(8,128)S(1)}, s32[64,128]{1,0:T(8,128)S(1)}, u32[]{:S(2)}, u32[]{:S(2)}) collective-permute-start(s32[64,128]{1,0:T(8,128)S(1)} %pad_add_fusion), channel_id=1, source_target_pairs={{0,4},{1,5},{2,6},{3,7},{4,0},{5,1},{6,2},{7,3},{8,12},{9,13},{10,... | collective-permute-start | bytes 98312 | tf_op jit(solution)/shard_map/ppermute | solution.py:270
  34.1 7.5 %collective-permute-start.4 = (f32[256,128]{1,0:T(8,128)S(1)}, f32[256,128]{1,0:T(8,128)S(1)}, u32[]{:S(2)}, u32[]{:S(2)}) collective-permute-start(f32[256,128]{1,0:T(8,128)S(1)} %get-tuple-element.62), channel_id=1, source_target_pairs={{0,1},{1,2},{2,3},{3,0},{4,5},{5,6},{6,7},{7,4},{8,9},{9,10},{10,1... | collective-permute-start | bytes 393224 | tf_op jit(solution)/shard_map/ppermute | solution.py:273
  36.1 5.5 %collective-permute-start.5 = (f32[256,128]{1,0:T(8,128)S(1)}, f32[256,128]{1,0:T(8,128)S(1)}, u32[]{:S(2)}, u32[]{:S(2)}) collective-permute-start(f32[256,128]{1,0:T(8,128)S(1)} %get-tuple-element.63), channel_id=1, source_target_pairs={{0,3},{1,0},{2,1},{3,2},{4,7},{5,4},{6,5},{7,6},{8,11},{9,8},{10,9... | collective-permute-start | bytes 393224 | tf_op jit(solution)/shard_map/ppermute | solution.py:273
  37.7 7.9 %collective-permute-start.6 = (f32[256,128]{1,0:T(8,128)S(1)}, f32[256,128]{1,0:T(8,128)S(1)}, u32[]{:S(2)}, u32[]{:S(2)}) collective-permute-start(f32[256,128]{1,0:T(8,128)S(1)} %get-tuple-element.64), channel_id=1, source_target_pairs={{0,2},{1,3},{2,0},{3,1},{4,6},{5,7},{6,4},{7,5},{8,10},{9,11},{10,... | collective-permute-start | bytes 393224 | tf_op jit(solution)/shard_map/ppermute | solution.py:273
  45.7 14.0 %copy-start.3 = (f32[128,128]{1,0:T(8,128)S(1)}, f32[128,128]{1,0:T(8,128)}, u32[]{:S(2)}) copy-start(f32[128,128]{1,0:T(8,128)} %w_root.3) | copy-start | bytes 196612
  45.7 14.0 %copy-start.4 = (f32[256,128]{1,0:T(8,128)S(1)}, f32[256,128]{1,0:T(8,128)}, u32[]{:S(2)}) copy-start(f32[256,128]{1,0:T(8,128)} %grad_out.1) | copy-start | bytes 393220
  45.7 9.2 %collective-permute-start.10 = (f32[256,128]{1,0:T(8,128)S(1)}, f32[256,128]{1,0:T(8,128)S(1)}, u32[]{:S(2)}, u32[]{:S(2)}) collective-permute-start(f32[256,128]{1,0:T(8,128)S(1)} %get-tuple-element.71), channel_id=1, source_target_pairs={{0,3},{1,0},{2,1},{3,2},{4,7},{5,4},{6,5},{7,6},{8,11},{9,8},{10,9... | collective-permute-start | bytes 393224 | tf_op jit(solution)/shard_map/ppermute | solution.py:273
  47.0 8.0 %collective-permute-start.7 = (f32[256,128]{1,0:T(8,128)S(1)}, f32[256,128]{1,0:T(8,128)S(1)}, u32[]{:S(2)}, u32[]{:S(2)}) collective-permute-start(f32[256,128]{1,0:T(8,128)S(1)} %add_add_fusion), channel_id=1, source_target_pairs={{0,4},{1,5},{2,6},{3,7},{4,0},{5,1},{6,2},{7,3},{8,12},{9,13},{10,... | collective-permute-start | bytes 393224 | tf_op jit(solution)/shard_map/ppermute | solution.py:270
  51.0 5.6 %collective-permute-start.8 = (f32[256,128]{1,0:T(8,128)S(1)}, f32[256,128]{1,0:T(8,128)S(1)}, u32[]{:S(2)}, u32[]{:S(2)}) collective-permute-start(f32[256,128]{1,0:T(8,128)S(1)} %get-tuple-element.69), channel_id=1, source_target_pairs={{0,2},{1,3},{2,0},{3,1},{4,6},{5,7},{6,4},{7,5},{8,10},{9,11},{10,... | collective-permute-start | bytes 393224 | tf_op jit(solution)/shard_map/ppermute | solution.py:273
  52.4 7.3 %collective-permute-start.9 = (f32[256,128]{1,0:T(8,128)S(1)}, f32[256,128]{1,0:T(8,128)S(1)}, u32[]{:S(2)}, u32[]{:S(2)}) collective-permute-start(f32[256,128]{1,0:T(8,128)S(1)} %get-tuple-element.70), channel_id=1, source_target_pairs={{0,1},{1,2},{2,3},{3,0},{4,5},{5,6},{6,7},{7,4},{8,9},{9,10},{10,1... | collective-permute-start | bytes 393224 | tf_op jit(solution)/shard_map/ppermute | solution.py:273
  62.7 22.7 %all-to-all-start.1 = ((f32[32,16,128]{2,1,0:T(8,128)}), f32[32,16,128]{2,1,0:T(8,128)S(1)}, u32[]{:S(2)}, u32[]{:S(2)}) async-start(f32[32,16,128]{2,1,0:T(8,128)} %shard_map.172), calls=%async_computation.1 | async-start | bytes 524288 | tf_op jit(solution)/shard_map/all_to_all | solution.py:276
  68.6 11.3 %collective-permute-start.11 = (f32[256,128]{1,0:T(8,128)S(1)}, f32[256,128]{1,0:T(8,128)}, u32[]{:S(2)}, u32[]{:S(2)}) collective-permute-start(f32[256,128]{1,0:T(8,128)S(1)} %get-tuple-element.75.grad_sum.g0), channel_id=1, source_target_pairs={{0,4},{1,5},{2,6},{3,7},{4,0},{5,1},{6,2},{7,3},{8,12},{9,13},{10,... | collective-permute-start | bytes 393224 | tf_op jit(solution)/shard_map/ppermute | solution.py:270
  71.1 8.8 %collective-permute-start.12 = (f32[256,128]{1,0:T(8,128)S(1)}, f32[256,128]{1,0:T(8,128)S(1)}, u32[]{:S(2)}, u32[]{:S(2)}) collective-permute-start(f32[256,128]{1,0:T(8,128)S(1)} %get-tuple-element.75.grad_sum.g0), channel_id=1, source_target_pairs={{0,3},{1,0},{2,1},{3,2},{4,7},{5,4},{6,5},{7,6},{8,11},{9,8},{10,9... | collective-permute-start | bytes 393224 | tf_op jit(solution)/shard_map/ppermute | solution.py:273
  71.4 9.2 %collective-permute-start.13 = (f32[256,128]{1,0:T(8,128)S(1)}, f32[256,128]{1,0:T(8,128)S(1)}, u32[]{:S(2)}, u32[]{:S(2)}) collective-permute-start(f32[256,128]{1,0:T(8,128)S(1)} %get-tuple-element.75.grad_sum.g0), channel_id=1, source_target_pairs={{0,2},{1,3},{2,0},{3,1},{4,6},{5,7},{6,4},{7,5},{8,10},{9,11},{10,... | collective-permute-start | bytes 393224 | tf_op jit(solution)/shard_map/ppermute | solution.py:273
  72.4 8.8 %collective-permute-start.14 = (f32[256,128]{1,0:T(8,128)S(1)}, f32[256,128]{1,0:T(8,128)S(1)}, u32[]{:S(2)}, u32[]{:S(2)}) collective-permute-start(f32[256,128]{1,0:T(8,128)S(1)} %get-tuple-element.75.grad_sum.g0), channel_id=1, source_target_pairs={{0,1},{1,2},{2,3},{3,0},{4,5},{5,6},{6,7},{7,4},{8,9},{9,10},{10,1... | collective-permute-start | bytes 393224 | tf_op jit(solution)/shard_map/ppermute | solution.py:273
  81.2 25.0 %copy-start.8 = (f32[256,128]{1,0:T(8,128)S(1)}, f32[256,128]{1,0:T(8,128)}, u32[]{:S(2)}) copy-start(f32[256,128]{1,0:T(8,128)} %copy-done.7) | copy-start | bytes 393220
  81.9 24.4 %copy-start.10 = (f32[256,128]{1,0:T(8,128)S(1)}, f32[256,128]{1,0:T(8,128)}, u32[]{:S(2)}) copy-start(f32[256,128]{1,0:T(8,128)} %copy-done.9) | copy-start | bytes 393220
  86.1 20.2 %copy-start.12 = (f32[256,128]{1,0:T(8,128)S(1)}, f32[256,128]{1,0:T(8,128)}, u32[]{:S(2)}) copy-start(f32[256,128]{1,0:T(8,128)} %copy-done.11) | copy-start | bytes 393220
  86.1 24.6 %all-to-all-start.3 = ((f32[32,32,128]{2,1,0:T(8,128)}), f32[32,32,128]{2,1,0:T(8,128)S(1)}, u32[]{:S(2)}, u32[]{:S(2)}) async-start(f32[32,32,128]{2,1,0:T(8,128)} %bitcast.11), calls=%async_computation.3 | async-start | bytes 1048576 | tf_op jit(solution)/shard_map/all_to_all | solution.py:276
  93.8 5.2 %collective-permute-start.18 = (f32[16,128]{1,0:T(8,128)S(1)}, f32[16,128]{1,0:T(8,128)S(1)}, u32[]{:S(2)}, u32[]{:S(2)}) collective-permute-start(f32[16,128]{1,0:T(8,128)S(1)} %shard_map.175), channel_id=1, source_target_pairs={{0,1},{1,2},{2,3},{3,0},{4,5},{5,6},{6,7},{7,4},{8,9},{9,10},{10,1... | collective-permute-start | bytes 24584 | tf_op jit(solution)/shard_map/ppermute | solution.py:273
  93.9 5.9 %collective-permute-start.19 = (f32[16,128]{1,0:T(8,128)S(1)}, f32[16,128]{1,0:T(8,128)S(1)}, u32[]{:S(2)}, u32[]{:S(2)}) collective-permute-start(f32[16,128]{1,0:T(8,128)S(1)} %shard_map.175), channel_id=1, source_target_pairs={{0,2},{1,3},{2,0},{3,1},{4,6},{5,7},{6,4},{7,5},{8,10},{9,11},{10,... | collective-permute-start | bytes 24584 | tf_op jit(solution)/shard_map/ppermute | solution.py:273
  95.4 4.4 %collective-permute-start.20 = (f32[16,128]{1,0:T(8,128)S(1)}, f32[16,128]{1,0:T(8,128)S(1)}, u32[]{:S(2)}, u32[]{:S(2)}) collective-permute-start(f32[16,128]{1,0:T(8,128)S(1)} %shard_map.175), channel_id=1, source_target_pairs={{0,3},{1,0},{2,1},{3,2},{4,7},{5,4},{6,5},{7,6},{8,11},{9,8},{10,9... | collective-permute-start | bytes 24584 | tf_op jit(solution)/shard_map/ppermute | solution.py:273
  96.6 6.4 %collective-permute-start.15 = (f32[256,128]{1,0:T(8,128)}, f32[256,128]{1,0:T(8,128)S(1)}, u32[]{:S(2)}, u32[]{:S(2)}) collective-permute-start(f32[256,128]{1,0:T(8,128)} %collective-permute-done.11.g4), channel_id=1, source_target_pairs={{0,3},{1,0},{2,1},{3,2},{4,7},{5,4},{6,5},{7,6},{8,11},{9,8},{10,9... | collective-permute-start | bytes 393224 | tf_op jit(solution)/shard_map/ppermute | solution.py:273
  97.3 5.8 %collective-permute-start.16 = (f32[256,128]{1,0:T(8,128)}, f32[256,128]{1,0:T(8,128)S(1)}, u32[]{:S(2)}, u32[]{:S(2)}) collective-permute-start(f32[256,128]{1,0:T(8,128)} %collective-permute-done.11.g4), channel_id=1, source_target_pairs={{0,2},{1,3},{2,0},{3,1},{4,6},{5,7},{6,4},{7,5},{8,10},{9,11},{10,... | collective-permute-start | bytes 393224 | tf_op jit(solution)/shard_map/ppermute | solution.py:273
  99.0 7.3 %collective-permute-start.17 = (f32[256,128]{1,0:T(8,128)}, f32[256,128]{1,0:T(8,128)S(1)}, u32[]{:S(2)}, u32[]{:S(2)}) collective-permute-start(f32[256,128]{1,0:T(8,128)} %collective-permute-done.11.g4), channel_id=1, source_target_pairs={{0,1},{1,2},{2,3},{3,0},{4,5},{5,6},{6,7},{7,4},{8,9},{9,10},{10,1... | collective-permute-start | bytes 393224 | tf_op jit(solution)/shard_map/ppermute | solution.py:273
  99.8 19.7 %copy-start.6 = (f32[256,128]{1,0:T(8,128)S(1)}, f32[256,128]{1,0:T(8,128)}, u32[]{:S(2)}) copy-start(f32[256,128]{1,0:T(8,128)} %copy-done.5) | copy-start | bytes 393220
  99.8 10.1 %collective-permute-start.21 = (f32[16,128]{1,0:T(8,128)S(1)}, f32[16,128]{1,0:T(8,128)S(1)}, u32[]{:S(2)}, u32[]{:S(2)}) collective-permute-start(f32[16,128]{1,0:T(8,128)S(1)} %add_add_fusion.1.near), channel_id=1, source_target_pairs={{0,4},{1,5},{2,6},{3,7},{4,0},{5,1},{6,2},{7,3},{8,12},{9,13},{10,... | collective-permute-start | bytes 24584 | tf_op jit(solution)/shard_map/ppermute | solution.py:270
  110.7 19.9 %all-to-all-start.2 = ((f32[32,16,128]{2,1,0:T(8,128)}), f32[32,16,128]{2,1,0:T(8,128)S(1)}, u32[]{:S(2)}, u32[]{:S(2)}) async-start(f32[32,16,128]{2,1,0:T(8,128)} %get-tuple-element.86), calls=%async_computation.2 | async-start | bytes 524288 | tf_op jit(solution)/shard_map/all_to_all | solution.py:276
  (26 other events, 154.5 us)
